TPU v7x, 32 devices: a whole 2x2x4 slice. The times are simulated.
32 devices in a mesh: gx: 4 (over x, core), gy: 8 (over z, y).
Axes of the slice: x: 2, y: 2, z: 4, core: 2. Of those that a mesh axis runs over, the one named last changes fastest.
Arguments:
- particles: float32 [16, 262144], P(None, ('gx', 'gy')), may hold values from -10 to 10
- migrant_index: int32 [128, 512], P(('gx', 'gy')), may hold values from 0 to 8191, as said below
- migrant_count: int32 [32, 4], P(('gx', 'gy')), may hold values from 170 to 512, as said below
- migrated_slot_cell: int32 [327680], P(('gx', 'gy')), may hold values from 0 to 12287
- source_tile_size: int32 [32, 256], P(('gx', 'gy')), may hold values from 1 to 64, 12288 in all within a row
- tile_owner: int32 [8192, 1], P(('gx', 'gy')), may hold values from 0 to 31; in each aligned block of 256 rows (0 to 255, 256 to 511, ...) at most 16 rows name the same one
- tile_offset: int32 [8192], P(('gx', 'gy')), may hold values from 0 to 8128, as said below
- closure: float32 [8, 16], replicated, may hold values from -1.5 to 1.5
- damping: float32 [8], replicated, may hold values from 0.5 to 1.5
Outputs:
- drag_field: bfloat16 [8, 32, 64, 128], P(None, 'gx', 'gy')
- particle_force: float32 [8, 327680], P(None, ('gx', 'gy'))
Inputs may be any that keep to these rules, and one draw needn't show every extreme that they name: `migrant_index`: on each device the first migrant_count entries of its four rows name distinct particles of that device. `migrant_count`: some device's count reaches 512. `source_tile_size`: the sizes of one device sum to 12288. `tile_owner`: among the tiles of one device no owner is named more than 16 times, a bound that some block reaches. Every tile lies in one vertical column of its owner's block: tile_offset % 128 + 64 <= 128.
All inputs are finite; a program needn't handle non-finite values.
Results may differ from a plain program's by a relative error of at most 0.0053.
Values may be sent and summed in bfloat16 or wider, within the bound.
No kernel may reach another device: no remote copies, remote signals or barrier semaphores. Data moves between devices by JAX's collectives and lax.ppermute only.
A program may use at most 64 MiB of HBM per device.

v0:
```python
import functools

import jax
import jax.numpy as jnp
from jax import lax
from jax.experimental import pallas as pl
from jax.experimental.pallas import tpu as pltpu
from jax.sharding import PartitionSpec as P

TILE = 64
FX = 8
FY = 8
FZ = 128
COLS = FX * FY
LANES = 128
GROUP = 256
CHUNK = 1024
VMEM = 48 * 1024 * 1024

NT = (((1,), (1,)), ((), ()))
TN = (((0,), (0,)), ((), ()))


def iota(shape, dim):
    return lax.broadcasted_iota(jnp.int32, shape, dim)


def dot(a, b, dims=(((1,), (0,)), ((), ()))):
    return lax.dot_general(a, b, dims, preferred_element_type=jnp.float32)


def one_hot(mask):
    return jnp.where(mask, 1.0, 0.0).astype(jnp.bfloat16)


def pick_kernel(part_ref, index_ref, count_ref, *out_refs):
    channels, parts = part_ref.shape
    migr = index_ref.shape[1]
    groups = parts // GROUP
    table = jnp.concatenate(
        [part_ref[:, g * GROUP : (g + 1) * GROUP].astype(jnp.bfloat16) for g in range(groups)], axis=0
    )
    for row in range(4):
        index = index_ref[row : row + 1, :]
        count = count_ref[0, row]
        low = one_hot(iota((GROUP, migr), 0) == index % GROUP)
        rows = dot(table, low)
        high = index // GROUP
        high = jnp.where(iota((1, migr), 1) < count, high, groups)
        picked = jnp.zeros((channels, migr), jnp.float32)
        for g in range(groups):
            picked = picked + jnp.where(high == g, rows[g * channels : (g + 1) * channels], 0.0)
        out_refs[row][:, :migr] = picked.astype(jnp.bfloat16)
        digits = jnp.where(iota((channels, LANES), 0) == 0, count // GROUP, count % GROUP)
        out_refs[row][:, migr:] = digits.astype(jnp.float32).astype(jnp.bfloat16)


def mix(closure_ref, state):
    state = state.astype(jnp.float32)
    mixed = closure_ref[:, 0:1] * state[0:1]
    for f in range(1, state.shape[0]):
        mixed = mixed + closure_ref[:, f : f + 1] * state[f : f + 1]
    return mixed, state[0:1]


def spread(mixed, first, place, width):
    hit = iota((TILE, width), 0) == place
    rows = [
        jnp.where(hit, mixed[r : r + 1], 0.0).astype(jnp.bfloat16) for r in range(mixed.shape[0])
    ]
    rows.append(jnp.where(hit, first, 0.0).astype(jnp.bfloat16))
    return jnp.concatenate(rows, axis=0)


def deposit_kernel(
    capacity, part_ref, index_ref, count_ref, cell_ref, size_ref, owner_ref, offset_ref, closure_ref,
    sum_ref, live_ref, code_ref, slot_ref, columns_ref,
):
    channels, parts = part_ref.shape
    migr = index_ref.shape[1]
    slots = cell_ref.shape[1]
    tiles = size_ref.shape[1]
    groups = parts // GROUP

    square = (tiles, tiles)
    below, across = iota(square, 0), iota(square, 1)
    same = below == across

    def column(row):
        return jnp.sum(jnp.where(same, row, 0), axis=1, keepdims=True)

    sizes = size_ref[...]
    owners = owner_ref[...]
    start = jnp.sum(jnp.where(across < below, sizes, 0), axis=1, keepdims=True)
    end = start + column(sizes)
    height = column(offset_ref[...] % FZ)
    code = iota((tiles, 1), 0) * TILE + (height - start) % TILE
    earlier = (column(owners) == owners) & (below < across)
    rank = jnp.sum(jnp.where(earlier, 1, 0), axis=0, keepdims=True)
    slot_ref[...] = owners * capacity + rank
    columns_ref[0] = jnp.broadcast_to(start, (tiles, LANES))
    columns_ref[1] = jnp.broadcast_to(end, (tiles, LANES))
    columns_ref[2] = jnp.broadcast_to(code, (tiles, LANES))

    hits = jnp.zeros((groups, GROUP), jnp.float32)
    for row in range(4):
        index = index_ref[row : row + 1, :]
        valid = iota((1, migr), 1) < count_ref[0, row]
        high = one_hot(iota((groups, migr), 0) == jnp.where(valid, index // GROUP, groups))
        low = one_hot(iota((GROUP, migr), 0) == index % GROUP)
        hits = hits + dot(high, low, NT)
    for g in range(groups):
        live_ref[:, g * GROUP : (g + 1) * GROUP] = 1.0 - hits[g : g + 1]

    def member(cell):
        def wide(k):
            return jnp.concatenate([columns_ref[k]] * (CHUNK // LANES), axis=1)

        inside = (cell >= wide(0)) & (cell < wide(1))
        found = jnp.sum(jnp.where(inside, wide(2), 0), axis=0, keepdims=True)
        place = (found + cell) % TILE
        return inside, found // TILE * TILE + place, place

    sum_ref[...] = jnp.zeros_like(sum_ref)

    @pl.loop(0, parts // CHUNK)
    def _(step):
        where = pl.ds(pl.multiple_of(step * CHUNK, CHUNK), CHUNK)
        inside, full, place = member(cell_ref[:, where])
        code_ref[:, where] = full
        state = (part_ref[:, where] * live_ref[:, where]).astype(jnp.bfloat16)
        mixed, first = mix(closure_ref, state)
        sum_ref[...] += dot(spread(mixed, first, place, CHUNK), one_hot(inside), NT)

    @pl.loop(parts // CHUNK, slots // CHUNK)
    def _(step):
        where = pl.ds(pl.multiple_of(step * CHUNK, CHUNK), CHUNK)
        _, full, _ = member(cell_ref[:, where])
        code_ref[:, where] = full


def pack_kernel(sum_ref, code_ref, slot_ref, offset_ref, closure_ref, *refs):
    state_refs, out_ref = refs[:4], refs[4]
    tiles = slot_ref.shape[1]
    migr = code_ref.shape[1] // 4
    total = sum_ref[...]
    for row in range(4):
        code = code_ref[:, row * migr : (row + 1) * migr]
        inside = iota((tiles, migr), 0) == code // TILE
        mixed, first = mix(closure_ref, state_refs[row][:, :migr])
        total = total + dot(spread(mixed, first, code % TILE, migr), one_hot(inside), NT)
    offset = offset_ref[...]
    spare = out_ref.shape[1] - total.shape[0]
    rows = iota((spare, tiles), 0)
    marks = jnp.where(rows == 0, offset // FZ, jnp.where(rows == 1, offset % FZ, 0))
    table = jnp.concatenate(
        [total.astype(jnp.bfloat16), marks.astype(jnp.float32).astype(jnp.bfloat16)], axis=0
    )
    match = one_hot(iota((out_ref.shape[0], tiles), 0) == slot_ref[...])
    out_ref[...] = dot(match, table, NT).astype(jnp.bfloat16)


def place_kernel(tile_ref, gas_ref, xlow_ref, xhigh_ref, ylow_ref, yhigh_ref):
    count, lanes = tile_ref.shape
    width = gas_ref.shape[1] // 2
    marks = tile_ref[:, lanes - LANES :].astype(jnp.float32)
    column = marks[:, width % LANES : width % LANES + 1]
    height = marks[:, width % LANES + 1 : width % LANES + 2]
    lane = iota((1, LANES), 1)
    target = jnp.where(
        lane < COLS,
        lane,
        jnp.where(
            lane < COLS + FX,
            (lane - COLS) * FY,
            jnp.where(lane < COLS + 2 * FX, (lane - COLS - FX) * FY + FY - 1, -1),
        ),
    )
    hot = one_hot(column == target.astype(jnp.float32))
    place = (iota((1, width), 1) % TILE).astype(jnp.float32)
    values = tile_ref[:, :width].astype(jnp.float32)
    for half, mask in enumerate((place >= height, place < height)):
        total = dot(hot, jnp.where(mask, values, 0.0).astype(jnp.bfloat16), TN)
        where = slice(half * width, (half + 1) * width)
        gas_ref[:, where] = total[:COLS]
        xlow_ref[:, where] = total[:FY]
        xhigh_ref[:, where] = total[COLS - FY : COLS]
        ylow_ref[:, where] = total[COLS : COLS + FX]
        yhigh_ref[:, where] = total[COLS + FX : COLS + 2 * FX]


def drag_kernel(mark_ref, gas_ref, xm_ref, xp_ref, ym_ref, yp_ref, drag_ref, back_ref):
    rows = drag_ref.shape[0]
    width = gas_ref.shape[1] // 2
    lanes = rows * TILE
    blocks = [xm_ref[...]] + [gas_ref[x * FY : (x + 1) * FY, :] for x in range(FX)] + [xp_ref[...]]
    along = [blocks[x] + 2.0 * blocks[x + 1] + blocks[x + 2] for x in range(FX)]

    def edge(ref):
        return ref[0:FX, :] + 2.0 * ref[1 : FX + 1, :] + ref[2 : FX + 2, :]

    before, after = edge(ym_ref), edge(yp_ref)
    smooth = []
    for x in range(FX):
        padded = jnp.concatenate([before[x : x + 1], along[x], after[x : x + 1]], axis=0)
        smooth.append((padded[0:FY] + 2.0 * padded[1 : FY + 1] + padded[2 : FY + 2]) / 16.0)
    smooth = jnp.concatenate(smooth, axis=0)
    halves = []
    for half in range(2):
        base = half * width
        density = smooth[:, base + lanes : base + lanes + TILE]
        below = 1.0 + density * density
        below = jnp.concatenate([below] * rows, axis=1)
        halves.append(smooth[:, base : base + lanes] / below)
    for r in range(rows):
        where = slice(r * TILE, (r + 1) * TILE)
        both = jnp.concatenate([halves[0][:, where], halves[1][:, where]], axis=1)
        drag_ref[r] = both.reshape(FX, FY, FZ).astype(jnp.bfloat16)
    mark = width % LANES
    marks = mark_ref[...].astype(jnp.float32)
    column, height = marks[:, mark : mark + 1], marks[:, mark + 1 : mark + 2]
    hot = one_hot(column == iota((1, COLS), 1).astype(jnp.float32))
    place = (iota((1, lanes), 1) % TILE).astype(jnp.float32)
    low = dot(hot, halves[0].astype(jnp.bfloat16))
    high = dot(hot, halves[1].astype(jnp.bfloat16))
    back_ref[...] = jnp.where(place >= height, low, high).astype(jnp.bfloat16)


def force_kernel(back_ref, slot_ref, code_ref, live_ref, part_ref, damping_ref, *refs):
    state_refs, out_ref, table_ref = refs[:4], refs[4], refs[5]
    rows, slots = out_ref.shape
    parts = part_ref.shape[1]
    tiles = slot_ref.shape[1]
    migr = (slots - parts) // 4
    match = one_hot(iota((back_ref.shape[0], tiles), 0) == slot_ref[...])
    table_ref[...] = dot(back_ref[...], match, TN).astype(jnp.bfloat16)
    damping = damping_ref[...]

    def look(code, width):
        inside = one_hot(iota((tiles, width), 0) == code // TILE)
        values = dot(table_ref[...], inside)
        hit = iota((TILE, width), 0) == code % TILE
        return jnp.concatenate(
            [
                jnp.sum(jnp.where(hit, values[r * TILE : (r + 1) * TILE], 0.0), axis=0, keepdims=True)
                for r in range(rows)
            ],
            axis=0,
        )

    @pl.loop(0, parts // CHUNK)
    def _(step):
        where = pl.ds(pl.multiple_of(step * CHUNK, CHUNK), CHUNK)
        drag = look(code_ref[:, where], CHUNK)
        out_ref[:, where] = live_ref[:, where] * (drag - damping * part_ref[:, where])

    for row in range(4):
        begin = parts + row * migr
        drag = look(code_ref[:, begin : begin + migr], migr)
        arrived = state_refs[row][:, :].astype(jnp.float32)
        count = arrived[0:1, migr : migr + 1] * GROUP + arrived[1:2, migr : migr + 1]
        live = iota((1, migr), 1).astype(jnp.float32) < count
        force = drag - damping * arrived[:rows, :migr]
        out_ref[:, begin : begin + migr] = jnp.where(live, force, 0.0)


def call(kernel, shapes, *operands, smem=(), scratch=()):
    in_specs = [
        pl.BlockSpec(memory_space=pltpu.SMEM if i in smem else pltpu.VMEM)
        for i in range(len(operands))
    ]
    return pl.pallas_call(
        kernel,
        out_shape=shapes,
        in_specs=in_specs,
        out_specs=[pl.BlockSpec(memory_space=pltpu.VMEM) for _ in shapes],
        scratch_shapes=scratch,
        compiler_params=pltpu.CompilerParams(vmem_limit_bytes=VMEM),
    )(*operands)


def shift(block, axis, step):
    size = lax.axis_size(axis)
    return lax.ppermute(block, axis, [(i, (i + step) % size) for i in range(size)])


def per_device(
    particles,
    migrant_index,
    migrant_count,
    migrated_slot_cell,
    source_tile_size,
    tile_owner,
    tile_offset,
    closure,
    damping,
):
    f32, bf16 = jnp.float32, jnp.bfloat16
    shape = jax.ShapeDtypeStruct
    channels, parts = particles.shape
    rows = closure.shape[0]
    migr = migrant_index.shape[1]
    slots = migrated_slot_cell.shape[0]
    tiles = source_tile_size.shape[1]
    devices = lax.axis_size("gx") * lax.axis_size("gy")
    capacity = max(2, 2 * tiles // devices)
    count = devices * capacity
    width = (rows + 1) * TILE
    lanes = (width + LANES) // LANES * LANES
    cells = migrated_slot_cell.reshape(1, slots)
    owners = tile_owner.reshape(1, tiles)
    offsets = tile_offset.reshape(1, tiles)

    leaving = call(
        pick_kernel, [shape((channels, migr + LANES), bf16)] * 4,
        particles, migrant_index, migrant_count, smem=(2,),
    )
    arrived = [
        shift(block, axis, step)
        for block, (axis, step) in zip(leaving, (("gx", 1), ("gx", -1), ("gy", 1), ("gy", -1)))
    ]
    sums, live, code, slot = call(
        functools.partial(deposit_kernel, capacity),
        [shape((width, tiles), f32), shape((1, parts), f32), shape((1, slots), jnp.int32),
         shape((1, tiles), jnp.int32)],
        particles, migrant_index, migrant_count, cells, source_tile_size, owners, offsets, closure,
        smem=(2,), scratch=[pltpu.VMEM((3, tiles, LANES), jnp.int32)],
    )
    (payload,) = call(
        pack_kernel, [shape((count, lanes), bf16)],
        sums, code[:, parts:], slot, offsets, closure, *arrived,
    )
    received = lax.all_to_all(
        payload.reshape(devices, capacity, lanes), ("gx", "gy"), split_axis=0, concat_axis=0, tiled=True
    ).reshape(count, lanes)
    edge = shape((FX, 2 * width), f32)
    gas, xlow, xhigh, ylow, yhigh = call(
        place_kernel, [shape((COLS, 2 * width), f32), edge, edge, edge, edge], received
    )
    xm, xp = shift(xhigh, "gx", 1), shift(xlow, "gx", -1)
    high = jnp.concatenate([xm[FY - 1 :], yhigh, xp[FY - 1 :]], axis=0)
    low = jnp.concatenate([xm[:1], ylow, xp[:1]], axis=0)
    ym, yp = shift(high, "gy", 1), shift(low, "gy", -1)
    drag, back = call(
        drag_kernel,
        [shape((rows, FX, FY, FZ), bf16), shape((count, rows * TILE), bf16)],
        received[:, lanes - LANES :], gas, xm, xp, ym, yp,
    )
    returned = lax.all_to_all(
        back.reshape(devices, capacity, rows * TILE), ("gx", "gy"), split_axis=0, concat_axis=0, tiled=True
    ).reshape(count, rows * TILE)
    (force,) = call(
        force_kernel, [shape((rows, slots), f32)],
        returned, slot, code, live, particles[:rows], damping.reshape(rows, 1), *arrived,
        scratch=[pltpu.VMEM((rows * TILE, tiles), bf16)],
    )
    return drag, force


def solution(mesh):
    both = ("gx", "gy")
    in_specs = (
        P(None, both),
        P(both, None),
        P(both, None),
        P(both),
        P(both, None),
        P(both, None),
        P(both),
        P(),
        P(),
    )
    out_specs = (P(None, "gx", "gy", None), P(None, both))
    return jax.shard_map(
        per_device, mesh=mesh, in_specs=in_specs, out_specs=out_specs, check_vma=False
    )
```

profile of v0, /device:TPU:0, one launch (start us, length us, event | category | flops | bytes accessed | tf_op | source)
XLA Modules:
  0.0 83.2 jit_solution(12244878245768695156)
XLA Ops:
  0.6 0.0 copy-start
  0.6 1.0 %copy-done = f32[16,8192]{1,0:T(8,128)S(1)} copy-done((f32[16,8192]{1,0:T(8,128)S(1)}, f32[16,8192]{1,0:T(8,128)}, u32[]{:S(2)}) %copy-start) | copy-done | bytes 524312
  1.7 0.7 copy-done.3
  2.4 0.7 copy-done.6
  3.0 1.4 %shard_map.105 = (bf16[16,640]{1,0:T(8,128)(2,1)S(1)}, bf16[16,640]{1,0:T(8,128)(2,1)S(1)}, bf16[16,640]{1,0:T(8,128)(2,1)S(1)}, bf16[16,640]{1,0:T(8,128)(2,1)S(1)}) custom-call(f32[16,8192]{1,0:T(8,128)S(1)} %copy-done, s32[4,512]{1,0:T(4,128)S(1)} %copy-done.3, s32[1,4]{1,0:T(1,128)S(1)} %copy-done.6), custom_call_target="tpu_custom_call" | custom-call | tf_op jit(solution)/shard_map/pallas_call | solution.py:272
  4.4 0.5 collective-permute-start
  4.9 2.0 %collective-permute-start.1 = (bf16[16,640]{1,0:T(8,128)(2,1)S(1)}, bf16[16,640]{1,0:T(8,128)(2,1)S(1)}, u32[]{:S(2)}, u32[]{:S(2)}) collective-permute-start(bf16[16,640]{1,0:T(8,128)(2,1)S(1)} %get-tuple-element.21), channel_id=1, source_target_pairs={{0,24},{8,0},{16,8},{24,16},{1,25},{9,1},{17,9},{25,17},{2,26},{10... | collective-permute-start | bytes 61448 | tf_op jit(solution)/shard_map/ppermute | solution.py:284
  6.9 2.3 %collective-permute-start.2 = (bf16[16,640]{1,0:T(8,128)(2,1)S(1)}, bf16[16,640]{1,0:T(8,128)(2,1)S(1)}, u32[]{:S(2)}, u32[]{:S(2)}) collective-permute-start(bf16[16,640]{1,0:T(8,128)(2,1)S(1)} %get-tuple-element.22), channel_id=1, source_target_pairs={{0,1},{1,2},{2,3},{3,4},{4,5},{5,6},{6,7},{7,0},{8,9},{9,10},{10,1... | collective-permute-start | bytes 61448 | tf_op jit(solution)/shard_map/ppermute | solution.py:284
  9.2 3.1 %collective-permute-start.3 = (bf16[16,640]{1,0:T(8,128)(2,1)S(1)}, bf16[16,640]{1,0:T(8,128)(2,1)S(1)}, u32[]{:S(2)}, u32[]{:S(2)}) collective-permute-start(bf16[16,640]{1,0:T(8,128)(2,1)S(1)} %get-tuple-element.23), channel_id=1, source_target_pairs={{0,7},{1,0},{2,1},{3,2},{4,3},{5,4},{6,5},{7,6},{8,15},{9,8},{10,9... | collective-permute-start | bytes 61448 | tf_op jit(solution)/shard_map/ppermute | solution.py:284
  12.3 0.7 copy-done.5
  13.0 7.0 %shard_map.104 = (f32[576,256]{1,0:T(8,128)S(1)}, f32[1,8192]{1,0:T(1,128)S(1)}, s32[1,10240]{1,0:T(1,128)S(1)}, s32[1,256]{1,0:T(1,128)S(1)}) custom-call(f32[16,8192]{1,0:T(8,128)S(1)} %copy-done, s32[4,512]{1,0:T(4,128)S(1)} %copy-done.3, s32[1,4]{1,0:T(1,128)S(1)} %copy-done.6, s32[1,10240]{1,0:T(1,128)S(1)} %bitcast.12, s32[1,256]{1,0:T(1,128)S(1)} %copy-done.7, ...), custom_call_target="tpu_custom_call" | custom-call | tf_op jit(solution)/shard_map/pallas_call | solution.py:272
  20.1 0.0 collective-permute-done.refs_0_
  20.1 0.0 collective-permute-done.1.refs_1_
  20.1 0.0 collective-permute-done.2.refs_2_
  20.1 1.6 %shard_map.106 = bf16[512,640]{1,0:T(8,128)(2,1)S(1)} custom-call(f32[576,256]{1,0:T(8,128)S(1)} %get-tuple-element.17.sum_ref, s32[1,2048]{1,0:T(1,128)S(1)} %slice.21.code_ref, s32[1,256]{1,0:T(1,128)S(1)} %get-tuple-element.19.slot_ref, s32[1,256]{1,0:T(1,128)S(1)} %bitcast.14, f32[8,16]{1,0:T(8,128)S(1)} %copy-done.4, ...), custom_call_target="tpu_custom_call" | custom-call | tf_op jit(solution)/shard_map/pallas_call | solution.py:272
  21.7 22.2 %all_to_all.10 = bf16[32,16,640]{2,1,0:T(8,128)(2,1)S(1)} all-to-all(bf16[32,16,640]{2,1,0:T(8,128)(2,1)S(1)} %bitcast.10), channel_id=1, replica_groups=mesh['gx'=4,'gy'=8] {'gx','gy'}, dimensions={0} | all-to-all | bytes 1310720 | tf_op jit(solution)/shard_map/all_to_all | solution.py:333
  44.0 0.6 shard_map.107
  44.6 0.1 collective-permute-start.4
  44.6 1.7 %collective-permute-start.5 = (f32[8,1152]{1,0:T(8,128)S(1)}, f32[8,1152]{1,0:T(8,128)S(1)}, u32[]{:S(2)}, u32[]{:S(2)}) collective-permute-start(f32[8,1152]{1,0:T(8,128)S(1)} %get-tuple-element.26), channel_id=1, source_target_pairs={{0,24},{8,0},{16,8},{24,16},{1,25},{9,1},{17,9},{25,17},{2,26},{10... | collective-permute-start | bytes 110600 | tf_op jit(solution)/shard_map/ppermute | solution.py:284
  46.4 1.6 %collective-permute-done.4.xm_ref = f32[8,1152]{1,0:T(8,128)S(1)} collective-permute-done((f32[8,1152]{1,0:T(8,128)S(1)}, f32[8,1152]{1,0:T(8,128)S(1)}, u32[]{:S(2)}, u32[]{:S(2)}) %collective-permute-start.4) | collective-permute-done | bytes 36896 | tf_op jit(solution)/shard_map/ppermute | solution.py:284
  48.0 0.0 collective-permute-done.5.xp_ref
  48.1 1.7 %collective-permute-start.7 = (f32[10,1152]{1,0:T(8,128)S(1)}, f32[10,1152]{1,0:T(8,128)S(1)}, u32[]{:S(2)}, u32[]{:S(2)}) collective-permute-start(f32[10,1152]{1,0:T(8,128)S(1)} %pad_maximum_fusion.1), channel_id=1, source_target_pairs={{0,7},{1,0},{2,1},{3,2},{4,3},{5,4},{6,5},{7,6},{8,15},{9,8},{10,9... | collective-permute-start | bytes 138248 | tf_op jit(solution)/shard_map/ppermute | solution.py:284
  49.8 0.4 collective-permute-start.6
  50.3 2.7 %collective-permute-done.7.yp_ref = f32[10,1152]{1,0:T(8,128)S(1)} collective-permute-done((f32[10,1152]{1,0:T(8,128)S(1)}, f32[10,1152]{1,0:T(8,128)S(1)}, u32[]{:S(2)}, u32[]{:S(2)}) %collective-permute-start.7) | collective-permute-done | bytes 46112 | tf_op jit(solution)/shard_map/ppermute | solution.py:284
  52.9 4.0 %collective-permute-done.6.ym_ref = f32[10,1152]{1,0:T(8,128)S(1)} collective-permute-done((f32[10,1152]{1,0:T(8,128)S(1)}, f32[10,1152]{1,0:T(8,128)S(1)}, u32[]{:S(2)}, u32[]{:S(2)}) %collective-permute-start.6) | collective-permute-done | bytes 46112 | tf_op jit(solution)/shard_map/ppermute | solution.py:284
  56.9 1.5 %shard_map.108 = (bf16[8,8,8,128]{3,2,1,0:T(8,128)(2,1)}, bf16[512,512]{1,0:T(8,128)(2,1)}) custom-call(bf16[512,128]{1,0:T(8,128)(2,1)S(1)} %slice.28.mark_ref, f32[64,1152]{1,0:T(8,128)S(1)} %get-tuple-element.24.gas_ref, f32[8,1152]{1,0:T(8,128)S(1)} %collective-permute-done.4.xm_ref, f32[8,1152]{1,0:T(8,128)S(1)} %collective-permute-done.5.xp_ref, ...), custom_call_target="tpu_custom_call" | custom-call | tf_op jit(solution)/shard_map/pallas_call | solution.py:272
  58.4 2.7 %all-to-all-start.1 = ((bf16[32,16,512]{2,1,0:T(8,128)(2,1)}), bf16[32,16,512]{2,1,0:T(8,128)(2,1)S(1)}, u32[]{:S(2)}, u32[]{:S(2)}) async-start(bf16[32,16,512]{2,1,0:T(8,128)(2,1)} %bitcast.5), calls=%async_computation.1 | async-start | bytes 1048576 | tf_op jit(solution)/shard_map/all_to_all | solution.py:349
  61.2 0.0 copy-start.9
  61.2 0.6 copy-done.9
  61.8 0.1 copy.11.damping_ref
  61.9 15.6 %all-to-all-done.1 = bf16[32,16,512]{2,1,0:T(8,128)(2,1)S(1)} async-done(((bf16[32,16,512]{2,1,0:T(8,128)(2,1)}), bf16[32,16,512]{2,1,0:T(8,128)(2,1)S(1)}, u32[]{:S(2)}, u32[]{:S(2)}) %all-to-all-start.1) | async-done | bytes 524320 | tf_op jit(solution)/shard_map/all_to_all | solution.py:349
  77.5 5.7 %shard_map.109 = f32[8,10240]{1,0:T(8,128)} custom-call(bf16[512,512]{1,0:T(8,128)(2,1)S(1)} %bitcast.11, s32[1,256]{1,0:T(1,128)S(1)} %get-tuple-element.19.slot_ref, s32[1,10240]{1,0:T(1,128)S(1)} %get-tuple-element.18.code_ref, f32[1,8192]{1,0:T(1,128)S(1)} %get-tuple-element.31.live_ref, f32[8,8192]{1,0:T(8,128)S(1)} %slice.27.part_ref, ...), custom_call_target="tpu_custom_call" | custom-call | tf_op jit(solution)/shard_map/pallas_call | solution.py:272
  (21 shorter events, 0.1 us)
Async XLA Ops:
  0.6 1.0 %copy-start = (f32[16,8192]{1,0:T(8,128)S(1)}, f32[16,8192]{1,0:T(8,128)}, u32[]{:S(2)}) copy-start(f32[16,8192]{1,0:T(8,128)} %part_ref.3) | copy-start | bytes 1572868
  1.7 0.7 copy-start.3
  2.4 0.7 copy-start.6
  3.0 9.3 %copy-start.2 = (s32[10240]{0:T(1024)S(1)}, s32[10240]{0:T(1024)}, u32[]{:S(2)}) copy-start(s32[10240]{0:T(1024)} %param.12) | copy-start | bytes 122884
  4.4 15.6 %collective-permute-start = (bf16[16,640]{1,0:T(8,128)(2,1)S(1)}, bf16[16,640]{1,0:T(8,128)(2,1)S(1)}, u32[]{:S(2)}, u32[]{:S(2)}) collective-permute-start(bf16[16,640]{1,0:T(8,128)(2,1)S(1)} %get-tuple-element.20), channel_id=1, source_target_pairs={{0,8},{8,16},{16,24},{24,0},{1,9},{9,17},{17,25},{25,1},{2,10},{10... | collective-permute-start | bytes 61448 | tf_op jit(solution)/shard_map/ppermute | solution.py:284
  4.9 15.1 %collective-permute-start.1 = (bf16[16,640]{1,0:T(8,128)(2,1)S(1)}, bf16[16,640]{1,0:T(8,128)(2,1)S(1)}, u32[]{:S(2)}, u32[]{:S(2)}) collective-permute-start(bf16[16,640]{1,0:T(8,128)(2,1)S(1)} %get-tuple-element.21), channel_id=1, source_target_pairs={{0,24},{8,0},{16,8},{24,16},{1,25},{9,1},{17,9},{25,17},{2,26},{10... | collective-permute-start | bytes 61448 | tf_op jit(solution)/shard_map/ppermute | solution.py:284
  6.9 5.4 %copy-start.4 = (f32[8,16]{1,0:T(8,128)S(1)}, f32[8,16]{1,0:T(8,128)}, u32[]{:S(2)}) copy-start(f32[8,16]{1,0:T(8,128)} %closure_ref.3) | copy-start | bytes 1540
  6.9 13.1 %collective-permute-start.2 = (bf16[16,640]{1,0:T(8,128)(2,1)S(1)}, bf16[16,640]{1,0:T(8,128)(2,1)S(1)}, u32[]{:S(2)}, u32[]{:S(2)}) collective-permute-start(bf16[16,640]{1,0:T(8,128)(2,1)S(1)} %get-tuple-element.22), channel_id=1, source_target_pairs={{0,1},{1,2},{2,3},{3,4},{4,5},{5,6},{6,7},{7,0},{8,9},{9,10},{10,1... | collective-permute-start | bytes 61448 | tf_op jit(solution)/shard_map/ppermute | solution.py:284
  9.2 3.1 %copy-start.7 = (s32[1,256]{1,0:T(1,128)S(1)}, s32[1,256]{1,0:T(1,128)}, u32[]{:S(2)}) copy-start(s32[1,256]{1,0:T(1,128)} %size_ref.1) | copy-start | bytes 3076
  9.2 3.1 %copy-start.8 = (s32[256,1]{0,1:T(1,128)S(1)}, s32[256,1]{0,1:T(1,128)}, u32[]{:S(2)}) copy-start(s32[256,1]{0,1:T(1,128)} %param.14) | copy-start | bytes 3076
  9.2 10.9 %collective-permute-start.3 = (bf16[16,640]{1,0:T(8,128)(2,1)S(1)}, bf16[16,640]{1,0:T(8,128)(2,1)S(1)}, u32[]{:S(2)}, u32[]{:S(2)}) collective-permute-start(bf16[16,640]{1,0:T(8,128)(2,1)S(1)} %get-tuple-element.23), channel_id=1, source_target_pairs={{0,7},{1,0},{2,1},{3,2},{4,3},{5,4},{6,5},{7,6},{8,15},{9,8},{10,9... | collective-permute-start | bytes 61448 | tf_op jit(solution)/shard_map/ppermute | solution.py:284
  12.3 0.7 copy-start.5
  44.6 3.4 %collective-permute-start.4 = (f32[8,1152]{1,0:T(8,128)S(1)}, f32[8,1152]{1,0:T(8,128)S(1)}, u32[]{:S(2)}, u32[]{:S(2)}) collective-permute-start(f32[8,1152]{1,0:T(8,128)S(1)} %get-tuple-element.25), channel_id=1, source_target_pairs={{0,8},{8,16},{16,24},{24,0},{1,9},{9,17},{17,25},{25,1},{2,10},{10... | collective-permute-start | bytes 110600 | tf_op jit(solution)/shard_map/ppermute | solution.py:284
  44.6 3.4 %collective-permute-start.5 = (f32[8,1152]{1,0:T(8,128)S(1)}, f32[8,1152]{1,0:T(8,128)S(1)}, u32[]{:S(2)}, u32[]{:S(2)}) collective-permute-start(f32[8,1152]{1,0:T(8,128)S(1)} %get-tuple-element.26), channel_id=1, source_target_pairs={{0,24},{8,0},{16,8},{24,16},{1,25},{9,1},{17,9},{25,17},{2,26},{10... | collective-permute-start | bytes 110600 | tf_op jit(solution)/shard_map/ppermute | solution.py:284
  48.1 4.9 %collective-permute-start.7 = (f32[10,1152]{1,0:T(8,128)S(1)}, f32[10,1152]{1,0:T(8,128)S(1)}, u32[]{:S(2)}, u32[]{:S(2)}) collective-permute-start(f32[10,1152]{1,0:T(8,128)S(1)} %pad_maximum_fusion.1), channel_id=1, source_target_pairs={{0,7},{1,0},{2,1},{3,2},{4,3},{5,4},{6,5},{7,6},{8,15},{9,8},{10,9... | collective-permute-start | bytes 138248 | tf_op jit(solution)/shard_map/ppermute | solution.py:284
  49.8 7.1 %collective-permute-start.6 = (f32[10,1152]{1,0:T(8,128)S(1)}, f32[10,1152]{1,0:T(8,128)S(1)}, u32[]{:S(2)}, u32[]{:S(2)}) collective-permute-start(f32[10,1152]{1,0:T(8,128)S(1)} %pad_maximum_fusion), channel_id=1, source_target_pairs={{0,1},{1,2},{2,3},{3,4},{4,5},{5,6},{6,7},{7,0},{8,9},{9,10},{10,1... | collective-permute-start | bytes 138248 | tf_op jit(solution)/shard_map/ppermute | solution.py:284
  58.4 2.7 %copy-start.1 = (f32[16,8192]{1,0:T(8,128)S(1)}, f32[16,8192]{1,0:T(8,128)}, u32[]{:S(2)}) copy-start(f32[16,8192]{1,0:T(8,128)} %part_ref.3) | copy-start | bytes 1572868
  58.4 19.1 %all-to-all-start.1 = ((bf16[32,16,512]{2,1,0:T(8,128)(2,1)}), bf16[32,16,512]{2,1,0:T(8,128)(2,1)S(1)}, u32[]{:S(2)}, u32[]{:S(2)}) async-start(bf16[32,16,512]{2,1,0:T(8,128)(2,1)} %bitcast.5), calls=%async_computation.1 | async-start | bytes 1048576 | tf_op jit(solution)/shard_map/all_to_all | solution.py:349
  61.2 0.7 copy-start.9
where the time goes:
time: 83.6 us; the launch traced here: 83.2 us
  waiting for transfers between devices  23.9 us (29%)
  blocking collectives  22.2 us (27%)
  Pallas kernels  17.9 us (21%)
  starting transfers between devices  14.5 us (17%)
  local copies, waits for them, and re-layouts  3.84 us (5%)
    all_to_all x1, blocking collectives, per_device(): lax.all_to_all(payload.reshape(devices, capacity, lanes), ('gx', 'gy'), s...  22.2 us
    pallas_call x6, Pallas kernels, call(): pl.pallas_call(kernel, out_shape=shapes, in_specs=in_specs, out_specs=[pl...  17.9 us
    all_to_all x1, waiting for transfers between devices, per_device(): lax.all_to_all(back.reshape(devices, capacity, rows * TILE), ('gx', 'gy')...  15.6 us
    ppermute x8, starting transfers between devices, shift(): lax.ppermute(block, axis, [(i, (i + step) % size) for i in range(size)])  11.8 us
    ppermute x8, waiting for transfers between devices, shift(): lax.ppermute(block, axis, [(i, (i + step) % size) for i in range(size)])  8.31 us
    unnamed x20, local copies, waits for them, and re-layouts  3.71 us
    all_to_all x1, starting transfers between devices, per_device(): lax.all_to_all(back.reshape(devices, capacity, rows * TILE), ('gx', 'gy')...  2.73 us
  transfers between devices with their start and end apart: 9, of which 4 were waited for; matrix products, arithmetic and copies ran while one was open for 0% of the time, Pallas kernels for 8%

commit v1 on v0

v1 whole, which is shorter than its diff:
```python
import functools

import jax
import jax.numpy as jnp
from jax import lax
from jax.experimental import pallas as pl
from jax.experimental.pallas import tpu as pltpu
from jax.sharding import PartitionSpec as P

TILE = 64
FX = 8
FY = 8
FZ = 128
COLS = FX * FY
LANES = 128
GROUP = 256
CHUNK = 2048
VMEM = 48 * 1024 * 1024

NT = (((1,), (1,)), ((), ()))
TN = (((0,), (0,)), ((), ()))


def iota(shape, dim):
    return lax.broadcasted_iota(jnp.int32, shape, dim)


def dot(a, b, dims=(((1,), (0,)), ((), ()))):
    return lax.dot_general(a, b, dims, preferred_element_type=jnp.float32)


def one_hot(mask):
    return jnp.where(mask, 1.0, 0.0).astype(jnp.bfloat16)


def fetch(sources, targets, sems):
    copies = [
        pltpu.make_async_copy(source, target, sems.at[i])
        for i, (source, target) in enumerate(zip(sources, targets))
    ]
    for copy in copies:
        copy.start()
    return copies


def pick_kernel(part_hbm, index_hbm, count_hbm, *refs):
    out_refs, (part_ref, index_ref, count_ref, sems) = refs[:4], refs[4:]
    channels, parts = part_ref.shape
    migr = index_ref.shape[1]
    groups = parts // GROUP
    piece = parts // 4
    sources, targets = [index_hbm, count_hbm], [index_ref, count_ref]
    for k in range(4):
        sources.append(part_hbm.at[:, k * piece : (k + 1) * piece])
        targets.append(part_ref.at[:, k * piece : (k + 1) * piece])
    copies = fetch(sources, targets, sems)
    for copy in copies[:2]:
        copy.wait()
    lows = [one_hot(iota((GROUP, migr), 0) == index_ref[r : r + 1, :] % GROUP) for r in range(4)]
    low = jnp.concatenate(lows, axis=1)
    lane = iota((1, migr), 1)
    highs = [
        jnp.where(lane < count_ref[0, r], index_ref[r : r + 1, :] // GROUP, groups) for r in range(4)
    ]
    high = jnp.concatenate(highs, axis=1)
    for copy in copies[2:]:
        copy.wait()
    table = jnp.concatenate(
        [part_ref[:, g * GROUP : (g + 1) * GROUP].astype(jnp.bfloat16) for g in range(groups)], axis=0
    )
    rows = dot(table, low)
    picked = jnp.zeros((channels, 4 * migr), jnp.float32)
    for g in range(groups):
        picked = jnp.where(high == g, rows[g * channels : (g + 1) * channels], picked)
    for r in range(4):
        count = count_ref[0, r]
        out_refs[r][:, :migr] = picked[:, r * migr : (r + 1) * migr].astype(jnp.bfloat16)
        digits = jnp.where(iota((channels, LANES), 0) == 0, count // GROUP, count % GROUP)
        out_refs[r][:, migr:] = digits.astype(jnp.float32).astype(jnp.bfloat16)


def mix(closure_ref, state):
    state = state.astype(jnp.float32)
    mixed = closure_ref[:, 0:1] * state[0:1]
    for f in range(1, state.shape[0]):
        mixed = mixed + closure_ref[:, f : f + 1] * state[f : f + 1]
    return mixed, state[0:1]


def equal(rows, row):
    numbers = iota((rows, row.shape[1]), 0).astype(jnp.float32).astype(jnp.bfloat16)
    return numbers == row.astype(jnp.float32).astype(jnp.bfloat16)


def ones(mask):
    return jnp.where(mask, jnp.bfloat16(1), jnp.bfloat16(0))


def spread(mixed, first, place):
    hit = equal(TILE, place)
    values = jnp.concatenate([mixed, first], axis=0).astype(jnp.bfloat16)
    return jnp.concatenate(
        [jnp.where(hit, values[r : r + 1], jnp.bfloat16(0)) for r in range(values.shape[0])], axis=0
    )


def deposit_kernel(
    capacity, part_ref, index_ref, count_ref, cell_ref, size_hbm, owner_hbm, offset_hbm, closure_hbm,
    sum_ref, live_ref, code_ref, slot_ref, size_ref, owner_ref, offset_ref, closure_ref, columns_ref, sems,
):
    channels, parts = part_ref.shape
    migr = index_ref.shape[1]
    slots = cell_ref.shape[1]
    tiles = size_ref.shape[1]
    groups = parts // GROUP
    copies = fetch(
        (size_hbm, owner_hbm, offset_hbm, closure_hbm), (size_ref, owner_ref, offset_ref, closure_ref), sems
    )

    highs, lows = [], []
    for row in range(4):
        index = index_ref[row : row + 1, :]
        valid = iota((1, migr), 1) < count_ref[0, row]
        highs.append(jnp.where(valid, index // GROUP, groups))
        lows.append(index % GROUP)
    high, low = jnp.concatenate(highs, axis=1), jnp.concatenate(lows, axis=1)
    hits = dot(ones(equal(groups, high)), ones(equal(GROUP, low)), NT)
    for g in range(groups):
        live_ref[:, g * GROUP : (g + 1) * GROUP] = 1.0 - hits[g : g + 1]

    for copy in copies:
        copy.wait()

    square = (tiles, tiles)
    below, across = iota(square, 0), iota(square, 1)

    def column(row):
        return jnp.sum(jnp.where(below == across, row, 0), axis=1, keepdims=True)

    sizes = size_ref[...]
    owners = owner_ref[...]
    start = jnp.sum(jnp.where(across < below, sizes, 0), axis=1, keepdims=True)
    height = column(offset_ref[...] % FZ)
    code = iota((tiles, 1), 0) * TILE + (height - start) % TILE
    code_step = code - jnp.concatenate([jnp.zeros((1, 1), jnp.int32), code[: tiles - 1]], axis=0)
    earlier = (column(owners) == owners) & (below < across)
    rank = jnp.sum(jnp.where(earlier, 1, 0), axis=0, keepdims=True)
    slot_ref[...] = owners * capacity + rank
    columns_ref[0] = jnp.broadcast_to(start, (tiles, LANES))
    columns_ref[1] = jnp.broadcast_to(code_step, (tiles, LANES))

    def find(cell):
        width = cell.shape[1]
        starts = jnp.concatenate([columns_ref[0]] * (width // LANES), axis=1)
        steps = jnp.concatenate([columns_ref[1]] * (width // LANES), axis=1)
        found = jnp.sum(jnp.where(cell >= starts, steps, 0), axis=0, keepdims=True)
        return found // TILE, (found + cell) % TILE

    for begin in range(parts, slots, CHUNK):
        tile, place = find(cell_ref[:, begin : begin + CHUNK])
        code_ref[:, begin : begin + CHUNK] = tile * TILE + place
    for begin in range(0, parts, CHUNK):
        tile, place = find(cell_ref[:, begin : begin + CHUNK])
        code_ref[:, begin : begin + CHUNK] = tile * TILE + place
        state = part_ref[:, begin : begin + CHUNK] * live_ref[:, begin : begin + CHUNK]
        mixed, first = mix(closure_ref, state.astype(jnp.bfloat16))
        added = dot(spread(mixed, first, place), ones(equal(tiles, tile)), NT)
        if begin == 0:
            sum_ref[...] = added
        else:
            sum_ref[...] += added


def pack_kernel(sum_ref, code_ref, slot_ref, offset_ref, closure_ref, *refs):
    state_refs, out_ref = refs[:4], refs[4]
    tiles = slot_ref.shape[1]
    migr = code_ref.shape[1] // 4
    code = code_ref[...]
    state = jnp.concatenate([ref[:, :migr] for ref in state_refs], axis=1)
    mixed, first = mix(closure_ref, state)
    total = sum_ref[...] + dot(spread(mixed, first, code % TILE), ones(equal(tiles, code // TILE)), NT)
    offset = offset_ref[...]
    spare = out_ref.shape[1] - total.shape[0]
    rows = iota((spare, tiles), 0)
    marks = jnp.where(rows == 0, offset // FZ, jnp.where(rows == 1, offset % FZ, 0))
    table = jnp.concatenate(
        [total.astype(jnp.bfloat16), marks.astype(jnp.float32).astype(jnp.bfloat16)], axis=0
    )
    match = one_hot(iota((out_ref.shape[0], tiles), 0) == slot_ref[...])
    out_ref[...] = dot(match, table, NT).astype(jnp.bfloat16)


def place_kernel(tile_ref, gas_ref, xlow_ref, xhigh_ref):
    count, lanes = tile_ref.shape
    width = gas_ref.shape[1] // 2
    marks = tile_ref[:, lanes - LANES :].astype(jnp.float32)
    column = marks[:, width % LANES : width % LANES + 1]
    height = marks[:, width % LANES + 1 : width % LANES + 2]
    lane = iota((1, LANES), 1)
    hot = one_hot(column == lane.astype(jnp.float32))
    place = (iota((1, width), 1) % TILE).astype(jnp.float32)
    values = tile_ref[:, :width].astype(jnp.float32)
    for half, mask in enumerate((place >= height, place < height)):
        total = dot(hot, jnp.where(mask, values, 0.0).astype(jnp.bfloat16), TN)
        where = slice(half * width, (half + 1) * width)
        gas_ref[:, where] = total[:COLS]
        xlow_ref[:, where] = total[:FY]
        xhigh_ref[:, where] = total[COLS - FY : COLS]


def along_kernel(gas_ref, xm_ref, xp_ref, out_ref, ylow_ref, yhigh_ref):
    blocks = [xm_ref[...]] + [gas_ref[x * FY : (x + 1) * FY, :] for x in range(FX)] + [xp_ref[...]]
    along = [blocks[x] + 2.0 * blocks[x + 1] + blocks[x + 2] for x in range(FX)]
    for x in range(FX):
        out_ref[x * FY : (x + 1) * FY, :] = along[x]
    ylow_ref[...] = jnp.concatenate([along[x][:1] for x in range(FX)], axis=0)
    yhigh_ref[...] = jnp.concatenate([along[x][FY - 1 :] for x in range(FX)], axis=0)


def drag_kernel(mark_ref, along_ref, ym_ref, yp_ref, drag_ref, back_ref):
    rows = drag_ref.shape[0]
    width = along_ref.shape[1] // 2
    lanes = rows * TILE
    before, after = ym_ref[...], yp_ref[...]
    smooth = []
    for x in range(FX):
        block = along_ref[x * FY : (x + 1) * FY, :]
        padded = jnp.concatenate([before[x : x + 1], block, after[x : x + 1]], axis=0)
        smooth.append((padded[0:FY] + 2.0 * block + padded[2 : FY + 2]) / 16.0)
    smooth = jnp.concatenate(smooth, axis=0)
    halves = []
    for half in range(2):
        base = half * width
        density = smooth[:, base + lanes : base + lanes + TILE]
        below = 1.0 + density * density
        below = jnp.concatenate([below] * rows, axis=1)
        halves.append(smooth[:, base : base + lanes] / below)
    for r in range(rows):
        where = slice(r * TILE, (r + 1) * TILE)
        both = jnp.concatenate([halves[0][:, where], halves[1][:, where]], axis=1)
        drag_ref[r] = both.reshape(FX, FY, FZ).astype(jnp.bfloat16)
    mark = width % LANES
    marks = mark_ref[...].astype(jnp.float32)
    column, height = marks[:, mark : mark + 1], marks[:, mark + 1 : mark + 2]
    hot = one_hot(column == iota((1, COLS), 1).astype(jnp.float32))
    place = (iota((1, lanes), 1) % TILE).astype(jnp.float32)
    low = dot(hot, halves[0].astype(jnp.bfloat16))
    high = dot(hot, halves[1].astype(jnp.bfloat16))
    back_ref[...] = jnp.where(place >= height, low, high).astype(jnp.bfloat16)


def force_kernel(back_ref, slot_ref, code_ref, live_ref, part_ref, damping_ref, *refs):
    state_refs, out_ref, table_ref = refs[:4], refs[4], refs[5]
    rows, slots = out_ref.shape
    parts = part_ref.shape[1]
    tiles = slot_ref.shape[1]
    migr = (slots - parts) // 4
    match = one_hot(iota((back_ref.shape[0], tiles), 0) == slot_ref[...])
    table_ref[...] = dot(back_ref[...], match, TN).astype(jnp.bfloat16)
    damping = damping_ref[...]

    def look(code):
        values = dot(table_ref[...], ones(equal(tiles, code // TILE))).astype(jnp.bfloat16)
        hit = equal(TILE, code % TILE)
        found = []
        for r in range(rows):
            picked = jnp.where(hit, values[r * TILE : (r + 1) * TILE], jnp.bfloat16(0))
            while picked.shape[0] > 16:
                half = picked.shape[0] // 2
                picked = picked[:half] + picked[half:]
            found.append(jnp.sum(picked.astype(jnp.float32), axis=0, keepdims=True))
        return jnp.concatenate(found, axis=0)

    for begin in range(0, parts, CHUNK):
        where = slice(begin, begin + CHUNK)
        out_ref[:, where] = live_ref[:, where] * (look(code_ref[:, where]) - damping * part_ref[:, where])
    drag = look(code_ref[:, parts:])
    for row in range(4):
        begin = parts + row * migr
        arrived = state_refs[row][:, :].astype(jnp.float32)
        count = arrived[0:1, migr : migr + 1] * GROUP + arrived[1:2, migr : migr + 1]
        live = iota((1, migr), 1).astype(jnp.float32) < count
        force = drag[:, row * migr : (row + 1) * migr] - damping * arrived[:rows, :migr]
        out_ref[:, begin : begin + migr] = jnp.where(live, force, 0.0)


def call(kernel, shapes, *operands, smem=(), hbm=(), scratch=()):
    def space(i):
        return pltpu.SMEM if i in smem else pltpu.HBM if i in hbm else pltpu.VMEM

    return pl.pallas_call(
        kernel,
        out_shape=shapes,
        in_specs=[pl.BlockSpec(memory_space=space(i)) for i in range(len(operands))],
        out_specs=[pl.BlockSpec(memory_space=pltpu.VMEM) for _ in shapes],
        scratch_shapes=scratch,
        compiler_params=pltpu.CompilerParams(vmem_limit_bytes=VMEM),
    )(*operands)


def shift(block, axis, step):
    size = lax.axis_size(axis)
    return lax.ppermute(block, axis, [(i, (i + step) % size) for i in range(size)])


def per_device(
    particles,
    migrant_index,
    migrant_count,
    migrated_slot_cell,
    source_tile_size,
    tile_owner,
    tile_offset,
    closure,
    damping,
):
    f32, bf16 = jnp.float32, jnp.bfloat16
    shape = jax.ShapeDtypeStruct
    channels, parts = particles.shape
    rows = closure.shape[0]
    migr = migrant_index.shape[1]
    slots = migrated_slot_cell.shape[0]
    tiles = source_tile_size.shape[1]
    devices = lax.axis_size("gx") * lax.axis_size("gy")
    capacity = max(2, 2 * tiles // devices)
    count = devices * capacity
    width = (rows + 1) * TILE
    lanes = (width + LANES) // LANES * LANES
    cells = migrated_slot_cell.reshape(1, slots)
    owners = tile_owner.reshape(1, tiles)
    offsets = tile_offset.reshape(1, tiles)

    leaving = call(
        pick_kernel, [shape((channels, migr + LANES), bf16)] * 4,
        particles, migrant_index, migrant_count, hbm=(0, 1, 2),
        scratch=[pltpu.VMEM(particles.shape, f32), pltpu.VMEM(migrant_index.shape, jnp.int32),
                 pltpu.SMEM(migrant_count.shape, jnp.int32), pltpu.SemaphoreType.DMA((6,))],
    )
    arrived = [
        shift(block, axis, step)
        for block, (axis, step) in zip(leaving, (("gx", 1), ("gx", -1), ("gy", 1), ("gy", -1)))
    ]
    sums, live, code, slot = call(
        functools.partial(deposit_kernel, capacity),
        [shape((width, tiles), f32), shape((1, parts), f32), shape((1, slots), jnp.int32),
         shape((1, tiles), jnp.int32)],
        particles, migrant_index, migrant_count, cells, source_tile_size, owners, offsets, closure,
        smem=(2,), hbm=(4, 5, 6, 7),
        scratch=[pltpu.VMEM((1, tiles), jnp.int32)] * 3
        + [pltpu.VMEM(closure.shape, f32), pltpu.VMEM((2, tiles, LANES), jnp.int32),
           pltpu.SemaphoreType.DMA((4,))],
    )
    (payload,) = call(
        pack_kernel, [shape((count, lanes), bf16)],
        sums, code[:, parts:], slot, offsets, closure, *arrived,
    )
    received = lax.all_to_all(
        payload.reshape(devices, capacity, lanes), ("gx", "gy"), split_axis=0, concat_axis=0, tiled=True
    ).reshape(count, lanes)
    grid, edge = shape((COLS, 2 * width), f32), shape((FX, 2 * width), f32)
    gas, xlow, xhigh = call(place_kernel, [grid, edge, edge], received)
    xm, xp = shift(xhigh, "gx", 1), shift(xlow, "gx", -1)
    along, ylow, yhigh = call(along_kernel, [grid, edge, edge], gas, xm, xp)
    ym, yp = shift(yhigh, "gy", 1), shift(ylow, "gy", -1)
    drag, back = call(
        drag_kernel,
        [shape((rows, FX, FY, FZ), bf16), shape((count, rows * TILE), bf16)],
        received[:, lanes - LANES :], along, ym, yp,
    )
    returned = lax.all_to_all(
        back.reshape(devices, capacity, rows * TILE), ("gx", "gy"), split_axis=0, concat_axis=0, tiled=True
    ).reshape(count, rows * TILE)
    (force,) = call(
        force_kernel, [shape((rows, slots), f32)],
        returned, slot, code, live, particles[:rows], damping.reshape(rows, 1), *arrived,
        scratch=[pltpu.VMEM((rows * TILE, tiles), bf16)],
    )
    return drag, force


def solution(mesh):
    both = ("gx", "gy")
    in_specs = (
        P(None, both),
        P(both, None),
        P(both, None),
        P(both),
        P(both, None),
        P(both, None),
        P(both),
        P(),
        P(),
    )
    out_specs = (P(None, "gx", "gy", None), P(None, both))
    return jax.shard_map(
        per_device, mesh=mesh, in_specs=in_specs, out_specs=out_specs, check_vma=False
    )
```

time: 83.6 us -> 80.4 us (0.962)
  starting transfers between devices: 14.5 us -> 19.7 us
  waiting for transfers between devices: 23.9 us -> 19 us
  Pallas kernels: 17.9 us -> 14.5 us
    ppermute x8, waiting for transfers between devices: 8.31 us -> 3.64 us  [shift(): lax.ppermute(block, axis, [(i, (i + step) % size) for i in range(size)])]
    pallas_call x6 -> x7, Pallas kernels: 17.9 us -> 14.5 us  [call(): pl.pallas_call(kernel, out_shape=shapes, in_specs=[pl.BlockSpec(memory_sp...]
    ppermute x8, starting transfers between devices: 11.8 us -> 14.4 us  [shift(): lax.ppermute(block, axis, [(i, (i + step) % size) for i in range(size)])]
    all_to_all x1, starting transfers between devices: 2.73 us -> 5.21 us  [per_device(): lax.all_to_all(back.reshape(devices, capacity, rows * TILE), ('gx', 'gy')...]
  transfers between devices with their start and end apart: 9 -> 9, of which waited for: 4 -> 3; matrix products, arithmetic and copies ran while one was open for 0% -> 0% of each run, Pallas kernels for 8% -> 6%
where the time goes in v1:
time: 80.4 us; the launch traced here: 80 us
  blocking collectives  22.2 us (28%)
  starting transfers between devices  19.7 us (25%)
  waiting for transfers between devices  19 us (24%)
  Pallas kernels  14.5 us (18%)
  local copies, waits for them, and re-layouts  3.83 us (5%)
    all_to_all x1, blocking collectives, per_device(): lax.all_to_all(payload.reshape(devices, capacity, lanes), ('gx', 'gy'), s...  22.2 us
    all_to_all x1, waiting for transfers between devices, per_device(): lax.all_to_all(back.reshape(devices, capacity, rows * TILE), ('gx', 'gy')...  15.4 us
    pallas_call x7, Pallas kernels, call(): pl.pallas_call(kernel, out_shape=shapes, in_specs=[pl.BlockSpec(memory_sp...  14.5 us
    ppermute x8, starting transfers between devices, shift(): lax.ppermute(block, axis, [(i, (i + step) % size) for i in range(size)])  14.4 us
    all_to_all x1, starting transfers between devices, per_device(): lax.all_to_all(back.reshape(devices, capacity, rows * TILE), ('gx', 'gy')...  5.21 us
    unnamed x20, local copies, waits for them, and re-layouts  3.71 us
    ppermute x8, waiting for transfers between devices, shift(): lax.ppermute(block, axis, [(i, (i + step) % size) for i in range(size)])  3.64 us
  transfers between devices with their start and end apart: 9, of which 3 were waited for; matrix products, arithmetic and copies ran while one was open for 0% of the time, Pallas kernels for 6%

profile of v1, /device:TPU:0, one launch (start us, length us, event | category | flops | bytes accessed | tf_op | source)
XLA Modules:
  0.0 80.0 jit_solution(4306017695760874396)
XLA Ops:
  0.6 0.0 copy-start
  0.6 1.0 %copy-done = f32[16,8192]{1,0:T(8,128)S(1)} copy-done((f32[16,8192]{1,0:T(8,128)S(1)}, f32[16,8192]{1,0:T(8,128)}, u32[]{:S(2)}) %copy-start) | copy-done | bytes 524312
  1.7 0.7 copy-done.3
  2.4 0.7 copy-done.6
  3.0 1.6 %shard_map.105 = (bf16[16,640]{1,0:T(8,128)(2,1)S(1)}, bf16[16,640]{1,0:T(8,128)(2,1)S(1)}, bf16[16,640]{1,0:T(8,128)(2,1)S(1)}, bf16[16,640]{1,0:T(8,128)(2,1)S(1)}) custom-call(f32[16,8192]{1,0:T(8,128)S(1)} %copy-done, s32[4,512]{1,0:T(4,128)S(1)} %copy-done.3, s32[1,4]{1,0:T(1,128)S(1)} %copy-done.6), custom_call_target="tpu_custom_call" | custom-call | tf_op jit(solution)/shard_map/pallas_call | solution.py:291
  4.7 0.5 collective-permute-start
  5.2 2.0 %collective-permute-start.1 = (bf16[16,640]{1,0:T(8,128)(2,1)S(1)}, bf16[16,640]{1,0:T(8,128)(2,1)S(1)}, u32[]{:S(2)}, u32[]{:S(2)}) collective-permute-start(bf16[16,640]{1,0:T(8,128)(2,1)S(1)} %get-tuple-element.22), channel_id=1, source_target_pairs={{0,24},{8,0},{16,8},{24,16},{1,25},{9,1},{17,9},{25,17},{2,26},{10... | collective-permute-start | bytes 61448 | tf_op jit(solution)/shard_map/ppermute | solution.py:303
  7.1 2.3 %collective-permute-start.2 = (bf16[16,640]{1,0:T(8,128)(2,1)S(1)}, bf16[16,640]{1,0:T(8,128)(2,1)S(1)}, u32[]{:S(2)}, u32[]{:S(2)}) collective-permute-start(bf16[16,640]{1,0:T(8,128)(2,1)S(1)} %get-tuple-element.23), channel_id=1, source_target_pairs={{0,1},{1,2},{2,3},{3,4},{4,5},{5,6},{6,7},{7,0},{8,9},{9,10},{10,1... | collective-permute-start | bytes 61448 | tf_op jit(solution)/shard_map/ppermute | solution.py:303
  9.4 3.1 %collective-permute-start.3 = (bf16[16,640]{1,0:T(8,128)(2,1)S(1)}, bf16[16,640]{1,0:T(8,128)(2,1)S(1)}, u32[]{:S(2)}, u32[]{:S(2)}) collective-permute-start(bf16[16,640]{1,0:T(8,128)(2,1)S(1)} %get-tuple-element.24), channel_id=1, source_target_pairs={{0,7},{1,0},{2,1},{3,2},{4,3},{5,4},{6,5},{7,6},{8,15},{9,8},{10,9... | collective-permute-start | bytes 61448 | tf_op jit(solution)/shard_map/ppermute | solution.py:303
  12.5 0.7 copy-done.5
  13.2 5.1 %shard_map.104 = (f32[576,256]{1,0:T(8,128)S(1)}, f32[1,8192]{1,0:T(1,128)S(1)}, s32[1,10240]{1,0:T(1,128)S(1)}, s32[1,256]{1,0:T(1,128)S(1)}) custom-call(f32[16,8192]{1,0:T(8,128)S(1)} %copy-done, s32[4,512]{1,0:T(4,128)S(1)} %copy-done.3, s32[1,4]{1,0:T(1,128)S(1)} %copy-done.6, s32[1,10240]{1,0:T(1,128)S(1)} %bitcast.12, s32[1,256]{1,0:T(1,128)S(1)} %copy-done.7, ...), custom_call_target="tpu_custom_call" | custom-call | tf_op jit(solution)/shard_map/pallas_call | solution.py:291
  18.3 0.0 collective-permute-done.refs_0_
  18.3 0.0 collective-permute-done.1.refs_1_
  18.3 0.0 collective-permute-done.2.refs_2_
  18.3 0.0 collective-permute-done.3.refs_3_
  18.3 1.6 %shard_map.106 = bf16[512,640]{1,0:T(8,128)(2,1)S(1)} custom-call(f32[576,256]{1,0:T(8,128)S(1)} %get-tuple-element.18.sum_ref, s32[1,2048]{1,0:T(1,128)S(1)} %slice.9.code_ref, s32[1,256]{1,0:T(1,128)S(1)} %get-tuple-element.20.slot_ref, s32[1,256]{1,0:T(1,128)S(1)} %bitcast.14, f32[8,16]{1,0:T(8,128)S(1)} %copy-done.4, ...), custom_call_target="tpu_custom_call" | custom-call | tf_op jit(solution)/shard_map/pallas_call | solution.py:291
  20.0 22.2 %all_to_all.10 = bf16[32,16,640]{2,1,0:T(8,128)(2,1)S(1)} all-to-all(bf16[32,16,640]{2,1,0:T(8,128)(2,1)S(1)} %bitcast.10), channel_id=1, replica_groups=mesh['gx'=4,'gy'=8] {'gx','gy'}, dimensions={0} | all-to-all | bytes 1310720 | tf_op jit(solution)/shard_map/all_to_all | solution.py:357
  42.2 0.6 shard_map.107
  42.8 0.1 collective-permute-start.4
  42.9 1.7 %collective-permute-start.5 = (f32[8,1152]{1,0:T(8,128)S(1)}, f32[8,1152]{1,0:T(8,128)S(1)}, u32[]{:S(2)}, u32[]{:S(2)}) collective-permute-start(f32[8,1152]{1,0:T(8,128)S(1)} %get-tuple-element.27), channel_id=1, source_target_pairs={{0,24},{8,0},{16,8},{24,16},{1,25},{9,1},{17,9},{25,17},{2,26},{10... | collective-permute-start | bytes 110600 | tf_op jit(solution)/shard_map/ppermute | solution.py:303
  44.6 1.6 %collective-permute-done.4.xm_ref = f32[8,1152]{1,0:T(8,128)S(1)} collective-permute-done((f32[8,1152]{1,0:T(8,128)S(1)}, f32[8,1152]{1,0:T(8,128)S(1)}, u32[]{:S(2)}, u32[]{:S(2)}) %collective-permute-start.4) | collective-permute-done | bytes 36896 | tf_op jit(solution)/shard_map/ppermute | solution.py:303
  46.3 0.1 shard_map.108
  46.3 0.8 %collective-permute-start.6 = (f32[8,1152]{1,0:T(8,128)S(1)}, f32[8,1152]{1,0:T(8,128)S(1)}, u32[]{:S(2)}, u32[]{:S(2)}) collective-permute-start(f32[8,1152]{1,0:T(8,128)S(1)} %get-tuple-element.29), channel_id=1, source_target_pairs={{0,1},{1,2},{2,3},{3,4},{4,5},{5,6},{6,7},{7,0},{8,9},{9,10},{10,1... | collective-permute-start | bytes 110600 | tf_op jit(solution)/shard_map/ppermute | solution.py:303
  47.2 3.9 %collective-permute-start.7 = (f32[8,1152]{1,0:T(8,128)S(1)}, f32[8,1152]{1,0:T(8,128)S(1)}, u32[]{:S(2)}, u32[]{:S(2)}) collective-permute-start(f32[8,1152]{1,0:T(8,128)S(1)} %get-tuple-element.30), channel_id=1, source_target_pairs={{0,7},{1,0},{2,1},{3,2},{4,3},{5,4},{6,5},{7,6},{8,15},{9,8},{10,9... | collective-permute-start | bytes 110600 | tf_op jit(solution)/shard_map/ppermute | solution.py:303
  51.2 2.0 %collective-permute-done.6.ym_ref = f32[8,1152]{1,0:T(8,128)S(1)} collective-permute-done((f32[8,1152]{1,0:T(8,128)S(1)}, f32[8,1152]{1,0:T(8,128)S(1)}, u32[]{:S(2)}, u32[]{:S(2)}) %collective-permute-start.6) | collective-permute-done | bytes 36896 | tf_op jit(solution)/shard_map/ppermute | solution.py:303
  53.1 1.4 %shard_map.109 = (bf16[8,8,8,128]{3,2,1,0:T(8,128)(2,1)}, bf16[512,512]{1,0:T(8,128)(2,1)}) custom-call(bf16[512,128]{1,0:T(8,128)(2,1)S(1)} %slice.12.mark_ref, f32[64,1152]{1,0:T(8,128)S(1)} %get-tuple-element.28.along_ref, f32[8,1152]{1,0:T(8,128)S(1)} %collective-permute-done.6.ym_ref, f32[8,1152]{1,0:T(8,128)S(1)} %collective-permute-done.7.yp_ref), custom_call_target="tpu_custom_call" | custom-call | tf_op jit(solution)/shard_map/pallas_call | solution.py:291
  54.5 5.2 %all-to-all-start.1 = ((bf16[32,16,512]{2,1,0:T(8,128)(2,1)}), bf16[32,16,512]{2,1,0:T(8,128)(2,1)S(1)}, u32[]{:S(2)}, u32[]{:S(2)}) async-start(bf16[32,16,512]{2,1,0:T(8,128)(2,1)} %bitcast.5), calls=%async_computation.1 | async-start | bytes 1048576 | tf_op jit(solution)/shard_map/all_to_all | solution.py:370
  59.8 0.0 copy-start.9
  59.8 0.6 copy-done.9
  60.5 0.1 copy.11.damping_ref
  60.5 15.4 %all-to-all-done.1 = bf16[32,16,512]{2,1,0:T(8,128)(2,1)S(1)} async-done(((bf16[32,16,512]{2,1,0:T(8,128)(2,1)}), bf16[32,16,512]{2,1,0:T(8,128)(2,1)S(1)}, u32[]{:S(2)}, u32[]{:S(2)}) %all-to-all-start.1) | async-done | bytes 524320 | tf_op jit(solution)/shard_map/all_to_all | solution.py:370
  75.9 4.1 %shard_map.110 = f32[8,10240]{1,0:T(8,128)} custom-call(bf16[512,512]{1,0:T(8,128)(2,1)S(1)} %bitcast.11, s32[1,256]{1,0:T(1,128)S(1)} %get-tuple-element.20.slot_ref, s32[1,10240]{1,0:T(1,128)S(1)} %get-tuple-element.19.code_ref, f32[1,8192]{1,0:T(1,128)S(1)} %get-tuple-element.33.live_ref, f32[8,8192]{1,0:T(8,128)S(1)} %slice.11.part_ref, ...), custom_call_target="tpu_custom_call" | custom-call | tf_op jit(solution)/shard_map/pallas_call | solution.py:291
  (18 shorter events, 0.1 us)
Async XLA Ops:
  0.6 1.0 %copy-start = (f32[16,8192]{1,0:T(8,128)S(1)}, f32[16,8192]{1,0:T(8,128)}, u32[]{:S(2)}) copy-start(f32[16,8192]{1,0:T(8,128)} %part_hbm.1) | copy-start | bytes 1572868
  1.7 0.7 copy-start.3
  2.4 0.7 copy-start.6
  3.0 9.5 %copy-start.2 = (s32[10240]{0:T(1024)S(1)}, s32[10240]{0:T(1024)}, u32[]{:S(2)}) copy-start(s32[10240]{0:T(1024)} %param.12) | copy-start | bytes 122884
  4.7 13.7 %collective-permute-start = (bf16[16,640]{1,0:T(8,128)(2,1)S(1)}, bf16[16,640]{1,0:T(8,128)(2,1)S(1)}, u32[]{:S(2)}, u32[]{:S(2)}) collective-permute-start(bf16[16,640]{1,0:T(8,128)(2,1)S(1)} %get-tuple-element.21), channel_id=1, source_target_pairs={{0,8},{8,16},{16,24},{24,0},{1,9},{9,17},{17,25},{25,1},{2,10},{10... | collective-permute-start | bytes 61448 | tf_op jit(solution)/shard_map/ppermute | solution.py:303
  5.2 13.2 %collective-permute-start.1 = (bf16[16,640]{1,0:T(8,128)(2,1)S(1)}, bf16[16,640]{1,0:T(8,128)(2,1)S(1)}, u32[]{:S(2)}, u32[]{:S(2)}) collective-permute-start(bf16[16,640]{1,0:T(8,128)(2,1)S(1)} %get-tuple-element.22), channel_id=1, source_target_pairs={{0,24},{8,0},{16,8},{24,16},{1,25},{9,1},{17,9},{25,17},{2,26},{10... | collective-permute-start | bytes 61448 | tf_op jit(solution)/shard_map/ppermute | solution.py:303
  7.1 5.4 %copy-start.4 = (f32[8,16]{1,0:T(8,128)S(1)}, f32[8,16]{1,0:T(8,128)}, u32[]{:S(2)}) copy-start(f32[8,16]{1,0:T(8,128)} %closure_ref.1) | copy-start | bytes 1540
  7.1 11.2 %collective-permute-start.2 = (bf16[16,640]{1,0:T(8,128)(2,1)S(1)}, bf16[16,640]{1,0:T(8,128)(2,1)S(1)}, u32[]{:S(2)}, u32[]{:S(2)}) collective-permute-start(bf16[16,640]{1,0:T(8,128)(2,1)S(1)} %get-tuple-element.23), channel_id=1, source_target_pairs={{0,1},{1,2},{2,3},{3,4},{4,5},{5,6},{6,7},{7,0},{8,9},{9,10},{10,1... | collective-permute-start | bytes 61448 | tf_op jit(solution)/shard_map/ppermute | solution.py:303
  9.4 3.1 %copy-start.7 = (s32[1,256]{1,0:T(1,128)S(1)}, s32[1,256]{1,0:T(1,128)}, u32[]{:S(2)}) copy-start(s32[1,256]{1,0:T(1,128)} %size_hbm.1) | copy-start | bytes 3076
  9.4 3.1 %copy-start.8 = (s32[256,1]{0,1:T(1,128)S(1)}, s32[256,1]{0,1:T(1,128)}, u32[]{:S(2)}) copy-start(s32[256,1]{0,1:T(1,128)} %param.14) | copy-start | bytes 3076
  9.4 8.9 %collective-permute-start.3 = (bf16[16,640]{1,0:T(8,128)(2,1)S(1)}, bf16[16,640]{1,0:T(8,128)(2,1)S(1)}, u32[]{:S(2)}, u32[]{:S(2)}) collective-permute-start(bf16[16,640]{1,0:T(8,128)(2,1)S(1)} %get-tuple-element.24), channel_id=1, source_target_pairs={{0,7},{1,0},{2,1},{3,2},{4,3},{5,4},{6,5},{7,6},{8,15},{9,8},{10,9... | collective-permute-start | bytes 61448 | tf_op jit(solution)/shard_map/ppermute | solution.py:303
  12.5 0.7 copy-start.5
  42.8 3.4 %collective-permute-start.4 = (f32[8,1152]{1,0:T(8,128)S(1)}, f32[8,1152]{1,0:T(8,128)S(1)}, u32[]{:S(2)}, u32[]{:S(2)}) collective-permute-start(f32[8,1152]{1,0:T(8,128)S(1)} %get-tuple-element.26), channel_id=1, source_target_pairs={{0,8},{8,16},{16,24},{24,0},{1,9},{9,17},{17,25},{25,1},{2,10},{10... | collective-permute-start | bytes 110600 | tf_op jit(solution)/shard_map/ppermute | solution.py:303
  42.9 3.4 %collective-permute-start.5 = (f32[8,1152]{1,0:T(8,128)S(1)}, f32[8,1152]{1,0:T(8,128)S(1)}, u32[]{:S(2)}, u32[]{:S(2)}) collective-permute-start(f32[8,1152]{1,0:T(8,128)S(1)} %get-tuple-element.27), channel_id=1, source_target_pairs={{0,24},{8,0},{16,8},{24,16},{1,25},{9,1},{17,9},{25,17},{2,26},{10... | collective-permute-start | bytes 110600 | tf_op jit(solution)/shard_map/ppermute | solution.py:303
  46.3 6.8 %collective-permute-start.6 = (f32[8,1152]{1,0:T(8,128)S(1)}, f32[8,1152]{1,0:T(8,128)S(1)}, u32[]{:S(2)}, u32[]{:S(2)}) collective-permute-start(f32[8,1152]{1,0:T(8,128)S(1)} %get-tuple-element.29), channel_id=1, source_target_pairs={{0,1},{1,2},{2,3},{3,4},{4,5},{5,6},{6,7},{7,0},{8,9},{9,10},{10,1... | collective-permute-start | bytes 110600 | tf_op jit(solution)/shard_map/ppermute | solution.py:303
  47.2 6.0 %collective-permute-start.7 = (f32[8,1152]{1,0:T(8,128)S(1)}, f32[8,1152]{1,0:T(8,128)S(1)}, u32[]{:S(2)}, u32[]{:S(2)}) collective-permute-start(f32[8,1152]{1,0:T(8,128)S(1)} %get-tuple-element.30), channel_id=1, source_target_pairs={{0,7},{1,0},{2,1},{3,2},{4,3},{5,4},{6,5},{7,6},{8,15},{9,8},{10,9... | collective-permute-start | bytes 110600 | tf_op jit(solution)/shard_map/ppermute | solution.py:303
  54.5 5.2 %copy-start.1 = (f32[16,8192]{1,0:T(8,128)S(1)}, f32[16,8192]{1,0:T(8,128)}, u32[]{:S(2)}) copy-start(f32[16,8192]{1,0:T(8,128)} %part_hbm.1) | copy-start | bytes 1572868
  54.5 21.4 %all-to-all-start.1 = ((bf16[32,16,512]{2,1,0:T(8,128)(2,1)}), bf16[32,16,512]{2,1,0:T(8,128)(2,1)S(1)}, u32[]{:S(2)}, u32[]{:S(2)}) async-start(bf16[32,16,512]{2,1,0:T(8,128)(2,1)} %bitcast.5), calls=%async_computation.1 | async-start | bytes 1048576 | tf_op jit(solution)/shard_map/all_to_all | solution.py:370
  59.8 0.7 copy-start.9

commit v2 on v1

--- a/solution.py
+++ b/solution.py
@@ -16,6 +16,7 @@
 GROUP = 256
 CHUNK = 2048
 VMEM = 48 * 1024 * 1024
+LARGE = 63 * 1024 * 1024
 
 NT = (((1,), (1,)), ((), ()))
 TN = (((0,), (0,)), ((), ()))
@@ -31,6 +32,15 @@
 
 def one_hot(mask):
     return jnp.where(mask, 1.0, 0.0).astype(jnp.bfloat16)
+
+
+def equal(rows, row):
+    numbers = iota((rows, row.shape[1]), 0).astype(jnp.float32).astype(jnp.bfloat16)
+    return numbers == row.astype(jnp.float32).astype(jnp.bfloat16)
+
+
+def ones(mask):
+    return jnp.where(mask, jnp.bfloat16(1), jnp.bfloat16(0))
 
 
 def fetch(sources, targets, sems):
@@ -43,8 +53,19 @@
     return copies
 
 
-def pick_kernel(part_hbm, index_hbm, count_hbm, *refs):
-    out_refs, (part_ref, index_ref, count_ref, sems) = refs[:4], refs[4:]
+def leaving_rows(index_ref, count_ref, groups):
+    migr = index_ref.shape[1]
+    lane = iota((1, migr), 1)
+    index = jnp.concatenate([index_ref[r : r + 1, :] for r in range(4)], axis=1)
+    leaves = jnp.concatenate([lane < count_ref[0, r] for r in range(4)], axis=1)
+    return jnp.where(leaves, index // GROUP, groups), index % GROUP
+
+
+def pick_kernel(
+    part_hbm, index_hbm, count_hbm, size_hbm, owner_hbm, offset_hbm, closure_hbm, damping_hbm, *refs
+):
+    out_refs, small_ref, refs = refs[:4], refs[4], refs[5:]
+    part_ref, index_ref, count_ref, size_ref, owner_ref, offset_ref, closure_ref, damping_ref, sems = refs
     channels, parts = part_ref.shape
     migr = index_ref.shape[1]
     groups = parts // GROUP
@@ -53,18 +74,22 @@
     for k in range(4):
         sources.append(part_hbm.at[:, k * piece : (k + 1) * piece])
         targets.append(part_ref.at[:, k * piece : (k + 1) * piece])
+    sources += [size_hbm, owner_hbm, offset_hbm, closure_hbm, damping_hbm]
+    targets += [size_ref, owner_ref, offset_ref, closure_ref, damping_ref]
     copies = fetch(sources, targets, sems)
     for copy in copies[:2]:
         copy.wait()
-    lows = [one_hot(iota((GROUP, migr), 0) == index_ref[r : r + 1, :] % GROUP) for r in range(4)]
-    low = jnp.concatenate(lows, axis=1)
-    lane = iota((1, migr), 1)
-    highs = [
-        jnp.where(lane < count_ref[0, r], index_ref[r : r + 1, :] // GROUP, groups) for r in range(4)
-    ]
-    high = jnp.concatenate(highs, axis=1)
+    high, low = leaving_rows(index_ref, count_ref, groups)
+    low = ones(equal(GROUP, low))
     for copy in copies[2:]:
         copy.wait()
+    for row, ref in enumerate((size_ref, owner_ref, offset_ref)):
+        small_ref[row : row + 1, :] = ref[...].astype(jnp.float32)
+    rows, width = closure_ref.shape
+    small_ref[rows : 2 * rows, :width] = closure_ref[...]
+    diagonal = iota((rows, rows), 0) == iota((rows, rows), 1)
+    damping = jnp.sum(jnp.where(diagonal, damping_ref[...], 0.0), axis=1, keepdims=True)
+    small_ref[rows : 2 * rows, width : width + 1] = damping
     table = jnp.concatenate(
         [part_ref[:, g * GROUP : (g + 1) * GROUP].astype(jnp.bfloat16) for g in range(groups)], axis=0
     )
@@ -79,21 +104,13 @@
         out_refs[r][:, migr:] = digits.astype(jnp.float32).astype(jnp.bfloat16)
 
 
-def mix(closure_ref, state):
+def mix(small_ref, state):
     state = state.astype(jnp.float32)
-    mixed = closure_ref[:, 0:1] * state[0:1]
+    closure = small_ref[small_ref.shape[0] // 2 :, :]
+    mixed = closure[:, 0:1] * state[0:1]
     for f in range(1, state.shape[0]):
-        mixed = mixed + closure_ref[:, f : f + 1] * state[f : f + 1]
+        mixed = mixed + closure[:, f : f + 1] * state[f : f + 1]
     return mixed, state[0:1]
-
-
-def equal(rows, row):
-    numbers = iota((rows, row.shape[1]), 0).astype(jnp.float32).astype(jnp.bfloat16)
-    return numbers == row.astype(jnp.float32).astype(jnp.bfloat16)
-
-
-def ones(mask):
-    return jnp.where(mask, jnp.bfloat16(1), jnp.bfloat16(0))
 
 
 def spread(mixed, first, place):
@@ -105,42 +122,28 @@
 
 
 def deposit_kernel(
-    capacity, part_ref, index_ref, count_ref, cell_ref, size_hbm, owner_hbm, offset_hbm, closure_hbm,
-    sum_ref, live_ref, code_ref, slot_ref, size_ref, owner_ref, offset_ref, closure_ref, columns_ref, sems,
+    capacity, part_ref, index_ref, count_ref, cell_ref, small_ref,
+    sum_ref, live_ref, code_ref, slot_ref, mark_ref, columns_ref,
 ):
     channels, parts = part_ref.shape
-    migr = index_ref.shape[1]
     slots = cell_ref.shape[1]
-    tiles = size_ref.shape[1]
+    tiles = slot_ref.shape[1]
     groups = parts // GROUP
-    copies = fetch(
-        (size_hbm, owner_hbm, offset_hbm, closure_hbm), (size_ref, owner_ref, offset_ref, closure_ref), sems
-    )
-
-    highs, lows = [], []
-    for row in range(4):
-        index = index_ref[row : row + 1, :]
-        valid = iota((1, migr), 1) < count_ref[0, row]
-        highs.append(jnp.where(valid, index // GROUP, groups))
-        lows.append(index % GROUP)
-    high, low = jnp.concatenate(highs, axis=1), jnp.concatenate(lows, axis=1)
+
+    high, low = leaving_rows(index_ref, count_ref, groups)
     hits = dot(ones(equal(groups, high)), ones(equal(GROUP, low)), NT)
     for g in range(groups):
         live_ref[:, g * GROUP : (g + 1) * GROUP] = 1.0 - hits[g : g + 1]
 
-    for copy in copies:
-        copy.wait()
-
     square = (tiles, tiles)
     below, across = iota(square, 0), iota(square, 1)
 
     def column(row):
         return jnp.sum(jnp.where(below == across, row, 0), axis=1, keepdims=True)
 
-    sizes = size_ref[...]
-    owners = owner_ref[...]
+    sizes, owners, offset = [small_ref[row : row + 1, :].astype(jnp.int32) for row in range(3)]
     start = jnp.sum(jnp.where(across < below, sizes, 0), axis=1, keepdims=True)
-    height = column(offset_ref[...] % FZ)
+    height = column(offset % FZ)
     code = iota((tiles, 1), 0) * TILE + (height - start) % TILE
     code_step = code - jnp.concatenate([jnp.zeros((1, 1), jnp.int32), code[: tiles - 1]], axis=0)
     earlier = (column(owners) == owners) & (below < across)
@@ -148,6 +151,9 @@
     slot_ref[...] = owners * capacity + rank
     columns_ref[0] = jnp.broadcast_to(start, (tiles, LANES))
     columns_ref[1] = jnp.broadcast_to(code_step, (tiles, LANES))
+    rows = iota(mark_ref.shape, 0)
+    marks = jnp.where(rows == 0, offset // FZ, jnp.where(rows == 1, offset % FZ, 0))
+    mark_ref[...] = marks.astype(jnp.float32).astype(jnp.bfloat16)
 
     def find(cell):
         width = cell.shape[1]
@@ -163,7 +169,7 @@
         tile, place = find(cell_ref[:, begin : begin + CHUNK])
         code_ref[:, begin : begin + CHUNK] = tile * TILE + place
         state = part_ref[:, begin : begin + CHUNK] * live_ref[:, begin : begin + CHUNK]
-        mixed, first = mix(closure_ref, state.astype(jnp.bfloat16))
+        mixed, first = mix(small_ref, state.astype(jnp.bfloat16))
         added = dot(spread(mixed, first, place), ones(equal(tiles, tile)), NT)
         if begin == 0:
             sum_ref[...] = added
@@ -171,21 +177,15 @@
             sum_ref[...] += added
 
 
-def pack_kernel(sum_ref, code_ref, slot_ref, offset_ref, closure_ref, *refs):
+def pack_kernel(sum_ref, code_ref, slot_ref, mark_ref, small_ref, *refs):
     state_refs, out_ref = refs[:4], refs[4]
     tiles = slot_ref.shape[1]
-    migr = code_ref.shape[1] // 4
-    code = code_ref[...]
+    migr = state_refs[0].shape[1] - LANES
+    code = code_ref[:, code_ref.shape[1] - 4 * migr :]
     state = jnp.concatenate([ref[:, :migr] for ref in state_refs], axis=1)
-    mixed, first = mix(closure_ref, state)
+    mixed, first = mix(small_ref, state)
     total = sum_ref[...] + dot(spread(mixed, first, code % TILE), ones(equal(tiles, code // TILE)), NT)
-    offset = offset_ref[...]
-    spare = out_ref.shape[1] - total.shape[0]
-    rows = iota((spare, tiles), 0)
-    marks = jnp.where(rows == 0, offset // FZ, jnp.where(rows == 1, offset % FZ, 0))
-    table = jnp.concatenate(
-        [total.astype(jnp.bfloat16), marks.astype(jnp.float32).astype(jnp.bfloat16)], axis=0
-    )
+    table = jnp.concatenate([total.astype(jnp.bfloat16), mark_ref[...]], axis=0)
     match = one_hot(iota((out_ref.shape[0], tiles), 0) == slot_ref[...])
     out_ref[...] = dot(match, table, NT).astype(jnp.bfloat16)
 
@@ -204,24 +204,34 @@
         total = dot(hot, jnp.where(mask, values, 0.0).astype(jnp.bfloat16), TN)
         where = slice(half * width, (half + 1) * width)
         gas_ref[:, where] = total[:COLS]
-        xlow_ref[:, where] = total[:FY]
-        xhigh_ref[:, where] = total[COLS - FY : COLS]
+        rows = slice(half * FY, (half + 1) * FY)
+        xlow_ref[rows, :] = total[:FY].astype(jnp.bfloat16)
+        xhigh_ref[rows, :] = total[COLS - FY : COLS].astype(jnp.bfloat16)
+
+
+def unfold(ref):
+    edge = ref[...].astype(jnp.float32)
+    half = edge.shape[0] // 2
+    return jnp.concatenate([edge[:half], edge[half:]], axis=1)
 
 
 def along_kernel(gas_ref, xm_ref, xp_ref, out_ref, ylow_ref, yhigh_ref):
-    blocks = [xm_ref[...]] + [gas_ref[x * FY : (x + 1) * FY, :] for x in range(FX)] + [xp_ref[...]]
+    blocks = [unfold(xm_ref)] + [gas_ref[x * FY : (x + 1) * FY, :] for x in range(FX)] + [unfold(xp_ref)]
     along = [blocks[x] + 2.0 * blocks[x + 1] + blocks[x + 2] for x in range(FX)]
     for x in range(FX):
         out_ref[x * FY : (x + 1) * FY, :] = along[x]
-    ylow_ref[...] = jnp.concatenate([along[x][:1] for x in range(FX)], axis=0)
-    yhigh_ref[...] = jnp.concatenate([along[x][FY - 1 :] for x in range(FX)], axis=0)
+    width = ylow_ref.shape[1]
+    for ref, row in ((ylow_ref, 0), (yhigh_ref, FY - 1)):
+        edge = jnp.concatenate([along[x][row : row + 1] for x in range(FX)], axis=0)
+        edge = jnp.concatenate([edge[:, :width], edge[:, width:]], axis=0)
+        ref[...] = edge.astype(jnp.bfloat16)
 
 
 def drag_kernel(mark_ref, along_ref, ym_ref, yp_ref, drag_ref, back_ref):
     rows = drag_ref.shape[0]
     width = along_ref.shape[1] // 2
     lanes = rows * TILE
-    before, after = ym_ref[...], yp_ref[...]
+    before, after = unfold(ym_ref), unfold(yp_ref)
     smooth = []
     for x in range(FX):
         block = along_ref[x * FY : (x + 1) * FY, :]
@@ -249,7 +259,7 @@
     back_ref[...] = jnp.where(place >= height, low, high).astype(jnp.bfloat16)
 
 
-def force_kernel(back_ref, slot_ref, code_ref, live_ref, part_ref, damping_ref, *refs):
+def force_kernel(back_ref, slot_ref, code_ref, live_ref, part_ref, small_ref, *refs):
     state_refs, out_ref, table_ref = refs[:4], refs[4], refs[5]
     rows, slots = out_ref.shape
     parts = part_ref.shape[1]
@@ -257,7 +267,8 @@
     migr = (slots - parts) // 4
     match = one_hot(iota((back_ref.shape[0], tiles), 0) == slot_ref[...])
     table_ref[...] = dot(back_ref[...], match, TN).astype(jnp.bfloat16)
-    damping = damping_ref[...]
+    channels = part_ref.shape[0]
+    damping = small_ref[rows:, channels : channels + 1]
 
     def look(code):
         values = dot(table_ref[...], ones(equal(tiles, code // TILE))).astype(jnp.bfloat16)
@@ -273,7 +284,7 @@
 
     for begin in range(0, parts, CHUNK):
         where = slice(begin, begin + CHUNK)
-        out_ref[:, where] = live_ref[:, where] * (look(code_ref[:, where]) - damping * part_ref[:, where])
+        out_ref[:, where] = live_ref[:, where] * (look(code_ref[:, where]) - damping * part_ref[:rows, where])
     drag = look(code_ref[:, parts:])
     for row in range(4):
         begin = parts + row * migr
@@ -284,7 +295,7 @@
         out_ref[:, begin : begin + migr] = jnp.where(live, force, 0.0)
 
 
-def call(kernel, shapes, *operands, smem=(), hbm=(), scratch=()):
+def call(kernel, shapes, *operands, smem=(), hbm=(), scratch=(), vmem=VMEM):
     def space(i):
         return pltpu.SMEM if i in smem else pltpu.HBM if i in hbm else pltpu.VMEM
 
@@ -294,7 +305,7 @@
         in_specs=[pl.BlockSpec(memory_space=space(i)) for i in range(len(operands))],
         out_specs=[pl.BlockSpec(memory_space=pltpu.VMEM) for _ in shapes],
         scratch_shapes=scratch,
-        compiler_params=pltpu.CompilerParams(vmem_limit_bytes=VMEM),
+        compiler_params=pltpu.CompilerParams(vmem_limit_bytes=vmem),
     )(*operands)
 
 
@@ -314,7 +325,7 @@
     closure,
     damping,
 ):
-    f32, bf16 = jnp.float32, jnp.bfloat16
+    f32, bf16, i32 = jnp.float32, jnp.bfloat16, jnp.int32
     shape = jax.ShapeDtypeStruct
     channels, parts = particles.shape
     rows = closure.shape[0]
@@ -326,38 +337,35 @@
     count = devices * capacity
     width = (rows + 1) * TILE
     lanes = (width + LANES) // LANES * LANES
-    cells = migrated_slot_cell.reshape(1, slots)
-    owners = tile_owner.reshape(1, tiles)
-    offsets = tile_offset.reshape(1, tiles)
-
-    leaving = call(
-        pick_kernel, [shape((channels, migr + LANES), bf16)] * 4,
-        particles, migrant_index, migrant_count, hbm=(0, 1, 2),
-        scratch=[pltpu.VMEM(particles.shape, f32), pltpu.VMEM(migrant_index.shape, jnp.int32),
-                 pltpu.SMEM(migrant_count.shape, jnp.int32), pltpu.SemaphoreType.DMA((6,))],
+    *leaving, small = call(
+        pick_kernel,
+        [shape((channels, migr + LANES), bf16)] * 4 + [shape((2 * rows, tiles), f32)],
+        particles, migrant_index, migrant_count, source_tile_size, tile_owner.reshape(1, tiles),
+        tile_offset.reshape(1, tiles), closure, damping.reshape(1, rows),
+        hbm=range(8), vmem=LARGE,
+        scratch=[pltpu.VMEM(particles.shape, f32), pltpu.VMEM(migrant_index.shape, i32),
+                 pltpu.SMEM(migrant_count.shape, i32)]
+        + [pltpu.VMEM((1, tiles), i32)] * 3
+        + [pltpu.VMEM(closure.shape, f32), pltpu.VMEM((1, rows), f32), pltpu.SemaphoreType.DMA((11,))],
     )
     arrived = [
         shift(block, axis, step)
         for block, (axis, step) in zip(leaving, (("gx", 1), ("gx", -1), ("gy", 1), ("gy", -1)))
     ]
-    sums, live, code, slot = call(
+    sums, live, code, slot, marks = call(
         functools.partial(deposit_kernel, capacity),
-        [shape((width, tiles), f32), shape((1, parts), f32), shape((1, slots), jnp.int32),
-         shape((1, tiles), jnp.int32)],
-        particles, migrant_index, migrant_count, cells, source_tile_size, owners, offsets, closure,
-        smem=(2,), hbm=(4, 5, 6, 7),
-        scratch=[pltpu.VMEM((1, tiles), jnp.int32)] * 3
-        + [pltpu.VMEM(closure.shape, f32), pltpu.VMEM((2, tiles, LANES), jnp.int32),
-           pltpu.SemaphoreType.DMA((4,))],
+        [shape((width, tiles), f32), shape((1, parts), f32), shape((1, slots), i32), shape((1, tiles), i32),
+         shape((lanes - width, tiles), bf16)],
+        particles, migrant_index, migrant_count, migrated_slot_cell.reshape(1, slots), small,
+        smem=(2,), scratch=[pltpu.VMEM((2, tiles, LANES), i32)],
     )
     (payload,) = call(
-        pack_kernel, [shape((count, lanes), bf16)],
-        sums, code[:, parts:], slot, offsets, closure, *arrived,
+        pack_kernel, [shape((count, lanes), bf16)], sums, code, slot, marks, small, *arrived
     )
     received = lax.all_to_all(
         payload.reshape(devices, capacity, lanes), ("gx", "gy"), split_axis=0, concat_axis=0, tiled=True
     ).reshape(count, lanes)
-    grid, edge = shape((COLS, 2 * width), f32), shape((FX, 2 * width), f32)
+    grid, edge = shape((COLS, 2 * width), f32), shape((2 * FX, width), bf16)
     gas, xlow, xhigh = call(place_kernel, [grid, edge, edge], received)
     xm, xp = shift(xhigh, "gx", 1), shift(xlow, "gx", -1)
     along, ylow, yhigh = call(along_kernel, [grid, edge, edge], gas, xm, xp)
@@ -372,7 +380,7 @@
     ).reshape(count, rows * TILE)
     (force,) = call(
         force_kernel, [shape((rows, slots), f32)],
-        returned, slot, code, live, particles[:rows], damping.reshape(rows, 1), *arrived,
+        returned, slot, code, live, particles, small, *arrived,
         scratch=[pltpu.VMEM((rows * TILE, tiles), bf16)],
     )
     return drag, force

time: 80.4 us -> 79.2 us (0.985)
  blocking collectives: 22.2 us -> 43.5 us
  waiting for transfers between devices: 19 us -> 3.22 us
  starting transfers between devices: 19.7 us -> 14.4 us
  local copies, waits for them, and re-layouts: 3.83 us -> 2.17 us
    all_to_all x0 -> x1, blocking collectives: none -> 21.2 us  [per_device(): lax.all_to_all(back.reshape(devices, capacity, rows * TILE), ('gx', 'gy')...]
    all_to_all x1 -> x0, waiting for transfers between devices: 15.4 us -> none  [per_device(): lax.all_to_all(back.reshape(devices, capacity, rows * TILE), ('gx', 'gy')...]
    all_to_all x1 -> x0, starting transfers between devices: 5.21 us -> none  [per_device(): lax.all_to_all(back.reshape(devices, capacity, rows * TILE), ('gx', 'gy')...]
    unnamed x20 -> x12, local copies, waits for them, and re-layouts: 3.71 us -> 2.16 us
  transfers between devices with their start and end apart: 9 -> 8, of which waited for: 3 -> 2; matrix products, arithmetic and copies ran while one was open for 0% -> 0% of each run, Pallas kernels for 6% -> 6%
where the time goes in v2:
time: 79.2 us; the launch traced here: 78.9 us
  blocking collectives  43.5 us (55%)
  Pallas kernels  14.9 us (19%)
  starting transfers between devices  14.4 us (18%)
  waiting for transfers between devices  3.22 us (4%)
  local copies, waits for them, and re-layouts  2.17 us (3%)
    all_to_all x1, blocking collectives, per_device(): lax.all_to_all(payload.reshape(devices, capacity, lanes), ('gx', 'gy'), s...  22.3 us
    all_to_all x1, blocking collectives, per_device(): lax.all_to_all(back.reshape(devices, capacity, rows * TILE), ('gx', 'gy')...  21.2 us
    pallas_call x7, Pallas kernels, call(): pl.pallas_call(kernel, out_shape=shapes, in_specs=[pl.BlockSpec(memory_sp...  14.9 us
    ppermute x8, starting transfers between devices, shift(): lax.ppermute(block, axis, [(i, (i + step) % size) for i in range(size)])  14.4 us
    ppermute x8, waiting for transfers between devices, shift(): lax.ppermute(block, axis, [(i, (i + step) % size) for i in range(size)])  3.22 us
    unnamed x12, local copies, waits for them, and re-layouts  2.16 us
  transfers between devices with their start and end apart: 8, of which 2 were waited for; matrix products, arithmetic and copies ran while one was open for 0% of the time, Pallas kernels for 6%

profile of v2, /device:TPU:0, one launch (start us, length us, event | category | flops | bytes accessed | tf_op | source)
XLA Modules:
  0.0 78.9 jit_solution(8820182931588021469)
XLA Ops:
  0.6 0.0 copy-start
  0.6 2.6 %shard_map.104 = (bf16[16,640]{1,0:T(8,128)(2,1)}, bf16[16,640]{1,0:T(8,128)(2,1)}, bf16[16,640]{1,0:T(8,128)(2,1)}, bf16[16,640]{1,0:T(8,128)(2,1)}, f32[16,256]{1,0:T(8,128)}) custom-call(f32[16,8192]{1,0:T(8,128)} %part_ref.3, s32[4,512]{1,0:T(4,128)} %index_ref.1, s32[1,4]{1,0:T(1,128)} %count_ref.1, s32[1,256]{1,0:T(1,128)} %size_hbm.1, ...), custom_call_target="tpu_custom_call" | custom-call | tf_op jit(solution)/shard_map/pallas_call | solution.py:302
  3.2 0.0 copy-start.4
  3.3 0.5 collective-permute-start
  3.8 2.0 %collective-permute-start.1 = (bf16[16,640]{1,0:T(8,128)(2,1)}, bf16[16,640]{1,0:T(8,128)(2,1)S(1)}, u32[]{:S(2)}, u32[]{:S(2)}) collective-permute-start(bf16[16,640]{1,0:T(8,128)(2,1)} %get-tuple-element.26), channel_id=1, source_target_pairs={{0,24},{8,0},{16,8},{24,16},{1,25},{9,1},{17,9},{25,17},{2,26},{10... | collective-permute-start | bytes 61448 | tf_op jit(solution)/shard_map/ppermute | solution.py:314
  5.8 2.3 %collective-permute-start.2 = (bf16[16,640]{1,0:T(8,128)(2,1)}, bf16[16,640]{1,0:T(8,128)(2,1)S(1)}, u32[]{:S(2)}, u32[]{:S(2)}) collective-permute-start(bf16[16,640]{1,0:T(8,128)(2,1)} %get-tuple-element.27), channel_id=1, source_target_pairs={{0,1},{1,2},{2,3},{3,4},{4,5},{5,6},{6,7},{7,0},{8,9},{9,10},{10,1... | collective-permute-start | bytes 61448 | tf_op jit(solution)/shard_map/ppermute | solution.py:314
  8.0 3.0 %collective-permute-start.3 = (bf16[16,640]{1,0:T(8,128)(2,1)}, bf16[16,640]{1,0:T(8,128)(2,1)S(1)}, u32[]{:S(2)}, u32[]{:S(2)}) collective-permute-start(bf16[16,640]{1,0:T(8,128)(2,1)} %get-tuple-element.28), channel_id=1, source_target_pairs={{0,7},{1,0},{2,1},{3,2},{4,3},{5,4},{6,5},{7,6},{8,15},{9,8},{10,9... | collective-permute-start | bytes 61448 | tf_op jit(solution)/shard_map/ppermute | solution.py:314
  11.1 0.0 copy-done
  11.1 0.0 copy-done.4
  11.1 0.6 copy-done.5
  11.7 0.7 copy-done.1
  12.4 0.8 copy-done.3
  13.2 4.6 %shard_map.105 = (f32[576,256]{1,0:T(8,128)S(1)}, f32[1,8192]{1,0:T(1,128)S(1)}, s32[1,10240]{1,0:T(1,128)S(1)}, s32[1,256]{1,0:T(1,128)S(1)}, bf16[64,256]{1,0:T(8,128)(2,1)S(1)}) custom-call(f32[16,8192]{1,0:T(8,128)S(1)} %copy-done, s32[4,512]{1,0:T(4,128)S(1)} %copy-done.4, s32[1,4]{1,0:T(1,128)S(1)} %copy-done.5, s32[1,10240]{1,0:T(1,128)S(1)} %bitcast.13, ...), custom_call_target="tpu_custom_call" | custom-call | tf_op jit(solution)/shard_map/pallas_call | solution.py:302
  17.8 0.0 collective-permute-done.refs_0_
  17.8 0.0 collective-permute-done.1.refs_1_
  17.8 0.0 collective-permute-done.2.refs_2_
  17.8 0.0 collective-permute-done.3.refs_3_
  17.9 1.6 %shard_map.106 = bf16[512,640]{1,0:T(8,128)(2,1)S(1)} custom-call(f32[576,256]{1,0:T(8,128)S(1)} %get-tuple-element.21.sum_ref, s32[1,10240]{1,0:T(1,128)S(1)} %get-tuple-element.22.code_ref, s32[1,256]{1,0:T(1,128)S(1)} %get-tuple-element.23.slot_ref, bf16[64,256]{1,0:T(8,128)(2,1)S(1)} %get-tuple-element.24.mark_ref, f32[16,256]{1,0:T(8,128)S(1)} %copy-done.1, ...), custom_call_target="tpu_custom_call" | custom-call | tf_op jit(solution)/shard_map/pallas_call | solution.py:302
  19.5 22.3 %all_to_all.10 = bf16[32,16,640]{2,1,0:T(8,128)(2,1)S(1)} all-to-all(bf16[32,16,640]{2,1,0:T(8,128)(2,1)S(1)} %bitcast.10), channel_id=1, replica_groups=mesh['gx'=4,'gy'=8] {'gx','gy'}, dimensions={0} | all-to-all | bytes 1310720 | tf_op jit(solution)/shard_map/all_to_all | solution.py:365
  41.8 0.6 shard_map.107
  42.4 0.1 collective-permute-start.4
  42.5 1.7 %collective-permute-start.5 = (bf16[16,576]{1,0:T(8,128)(2,1)S(1)}, bf16[16,576]{1,0:T(8,128)(2,1)S(1)}, u32[]{:S(2)}, u32[]{:S(2)}) collective-permute-start(bf16[16,576]{1,0:T(8,128)(2,1)S(1)} %get-tuple-element.31), channel_id=1, source_target_pairs={{0,24},{8,0},{16,8},{24,16},{1,25},{9,1},{17,9},{25,17},{2,26},{10... | collective-permute-start | bytes 55304 | tf_op jit(solution)/shard_map/ppermute | solution.py:314
  44.2 1.5 %collective-permute-done.4.xm_ref = bf16[16,576]{1,0:T(8,128)(2,1)S(1)} collective-permute-done((bf16[16,576]{1,0:T(8,128)(2,1)S(1)}, bf16[16,576]{1,0:T(8,128)(2,1)S(1)}, u32[]{:S(2)}, u32[]{:S(2)}) %collective-permute-start.4) | collective-permute-done | bytes 18464 | tf_op jit(solution)/shard_map/ppermute | solution.py:314
  45.7 0.0 collective-permute-done.5.xp_ref
  45.7 0.2 shard_map.108
  45.9 0.8 %collective-permute-start.6 = (bf16[16,576]{1,0:T(8,128)(2,1)S(1)}, bf16[16,576]{1,0:T(8,128)(2,1)S(1)}, u32[]{:S(2)}, u32[]{:S(2)}) collective-permute-start(bf16[16,576]{1,0:T(8,128)(2,1)S(1)} %get-tuple-element.33), channel_id=1, source_target_pairs={{0,1},{1,2},{2,3},{3,4},{4,5},{5,6},{6,7},{7,0},{8,9},{9,10},{10,1... | collective-permute-start | bytes 55304 | tf_op jit(solution)/shard_map/ppermute | solution.py:314
  46.7 3.9 %collective-permute-start.7 = (bf16[16,576]{1,0:T(8,128)(2,1)S(1)}, bf16[16,576]{1,0:T(8,128)(2,1)S(1)}, u32[]{:S(2)}, u32[]{:S(2)}) collective-permute-start(bf16[16,576]{1,0:T(8,128)(2,1)S(1)} %get-tuple-element.34), channel_id=1, source_target_pairs={{0,7},{1,0},{2,1},{3,2},{4,3},{5,4},{6,5},{7,6},{8,15},{9,8},{10,9... | collective-permute-start | bytes 55304 | tf_op jit(solution)/shard_map/ppermute | solution.py:314
  50.7 1.7 %collective-permute-done.6.ym_ref = bf16[16,576]{1,0:T(8,128)(2,1)S(1)} collective-permute-done((bf16[16,576]{1,0:T(8,128)(2,1)S(1)}, bf16[16,576]{1,0:T(8,128)(2,1)S(1)}, u32[]{:S(2)}, u32[]{:S(2)}) %collective-permute-start.6) | collective-permute-done | bytes 18464 | tf_op jit(solution)/shard_map/ppermute | solution.py:314
  52.4 0.0 collective-permute-done.7.yp_ref
  52.4 1.2 %shard_map.109 = (bf16[8,8,8,128]{3,2,1,0:T(8,128)(2,1)}, bf16[512,512]{1,0:T(8,128)(2,1)S(1)}) custom-call(bf16[512,128]{1,0:T(8,128)(2,1)S(1)} %slice.4.mark_ref, f32[64,1152]{1,0:T(8,128)S(1)} %get-tuple-element.32.along_ref, bf16[16,576]{1,0:T(8,128)(2,1)S(1)} %collective-permute-done.6.ym_ref, bf16[16,576]{1,0:T(8,128)(2,1)S(1)} %collective-permute-done.7.yp_ref), custom_call_target="tpu_custom_call" | custom-call | tf_op jit(solution)/shard_map/pallas_call | solution.py:302
  53.6 21.2 %all_to_all.11 = bf16[32,16,512]{2,1,0:T(8,128)(2,1)S(1)} all-to-all(bf16[32,16,512]{2,1,0:T(8,128)(2,1)S(1)} %bitcast.12), channel_id=1, replica_groups=mesh['gx'=4,'gy'=8] {'gx','gy'}, dimensions={0} | all-to-all | bytes 1048576 | tf_op jit(solution)/shard_map/all_to_all | solution.py:378
  74.8 4.1 %shard_map.110 = f32[8,10240]{1,0:T(8,128)} custom-call(bf16[512,512]{1,0:T(8,128)(2,1)S(1)} %bitcast.11, s32[1,256]{1,0:T(1,128)S(1)} %get-tuple-element.23.slot_ref, s32[1,10240]{1,0:T(1,128)S(1)} %get-tuple-element.22.code_ref, f32[1,8192]{1,0:T(1,128)S(1)} %get-tuple-element.37.live_ref, f32[16,8192]{1,0:T(8,128)S(1)} %copy-done, ...), custom_call_target="tpu_custom_call" | custom-call | tf_op jit(solution)/shard_map/pallas_call | solution.py:302
  (6 shorter events, 0.0 us)
Async XLA Ops:
  0.6 10.4 %copy-start = (f32[16,8192]{1,0:T(8,128)S(1)}, f32[16,8192]{1,0:T(8,128)}, u32[]{:S(2)}) copy-start(f32[16,8192]{1,0:T(8,128)} %part_ref.3) | copy-start | bytes 1572868
  3.2 7.8 %copy-start.4 = (s32[4,512]{1,0:T(4,128)S(1)}, s32[4,512]{1,0:T(4,128)}, u32[]{:S(2)}) copy-start(s32[4,512]{1,0:T(4,128)} %index_ref.1) | copy-start | bytes 24580
  3.3 14.6 %collective-permute-start = (bf16[16,640]{1,0:T(8,128)(2,1)}, bf16[16,640]{1,0:T(8,128)(2,1)S(1)}, u32[]{:S(2)}, u32[]{:S(2)}) collective-permute-start(bf16[16,640]{1,0:T(8,128)(2,1)} %get-tuple-element.25), channel_id=1, source_target_pairs={{0,8},{8,16},{16,24},{24,0},{1,9},{9,17},{17,25},{25,1},{2,10},{10... | collective-permute-start | bytes 61448 | tf_op jit(solution)/shard_map/ppermute | solution.py:314
  3.8 14.1 %collective-permute-start.1 = (bf16[16,640]{1,0:T(8,128)(2,1)}, bf16[16,640]{1,0:T(8,128)(2,1)S(1)}, u32[]{:S(2)}, u32[]{:S(2)}) collective-permute-start(bf16[16,640]{1,0:T(8,128)(2,1)} %get-tuple-element.26), channel_id=1, source_target_pairs={{0,24},{8,0},{16,8},{24,16},{1,25},{9,1},{17,9},{25,17},{2,26},{10... | collective-permute-start | bytes 61448 | tf_op jit(solution)/shard_map/ppermute | solution.py:314
  5.8 12.1 %collective-permute-start.2 = (bf16[16,640]{1,0:T(8,128)(2,1)}, bf16[16,640]{1,0:T(8,128)(2,1)S(1)}, u32[]{:S(2)}, u32[]{:S(2)}) collective-permute-start(bf16[16,640]{1,0:T(8,128)(2,1)} %get-tuple-element.27), channel_id=1, source_target_pairs={{0,1},{1,2},{2,3},{3,4},{4,5},{5,6},{6,7},{7,0},{8,9},{9,10},{10,1... | collective-permute-start | bytes 61448 | tf_op jit(solution)/shard_map/ppermute | solution.py:314
  8.0 9.8 %collective-permute-start.3 = (bf16[16,640]{1,0:T(8,128)(2,1)}, bf16[16,640]{1,0:T(8,128)(2,1)S(1)}, u32[]{:S(2)}, u32[]{:S(2)}) collective-permute-start(bf16[16,640]{1,0:T(8,128)(2,1)} %get-tuple-element.28), channel_id=1, source_target_pairs={{0,7},{1,0},{2,1},{3,2},{4,3},{5,4},{6,5},{7,6},{8,15},{9,8},{10,9... | collective-permute-start | bytes 61448 | tf_op jit(solution)/shard_map/ppermute | solution.py:314
  11.1 0.7 copy-start.5
  11.7 0.7 copy-start.1
  12.4 0.8 copy-start.3
  42.4 3.3 %collective-permute-start.4 = (bf16[16,576]{1,0:T(8,128)(2,1)S(1)}, bf16[16,576]{1,0:T(8,128)(2,1)S(1)}, u32[]{:S(2)}, u32[]{:S(2)}) collective-permute-start(bf16[16,576]{1,0:T(8,128)(2,1)S(1)} %get-tuple-element.30), channel_id=1, source_target_pairs={{0,8},{8,16},{16,24},{24,0},{1,9},{9,17},{17,25},{25,1},{2,10},{10... | collective-permute-start | bytes 55304 | tf_op jit(solution)/shard_map/ppermute | solution.py:314
  42.5 3.2 %collective-permute-start.5 = (bf16[16,576]{1,0:T(8,128)(2,1)S(1)}, bf16[16,576]{1,0:T(8,128)(2,1)S(1)}, u32[]{:S(2)}, u32[]{:S(2)}) collective-permute-start(bf16[16,576]{1,0:T(8,128)(2,1)S(1)} %get-tuple-element.31), channel_id=1, source_target_pairs={{0,24},{8,0},{16,8},{24,16},{1,25},{9,1},{17,9},{25,17},{2,26},{10... | collective-permute-start | bytes 55304 | tf_op jit(solution)/shard_map/ppermute | solution.py:314
  45.9 6.5 %collective-permute-start.6 = (bf16[16,576]{1,0:T(8,128)(2,1)S(1)}, bf16[16,576]{1,0:T(8,128)(2,1)S(1)}, u32[]{:S(2)}, u32[]{:S(2)}) collective-permute-start(bf16[16,576]{1,0:T(8,128)(2,1)S(1)} %get-tuple-element.33), channel_id=1, source_target_pairs={{0,1},{1,2},{2,3},{3,4},{4,5},{5,6},{6,7},{7,0},{8,9},{9,10},{10,1... | collective-permute-start | bytes 55304 | tf_op jit(solution)/shard_map/ppermute | solution.py:314
  46.7 5.7 %collective-permute-start.7 = (bf16[16,576]{1,0:T(8,128)(2,1)S(1)}, bf16[16,576]{1,0:T(8,128)(2,1)S(1)}, u32[]{:S(2)}, u32[]{:S(2)}) collective-permute-start(bf16[16,576]{1,0:T(8,128)(2,1)S(1)} %get-tuple-element.34), channel_id=1, source_target_pairs={{0,7},{1,0},{2,1},{3,2},{4,3},{5,4},{6,5},{7,6},{8,15},{9,8},{10,9... | collective-permute-start | bytes 55304 | tf_op jit(solution)/shard_map/ppermute | solution.py:314
  53.6 21.3 %copy-start.2 = (f32[16,256]{1,0:T(8,128)S(1)}, f32[16,256]{1,0:T(8,128)}, u32[]{:S(2)}) copy-start(f32[16,256]{1,0:T(8,128)} %get-tuple-element.20.small_ref) | copy-start | bytes 49156

commit v3 on v2

v3 whole, which is shorter than its diff:
```python
import functools

import jax
import jax.numpy as jnp
from jax import lax
from jax.experimental import pallas as pl
from jax.experimental.pallas import tpu as pltpu
from jax.sharding import PartitionSpec as P

TILE = 64
FX = 8
FY = 8
FZ = 128
COLS = FX * FY
LANES = 128
GROUP = 256
CHUNK = 2048
VMEM = 48 * 1024 * 1024
LARGE = 63 * 1024 * 1024

NT = (((1,), (1,)), ((), ()))
TN = (((0,), (0,)), ((), ()))


def iota(shape, dim):
    return lax.broadcasted_iota(jnp.int32, shape, dim)


def dot(a, b, dims=(((1,), (0,)), ((), ()))):
    return lax.dot_general(a, b, dims, preferred_element_type=jnp.float32)


def one_hot(mask):
    return jnp.where(mask, 1.0, 0.0).astype(jnp.bfloat16)


def equal(rows, row):
    numbers = iota((rows, row.shape[1]), 0).astype(jnp.float32).astype(jnp.bfloat16)
    return numbers == row.astype(jnp.float32).astype(jnp.bfloat16)


def ones(mask):
    return jnp.where(mask, jnp.bfloat16(1), jnp.bfloat16(0))


def fetch(sources, targets, sems):
    copies = [
        pltpu.make_async_copy(source, target, sems.at[i])
        for i, (source, target) in enumerate(zip(sources, targets))
    ]
    for copy in copies:
        copy.start()
    return copies


def pieces(hbm, vmem):
    width = hbm.shape[1] // 4
    cuts = [slice(k * width, (k + 1) * width) for k in range(4)]
    return [hbm.at[:, cut] for cut in cuts], [vmem.at[:, cut] for cut in cuts]


def leaving_row(index_ref, count_ref, parts):
    migr = index_ref.shape[1]
    lane = iota((1, migr), 1)
    rows = [jnp.where(lane < count_ref[0, r], index_ref[r : r + 1, :], parts) for r in range(4)]
    return jnp.concatenate(rows, axis=1)


def small_rows(rows, groups, slots):
    live = 2 * rows
    cells = live + groups
    return rows, live, cells, cells + slots // GROUP


def pick_kernel(
    part_hbm, index_hbm, count_hbm, size_hbm, owner_hbm, offset_hbm, closure_hbm, damping_hbm, cell_hbm, *refs
):
    out_refs, small_ref, refs = refs[:4], refs[4], refs[5:]
    part_ref, index_ref, count_ref, size_ref, owner_ref, offset_ref = refs[:6]
    closure_ref, damping_ref, cell_ref, sems = refs[6:]
    channels, parts = part_ref.shape
    migr = index_ref.shape[1]
    slots = cell_ref.shape[1]
    groups = parts // GROUP
    rows, width = closure_ref.shape
    closure_row, live_row, cell_row, _ = small_rows(rows, groups, slots)
    sources, targets = pieces(part_hbm, part_ref)
    copies = fetch(
        [index_hbm, count_hbm, size_hbm, owner_hbm, offset_hbm, closure_hbm, damping_hbm, cell_hbm] + sources,
        [index_ref, count_ref, size_ref, owner_ref, offset_ref, closure_ref, damping_ref, cell_ref] + targets,
        sems,
    )
    for copy in copies[:8]:
        copy.wait()
    for row, ref in enumerate((size_ref, owner_ref, offset_ref)):
        small_ref[row : row + 1, :] = ref[...].astype(jnp.float32)
    small_ref[closure_row:live_row, :width] = closure_ref[...]
    diagonal = iota((rows, rows), 0) == iota((rows, rows), 1)
    damping = jnp.sum(jnp.where(diagonal, damping_ref[...], 0.0), axis=1, keepdims=True)
    small_ref[closure_row:live_row, width : width + 1] = damping
    for k in range(slots // GROUP):
        row = cell_ref[:, k * GROUP : (k + 1) * GROUP]
        small_ref[cell_row + k : cell_row + k + 1, :] = row.astype(jnp.float32)
    leave = leaving_row(index_ref, count_ref, parts)
    high = leave // GROUP
    low = ones(equal(GROUP, leave % GROUP))
    small_ref[live_row:cell_row, :] = 1.0 - dot(ones(equal(groups, high)), low, NT)
    for copy in copies[8:]:
        copy.wait()
    table = jnp.concatenate(
        [part_ref[:, g * GROUP : (g + 1) * GROUP].astype(jnp.bfloat16) for g in range(groups)], axis=0
    )
    rows = dot(table, low)
    picked = jnp.zeros((channels, 4 * migr), jnp.float32)
    for g in range(groups):
        picked = jnp.where(high == g, rows[g * channels : (g + 1) * channels], picked)
    live = jnp.where(leave < parts, 1.0, 0.0)
    for r in range(4):
        out_refs[r][:, :migr] = picked[:, r * migr : (r + 1) * migr].astype(jnp.bfloat16)
        flags = [live[:, k : k + LANES] for k in range(r * migr, (r + 1) * migr, LANES)]
        flags.append(jnp.zeros((channels - len(flags), LANES), jnp.float32))
        out_refs[r][:, migr:] = jnp.concatenate(flags, axis=0).astype(jnp.bfloat16)


def mix(closure, state):
    state = state.astype(jnp.float32)
    mixed = closure[:, 0:1] * state[0:1]
    for f in range(1, state.shape[0]):
        mixed = mixed + closure[:, f : f + 1] * state[f : f + 1]
    return mixed, state[0:1]


def side_by_side(ref, first, begin, width):
    first = first + begin // GROUP
    rows = [ref[r : r + 1, :] for r in range(first, first + width // GROUP)]
    return jnp.concatenate(rows, axis=1)


def spread(mixed, first, place):
    hit = equal(TILE, place)
    values = jnp.concatenate([mixed, first], axis=0).astype(jnp.bfloat16)
    return jnp.concatenate(
        [jnp.where(hit, values[r : r + 1], jnp.bfloat16(0)) for r in range(values.shape[0])], axis=0
    )


def deposit_kernel(
    capacity, rows, part_ref, small_ref, sum_ref, code_ref, slot_ref, mark_ref, columns_ref,
):
    channels, parts = part_ref.shape
    slots = code_ref.shape[1]
    tiles = slot_ref.shape[1]
    closure_row, live_row, cell_row, _ = small_rows(rows, parts // GROUP, slots)
    closure = small_ref[closure_row:live_row, :channels]

    square = (tiles, tiles)
    below, across = iota(square, 0), iota(square, 1)

    def column(row):
        return jnp.sum(jnp.where(below == across, row, 0), axis=1, keepdims=True)

    sizes, owners, offset = [small_ref[r : r + 1, :].astype(jnp.int32) for r in range(3)]
    start = jnp.sum(jnp.where(across < below, sizes, 0), axis=1, keepdims=True)
    height = column(offset % FZ)
    code = iota((tiles, 1), 0) * TILE + (height - start) % TILE
    code_step = code - jnp.concatenate([jnp.zeros((1, 1), jnp.int32), code[: tiles - 1]], axis=0)
    earlier = (column(owners) == owners) & (below < across)
    rank = jnp.sum(jnp.where(earlier, 1, 0), axis=0, keepdims=True)
    slot_ref[...] = owners * capacity + rank
    columns_ref[0] = jnp.broadcast_to(start, (tiles, LANES))
    columns_ref[1] = jnp.broadcast_to(code_step, (tiles, LANES))
    rows = iota(mark_ref.shape, 0)
    marks = jnp.where(rows == 0, offset // FZ, jnp.where(rows == 1, offset % FZ, 0))
    mark_ref[...] = marks.astype(jnp.float32).astype(jnp.bfloat16)

    def find(begin):
        cell = side_by_side(small_ref, cell_row, begin, CHUNK).astype(jnp.int32)
        starts = jnp.concatenate([columns_ref[0]] * (CHUNK // LANES), axis=1)
        steps = jnp.concatenate([columns_ref[1]] * (CHUNK // LANES), axis=1)
        found = jnp.sum(jnp.where(cell >= starts, steps, 0), axis=0, keepdims=True)
        return found // TILE, (found + cell) % TILE

    for begin in range(parts, slots, CHUNK):
        tile, place = find(begin)
        code_ref[:, begin : begin + CHUNK] = tile * TILE + place
    for begin in range(0, parts, CHUNK):
        tile, place = find(begin)
        code_ref[:, begin : begin + CHUNK] = tile * TILE + place
        live = side_by_side(small_ref, live_row, begin, CHUNK)
        state = part_ref[:, begin : begin + CHUNK] * live
        mixed, first = mix(closure, state.astype(jnp.bfloat16))
        added = dot(spread(mixed, first, place), ones(equal(tiles, tile)), NT)
        if begin == 0:
            sum_ref[...] = added
        else:
            sum_ref[...] += added


def pack_kernel(rows, sum_ref, code_ref, slot_ref, mark_ref, small_ref, *refs):
    state_refs, out_ref = refs[:4], refs[4]
    channels, tiles = state_refs[0].shape[0], slot_ref.shape[1]
    closure = small_ref[rows : 2 * rows, :channels]
    migr = state_refs[0].shape[1] - LANES
    code = code_ref[:, code_ref.shape[1] - 4 * migr :]
    state = jnp.concatenate([ref[:, :migr] for ref in state_refs], axis=1)
    mixed, first = mix(closure, state)
    total = sum_ref[...] + dot(spread(mixed, first, code % TILE), ones(equal(tiles, code // TILE)), NT)
    table = jnp.concatenate([total.astype(jnp.bfloat16), mark_ref[...]], axis=0)
    match = one_hot(iota((out_ref.shape[0], tiles), 0) == slot_ref[...])
    out_ref[...] = dot(match, table, NT).astype(jnp.bfloat16)


def is_even(axis):
    return lax.axis_index(axis) % 2 == 0


def exchange(block_a, block_b, axis):
    size = lax.axis_size(axis)
    blocks = []
    for odd, block in enumerate((block_a, block_b)):
        pairs = [(i, (i + 1) % size if i % 2 == odd else (i - 1) % size) for i in range(size)]
        blocks.append(lax.ppermute(block, axis, pairs))
    return blocks


def place_kernel(tile_ref, gas_ref, xa_ref, xb_ref):
    even = is_even("gx")
    count, lanes = tile_ref.shape
    width = gas_ref.shape[1] // 2
    marks = tile_ref[:, lanes - LANES :].astype(jnp.float32)
    column = marks[:, width % LANES : width % LANES + 1]
    height = marks[:, width % LANES + 1 : width % LANES + 2]
    lane = iota((1, LANES), 1)
    hot = one_hot(column == lane.astype(jnp.float32))
    place = (iota((1, width), 1) % TILE).astype(jnp.float32)
    values = tile_ref[:, :width].astype(jnp.float32)
    for half, mask in enumerate((place >= height, place < height)):
        total = dot(hot, jnp.where(mask, values, 0.0).astype(jnp.bfloat16), TN)
        where = slice(half * width, (half + 1) * width)
        gas_ref[:, where] = total[:COLS]
        rows = slice(half * FY, (half + 1) * FY)
        low, high = total[:FY], total[COLS - FY : COLS]
        xa_ref[rows, :] = jnp.where(even, high, low).astype(jnp.bfloat16)
        xb_ref[rows, :] = jnp.where(even, low, high).astype(jnp.bfloat16)


def unfold(ref):
    edge = ref[...].astype(jnp.float32)
    half = edge.shape[0] // 2
    return jnp.concatenate([edge[:half], edge[half:]], axis=1)


def along_kernel(gas_ref, xa_ref, xb_ref, out_ref, ya_ref, yb_ref):
    even = is_even("gx")
    xa, xb = unfold(xa_ref), unfold(xb_ref)
    blocks = [gas_ref[x * FY : (x + 1) * FY, :] for x in range(FX)]
    blocks = [jnp.where(even, xb, xa)] + blocks + [jnp.where(even, xa, xb)]
    along = [blocks[x] + 2.0 * blocks[x + 1] + blocks[x + 2] for x in range(FX)]
    for x in range(FX):
        out_ref[x * FY : (x + 1) * FY, :] = along[x]
    width = ya_ref.shape[1]
    edges = []
    for row in (0, FY - 1):
        edge = jnp.concatenate([along[x][row : row + 1] for x in range(FX)], axis=0)
        edges.append(jnp.concatenate([edge[:, :width], edge[:, width:]], axis=0))
    even = is_even("gy")
    ya_ref[...] = jnp.where(even, edges[1], edges[0]).astype(jnp.bfloat16)
    yb_ref[...] = jnp.where(even, edges[0], edges[1]).astype(jnp.bfloat16)


def drag_kernel(mark_ref, along_ref, ya_ref, yb_ref, drag_ref, back_ref):
    rows = drag_ref.shape[0]
    width = along_ref.shape[1] // 2
    lanes = rows * TILE
    even = is_even("gy")
    ya, yb = unfold(ya_ref), unfold(yb_ref)
    before, after = jnp.where(even, yb, ya), jnp.where(even, ya, yb)
    smooth = []
    for x in range(FX):
        block = along_ref[x * FY : (x + 1) * FY, :]
        padded = jnp.concatenate([before[x : x + 1], block, after[x : x + 1]], axis=0)
        smooth.append((padded[0:FY] + 2.0 * block + padded[2 : FY + 2]) / 16.0)
    smooth = jnp.concatenate(smooth, axis=0)
    halves = []
    for half in range(2):
        base = half * width
        density = smooth[:, base + lanes : base + lanes + TILE]
        below = 1.0 + density * density
        below = jnp.concatenate([below] * rows, axis=1)
        halves.append(smooth[:, base : base + lanes] / below)
    for r in range(rows):
        where = slice(r * TILE, (r + 1) * TILE)
        both = jnp.concatenate([halves[0][:, where], halves[1][:, where]], axis=1)
        drag_ref[r] = both.reshape(FX, FY, FZ).astype(jnp.bfloat16)
    mark = width % LANES
    marks = mark_ref[...].astype(jnp.float32)
    column, height = marks[:, mark : mark + 1], marks[:, mark + 1 : mark + 2]
    hot = one_hot(column == iota((1, COLS), 1).astype(jnp.float32))
    place = (iota((1, lanes), 1) % TILE).astype(jnp.float32)
    low = dot(hot, halves[0].astype(jnp.bfloat16))
    high = dot(hot, halves[1].astype(jnp.bfloat16))
    back_ref[...] = jnp.where(place >= height, low, high).astype(jnp.bfloat16)


def force_kernel(back_ref, slot_ref, code_ref, part_ref, small_ref, *refs):
    state_refs, out_ref, table_ref = refs[:4], refs[4], refs[5]
    rows, slots = out_ref.shape
    parts = part_ref.shape[1]
    tiles = slot_ref.shape[1]
    migr = (slots - parts) // 4
    match = one_hot(iota((back_ref.shape[0], tiles), 0) == slot_ref[...])
    table_ref[...] = dot(back_ref[...], match, TN).astype(jnp.bfloat16)
    channels = part_ref.shape[0]
    closure_row, live_row, _, _ = small_rows(rows, parts // GROUP, slots)
    damping = small_ref[closure_row:live_row, channels : channels + 1]

    def look(code):
        values = dot(table_ref[...], ones(equal(tiles, code // TILE))).astype(jnp.bfloat16)
        hit = equal(TILE, code % TILE)
        found = []
        for r in range(rows):
            picked = jnp.where(hit, values[r * TILE : (r + 1) * TILE], jnp.bfloat16(0))
            while picked.shape[0] > 16:
                half = picked.shape[0] // 2
                picked = picked[:half] + picked[half:]
            found.append(jnp.sum(picked.astype(jnp.float32), axis=0, keepdims=True))
        return jnp.concatenate(found, axis=0)

    for begin in range(0, parts, CHUNK):
        where = slice(begin, begin + CHUNK)
        live = side_by_side(small_ref, live_row, begin, CHUNK)
        out_ref[:, where] = live * (look(code_ref[:, where]) - damping * part_ref[:rows, where])
    drag = look(code_ref[:, parts:])
    for row in range(4):
        begin = parts + row * migr
        arrived = state_refs[row][:, :].astype(jnp.float32)
        live = jnp.concatenate([arrived[k : k + 1, migr:] for k in range(migr // LANES)], axis=1)
        force = drag[:, row * migr : (row + 1) * migr] - damping * arrived[:rows, :migr]
        out_ref[:, begin : begin + migr] = live * force


def call(kernel, shapes, *operands, limit=None, scratch=()):
    vmem = pl.BlockSpec(memory_space=pltpu.VMEM)
    operand = pl.BlockSpec(memory_space=pltpu.HBM) if limit else vmem
    return pl.pallas_call(
        kernel,
        out_shape=shapes,
        in_specs=[operand] * len(operands),
        out_specs=[vmem] * len(shapes),
        scratch_shapes=scratch,
        compiler_params=pltpu.CompilerParams(vmem_limit_bytes=limit or VMEM),
    )(*operands)


def shift(block, axis, step):
    size = lax.axis_size(axis)
    return lax.ppermute(block, axis, [(i, (i + step) % size) for i in range(size)])


def per_device(
    particles,
    migrant_index,
    migrant_count,
    migrated_slot_cell,
    source_tile_size,
    tile_owner,
    tile_offset,
    closure,
    damping,
):
    f32, bf16, i32 = jnp.float32, jnp.bfloat16, jnp.int32
    shape = jax.ShapeDtypeStruct
    channels, parts = particles.shape
    rows = closure.shape[0]
    migr = migrant_index.shape[1]
    slots = migrated_slot_cell.shape[0]
    tiles = source_tile_size.shape[1]
    devices = lax.axis_size("gx") * lax.axis_size("gy")
    capacity = max(2, 2 * tiles // devices)
    count = devices * capacity
    width = (rows + 1) * TILE
    lanes = (width + LANES) // LANES * LANES
    small_count = small_rows(rows, parts // GROUP, slots)[-1]
    operands = (
        particles, migrant_index, migrant_count, source_tile_size, tile_owner.reshape(1, tiles),
        tile_offset.reshape(1, tiles), closure, damping.reshape(1, rows), migrated_slot_cell.reshape(1, slots),
    )
    *leaving, small = call(
        pick_kernel,
        [shape((channels, migr + LANES), bf16)] * 4 + [shape((small_count, GROUP), f32)],
        *operands, limit=LARGE,
        scratch=[(pltpu.SMEM if i == 2 else pltpu.VMEM)(x.shape, x.dtype) for i, x in enumerate(operands)]
        + [pltpu.SemaphoreType.DMA((12,))],
    )
    arrived = [
        shift(block, axis, step)
        for block, (axis, step) in zip(leaving, (("gx", 1), ("gx", -1), ("gy", 1), ("gy", -1)))
    ]
    sums, code, slot, marks = call(
        functools.partial(deposit_kernel, capacity, rows),
        [shape((width, tiles), f32), shape((1, slots), i32), shape((1, tiles), i32),
         shape((lanes - width, tiles), bf16)],
        particles, small, scratch=[pltpu.VMEM((2, tiles, LANES), i32)],
    )
    (payload,) = call(
        functools.partial(pack_kernel, rows), [shape((count, lanes), bf16)],
        sums, code, slot, marks, small, *arrived,
    )
    received = lax.all_to_all(
        payload.reshape(devices, capacity, lanes), ("gx", "gy"), split_axis=0, concat_axis=0, tiled=True
    ).reshape(count, lanes)
    grid, edge = shape((COLS, 2 * width), f32), shape((2 * FX, width), bf16)
    gas, xa, xb = call(place_kernel, [grid, edge, edge], received)
    xa, xb = exchange(xa, xb, "gx")
    along, ya, yb = call(along_kernel, [grid, edge, edge], gas, xa, xb)
    ya, yb = exchange(ya, yb, "gy")
    drag, back = call(
        drag_kernel,
        [shape((rows, FX, FY, FZ), bf16), shape((count, rows * TILE), bf16)],
        received[:, lanes - LANES :], along, ya, yb,
    )
    returned = lax.all_to_all(
        back.reshape(devices, capacity, rows * TILE), ("gx", "gy"), split_axis=0, concat_axis=0, tiled=True
    ).reshape(count, rows * TILE)
    (force,) = call(
        force_kernel, [shape((rows, slots), f32)],
        returned, slot, code, particles, small, *arrived,
        scratch=[pltpu.VMEM((rows * TILE, tiles), bf16)],
    )
    return drag, force


def solution(mesh):
    both = ("gx", "gy")
    in_specs = (
        P(None, both),
        P(both, None),
        P(both, None),
        P(both),
        P(both, None),
        P(both, None),
        P(both),
        P(),
        P(),
    )
    out_specs = (P(None, "gx", "gy", None), P(None, both))
    return jax.shard_map(
        per_device, mesh=mesh, in_specs=in_specs, out_specs=out_specs, check_vma=False
    )
```

time: 79.2 us -> 76.6 us (0.967)
  waiting for transfers between devices: 3.22 us -> 7.5 us
  starting transfers between devices: 14.4 us -> 11.1 us
  blocking collectives: 43.5 us -> 41.5 us
  local copies, waits for them, and re-layouts: 2.17 us -> 0.91 us
    ppermute x0 -> x4, waiting for transfers between devices: none -> 7.49 us  [exchange(): blocks.append(lax.ppermute(block, axis, pairs))]
    ppermute x8 -> x4, starting transfers between devices: 14.4 us -> 7.81 us  [shift(): lax.ppermute(block, axis, [(i, (i + step) % size) for i in range(size)])]
    ppermute x0 -> x4, starting transfers between devices: none -> 3.25 us  [exchange(): blocks.append(lax.ppermute(block, axis, pairs))]
    ppermute x8 -> x4, waiting for transfers between devices: 3.22 us -> 0.01 us  [shift(): lax.ppermute(block, axis, [(i, (i + step) % size) for i in range(size)])]
    all_to_all x1, blocking collectives: 21.2 us -> 19 us  [per_device(): lax.all_to_all(back.reshape(devices, capacity, rows * TILE), ('gx', 'gy')...]
    unnamed x12 -> x6, local copies, waits for them, and re-layouts: 2.16 us -> 0.9 us
  transfers between devices with their start and end apart: 8 -> 8, of which waited for: 2 -> 4; matrix products, arithmetic and copies ran while one was open for 0% -> 0% of each run, Pallas kernels for 6% -> 5%
where the time goes in v3:
time: 76.6 us; the launch traced here: 76.4 us
  blocking collectives  41.5 us (54%)
  Pallas kernels  14.7 us (19%)
  starting transfers between devices  11.1 us (14%)
  waiting for transfers between devices  7.5 us (10%)
  local copies, waits for them, and re-layouts  0.91 us (1%)
    all_to_all x1, blocking collectives, per_device(): lax.all_to_all(payload.reshape(devices, capacity, lanes), ('gx', 'gy'), s...  22.5 us
    all_to_all x1, blocking collectives, per_device(): lax.all_to_all(back.reshape(devices, capacity, rows * TILE), ('gx', 'gy')...  19 us
    pallas_call x7, Pallas kernels, call(): pl.pallas_call(kernel, out_shape=shapes, in_specs=[operand] * len(operand...  14.7 us
    ppermute x4, starting transfers between devices, shift(): lax.ppermute(block, axis, [(i, (i + step) % size) for i in range(size)])  7.81 us
    ppermute x4, waiting for transfers between devices, exchange(): blocks.append(lax.ppermute(block, axis, pairs))  7.49 us
    ppermute x4, starting transfers between devices, exchange(): blocks.append(lax.ppermute(block, axis, pairs))  3.25 us
  transfers between devices with their start and end apart: 8, of which 4 were waited for; matrix products, arithmetic and copies ran while one was open for 0% of the time, Pallas kernels for 5%

profile of v3, /device:TPU:0, one launch (start us, length us, event | category | flops | bytes accessed | tf_op | source)
XLA Modules:
  0.0 76.4 jit_solution(6613777517298870469)
XLA Ops:
  0.6 0.0 copy-start
  0.6 3.4 %shard_map.104 = (bf16[16,640]{1,0:T(8,128)(2,1)}, bf16[16,640]{1,0:T(8,128)(2,1)}, bf16[16,640]{1,0:T(8,128)(2,1)}, bf16[16,640]{1,0:T(8,128)(2,1)}, f32[88,256]{1,0:T(8,128)}) custom-call(f32[16,8192]{1,0:T(8,128)} %part_ref.3, s32[4,512]{1,0:T(4,128)} %index_hbm.1, s32[1,4]{1,0:T(1,128)} %count_hbm.1, s32[1,256]{1,0:T(1,128)} %size_hbm.1, ...), custom_call_target="tpu_custom_call" | custom-call | tf_op jit(solution)/shard_map/pallas_call | solution.py:345
  4.0 0.5 collective-permute-start
  4.5 2.0 %collective-permute-start.1 = (bf16[16,640]{1,0:T(8,128)(2,1)}, bf16[16,640]{1,0:T(8,128)(2,1)S(1)}, u32[]{:S(2)}, u32[]{:S(2)}) collective-permute-start(bf16[16,640]{1,0:T(8,128)(2,1)} %get-tuple-element.25), channel_id=1, source_target_pairs={{0,24},{8,0},{16,8},{24,16},{1,25},{9,1},{17,9},{25,17},{2,26},{10... | collective-permute-start | bytes 61448 | tf_op jit(solution)/shard_map/ppermute | solution.py:357
  6.5 2.3 %collective-permute-start.2 = (bf16[16,640]{1,0:T(8,128)(2,1)}, bf16[16,640]{1,0:T(8,128)(2,1)S(1)}, u32[]{:S(2)}, u32[]{:S(2)}) collective-permute-start(bf16[16,640]{1,0:T(8,128)(2,1)} %get-tuple-element.26), channel_id=1, source_target_pairs={{0,1},{1,2},{2,3},{3,4},{4,5},{5,6},{6,7},{7,0},{8,9},{9,10},{10,1... | collective-permute-start | bytes 61448 | tf_op jit(solution)/shard_map/ppermute | solution.py:357
  8.8 3.0 %collective-permute-start.3 = (bf16[16,640]{1,0:T(8,128)(2,1)}, bf16[16,640]{1,0:T(8,128)(2,1)S(1)}, u32[]{:S(2)}, u32[]{:S(2)}) collective-permute-start(bf16[16,640]{1,0:T(8,128)(2,1)} %get-tuple-element.27), channel_id=1, source_target_pairs={{0,7},{1,0},{2,1},{3,2},{4,3},{5,4},{6,5},{7,6},{8,15},{9,8},{10,9... | collective-permute-start | bytes 61448 | tf_op jit(solution)/shard_map/ppermute | solution.py:357
  11.8 0.0 copy-done
  11.8 0.0 copy-start.1
  11.8 0.9 %copy-done.1 = f32[88,256]{1,0:T(8,128)S(1)} copy-done((f32[88,256]{1,0:T(8,128)S(1)}, f32[88,256]{1,0:T(8,128)}, u32[]{:S(2)}) %copy-start.1) | copy-done | bytes 90136
  12.7 3.7 %shard_map.105 = (f32[576,256]{1,0:T(8,128)S(1)}, s32[1,10240]{1,0:T(1,128)S(1)}, s32[1,256]{1,0:T(1,128)S(1)}, bf16[64,256]{1,0:T(8,128)(2,1)S(1)}) custom-call(f32[16,8192]{1,0:T(8,128)S(1)} %copy-done, f32[88,256]{1,0:T(8,128)S(1)} %copy-done.1), custom_call_target="tpu_custom_call" | custom-call | tf_op jit(solution)/shard_map/pallas_call | solution.py:345
  16.4 0.0 collective-permute-done.refs_0_
  16.4 0.0 collective-permute-done.1.refs_1_
  16.4 0.0 collective-permute-done.2.refs_2_
  16.4 0.0 collective-permute-done.3.refs_3_
  16.4 1.6 %shard_map.106 = bf16[512,640]{1,0:T(8,128)(2,1)S(1)} custom-call(f32[576,256]{1,0:T(8,128)S(1)} %get-tuple-element.20.sum_ref, s32[1,10240]{1,0:T(1,128)S(1)} %get-tuple-element.21.code_ref, s32[1,256]{1,0:T(1,128)S(1)} %get-tuple-element.22.slot_ref, bf16[64,256]{1,0:T(8,128)(2,1)S(1)} %get-tuple-element.23.mark_ref, f32[88,256]{1,0:T(8,128)S(1)} %copy-done.1, ...), custom_call_target="tpu_custom_call" | custom-call | tf_op jit(solution)/shard_map/pallas_call | solution.py:345
  18.0 22.5 %all_to_all.10 = bf16[32,16,640]{2,1,0:T(8,128)(2,1)S(1)} all-to-all(bf16[32,16,640]{2,1,0:T(8,128)(2,1)S(1)} %bitcast.10), channel_id=1, replica_groups=mesh['gx'=4,'gy'=8] {'gx','gy'}, dimensions={0} | all-to-all | bytes 1310720 | tf_op jit(solution)/shard_map/all_to_all | solution.py:409
  40.6 0.6 shard_map.107
  41.2 0.1 collective-permute-start.4
  41.3 0.6 collective-permute-start.5
  41.9 0.5 collective-permute-done.4.xa_ref
  42.4 2.1 %collective-permute-done.5.xb_ref = bf16[16,576]{1,0:T(8,128)(2,1)S(1)} collective-permute-done((bf16[16,576]{1,0:T(8,128)(2,1)S(1)}, bf16[16,576]{1,0:T(8,128)(2,1)S(1)}, u32[]{:S(2)}, u32[]{:S(2)}) %collective-permute-start.5) | collective-permute-done | bytes 18464 | tf_op jit(solution)/shard_map/ppermute | solution.py:222
  44.5 0.2 shard_map.108
  44.7 0.9 %collective-permute-start.6 = (bf16[16,576]{1,0:T(8,128)(2,1)S(1)}, bf16[16,576]{1,0:T(8,128)(2,1)S(1)}, u32[]{:S(2)}, u32[]{:S(2)}) collective-permute-start(bf16[16,576]{1,0:T(8,128)(2,1)S(1)} %get-tuple-element.32), channel_id=1, source_target_pairs={{0,1},{1,0},{2,3},{3,2},{4,5},{5,4},{6,7},{7,6},{8,9},{9,8},{10,11... | collective-permute-start | bytes 55304 | tf_op jit(solution)/shard_map/ppermute | solution.py:222
  45.7 1.6 %collective-permute-start.7 = (bf16[16,576]{1,0:T(8,128)(2,1)S(1)}, bf16[16,576]{1,0:T(8,128)(2,1)S(1)}, u32[]{:S(2)}, u32[]{:S(2)}) collective-permute-start(bf16[16,576]{1,0:T(8,128)(2,1)S(1)} %get-tuple-element.33), channel_id=1, source_target_pairs={{0,7},{1,2},{2,1},{3,4},{4,3},{5,6},{6,5},{7,0},{8,15},{9,10},{10,... | collective-permute-start | bytes 55304 | tf_op jit(solution)/shard_map/ppermute | solution.py:222
  47.3 1.3 %collective-permute-done.6.ya_ref = bf16[16,576]{1,0:T(8,128)(2,1)S(1)} collective-permute-done((bf16[16,576]{1,0:T(8,128)(2,1)S(1)}, bf16[16,576]{1,0:T(8,128)(2,1)S(1)}, u32[]{:S(2)}, u32[]{:S(2)}) %collective-permute-start.6) | collective-permute-done | bytes 18464 | tf_op jit(solution)/shard_map/ppermute | solution.py:222
  48.6 3.6 %collective-permute-done.7.yb_ref = bf16[16,576]{1,0:T(8,128)(2,1)S(1)} collective-permute-done((bf16[16,576]{1,0:T(8,128)(2,1)S(1)}, bf16[16,576]{1,0:T(8,128)(2,1)S(1)}, u32[]{:S(2)}, u32[]{:S(2)}) %collective-permute-start.7) | collective-permute-done | bytes 18464 | tf_op jit(solution)/shard_map/ppermute | solution.py:222
  52.2 1.2 %shard_map.109 = (bf16[8,8,8,128]{3,2,1,0:T(8,128)(2,1)}, bf16[512,512]{1,0:T(8,128)(2,1)S(1)}) custom-call(bf16[512,128]{1,0:T(8,128)(2,1)S(1)} %slice.4.mark_ref, f32[64,1152]{1,0:T(8,128)S(1)} %get-tuple-element.31.along_ref, bf16[16,576]{1,0:T(8,128)(2,1)S(1)} %collective-permute-done.6.ya_ref, bf16[16,576]{1,0:T(8,128)(2,1)S(1)} %collective-permute-done.7.yb_ref), custom_call_target="tpu_custom_call" | custom-call | tf_op jit(solution)/shard_map/pallas_call | solution.py:345
  53.3 0.0 copy-start.2
  53.3 19.0 %all_to_all.11 = bf16[32,16,512]{2,1,0:T(8,128)(2,1)S(1)} all-to-all(bf16[32,16,512]{2,1,0:T(8,128)(2,1)S(1)} %bitcast.12), channel_id=1, replica_groups=mesh['gx'=4,'gy'=8] {'gx','gy'}, dimensions={0} | all-to-all | bytes 1048576 | tf_op jit(solution)/shard_map/all_to_all | solution.py:422
  72.4 0.0 copy-done.2
  72.4 4.1 %shard_map.110 = f32[8,10240]{1,0:T(8,128)} custom-call(bf16[512,512]{1,0:T(8,128)(2,1)S(1)} %bitcast.11, s32[1,256]{1,0:T(1,128)S(1)} %get-tuple-element.22.slot_ref, s32[1,10240]{1,0:T(1,128)S(1)} %get-tuple-element.21.code_ref, f32[16,8192]{1,0:T(8,128)S(1)} %copy-done, f32[88,256]{1,0:T(8,128)S(1)} %copy-done.2, ...), custom_call_target="tpu_custom_call" | custom-call | tf_op jit(solution)/shard_map/pallas_call | solution.py:345
  (1 shorter events, 0.0 us)
Async XLA Ops:
  0.6 11.2 %copy-start = (f32[16,8192]{1,0:T(8,128)S(1)}, f32[16,8192]{1,0:T(8,128)}, u32[]{:S(2)}) copy-start(f32[16,8192]{1,0:T(8,128)} %part_ref.3) | copy-start | bytes 1572868
  4.0 12.4 %collective-permute-start = (bf16[16,640]{1,0:T(8,128)(2,1)}, bf16[16,640]{1,0:T(8,128)(2,1)S(1)}, u32[]{:S(2)}, u32[]{:S(2)}) collective-permute-start(bf16[16,640]{1,0:T(8,128)(2,1)} %get-tuple-element.24), channel_id=1, source_target_pairs={{0,8},{8,16},{16,24},{24,0},{1,9},{9,17},{17,25},{25,1},{2,10},{10... | collective-permute-start | bytes 61448 | tf_op jit(solution)/shard_map/ppermute | solution.py:357
  4.5 11.9 %collective-permute-start.1 = (bf16[16,640]{1,0:T(8,128)(2,1)}, bf16[16,640]{1,0:T(8,128)(2,1)S(1)}, u32[]{:S(2)}, u32[]{:S(2)}) collective-permute-start(bf16[16,640]{1,0:T(8,128)(2,1)} %get-tuple-element.25), channel_id=1, source_target_pairs={{0,24},{8,0},{16,8},{24,16},{1,25},{9,1},{17,9},{25,17},{2,26},{10... | collective-permute-start | bytes 61448 | tf_op jit(solution)/shard_map/ppermute | solution.py:357
  6.5 9.9 %collective-permute-start.2 = (bf16[16,640]{1,0:T(8,128)(2,1)}, bf16[16,640]{1,0:T(8,128)(2,1)S(1)}, u32[]{:S(2)}, u32[]{:S(2)}) collective-permute-start(bf16[16,640]{1,0:T(8,128)(2,1)} %get-tuple-element.26), channel_id=1, source_target_pairs={{0,1},{1,2},{2,3},{3,4},{4,5},{5,6},{6,7},{7,0},{8,9},{9,10},{10,1... | collective-permute-start | bytes 61448 | tf_op jit(solution)/shard_map/ppermute | solution.py:357
  8.8 7.6 %collective-permute-start.3 = (bf16[16,640]{1,0:T(8,128)(2,1)}, bf16[16,640]{1,0:T(8,128)(2,1)S(1)}, u32[]{:S(2)}, u32[]{:S(2)}) collective-permute-start(bf16[16,640]{1,0:T(8,128)(2,1)} %get-tuple-element.27), channel_id=1, source_target_pairs={{0,7},{1,0},{2,1},{3,2},{4,3},{5,4},{6,5},{7,6},{8,15},{9,8},{10,9... | collective-permute-start | bytes 61448 | tf_op jit(solution)/shard_map/ppermute | solution.py:357
  11.8 0.9 %copy-start.1 = (f32[88,256]{1,0:T(8,128)S(1)}, f32[88,256]{1,0:T(8,128)}, u32[]{:S(2)}) copy-start(f32[88,256]{1,0:T(8,128)} %get-tuple-element.19.small_ref) | copy-start | bytes 270340
  41.2 1.3 %collective-permute-start.4 = (bf16[16,576]{1,0:T(8,128)(2,1)S(1)}, bf16[16,576]{1,0:T(8,128)(2,1)S(1)}, u32[]{:S(2)}, u32[]{:S(2)}) collective-permute-start(bf16[16,576]{1,0:T(8,128)(2,1)S(1)} %get-tuple-element.29), channel_id=1, source_target_pairs={{0,8},{8,0},{16,24},{24,16},{1,9},{9,1},{17,25},{25,17},{2,10},{10... | collective-permute-start | bytes 55304 | tf_op jit(solution)/shard_map/ppermute | solution.py:222
  41.3 3.3 %collective-permute-start.5 = (bf16[16,576]{1,0:T(8,128)(2,1)S(1)}, bf16[16,576]{1,0:T(8,128)(2,1)S(1)}, u32[]{:S(2)}, u32[]{:S(2)}) collective-permute-start(bf16[16,576]{1,0:T(8,128)(2,1)S(1)} %get-tuple-element.30), channel_id=1, source_target_pairs={{0,24},{8,16},{16,8},{24,0},{1,25},{9,17},{17,9},{25,1},{2,26},{10... | collective-permute-start | bytes 55304 | tf_op jit(solution)/shard_map/ppermute | solution.py:222
  44.7 3.8 %collective-permute-start.6 = (bf16[16,576]{1,0:T(8,128)(2,1)S(1)}, bf16[16,576]{1,0:T(8,128)(2,1)S(1)}, u32[]{:S(2)}, u32[]{:S(2)}) collective-permute-start(bf16[16,576]{1,0:T(8,128)(2,1)S(1)} %get-tuple-element.32), channel_id=1, source_target_pairs={{0,1},{1,0},{2,3},{3,2},{4,5},{5,4},{6,7},{7,6},{8,9},{9,8},{10,11... | collective-permute-start | bytes 55304 | tf_op jit(solution)/shard_map/ppermute | solution.py:222
  45.7 6.5 %collective-permute-start.7 = (bf16[16,576]{1,0:T(8,128)(2,1)S(1)}, bf16[16,576]{1,0:T(8,128)(2,1)S(1)}, u32[]{:S(2)}, u32[]{:S(2)}) collective-permute-start(bf16[16,576]{1,0:T(8,128)(2,1)S(1)} %get-tuple-element.33), channel_id=1, source_target_pairs={{0,7},{1,2},{2,1},{3,4},{4,3},{5,6},{6,5},{7,0},{8,15},{9,10},{10,... | collective-permute-start | bytes 55304 | tf_op jit(solution)/shard_map/ppermute | solution.py:222
  53.3 19.0 %copy-start.2 = (f32[88,256]{1,0:T(8,128)S(1)}, f32[88,256]{1,0:T(8,128)}, u32[]{:S(2)}) copy-start(f32[88,256]{1,0:T(8,128)} %get-tuple-element.19.small_ref) | copy-start | bytes 270340

commit v4 on v3

--- a/solution.py
+++ b/solution.py
@@ -75,9 +75,9 @@
 def pick_kernel(
     part_hbm, index_hbm, count_hbm, size_hbm, owner_hbm, offset_hbm, closure_hbm, damping_hbm, cell_hbm, *refs
 ):
-    out_refs, small_ref, refs = refs[:4], refs[4], refs[5:]
+    out_hbm, small_hbm, refs = refs[:4], refs[4], refs[5:]
     part_ref, index_ref, count_ref, size_ref, owner_ref, offset_ref = refs[:6]
-    closure_ref, damping_ref, cell_ref, sems = refs[6:]
+    closure_ref, damping_ref, cell_ref, out_ref, small_ref, sems, out_sems = refs[6:]
     channels, parts = part_ref.shape
     migr = index_ref.shape[1]
     slots = cell_ref.shape[1]
@@ -90,7 +90,13 @@
         [index_ref, count_ref, size_ref, owner_ref, offset_ref, closure_ref, damping_ref, cell_ref] + targets,
         sems,
     )
-    for copy in copies[:8]:
+    copies[0].wait()
+    copies[1].wait()
+    leave = leaving_row(index_ref, count_ref, parts)
+    high = leave // GROUP
+    low = ones(equal(GROUP, leave % GROUP))
+    small_ref[live_row:cell_row, :] = 1.0 - dot(ones(equal(groups, high)), low, NT)
+    for copy in copies[2:8]:
         copy.wait()
     for row, ref in enumerate((size_ref, owner_ref, offset_ref)):
         small_ref[row : row + 1, :] = ref[...].astype(jnp.float32)
@@ -101,10 +107,8 @@
     for k in range(slots // GROUP):
         row = cell_ref[:, k * GROUP : (k + 1) * GROUP]
         small_ref[cell_row + k : cell_row + k + 1, :] = row.astype(jnp.float32)
-    leave = leaving_row(index_ref, count_ref, parts)
-    high = leave // GROUP
-    low = ones(equal(GROUP, leave % GROUP))
-    small_ref[live_row:cell_row, :] = 1.0 - dot(ones(equal(groups, high)), low, NT)
+    stores = [pltpu.make_async_copy(small_ref, small_hbm, out_sems.at[4])]
+    stores[0].start()
     for copy in copies[8:]:
         copy.wait()
     table = jnp.concatenate(
@@ -116,10 +120,14 @@
         picked = jnp.where(high == g, rows[g * channels : (g + 1) * channels], picked)
     live = jnp.where(leave < parts, 1.0, 0.0)
     for r in range(4):
-        out_refs[r][:, :migr] = picked[:, r * migr : (r + 1) * migr].astype(jnp.bfloat16)
+        out_ref[r, :, :migr] = picked[:, r * migr : (r + 1) * migr].astype(jnp.bfloat16)
         flags = [live[:, k : k + LANES] for k in range(r * migr, (r + 1) * migr, LANES)]
         flags.append(jnp.zeros((channels - len(flags), LANES), jnp.float32))
-        out_refs[r][:, migr:] = jnp.concatenate(flags, axis=0).astype(jnp.bfloat16)
+        out_ref[r, :, migr:] = jnp.concatenate(flags, axis=0).astype(jnp.bfloat16)
+        stores.append(pltpu.make_async_copy(out_ref.at[r], out_hbm[r], out_sems.at[r]))
+        stores[-1].start()
+    for store in stores:
+        store.wait()
 
 
 def mix(closure, state):
@@ -216,11 +224,11 @@
 
 def exchange(block_a, block_b, axis):
     size = lax.axis_size(axis)
-    blocks = []
-    for odd, block in enumerate((block_a, block_b)):
+    blocks = {}
+    for odd, block in ((1, block_b), (0, block_a)):
         pairs = [(i, (i + 1) % size if i % 2 == odd else (i - 1) % size) for i in range(size)]
-        blocks.append(lax.ppermute(block, axis, pairs))
-    return blocks
+        blocks[odd] = lax.ppermute(block, axis, pairs)
+    return blocks[0], blocks[1]
 
 
 def place_kernel(tile_ref, gas_ref, xa_ref, xb_ref):
@@ -285,9 +293,8 @@
     for half in range(2):
         base = half * width
         density = smooth[:, base + lanes : base + lanes + TILE]
-        below = 1.0 + density * density
-        below = jnp.concatenate([below] * rows, axis=1)
-        halves.append(smooth[:, base : base + lanes] / below)
+        scale = 1.0 / (1.0 + density * density)
+        halves.append(smooth[:, base : base + lanes] * jnp.concatenate([scale] * rows, axis=1))
     for r in range(rows):
         where = slice(r * TILE, (r + 1) * TILE)
         both = jnp.concatenate([halves[0][:, where], halves[1][:, where]], axis=1)
@@ -302,8 +309,10 @@
     back_ref[...] = jnp.where(place >= height, low, high).astype(jnp.bfloat16)
 
 
-def force_kernel(back_ref, slot_ref, code_ref, part_ref, small_ref, *refs):
-    state_refs, out_ref, table_ref = refs[:4], refs[4], refs[5]
+def force_kernel(back_ref, slot_ref, code_ref, part_ref, small_ref, drag_ref, *refs):
+    state_refs, out_ref, drag_hbm, table_ref, sem = refs[:4], refs[4], refs[5], refs[6], refs[7]
+    store = pltpu.make_async_copy(drag_ref, drag_hbm, sem)
+    store.start()
     rows, slots = out_ref.shape
     parts = part_ref.shape[1]
     tiles = slot_ref.shape[1]
@@ -337,16 +346,16 @@
         live = jnp.concatenate([arrived[k : k + 1, migr:] for k in range(migr // LANES)], axis=1)
         force = drag[:, row * migr : (row + 1) * migr] - damping * arrived[:rows, :migr]
         out_ref[:, begin : begin + migr] = live * force
-
-
-def call(kernel, shapes, *operands, limit=None, scratch=()):
-    vmem = pl.BlockSpec(memory_space=pltpu.VMEM)
-    operand = pl.BlockSpec(memory_space=pltpu.HBM) if limit else vmem
+    store.wait()
+
+
+def call(kernel, shapes, *operands, limit=None, late=(), scratch=()):
+    vmem, hbm = pl.BlockSpec(memory_space=pltpu.VMEM), pl.BlockSpec(memory_space=pltpu.HBM)
     return pl.pallas_call(
         kernel,
         out_shape=shapes,
-        in_specs=[operand] * len(operands),
-        out_specs=[vmem] * len(shapes),
+        in_specs=[hbm if limit else vmem] * len(operands),
+        out_specs=[hbm if limit or i in late else vmem for i in range(len(shapes))],
         scratch_shapes=scratch,
         compiler_params=pltpu.CompilerParams(vmem_limit_bytes=limit or VMEM),
     )(*operands)
@@ -390,7 +399,8 @@
         [shape((channels, migr + LANES), bf16)] * 4 + [shape((small_count, GROUP), f32)],
         *operands, limit=LARGE,
         scratch=[(pltpu.SMEM if i == 2 else pltpu.VMEM)(x.shape, x.dtype) for i, x in enumerate(operands)]
-        + [pltpu.SemaphoreType.DMA((12,))],
+        + [pltpu.VMEM((4, channels, migr + LANES), bf16), pltpu.VMEM((small_count, GROUP), f32),
+           pltpu.SemaphoreType.DMA((12,)), pltpu.SemaphoreType.DMA((5,))],
     )
     arrived = [
         shift(block, axis, step)
@@ -422,10 +432,10 @@
     returned = lax.all_to_all(
         back.reshape(devices, capacity, rows * TILE), ("gx", "gy"), split_axis=0, concat_axis=0, tiled=True
     ).reshape(count, rows * TILE)
-    (force,) = call(
-        force_kernel, [shape((rows, slots), f32)],
-        returned, slot, code, particles, small, *arrived,
-        scratch=[pltpu.VMEM((rows * TILE, tiles), bf16)],
+    force, drag = call(
+        force_kernel, [shape((rows, slots), f32), shape(drag.shape, bf16)],
+        returned, slot, code, particles, small, drag, *arrived, late=(1,),
+        scratch=[pltpu.VMEM((rows * TILE, tiles), bf16), pltpu.SemaphoreType.DMA],
     )
     return drag, force
 

time: 76.6 us -> 76.4 us (level)
  no operation moved by 1% of the time
where the time goes in v4:
time: 76.4 us; the launch traced here: 76.1 us
  blocking collectives  41.6 us (54%)
  Pallas kernels  14.2 us (19%)
  starting transfers between devices  11.1 us (15%)
  waiting for transfers between devices  7.46 us (10%)
  local copies, waits for them, and re-layouts  0.91 us (1%)
  between operations  0.89 us (1%)
    all_to_all x1, blocking collectives, per_device(): lax.all_to_all(payload.reshape(devices, capacity, lanes), ('gx', 'gy'), s...  22.5 us
    all_to_all x1, blocking collectives, per_device(): lax.all_to_all(back.reshape(devices, capacity, rows * TILE), ('gx', 'gy')...  19.1 us
    pallas_call x7, Pallas kernels, call(): pl.pallas_call(kernel, out_shape=shapes, in_specs=[hbm if limit else vmem...  14.2 us
    ppermute x4, starting transfers between devices, shift(): lax.ppermute(block, axis, [(i, (i + step) % size) for i in range(size)])  7.81 us
    ppermute x4, waiting for transfers between devices, exchange(): blocks[odd] = lax.ppermute(block, axis, pairs)  7.45 us
    ppermute x4, starting transfers between devices, exchange(): blocks[odd] = lax.ppermute(block, axis, pairs)  3.25 us
  transfers between devices with their start and end apart: 8, of which 4 were waited for; matrix products, arithmetic and copies ran while one was open for 0% of the time, Pallas kernels for 5%

profile of v4, /device:TPU:0, one launch (start us, length us, event | category | flops | bytes accessed | tf_op | source)
XLA Modules:
  0.0 76.1 jit_solution(2850604615612711701)
XLA Ops:
  0.6 0.0 copy-start
  0.6 3.3 %shard_map.104 = (bf16[16,640]{1,0:T(8,128)(2,1)}, bf16[16,640]{1,0:T(8,128)(2,1)}, bf16[16,640]{1,0:T(8,128)(2,1)}, bf16[16,640]{1,0:T(8,128)(2,1)}, f32[88,256]{1,0:T(8,128)}) custom-call(f32[16,8192]{1,0:T(8,128)} %part_ref.3, s32[4,512]{1,0:T(4,128)} %index_hbm.1, s32[1,4]{1,0:T(1,128)} %count_hbm.1, s32[1,256]{1,0:T(1,128)} %size_hbm.1, ...), custom_call_target="tpu_custom_call" | custom-call | tf_op jit(solution)/shard_map/pallas_call | solution.py:354
  4.0 0.5 collective-permute-start
  4.5 2.0 %collective-permute-start.1 = (bf16[16,640]{1,0:T(8,128)(2,1)}, bf16[16,640]{1,0:T(8,128)(2,1)S(1)}, u32[]{:S(2)}, u32[]{:S(2)}) collective-permute-start(bf16[16,640]{1,0:T(8,128)(2,1)} %get-tuple-element.27), channel_id=1, source_target_pairs={{0,24},{8,0},{16,8},{24,16},{1,25},{9,1},{17,9},{25,17},{2,26},{10... | collective-permute-start | bytes 61448 | tf_op jit(solution)/shard_map/ppermute | solution.py:366
  6.5 2.3 %collective-permute-start.2 = (bf16[16,640]{1,0:T(8,128)(2,1)}, bf16[16,640]{1,0:T(8,128)(2,1)S(1)}, u32[]{:S(2)}, u32[]{:S(2)}) collective-permute-start(bf16[16,640]{1,0:T(8,128)(2,1)} %get-tuple-element.28), channel_id=1, source_target_pairs={{0,1},{1,2},{2,3},{3,4},{4,5},{5,6},{6,7},{7,0},{8,9},{9,10},{10,1... | collective-permute-start | bytes 61448 | tf_op jit(solution)/shard_map/ppermute | solution.py:366
  8.7 3.0 %collective-permute-start.3 = (bf16[16,640]{1,0:T(8,128)(2,1)}, bf16[16,640]{1,0:T(8,128)(2,1)S(1)}, u32[]{:S(2)}, u32[]{:S(2)}) collective-permute-start(bf16[16,640]{1,0:T(8,128)(2,1)} %get-tuple-element.29), channel_id=1, source_target_pairs={{0,7},{1,0},{2,1},{3,2},{4,3},{5,4},{6,5},{7,6},{8,15},{9,8},{10,9... | collective-permute-start | bytes 61448 | tf_op jit(solution)/shard_map/ppermute | solution.py:366
  11.8 0.0 copy-done
  11.8 0.0 copy-start.1
  11.8 0.9 %copy-done.1 = f32[88,256]{1,0:T(8,128)S(1)} copy-done((f32[88,256]{1,0:T(8,128)S(1)}, f32[88,256]{1,0:T(8,128)}, u32[]{:S(2)}) %copy-start.1) | copy-done | bytes 90136
  12.7 3.7 %shard_map.105 = (f32[576,256]{1,0:T(8,128)S(1)}, s32[1,10240]{1,0:T(1,128)S(1)}, s32[1,256]{1,0:T(1,128)S(1)}, bf16[64,256]{1,0:T(8,128)(2,1)S(1)}) custom-call(f32[16,8192]{1,0:T(8,128)S(1)} %copy-done, f32[88,256]{1,0:T(8,128)S(1)} %copy-done.1), custom_call_target="tpu_custom_call" | custom-call | tf_op jit(solution)/shard_map/pallas_call | solution.py:354
  16.3 0.0 collective-permute-done.refs_0_
  16.3 0.0 collective-permute-done.1.refs_1_
  16.3 0.0 collective-permute-done.2.refs_2_
  16.4 0.0 collective-permute-done.3.refs_3_
  16.4 1.6 %shard_map.106 = bf16[512,640]{1,0:T(8,128)(2,1)S(1)} custom-call(f32[576,256]{1,0:T(8,128)S(1)} %get-tuple-element.22.sum_ref, s32[1,10240]{1,0:T(1,128)S(1)} %get-tuple-element.23.code_ref, s32[1,256]{1,0:T(1,128)S(1)} %get-tuple-element.24.slot_ref, bf16[64,256]{1,0:T(8,128)(2,1)S(1)} %get-tuple-element.25.mark_ref, f32[88,256]{1,0:T(8,128)S(1)} %copy-done.1, ...), custom_call_target="tpu_custom_call" | custom-call | tf_op jit(solution)/shard_map/pallas_call | solution.py:354
  18.0 22.5 %all_to_all.10 = bf16[32,16,640]{2,1,0:T(8,128)(2,1)S(1)} all-to-all(bf16[32,16,640]{2,1,0:T(8,128)(2,1)S(1)} %bitcast.10), channel_id=1, replica_groups=mesh['gx'=4,'gy'=8] {'gx','gy'}, dimensions={0} | all-to-all | bytes 1310720 | tf_op jit(solution)/shard_map/all_to_all | solution.py:419
  40.5 0.6 shard_map.107
  41.1 0.1 collective-permute-start.4
  41.2 0.7 collective-permute-start.5
  41.9 0.5 collective-permute-done.4.xa_ref
  42.4 2.1 %collective-permute-done.5.xb_ref = bf16[16,576]{1,0:T(8,128)(2,1)S(1)} collective-permute-done((bf16[16,576]{1,0:T(8,128)(2,1)S(1)}, bf16[16,576]{1,0:T(8,128)(2,1)S(1)}, u32[]{:S(2)}, u32[]{:S(2)}) %collective-permute-start.5) | collective-permute-done | bytes 18464 | tf_op jit(solution)/shard_map/ppermute | solution.py:230
  44.5 0.2 shard_map.108
  44.7 0.9 %collective-permute-start.6 = (bf16[16,576]{1,0:T(8,128)(2,1)S(1)}, bf16[16,576]{1,0:T(8,128)(2,1)S(1)}, u32[]{:S(2)}, u32[]{:S(2)}) collective-permute-start(bf16[16,576]{1,0:T(8,128)(2,1)S(1)} %get-tuple-element.34), channel_id=1, source_target_pairs={{0,1},{1,0},{2,3},{3,2},{4,5},{5,4},{6,7},{7,6},{8,9},{9,8},{10,11... | collective-permute-start | bytes 55304 | tf_op jit(solution)/shard_map/ppermute | solution.py:230
  45.6 1.6 %collective-permute-start.7 = (bf16[16,576]{1,0:T(8,128)(2,1)S(1)}, bf16[16,576]{1,0:T(8,128)(2,1)S(1)}, u32[]{:S(2)}, u32[]{:S(2)}) collective-permute-start(bf16[16,576]{1,0:T(8,128)(2,1)S(1)} %get-tuple-element.35), channel_id=1, source_target_pairs={{0,7},{1,2},{2,1},{3,4},{4,3},{5,6},{6,5},{7,0},{8,15},{9,10},{10,... | collective-permute-start | bytes 55304 | tf_op jit(solution)/shard_map/ppermute | solution.py:230
  47.2 1.3 %collective-permute-done.6.ya_ref = bf16[16,576]{1,0:T(8,128)(2,1)S(1)} collective-permute-done((bf16[16,576]{1,0:T(8,128)(2,1)S(1)}, bf16[16,576]{1,0:T(8,128)(2,1)S(1)}, u32[]{:S(2)}, u32[]{:S(2)}) %collective-permute-start.6) | collective-permute-done | bytes 18464 | tf_op jit(solution)/shard_map/ppermute | solution.py:230
  48.5 3.5 %collective-permute-done.7.yb_ref = bf16[16,576]{1,0:T(8,128)(2,1)S(1)} collective-permute-done((bf16[16,576]{1,0:T(8,128)(2,1)S(1)}, bf16[16,576]{1,0:T(8,128)(2,1)S(1)}, u32[]{:S(2)}, u32[]{:S(2)}) %collective-permute-start.7) | collective-permute-done | bytes 18464 | tf_op jit(solution)/shard_map/ppermute | solution.py:230
  52.1 0.7 shard_map.109
  52.8 0.0 copy-start.2
  52.8 19.1 %all_to_all.11 = bf16[32,16,512]{2,1,0:T(8,128)(2,1)S(1)} all-to-all(bf16[32,16,512]{2,1,0:T(8,128)(2,1)S(1)} %bitcast.12), channel_id=1, replica_groups=mesh['gx'=4,'gy'=8] {'gx','gy'}, dimensions={0} | all-to-all | bytes 1048576 | tf_op jit(solution)/shard_map/all_to_all | solution.py:432
  71.9 0.0 copy-done.2
  71.9 4.1 %shard_map.110 = (f32[8,10240]{1,0:T(8,128)}, bf16[8,8,8,128]{3,2,1,0:T(8,128)(2,1)}) custom-call(bf16[512,512]{1,0:T(8,128)(2,1)S(1)} %bitcast.11, s32[1,256]{1,0:T(1,128)S(1)} %get-tuple-element.24.slot_ref, s32[1,10240]{1,0:T(1,128)S(1)} %get-tuple-element.23.code_ref, f32[16,8192]{1,0:T(8,128)S(1)} %copy-done, f32[88,256]{1,0:T(8,128)S(1)} %copy-done.2, ...), custom_call_target="tpu_custom_call" | custom-call | tf_op jit(solution)/shard_map/pallas_call | solution.py:354
  (1 shorter events, 0.0 us)
Async XLA Ops:
  0.6 11.1 %copy-start = (f32[16,8192]{1,0:T(8,128)S(1)}, f32[16,8192]{1,0:T(8,128)}, u32[]{:S(2)}) copy-start(f32[16,8192]{1,0:T(8,128)} %part_ref.3) | copy-start | bytes 1572868
  4.0 12.4 %collective-permute-start = (bf16[16,640]{1,0:T(8,128)(2,1)}, bf16[16,640]{1,0:T(8,128)(2,1)S(1)}, u32[]{:S(2)}, u32[]{:S(2)}) collective-permute-start(bf16[16,640]{1,0:T(8,128)(2,1)} %get-tuple-element.26), channel_id=1, source_target_pairs={{0,8},{8,16},{16,24},{24,0},{1,9},{9,17},{17,25},{25,1},{2,10},{10... | collective-permute-start | bytes 61448 | tf_op jit(solution)/shard_map/ppermute | solution.py:366
  4.5 11.9 %collective-permute-start.1 = (bf16[16,640]{1,0:T(8,128)(2,1)}, bf16[16,640]{1,0:T(8,128)(2,1)S(1)}, u32[]{:S(2)}, u32[]{:S(2)}) collective-permute-start(bf16[16,640]{1,0:T(8,128)(2,1)} %get-tuple-element.27), channel_id=1, source_target_pairs={{0,24},{8,0},{16,8},{24,16},{1,25},{9,1},{17,9},{25,17},{2,26},{10... | collective-permute-start | bytes 61448 | tf_op jit(solution)/shard_map/ppermute | solution.py:366
  6.5 9.9 %collective-permute-start.2 = (bf16[16,640]{1,0:T(8,128)(2,1)}, bf16[16,640]{1,0:T(8,128)(2,1)S(1)}, u32[]{:S(2)}, u32[]{:S(2)}) collective-permute-start(bf16[16,640]{1,0:T(8,128)(2,1)} %get-tuple-element.28), channel_id=1, source_target_pairs={{0,1},{1,2},{2,3},{3,4},{4,5},{5,6},{6,7},{7,0},{8,9},{9,10},{10,1... | collective-permute-start | bytes 61448 | tf_op jit(solution)/shard_map/ppermute | solution.py:366
  8.7 7.6 %collective-permute-start.3 = (bf16[16,640]{1,0:T(8,128)(2,1)}, bf16[16,640]{1,0:T(8,128)(2,1)S(1)}, u32[]{:S(2)}, u32[]{:S(2)}) collective-permute-start(bf16[16,640]{1,0:T(8,128)(2,1)} %get-tuple-element.29), channel_id=1, source_target_pairs={{0,7},{1,0},{2,1},{3,2},{4,3},{5,4},{6,5},{7,6},{8,15},{9,8},{10,9... | collective-permute-start | bytes 61448 | tf_op jit(solution)/shard_map/ppermute | solution.py:366
  11.8 0.9 %copy-start.1 = (f32[88,256]{1,0:T(8,128)S(1)}, f32[88,256]{1,0:T(8,128)}, u32[]{:S(2)}) copy-start(f32[88,256]{1,0:T(8,128)} %get-tuple-element.21.small_ref) | copy-start | bytes 270340
  41.1 1.3 %collective-permute-start.4 = (bf16[16,576]{1,0:T(8,128)(2,1)S(1)}, bf16[16,576]{1,0:T(8,128)(2,1)S(1)}, u32[]{:S(2)}, u32[]{:S(2)}) collective-permute-start(bf16[16,576]{1,0:T(8,128)(2,1)S(1)} %get-tuple-element.31), channel_id=1, source_target_pairs={{0,8},{8,0},{16,24},{24,16},{1,9},{9,1},{17,25},{25,17},{2,10},{10... | collective-permute-start | bytes 55304 | tf_op jit(solution)/shard_map/ppermute | solution.py:230
  41.2 3.3 %collective-permute-start.5 = (bf16[16,576]{1,0:T(8,128)(2,1)S(1)}, bf16[16,576]{1,0:T(8,128)(2,1)S(1)}, u32[]{:S(2)}, u32[]{:S(2)}) collective-permute-start(bf16[16,576]{1,0:T(8,128)(2,1)S(1)} %get-tuple-element.32), channel_id=1, source_target_pairs={{0,24},{8,16},{16,8},{24,0},{1,25},{9,17},{17,9},{25,1},{2,26},{10... | collective-permute-start | bytes 55304 | tf_op jit(solution)/shard_map/ppermute | solution.py:230
  44.7 3.8 %collective-permute-start.6 = (bf16[16,576]{1,0:T(8,128)(2,1)S(1)}, bf16[16,576]{1,0:T(8,128)(2,1)S(1)}, u32[]{:S(2)}, u32[]{:S(2)}) collective-permute-start(bf16[16,576]{1,0:T(8,128)(2,1)S(1)} %get-tuple-element.34), channel_id=1, source_target_pairs={{0,1},{1,0},{2,3},{3,2},{4,5},{5,4},{6,7},{7,6},{8,9},{9,8},{10,11... | collective-permute-start | bytes 55304 | tf_op jit(solution)/shard_map/ppermute | solution.py:230
  45.6 6.5 %collective-permute-start.7 = (bf16[16,576]{1,0:T(8,128)(2,1)S(1)}, bf16[16,576]{1,0:T(8,128)(2,1)S(1)}, u32[]{:S(2)}, u32[]{:S(2)}) collective-permute-start(bf16[16,576]{1,0:T(8,128)(2,1)S(1)} %get-tuple-element.35), channel_id=1, source_target_pairs={{0,7},{1,2},{2,1},{3,4},{4,3},{5,6},{6,5},{7,0},{8,15},{9,10},{10,... | collective-permute-start | bytes 55304 | tf_op jit(solution)/shard_map/ppermute | solution.py:230
  52.8 19.1 %copy-start.2 = (f32[88,256]{1,0:T(8,128)S(1)}, f32[88,256]{1,0:T(8,128)}, u32[]{:S(2)}) copy-start(f32[88,256]{1,0:T(8,128)} %get-tuple-element.21.small_ref) | copy-start | bytes 270340

commit v5 on v4

--- a/solution.py
+++ b/solution.py
@@ -53,12 +53,6 @@
     return copies
 
 
-def pieces(hbm, vmem):
-    width = hbm.shape[1] // 4
-    cuts = [slice(k * width, (k + 1) * width) for k in range(4)]
-    return [hbm.at[:, cut] for cut in cuts], [vmem.at[:, cut] for cut in cuts]
-
-
 def leaving_row(index_ref, count_ref, parts):
     migr = index_ref.shape[1]
     lane = iota((1, migr), 1)
@@ -66,10 +60,10 @@
     return jnp.concatenate(rows, axis=1)
 
 
-def small_rows(rows, groups, slots):
-    live = 2 * rows
-    cells = live + groups
-    return rows, live, cells, cells + slots // GROUP
+def small_rows(rows, leaving, slots):
+    leave = 2 * rows
+    cells = leave + leaving // GROUP
+    return rows, leave, cells, cells + slots // GROUP
 
 
 def pick_kernel(
@@ -83,11 +77,10 @@
     slots = cell_ref.shape[1]
     groups = parts // GROUP
     rows, width = closure_ref.shape
-    closure_row, live_row, cell_row, _ = small_rows(rows, groups, slots)
-    sources, targets = pieces(part_hbm, part_ref)
+    closure_row, leave_row, cell_row, _ = small_rows(rows, 4 * migr, slots)
     copies = fetch(
-        [index_hbm, count_hbm, size_hbm, owner_hbm, offset_hbm, closure_hbm, damping_hbm, cell_hbm] + sources,
-        [index_ref, count_ref, size_ref, owner_ref, offset_ref, closure_ref, damping_ref, cell_ref] + targets,
+        [index_hbm, count_hbm, part_hbm, size_hbm, owner_hbm, offset_hbm, closure_hbm, damping_hbm, cell_hbm],
+        [index_ref, count_ref, part_ref, size_ref, owner_ref, offset_ref, closure_ref, damping_ref, cell_ref],
         sems,
     )
     copies[0].wait()
@@ -95,32 +88,32 @@
     leave = leaving_row(index_ref, count_ref, parts)
     high = leave // GROUP
     low = ones(equal(GROUP, leave % GROUP))
-    small_ref[live_row:cell_row, :] = 1.0 - dot(ones(equal(groups, high)), low, NT)
-    for copy in copies[2:8]:
+    for copy in copies[3:]:
         copy.wait()
     for row, ref in enumerate((size_ref, owner_ref, offset_ref)):
         small_ref[row : row + 1, :] = ref[...].astype(jnp.float32)
-    small_ref[closure_row:live_row, :width] = closure_ref[...]
+    small_ref[closure_row:leave_row, :width] = closure_ref[...]
     diagonal = iota((rows, rows), 0) == iota((rows, rows), 1)
     damping = jnp.sum(jnp.where(diagonal, damping_ref[...], 0.0), axis=1, keepdims=True)
-    small_ref[closure_row:live_row, width : width + 1] = damping
-    for k in range(slots // GROUP):
-        row = cell_ref[:, k * GROUP : (k + 1) * GROUP]
-        small_ref[cell_row + k : cell_row + k + 1, :] = row.astype(jnp.float32)
+    small_ref[closure_row:leave_row, width : width + 1] = damping
+    for first, line in ((leave_row, leave), (cell_row, cell_ref[...])):
+        for k in range(line.shape[1] // GROUP):
+            part = line[:, k * GROUP : (k + 1) * GROUP]
+            small_ref[first + k : first + k + 1, :] = part.astype(jnp.float32)
     stores = [pltpu.make_async_copy(small_ref, small_hbm, out_sems.at[4])]
     stores[0].start()
-    for copy in copies[8:]:
-        copy.wait()
+    copies[2].wait()
     table = jnp.concatenate(
         [part_ref[:, g * GROUP : (g + 1) * GROUP].astype(jnp.bfloat16) for g in range(groups)], axis=0
     )
-    rows = dot(table, low)
-    picked = jnp.zeros((channels, 4 * migr), jnp.float32)
-    for g in range(groups):
-        picked = jnp.where(high == g, rows[g * channels : (g + 1) * channels], picked)
     live = jnp.where(leave < parts, 1.0, 0.0)
     for r in range(4):
-        out_ref[r, :, :migr] = picked[:, r * migr : (r + 1) * migr].astype(jnp.bfloat16)
+        where = slice(r * migr, (r + 1) * migr)
+        found = dot(table, low[:, where])
+        picked = jnp.zeros((channels, migr), jnp.float32)
+        for g in range(groups):
+            picked = jnp.where(high[:, where] == g, found[g * channels : (g + 1) * channels], picked)
+        out_ref[r, :, :migr] = picked.astype(jnp.bfloat16)
         flags = [live[:, k : k + LANES] for k in range(r * migr, (r + 1) * migr, LANES)]
         flags.append(jnp.zeros((channels - len(flags), LANES), jnp.float32))
         out_ref[r, :, migr:] = jnp.concatenate(flags, axis=0).astype(jnp.bfloat16)
@@ -153,39 +146,53 @@
 
 
 def deposit_kernel(
-    capacity, rows, part_ref, small_ref, sum_ref, code_ref, slot_ref, mark_ref, columns_ref,
+    capacity, rows, leaving, part_ref, small_ref, sum_ref, code_ref, slot_ref, mark_ref, live_ref, columns_ref
 ):
     channels, parts = part_ref.shape
     slots = code_ref.shape[1]
     tiles = slot_ref.shape[1]
-    closure_row, live_row, cell_row, _ = small_rows(rows, parts // GROUP, slots)
-    closure = small_ref[closure_row:live_row, :channels]
-
+    groups = parts // GROUP
+    closure_row, leave_row, cell_row, _ = small_rows(rows, leaving, slots)
+    closure = small_ref[closure_row:leave_row, :channels]
+
+    leave = side_by_side(small_ref, leave_row, 0, leaving).astype(jnp.int32)
+    pieces = leaving // LANES
+    columns = [leave[:, k * LANES : (k + 1) * LANES] % GROUP for k in range(pieces)]
+    columns.append(jnp.zeros((LANES - pieces, LANES), jnp.int32))
+    columns = jnp.concatenate(columns, axis=0).astype(jnp.float32).T
+    lane = iota((LANES, GROUP), 1).astype(jnp.float32)
+    low = jnp.concatenate([one_hot(lane == columns[:, k : k + 1]) for k in range(pieces)], axis=0)
+    live_ref[...] = 1.0 - dot(ones(equal(groups, leave // GROUP)), low)
+
+    sizes, owners, offset = [small_ref[r : r + 1, :] for r in range(3)]
+    offset = offset.astype(jnp.int32)
     square = (tiles, tiles)
     below, across = iota(square, 0), iota(square, 1)
-
-    def column(row):
-        return jnp.sum(jnp.where(below == across, row, 0), axis=1, keepdims=True)
-
-    sizes, owners, offset = [small_ref[r : r + 1, :].astype(jnp.int32) for r in range(3)]
-    start = jnp.sum(jnp.where(across < below, sizes, 0), axis=1, keepdims=True)
-    height = column(offset % FZ)
+    inputs = [sizes, owners, (offset % FZ).astype(jnp.float32), jnp.zeros((5, tiles), jnp.float32)]
+    inputs = jnp.concatenate(inputs, axis=0).astype(jnp.bfloat16)
+    turned = dot(ones(below == across), inputs, NT)
+    start = dot(ones(across < below), inputs, NT)[:, 0:1].astype(jnp.int32)
+    height = turned[:, 2:3].astype(jnp.int32)
     code = iota((tiles, 1), 0) * TILE + (height - start) % TILE
     code_step = code - jnp.concatenate([jnp.zeros((1, 1), jnp.int32), code[: tiles - 1]], axis=0)
-    earlier = (column(owners) == owners) & (below < across)
-    rank = jnp.sum(jnp.where(earlier, 1, 0), axis=0, keepdims=True)
-    slot_ref[...] = owners * capacity + rank
-    columns_ref[0] = jnp.broadcast_to(start, (tiles, LANES))
-    columns_ref[1] = jnp.broadcast_to(code_step, (tiles, LANES))
-    rows = iota(mark_ref.shape, 0)
-    marks = jnp.where(rows == 0, offset // FZ, jnp.where(rows == 1, offset % FZ, 0))
+    earlier = ones((turned[:, 1:2] == owners) & (below < across))
+    rank = dot(jnp.ones((8, tiles), jnp.bfloat16), earlier)[0:1]
+    slot_ref[...] = (owners * capacity + rank).astype(jnp.int32)
+    columns_ref[0] = jnp.broadcast_to(start, (tiles, LANES)).astype(jnp.int16)
+    columns_ref[1] = jnp.broadcast_to(code_step, (tiles, LANES)).astype(jnp.int16)
+    lines = iota(mark_ref.shape, 0)
+    marks = jnp.where(lines == 0, offset // FZ, jnp.where(lines == 1, offset % FZ, 0))
     mark_ref[...] = marks.astype(jnp.float32).astype(jnp.bfloat16)
 
     def find(begin):
         cell = side_by_side(small_ref, cell_row, begin, CHUNK).astype(jnp.int32)
         starts = jnp.concatenate([columns_ref[0]] * (CHUNK // LANES), axis=1)
         steps = jnp.concatenate([columns_ref[1]] * (CHUNK // LANES), axis=1)
-        found = jnp.sum(jnp.where(cell >= starts, steps, 0), axis=0, keepdims=True)
+        found = jnp.where(cell.astype(jnp.int16) >= starts, steps, jnp.int16(0))
+        while found.shape[0] > 16:
+            half = found.shape[0] // 2
+            found = found[:half] + found[half:]
+        found = jnp.sum(found.astype(jnp.int32), axis=0, keepdims=True) & 0xFFFF
         return found // TILE, (found + cell) % TILE
 
     for begin in range(parts, slots, CHUNK):
@@ -194,7 +201,7 @@
     for begin in range(0, parts, CHUNK):
         tile, place = find(begin)
         code_ref[:, begin : begin + CHUNK] = tile * TILE + place
-        live = side_by_side(small_ref, live_row, begin, CHUNK)
+        live = side_by_side(live_ref, 0, begin, CHUNK)
         state = part_ref[:, begin : begin + CHUNK] * live
         mixed, first = mix(closure, state.astype(jnp.bfloat16))
         added = dot(spread(mixed, first, place), ones(equal(tiles, tile)), NT)
@@ -258,7 +265,7 @@
     return jnp.concatenate([edge[:half], edge[half:]], axis=1)
 
 
-def along_kernel(gas_ref, xa_ref, xb_ref, out_ref, ya_ref, yb_ref):
+def along_kernel(gas_ref, xb_ref, xa_ref, out_ref, ya_ref, yb_ref):
     even = is_even("gx")
     xa, xb = unfold(xa_ref), unfold(xb_ref)
     blocks = [gas_ref[x * FY : (x + 1) * FY, :] for x in range(FX)]
@@ -276,7 +283,7 @@
     yb_ref[...] = jnp.where(even, edges[0], edges[1]).astype(jnp.bfloat16)
 
 
-def drag_kernel(mark_ref, along_ref, ya_ref, yb_ref, drag_ref, back_ref):
+def drag_kernel(mark_ref, along_ref, yb_ref, ya_ref, drag_ref, back_ref):
     rows = drag_ref.shape[0]
     width = along_ref.shape[1] // 2
     lanes = rows * TILE
@@ -309,10 +316,15 @@
     back_ref[...] = jnp.where(place >= height, low, high).astype(jnp.bfloat16)
 
 
-def force_kernel(back_ref, slot_ref, code_ref, part_ref, small_ref, drag_ref, *refs):
-    state_refs, out_ref, drag_hbm, table_ref, sem = refs[:4], refs[4], refs[5], refs[6], refs[7]
-    store = pltpu.make_async_copy(drag_ref, drag_hbm, sem)
-    store.start()
+def force_kernel(back_ref, slot_ref, code_ref, part_ref, small_ref, live_ref, drag_ref, *refs):
+    state_refs, (out_hbm, drag_hbm, out_ref, table_ref, sems) = refs[:4], refs[4:]
+    stores = [pltpu.make_async_copy(drag_ref, drag_hbm, sems.at[0])]
+    stores[0].start()
+
+    def store(where):
+        stores.append(pltpu.make_async_copy(out_ref.at[:, where], out_hbm.at[:, where], sems.at[len(stores)]))
+        stores[-1].start()
+
     rows, slots = out_ref.shape
     parts = part_ref.shape[1]
     tiles = slot_ref.shape[1]
@@ -320,8 +332,7 @@
     match = one_hot(iota((back_ref.shape[0], tiles), 0) == slot_ref[...])
     table_ref[...] = dot(back_ref[...], match, TN).astype(jnp.bfloat16)
     channels = part_ref.shape[0]
-    closure_row, live_row, _, _ = small_rows(rows, parts // GROUP, slots)
-    damping = small_ref[closure_row:live_row, channels : channels + 1]
+    damping = small_ref[rows : 2 * rows, channels : channels + 1]
 
     def look(code):
         values = dot(table_ref[...], ones(equal(tiles, code // TILE))).astype(jnp.bfloat16)
@@ -337,8 +348,9 @@
 
     for begin in range(0, parts, CHUNK):
         where = slice(begin, begin + CHUNK)
-        live = side_by_side(small_ref, live_row, begin, CHUNK)
+        live = side_by_side(live_ref, 0, begin, CHUNK)
         out_ref[:, where] = live * (look(code_ref[:, where]) - damping * part_ref[:rows, where])
+        store(where)
     drag = look(code_ref[:, parts:])
     for row in range(4):
         begin = parts + row * migr
@@ -346,7 +358,9 @@
         live = jnp.concatenate([arrived[k : k + 1, migr:] for k in range(migr // LANES)], axis=1)
         force = drag[:, row * migr : (row + 1) * migr] - damping * arrived[:rows, :migr]
         out_ref[:, begin : begin + migr] = live * force
-    store.wait()
+    store(slice(parts, slots))
+    for copy in stores:
+        copy.wait()
 
 
 def call(kernel, shapes, *operands, limit=None, late=(), scratch=()):
@@ -389,7 +403,7 @@
     count = devices * capacity
     width = (rows + 1) * TILE
     lanes = (width + LANES) // LANES * LANES
-    small_count = small_rows(rows, parts // GROUP, slots)[-1]
+    small_count = small_rows(rows, 4 * migr, slots)[-1]
     operands = (
         particles, migrant_index, migrant_count, source_tile_size, tile_owner.reshape(1, tiles),
         tile_offset.reshape(1, tiles), closure, damping.reshape(1, rows), migrated_slot_cell.reshape(1, slots),
@@ -400,17 +414,17 @@
         *operands, limit=LARGE,
         scratch=[(pltpu.SMEM if i == 2 else pltpu.VMEM)(x.shape, x.dtype) for i, x in enumerate(operands)]
         + [pltpu.VMEM((4, channels, migr + LANES), bf16), pltpu.VMEM((small_count, GROUP), f32),
-           pltpu.SemaphoreType.DMA((12,)), pltpu.SemaphoreType.DMA((5,))],
+           pltpu.SemaphoreType.DMA((9,)), pltpu.SemaphoreType.DMA((5,))],
     )
     arrived = [
         shift(block, axis, step)
         for block, (axis, step) in zip(leaving, (("gx", 1), ("gx", -1), ("gy", 1), ("gy", -1)))
     ]
-    sums, code, slot, marks = call(
-        functools.partial(deposit_kernel, capacity, rows),
+    sums, code, slot, marks, live = call(
+        functools.partial(deposit_kernel, capacity, rows, 4 * migr),
         [shape((width, tiles), f32), shape((1, slots), i32), shape((1, tiles), i32),
-         shape((lanes - width, tiles), bf16)],
-        particles, small, scratch=[pltpu.VMEM((2, tiles, LANES), i32)],
+         shape((lanes - width, tiles), bf16), shape((parts // GROUP, GROUP), f32)],
+        particles, small, scratch=[pltpu.VMEM((2, tiles, LANES), jnp.int16)],
     )
     (payload,) = call(
         functools.partial(pack_kernel, rows), [shape((count, lanes), bf16)],
@@ -422,20 +436,21 @@
     grid, edge = shape((COLS, 2 * width), f32), shape((2 * FX, width), bf16)
     gas, xa, xb = call(place_kernel, [grid, edge, edge], received)
     xa, xb = exchange(xa, xb, "gx")
-    along, ya, yb = call(along_kernel, [grid, edge, edge], gas, xa, xb)
+    along, ya, yb = call(along_kernel, [grid, edge, edge], gas, xb, xa)
     ya, yb = exchange(ya, yb, "gy")
     drag, back = call(
         drag_kernel,
         [shape((rows, FX, FY, FZ), bf16), shape((count, rows * TILE), bf16)],
-        received[:, lanes - LANES :], along, ya, yb,
+        received[:, lanes - LANES :], along, yb, ya,
     )
     returned = lax.all_to_all(
         back.reshape(devices, capacity, rows * TILE), ("gx", "gy"), split_axis=0, concat_axis=0, tiled=True
     ).reshape(count, rows * TILE)
     force, drag = call(
         force_kernel, [shape((rows, slots), f32), shape(drag.shape, bf16)],
-        returned, slot, code, particles, small, drag, *arrived, late=(1,),
-        scratch=[pltpu.VMEM((rows * TILE, tiles), bf16), pltpu.SemaphoreType.DMA],
+        returned, slot, code, particles, small, live, drag, *arrived, late=(0, 1),
+        scratch=[pltpu.VMEM((rows, slots), f32), pltpu.VMEM((rows * TILE, tiles), bf16),
+                 pltpu.SemaphoreType.DMA((2 + parts // CHUNK,))],
     )
     return drag, force
 

time: 76.4 us -> 74.3 us (0.973)
  blocking collectives: 41.6 us -> 40.8 us
  transfers between devices with their start and end apart: 8 -> 8, of which waited for: 4 -> 2; matrix products, arithmetic and copies ran while one was open for 0% -> 0% of each run, Pallas kernels for 5% -> 6%
where the time goes in v5:
time: 74.3 us; the launch traced here: 74.1 us
  blocking collectives  40.8 us (55%)
  Pallas kernels  13.9 us (19%)
  starting transfers between devices  10.6 us (14%)
  waiting for transfers between devices  7.11 us (10%)
  local copies, waits for them, and re-layouts  0.86 us (1%)
    all_to_all x1, blocking collectives, per_device(): lax.all_to_all(payload.reshape(devices, capacity, lanes), ('gx', 'gy'), s...  22.3 us
    all_to_all x1, blocking collectives, per_device(): lax.all_to_all(back.reshape(devices, capacity, rows * TILE), ('gx', 'gy')...  18.5 us
    pallas_call x7, Pallas kernels, call(): pl.pallas_call(kernel, out_shape=shapes, in_specs=[hbm if limit else vmem...  13.9 us
    ppermute x4, starting transfers between devices, shift(): lax.ppermute(block, axis, [(i, (i + step) % size) for i in range(size)])  7.81 us
    ppermute x4, waiting for transfers between devices, exchange(): blocks[odd] = lax.ppermute(block, axis, pairs)  7.1 us
    ppermute x4, starting transfers between devices, exchange(): blocks[odd] = lax.ppermute(block, axis, pairs)  2.78 us
  transfers between devices with their start and end apart: 8, of which 2 were waited for; matrix products, arithmetic and copies ran while one was open for 0% of the time, Pallas kernels for 6%

profile of v5, /device:TPU:0, one launch (start us, length us, event | category | flops | bytes accessed | tf_op | source)
XLA Modules:
  0.0 74.1 jit_solution(16415094471011567016)
XLA Ops:
  0.6 0.0 copy-start
  0.6 2.6 %shard_map.104 = (bf16[16,640]{1,0:T(8,128)(2,1)}, bf16[16,640]{1,0:T(8,128)(2,1)}, bf16[16,640]{1,0:T(8,128)(2,1)}, bf16[16,640]{1,0:T(8,128)(2,1)}, f32[64,256]{1,0:T(8,128)}) custom-call(f32[16,8192]{1,0:T(8,128)} %part_ref.3, s32[4,512]{1,0:T(4,128)} %index_hbm.1, s32[1,4]{1,0:T(1,128)} %count_hbm.1, s32[1,256]{1,0:T(1,128)} %size_hbm.1, ...), custom_call_target="tpu_custom_call" | custom-call | tf_op jit(solution)/shard_map/pallas_call | solution.py:368
  3.3 0.5 collective-permute-start
  3.8 2.0 %collective-permute-start.1 = (bf16[16,640]{1,0:T(8,128)(2,1)}, bf16[16,640]{1,0:T(8,128)(2,1)S(1)}, u32[]{:S(2)}, u32[]{:S(2)}) collective-permute-start(bf16[16,640]{1,0:T(8,128)(2,1)} %get-tuple-element.28), channel_id=1, source_target_pairs={{0,24},{8,0},{16,8},{24,16},{1,25},{9,1},{17,9},{25,17},{2,26},{10... | collective-permute-start | bytes 61448 | tf_op jit(solution)/shard_map/ppermute | solution.py:380
  5.8 2.3 %collective-permute-start.2 = (bf16[16,640]{1,0:T(8,128)(2,1)}, bf16[16,640]{1,0:T(8,128)(2,1)S(1)}, u32[]{:S(2)}, u32[]{:S(2)}) collective-permute-start(bf16[16,640]{1,0:T(8,128)(2,1)} %get-tuple-element.29), channel_id=1, source_target_pairs={{0,1},{1,2},{2,3},{3,4},{4,5},{5,6},{6,7},{7,0},{8,9},{9,10},{10,1... | collective-permute-start | bytes 61448 | tf_op jit(solution)/shard_map/ppermute | solution.py:380
  8.0 3.0 %collective-permute-start.3 = (bf16[16,640]{1,0:T(8,128)(2,1)}, bf16[16,640]{1,0:T(8,128)(2,1)S(1)}, u32[]{:S(2)}, u32[]{:S(2)}) collective-permute-start(bf16[16,640]{1,0:T(8,128)(2,1)} %get-tuple-element.30), channel_id=1, source_target_pairs={{0,7},{1,0},{2,1},{3,2},{4,3},{5,4},{6,5},{7,6},{8,15},{9,8},{10,9... | collective-permute-start | bytes 61448 | tf_op jit(solution)/shard_map/ppermute | solution.py:380
  11.1 0.0 copy-done
  11.1 0.0 copy-start.1
  11.1 0.8 %copy-done.1 = f32[64,256]{1,0:T(8,128)S(1)} copy-done((f32[64,256]{1,0:T(8,128)S(1)}, f32[64,256]{1,0:T(8,128)}, u32[]{:S(2)}) %copy-start.1) | copy-done | bytes 65560
  11.9 4.1 %shard_map.105 = (f32[576,256]{1,0:T(8,128)S(1)}, s32[1,10240]{1,0:T(1,128)S(1)}, s32[1,256]{1,0:T(1,128)S(1)}, bf16[64,256]{1,0:T(8,128)(2,1)S(1)}, f32[32,256]{1,0:T(8,128)S(1)}) custom-call(f32[16,8192]{1,0:T(8,128)S(1)} %copy-done, f32[64,256]{1,0:T(8,128)S(1)} %copy-done.1), custom_call_target="tpu_custom_call" | custom-call | tf_op jit(solution)/shard_map/pallas_call | solution.py:368
  16.0 0.0 collective-permute-done.refs_0_
  16.1 0.0 collective-permute-done.1.refs_1_
  16.1 0.0 collective-permute-done.2.refs_2_
  16.1 0.0 collective-permute-done.3.refs_3_
  16.1 1.6 %shard_map.106 = bf16[512,640]{1,0:T(8,128)(2,1)S(1)} custom-call(f32[576,256]{1,0:T(8,128)S(1)} %get-tuple-element.23.sum_ref, s32[1,10240]{1,0:T(1,128)S(1)} %get-tuple-element.24.code_ref, s32[1,256]{1,0:T(1,128)S(1)} %get-tuple-element.25.slot_ref, bf16[64,256]{1,0:T(8,128)(2,1)S(1)} %get-tuple-element.26.mark_ref, f32[64,256]{1,0:T(8,128)S(1)} %copy-done.1, ...), custom_call_target="tpu_custom_call" | custom-call | tf_op jit(solution)/shard_map/pallas_call | solution.py:368
  17.7 22.3 %all_to_all.10 = bf16[32,16,640]{2,1,0:T(8,128)(2,1)S(1)} all-to-all(bf16[32,16,640]{2,1,0:T(8,128)(2,1)S(1)} %bitcast.10), channel_id=1, replica_groups=mesh['gx'=4,'gy'=8] {'gx','gy'}, dimensions={0} | all-to-all | bytes 1310720 | tf_op jit(solution)/shard_map/all_to_all | solution.py:433
  40.0 0.6 shard_map.107
  40.6 0.5 collective-permute-start.4
  41.1 0.2 collective-permute-start.5
  41.3 2.6 %collective-permute-done.4.xb_ref = bf16[16,576]{1,0:T(8,128)(2,1)S(1)} collective-permute-done((bf16[16,576]{1,0:T(8,128)(2,1)S(1)}, bf16[16,576]{1,0:T(8,128)(2,1)S(1)}, u32[]{:S(2)}, u32[]{:S(2)}) %collective-permute-start.4) | collective-permute-done | bytes 18464 | tf_op jit(solution)/shard_map/ppermute | solution.py:237
  44.0 0.0 collective-permute-done.5.xa_ref
  44.0 0.2 shard_map.108
  44.2 1.7 %collective-permute-start.6 = (bf16[16,576]{1,0:T(8,128)(2,1)S(1)}, bf16[16,576]{1,0:T(8,128)(2,1)S(1)}, u32[]{:S(2)}, u32[]{:S(2)}) collective-permute-start(bf16[16,576]{1,0:T(8,128)(2,1)S(1)} %get-tuple-element.35), channel_id=1, source_target_pairs={{0,7},{1,2},{2,1},{3,4},{4,3},{5,6},{6,5},{7,0},{8,15},{9,10},{10,... | collective-permute-start | bytes 55304 | tf_op jit(solution)/shard_map/ppermute | solution.py:237
  45.8 0.4 collective-permute-start.7
  46.2 4.5 %collective-permute-done.6.yb_ref = bf16[16,576]{1,0:T(8,128)(2,1)S(1)} collective-permute-done((bf16[16,576]{1,0:T(8,128)(2,1)S(1)}, bf16[16,576]{1,0:T(8,128)(2,1)S(1)}, u32[]{:S(2)}, u32[]{:S(2)}) %collective-permute-start.6) | collective-permute-done | bytes 18464 | tf_op jit(solution)/shard_map/ppermute | solution.py:237
  50.7 0.0 collective-permute-done.7.ya_ref
  50.7 0.8 %shard_map.109 = (bf16[8,8,8,128]{3,2,1,0:T(8,128)(2,1)S(1)}, bf16[512,512]{1,0:T(8,128)(2,1)S(1)}) custom-call(bf16[512,128]{1,0:T(8,128)(2,1)S(1)} %slice.4.mark_ref, f32[64,1152]{1,0:T(8,128)S(1)} %get-tuple-element.34.along_ref, bf16[16,576]{1,0:T(8,128)(2,1)S(1)} %collective-permute-done.6.yb_ref, bf16[16,576]{1,0:T(8,128)(2,1)S(1)} %collective-permute-done.7.ya_ref), custom_call_target="tpu_custom_call" | custom-call | tf_op jit(solution)/shard_map/pallas_call | solution.py:368
  51.5 0.0 copy-start.2
  51.5 18.5 %all_to_all.11 = bf16[32,16,512]{2,1,0:T(8,128)(2,1)S(1)} all-to-all(bf16[32,16,512]{2,1,0:T(8,128)(2,1)S(1)} %bitcast.12), channel_id=1, replica_groups=mesh['gx'=4,'gy'=8] {'gx','gy'}, dimensions={0} | all-to-all | bytes 1048576 | tf_op jit(solution)/shard_map/all_to_all | solution.py:446
  70.0 0.0 copy-done.2
  70.0 4.0 %shard_map.110 = (f32[8,10240]{1,0:T(8,128)}, bf16[8,8,8,128]{3,2,1,0:T(8,128)(2,1)}) custom-call(bf16[512,512]{1,0:T(8,128)(2,1)S(1)} %bitcast.11, s32[1,256]{1,0:T(1,128)S(1)} %get-tuple-element.25.slot_ref, s32[1,10240]{1,0:T(1,128)S(1)} %get-tuple-element.24.code_ref, f32[16,8192]{1,0:T(8,128)S(1)} %copy-done, f32[64,256]{1,0:T(8,128)S(1)} %copy-done.2, ...), custom_call_target="tpu_custom_call" | custom-call | tf_op jit(solution)/shard_map/pallas_call | solution.py:368
  (1 shorter events, 0.0 us)
Async XLA Ops:
  0.6 10.4 %copy-start = (f32[16,8192]{1,0:T(8,128)S(1)}, f32[16,8192]{1,0:T(8,128)}, u32[]{:S(2)}) copy-start(f32[16,8192]{1,0:T(8,128)} %part_ref.3) | copy-start | bytes 1572868
  3.3 12.8 %collective-permute-start = (bf16[16,640]{1,0:T(8,128)(2,1)}, bf16[16,640]{1,0:T(8,128)(2,1)S(1)}, u32[]{:S(2)}, u32[]{:S(2)}) collective-permute-start(bf16[16,640]{1,0:T(8,128)(2,1)} %get-tuple-element.27), channel_id=1, source_target_pairs={{0,8},{8,16},{16,24},{24,0},{1,9},{9,17},{17,25},{25,1},{2,10},{10... | collective-permute-start | bytes 61448 | tf_op jit(solution)/shard_map/ppermute | solution.py:380
  3.8 12.3 %collective-permute-start.1 = (bf16[16,640]{1,0:T(8,128)(2,1)}, bf16[16,640]{1,0:T(8,128)(2,1)S(1)}, u32[]{:S(2)}, u32[]{:S(2)}) collective-permute-start(bf16[16,640]{1,0:T(8,128)(2,1)} %get-tuple-element.28), channel_id=1, source_target_pairs={{0,24},{8,0},{16,8},{24,16},{1,25},{9,1},{17,9},{25,17},{2,26},{10... | collective-permute-start | bytes 61448 | tf_op jit(solution)/shard_map/ppermute | solution.py:380
  5.8 10.3 %collective-permute-start.2 = (bf16[16,640]{1,0:T(8,128)(2,1)}, bf16[16,640]{1,0:T(8,128)(2,1)S(1)}, u32[]{:S(2)}, u32[]{:S(2)}) collective-permute-start(bf16[16,640]{1,0:T(8,128)(2,1)} %get-tuple-element.29), channel_id=1, source_target_pairs={{0,1},{1,2},{2,3},{3,4},{4,5},{5,6},{6,7},{7,0},{8,9},{9,10},{10,1... | collective-permute-start | bytes 61448 | tf_op jit(solution)/shard_map/ppermute | solution.py:380
  8.0 8.1 %collective-permute-start.3 = (bf16[16,640]{1,0:T(8,128)(2,1)}, bf16[16,640]{1,0:T(8,128)(2,1)S(1)}, u32[]{:S(2)}, u32[]{:S(2)}) collective-permute-start(bf16[16,640]{1,0:T(8,128)(2,1)} %get-tuple-element.30), channel_id=1, source_target_pairs={{0,7},{1,0},{2,1},{3,2},{4,3},{5,4},{6,5},{7,6},{8,15},{9,8},{10,9... | collective-permute-start | bytes 61448 | tf_op jit(solution)/shard_map/ppermute | solution.py:380
  11.1 0.8 %copy-start.1 = (f32[64,256]{1,0:T(8,128)S(1)}, f32[64,256]{1,0:T(8,128)}, u32[]{:S(2)}) copy-start(f32[64,256]{1,0:T(8,128)} %get-tuple-element.22.small_ref) | copy-start | bytes 196612
  40.6 3.4 %collective-permute-start.4 = (bf16[16,576]{1,0:T(8,128)(2,1)S(1)}, bf16[16,576]{1,0:T(8,128)(2,1)S(1)}, u32[]{:S(2)}, u32[]{:S(2)}) collective-permute-start(bf16[16,576]{1,0:T(8,128)(2,1)S(1)} %get-tuple-element.32), channel_id=1, source_target_pairs={{0,24},{8,16},{16,8},{24,0},{1,25},{9,17},{17,9},{25,1},{2,26},{10... | collective-permute-start | bytes 55304 | tf_op jit(solution)/shard_map/ppermute | solution.py:237
  41.1 2.8 %collective-permute-start.5 = (bf16[16,576]{1,0:T(8,128)(2,1)S(1)}, bf16[16,576]{1,0:T(8,128)(2,1)S(1)}, u32[]{:S(2)}, u32[]{:S(2)}) collective-permute-start(bf16[16,576]{1,0:T(8,128)(2,1)S(1)} %get-tuple-element.33), channel_id=1, source_target_pairs={{0,8},{8,0},{16,24},{24,16},{1,9},{9,1},{17,25},{25,17},{2,10},{10... | collective-permute-start | bytes 55304 | tf_op jit(solution)/shard_map/ppermute | solution.py:237
  44.2 6.5 %collective-permute-start.6 = (bf16[16,576]{1,0:T(8,128)(2,1)S(1)}, bf16[16,576]{1,0:T(8,128)(2,1)S(1)}, u32[]{:S(2)}, u32[]{:S(2)}) collective-permute-start(bf16[16,576]{1,0:T(8,128)(2,1)S(1)} %get-tuple-element.35), channel_id=1, source_target_pairs={{0,7},{1,2},{2,1},{3,4},{4,3},{5,6},{6,5},{7,0},{8,15},{9,10},{10,... | collective-permute-start | bytes 55304 | tf_op jit(solution)/shard_map/ppermute | solution.py:237
  45.8 4.9 %collective-permute-start.7 = (bf16[16,576]{1,0:T(8,128)(2,1)S(1)}, bf16[16,576]{1,0:T(8,128)(2,1)S(1)}, u32[]{:S(2)}, u32[]{:S(2)}) collective-permute-start(bf16[16,576]{1,0:T(8,128)(2,1)S(1)} %get-tuple-element.36), channel_id=1, source_target_pairs={{0,1},{1,0},{2,3},{3,2},{4,5},{5,4},{6,7},{7,6},{8,9},{9,8},{10,11... | collective-permute-start | bytes 55304 | tf_op jit(solution)/shard_map/ppermute | solution.py:237
  51.5 18.6 %copy-start.2 = (f32[64,256]{1,0:T(8,128)S(1)}, f32[64,256]{1,0:T(8,128)}, u32[]{:S(2)}) copy-start(f32[64,256]{1,0:T(8,128)} %get-tuple-element.22.small_ref) | copy-start | bytes 196612

commit v6 on v5

--- a/solution.py
+++ b/solution.py
@@ -53,11 +53,37 @@
     return copies
 
 
+def is_even(axis):
+    return lax.axis_index(axis) % 2 == 0
+
+
+def exchange(block_a, block_b, axis):
+    size = lax.axis_size(axis)
+    blocks = {}
+    for odd, block in ((1, block_b), (0, block_a)):
+        pairs = [(i, (i + 1) % size if i % 2 == odd else (i - 1) % size) for i in range(size)]
+        blocks[odd] = lax.ppermute(block, axis, pairs)
+    return blocks[0], blocks[1]
+
+
+def ordered(first, second, axis):
+    even = is_even(axis)
+    return jnp.where(even, second, first), jnp.where(even, first, second)
+
+
 def leaving_row(index_ref, count_ref, parts):
     migr = index_ref.shape[1]
     lane = iota((1, migr), 1)
-    rows = [jnp.where(lane < count_ref[0, r], index_ref[r : r + 1, :], parts) for r in range(4)]
+    odd = [jnp.where(is_even(axis), 0, 1) for axis in ("gx", "gy")]
+    rows = []
+    for row in (odd[0], 1 - odd[0], 2 + odd[1], 3 - odd[1]):
+        rows.append(jnp.where(lane < count_ref[0, row], index_ref[pl.ds(row, 1), :], parts))
     return jnp.concatenate(rows, axis=1)
+
+
+def arrived_blocks(refs):
+    blocks = [ref[...].astype(jnp.float32) for ref in refs]
+    return ordered(blocks[0], blocks[1], "gx") + ordered(blocks[2], blocks[3], "gy")
 
 
 def small_rows(rows, leaving, slots):
@@ -217,25 +243,12 @@
     closure = small_ref[rows : 2 * rows, :channels]
     migr = state_refs[0].shape[1] - LANES
     code = code_ref[:, code_ref.shape[1] - 4 * migr :]
-    state = jnp.concatenate([ref[:, :migr] for ref in state_refs], axis=1)
+    state = jnp.concatenate([block[:, :migr] for block in arrived_blocks(state_refs)], axis=1)
     mixed, first = mix(closure, state)
     total = sum_ref[...] + dot(spread(mixed, first, code % TILE), ones(equal(tiles, code // TILE)), NT)
     table = jnp.concatenate([total.astype(jnp.bfloat16), mark_ref[...]], axis=0)
     match = one_hot(iota((out_ref.shape[0], tiles), 0) == slot_ref[...])
     out_ref[...] = dot(match, table, NT).astype(jnp.bfloat16)
-
-
-def is_even(axis):
-    return lax.axis_index(axis) % 2 == 0
-
-
-def exchange(block_a, block_b, axis):
-    size = lax.axis_size(axis)
-    blocks = {}
-    for odd, block in ((1, block_b), (0, block_a)):
-        pairs = [(i, (i + 1) % size if i % 2 == odd else (i - 1) % size) for i in range(size)]
-        blocks[odd] = lax.ppermute(block, axis, pairs)
-    return blocks[0], blocks[1]
 
 
 def place_kernel(tile_ref, gas_ref, xa_ref, xb_ref):
@@ -266,10 +279,8 @@
 
 
 def along_kernel(gas_ref, xb_ref, xa_ref, out_ref, ya_ref, yb_ref):
-    even = is_even("gx")
-    xa, xb = unfold(xa_ref), unfold(xb_ref)
-    blocks = [gas_ref[x * FY : (x + 1) * FY, :] for x in range(FX)]
-    blocks = [jnp.where(even, xb, xa)] + blocks + [jnp.where(even, xa, xb)]
+    before, after = ordered(unfold(xa_ref), unfold(xb_ref), "gx")
+    blocks = [before] + [gas_ref[x * FY : (x + 1) * FY, :] for x in range(FX)] + [after]
     along = [blocks[x] + 2.0 * blocks[x + 1] + blocks[x + 2] for x in range(FX)]
     for x in range(FX):
         out_ref[x * FY : (x + 1) * FY, :] = along[x]
@@ -287,9 +298,7 @@
     rows = drag_ref.shape[0]
     width = along_ref.shape[1] // 2
     lanes = rows * TILE
-    even = is_even("gy")
-    ya, yb = unfold(ya_ref), unfold(yb_ref)
-    before, after = jnp.where(even, yb, ya), jnp.where(even, ya, yb)
+    before, after = ordered(unfold(ya_ref), unfold(yb_ref), "gy")
     smooth = []
     for x in range(FX):
         block = along_ref[x * FY : (x + 1) * FY, :]
@@ -352,9 +361,8 @@
         out_ref[:, where] = live * (look(code_ref[:, where]) - damping * part_ref[:rows, where])
         store(where)
     drag = look(code_ref[:, parts:])
-    for row in range(4):
+    for row, arrived in enumerate(arrived_blocks(state_refs)):
         begin = parts + row * migr
-        arrived = state_refs[row][:, :].astype(jnp.float32)
         live = jnp.concatenate([arrived[k : k + 1, migr:] for k in range(migr // LANES)], axis=1)
         force = drag[:, row * migr : (row + 1) * migr] - damping * arrived[:rows, :migr]
         out_ref[:, begin : begin + migr] = live * force
@@ -373,11 +381,6 @@
         scratch_shapes=scratch,
         compiler_params=pltpu.CompilerParams(vmem_limit_bytes=limit or VMEM),
     )(*operands)
-
-
-def shift(block, axis, step):
-    size = lax.axis_size(axis)
-    return lax.ppermute(block, axis, [(i, (i + step) % size) for i in range(size)])
 
 
 def per_device(
@@ -416,10 +419,7 @@
         + [pltpu.VMEM((4, channels, migr + LANES), bf16), pltpu.VMEM((small_count, GROUP), f32),
            pltpu.SemaphoreType.DMA((9,)), pltpu.SemaphoreType.DMA((5,))],
     )
-    arrived = [
-        shift(block, axis, step)
-        for block, (axis, step) in zip(leaving, (("gx", 1), ("gx", -1), ("gy", 1), ("gy", -1)))
-    ]
+    arrived = exchange(*leaving[:2], "gx") + exchange(*leaving[2:], "gy")
     sums, code, slot, marks, live = call(
         functools.partial(deposit_kernel, capacity, rows, 4 * migr),
         [shape((width, tiles), f32), shape((1, slots), i32), shape((1, tiles), i32),

time: 74.3 us -> 73.4 us (0.988)
  blocking collectives: 40.8 us -> 39.6 us
    ppermute x4 -> x8, starting transfers between devices: 2.78 us -> 11 us  [exchange(): blocks[odd] = lax.ppermute(block, axis, pairs)]
    ppermute x4 -> x0, starting transfers between devices: 7.81 us -> none  [shift(): lax.ppermute(block, axis, [(i, (i + step) % size) for i in range(size)])]
    all_to_all x1, blocking collectives: 22.3 us -> 21 us  [per_device(): lax.all_to_all(payload.reshape(devices, capacity, lanes), ('gx', 'gy'), s...]
    ppermute x4 -> x8, waiting for transfers between devices: 7.1 us -> 7.11 us  [exchange(): blocks[odd] = lax.ppermute(block, axis, pairs)]
where the time goes in v6:
time: 73.4 us; the launch traced here: 73.2 us
  blocking collectives  39.6 us (54%)
  Pallas kernels  13.9 us (19%)
  starting transfers between devices  11 us (15%)
  waiting for transfers between devices  7.11 us (10%)
  local copies, waits for them, and re-layouts  0.86 us (1%)
    all_to_all x1, blocking collectives, per_device(): lax.all_to_all(payload.reshape(devices, capacity, lanes), ('gx', 'gy'), s...  21 us
    all_to_all x1, blocking collectives, per_device(): lax.all_to_all(back.reshape(devices, capacity, rows * TILE), ('gx', 'gy')...  18.5 us
    pallas_call x7, Pallas kernels, call(): pl.pallas_call(kernel, out_shape=shapes, in_specs=[hbm if limit else vmem...  13.9 us
    ppermute x8, starting transfers between devices, exchange(): blocks[odd] = lax.ppermute(block, axis, pairs)  11 us
    ppermute x8, waiting for transfers between devices, exchange(): blocks[odd] = lax.ppermute(block, axis, pairs)  7.11 us
  transfers between devices with their start and end apart: 8, of which 2 were waited for; matrix products, arithmetic and copies ran while one was open for 0% of the time, Pallas kernels for 6%

profile of v6, /device:TPU:0, one launch (start us, length us, event | category | flops | bytes accessed | tf_op | source)
XLA Modules:
  0.0 73.2 jit_solution(13161345567784785023)
XLA Ops:
  0.6 0.0 copy-start
  0.6 2.6 %shard_map.104 = (bf16[16,640]{1,0:T(8,128)(2,1)}, bf16[16,640]{1,0:T(8,128)(2,1)}, bf16[16,640]{1,0:T(8,128)(2,1)}, bf16[16,640]{1,0:T(8,128)(2,1)}, f32[64,256]{1,0:T(8,128)}) custom-call(f32[16,8192]{1,0:T(8,128)} %part_ref.3, s32[4,512]{1,0:T(4,128)} %index_hbm.1, s32[1,4]{1,0:T(1,128)} %count_hbm.1, s32[1,256]{1,0:T(1,128)} %size_hbm.1, ...), custom_call_target="tpu_custom_call" | custom-call | tf_op jit(solution)/shard_map/pallas_call | solution.py:376
  3.3 0.5 collective-permute-start
  3.8 2.6 %collective-permute-start.1 = (bf16[16,640]{1,0:T(8,128)(2,1)}, bf16[16,640]{1,0:T(8,128)(2,1)S(1)}, u32[]{:S(2)}, u32[]{:S(2)}) collective-permute-start(bf16[16,640]{1,0:T(8,128)(2,1)} %get-tuple-element.28), channel_id=1, source_target_pairs={{0,24},{8,16},{16,8},{24,0},{1,25},{9,17},{17,9},{25,1},{2,26},{10... | collective-permute-start | bytes 61448 | tf_op jit(solution)/shard_map/ppermute | solution.py:65
  6.4 1.5 %collective-permute-start.2 = (bf16[16,640]{1,0:T(8,128)(2,1)}, bf16[16,640]{1,0:T(8,128)(2,1)S(1)}, u32[]{:S(2)}, u32[]{:S(2)}) collective-permute-start(bf16[16,640]{1,0:T(8,128)(2,1)} %get-tuple-element.29), channel_id=1, source_target_pairs={{0,1},{1,0},{2,3},{3,2},{4,5},{5,4},{6,7},{7,6},{8,9},{9,8},{10,11... | collective-permute-start | bytes 61448 | tf_op jit(solution)/shard_map/ppermute | solution.py:65
  7.9 3.5 %collective-permute-start.3 = (bf16[16,640]{1,0:T(8,128)(2,1)}, bf16[16,640]{1,0:T(8,128)(2,1)S(1)}, u32[]{:S(2)}, u32[]{:S(2)}) collective-permute-start(bf16[16,640]{1,0:T(8,128)(2,1)} %get-tuple-element.30), channel_id=1, source_target_pairs={{0,7},{1,2},{2,1},{3,4},{4,3},{5,6},{6,5},{7,0},{8,15},{9,10},{10,... | collective-permute-start | bytes 61448 | tf_op jit(solution)/shard_map/ppermute | solution.py:65
  11.5 0.0 copy-done
  11.5 0.0 copy-start.1
  11.5 0.8 %copy-done.1 = f32[64,256]{1,0:T(8,128)S(1)} copy-done((f32[64,256]{1,0:T(8,128)S(1)}, f32[64,256]{1,0:T(8,128)}, u32[]{:S(2)}) %copy-start.1) | copy-done | bytes 65560
  12.3 4.1 %shard_map.105 = (f32[576,256]{1,0:T(8,128)S(1)}, s32[1,10240]{1,0:T(1,128)S(1)}, s32[1,256]{1,0:T(1,128)S(1)}, bf16[64,256]{1,0:T(8,128)(2,1)S(1)}, f32[32,256]{1,0:T(8,128)S(1)}) custom-call(f32[16,8192]{1,0:T(8,128)S(1)} %copy-done, f32[64,256]{1,0:T(8,128)S(1)} %copy-done.1), custom_call_target="tpu_custom_call" | custom-call | tf_op jit(solution)/shard_map/pallas_call | solution.py:376
  16.4 0.0 collective-permute-done.refs_0_
  16.4 0.0 collective-permute-done.1.refs_1_
  16.5 0.0 collective-permute-done.2.refs_2_
  16.5 0.0 collective-permute-done.3.refs_3_
  16.5 1.6 %shard_map.106 = bf16[512,640]{1,0:T(8,128)(2,1)S(1)} custom-call(f32[576,256]{1,0:T(8,128)S(1)} %get-tuple-element.23.sum_ref, s32[1,10240]{1,0:T(1,128)S(1)} %get-tuple-element.24.code_ref, s32[1,256]{1,0:T(1,128)S(1)} %get-tuple-element.25.slot_ref, bf16[64,256]{1,0:T(8,128)(2,1)S(1)} %get-tuple-element.26.mark_ref, f32[64,256]{1,0:T(8,128)S(1)} %copy-done.1, ...), custom_call_target="tpu_custom_call" | custom-call | tf_op jit(solution)/shard_map/pallas_call | solution.py:376
  18.1 21.0 %all_to_all.10 = bf16[32,16,640]{2,1,0:T(8,128)(2,1)S(1)} all-to-all(bf16[32,16,640]{2,1,0:T(8,128)(2,1)S(1)} %bitcast.10), channel_id=1, replica_groups=mesh['gx'=4,'gy'=8] {'gx','gy'}, dimensions={0} | all-to-all | bytes 1310720 | tf_op jit(solution)/shard_map/all_to_all | solution.py:433
  39.1 0.6 shard_map.107
  39.7 0.5 collective-permute-start.4
  40.3 0.2 collective-permute-start.5
  40.5 2.6 %collective-permute-done.4.xb_ref = bf16[16,576]{1,0:T(8,128)(2,1)S(1)} collective-permute-done((bf16[16,576]{1,0:T(8,128)(2,1)S(1)}, bf16[16,576]{1,0:T(8,128)(2,1)S(1)}, u32[]{:S(2)}, u32[]{:S(2)}) %collective-permute-start.4) | collective-permute-done | bytes 18464 | tf_op jit(solution)/shard_map/ppermute | solution.py:65
  43.1 0.0 collective-permute-done.5.xa_ref
  43.1 0.2 shard_map.108
  43.3 1.7 %collective-permute-start.6 = (bf16[16,576]{1,0:T(8,128)(2,1)S(1)}, bf16[16,576]{1,0:T(8,128)(2,1)S(1)}, u32[]{:S(2)}, u32[]{:S(2)}) collective-permute-start(bf16[16,576]{1,0:T(8,128)(2,1)S(1)} %get-tuple-element.35), channel_id=1, source_target_pairs={{0,7},{1,2},{2,1},{3,4},{4,3},{5,6},{6,5},{7,0},{8,15},{9,10},{10,... | collective-permute-start | bytes 55304 | tf_op jit(solution)/shard_map/ppermute | solution.py:65
  44.9 0.4 collective-permute-start.7
  45.3 4.5 %collective-permute-done.6.yb_ref = bf16[16,576]{1,0:T(8,128)(2,1)S(1)} collective-permute-done((bf16[16,576]{1,0:T(8,128)(2,1)S(1)}, bf16[16,576]{1,0:T(8,128)(2,1)S(1)}, u32[]{:S(2)}, u32[]{:S(2)}) %collective-permute-start.6) | collective-permute-done | bytes 18464 | tf_op jit(solution)/shard_map/ppermute | solution.py:65
  49.8 0.0 collective-permute-done.7.ya_ref
  49.8 0.8 %shard_map.109 = (bf16[8,8,8,128]{3,2,1,0:T(8,128)(2,1)S(1)}, bf16[512,512]{1,0:T(8,128)(2,1)S(1)}) custom-call(bf16[512,128]{1,0:T(8,128)(2,1)S(1)} %slice.4.mark_ref, f32[64,1152]{1,0:T(8,128)S(1)} %get-tuple-element.34.along_ref, bf16[16,576]{1,0:T(8,128)(2,1)S(1)} %collective-permute-done.6.yb_ref, bf16[16,576]{1,0:T(8,128)(2,1)S(1)} %collective-permute-done.7.ya_ref), custom_call_target="tpu_custom_call" | custom-call | tf_op jit(solution)/shard_map/pallas_call | solution.py:376
  50.6 0.0 copy-start.2
  50.6 18.5 %all_to_all.11 = bf16[32,16,512]{2,1,0:T(8,128)(2,1)S(1)} all-to-all(bf16[32,16,512]{2,1,0:T(8,128)(2,1)S(1)} %bitcast.12), channel_id=1, replica_groups=mesh['gx'=4,'gy'=8] {'gx','gy'}, dimensions={0} | all-to-all | bytes 1048576 | tf_op jit(solution)/shard_map/all_to_all | solution.py:446
  69.1 0.0 copy-done.2
  69.1 4.0 %shard_map.110 = (f32[8,10240]{1,0:T(8,128)}, bf16[8,8,8,128]{3,2,1,0:T(8,128)(2,1)}) custom-call(bf16[512,512]{1,0:T(8,128)(2,1)S(1)} %bitcast.11, s32[1,256]{1,0:T(1,128)S(1)} %get-tuple-element.25.slot_ref, s32[1,10240]{1,0:T(1,128)S(1)} %get-tuple-element.24.code_ref, f32[16,8192]{1,0:T(8,128)S(1)} %copy-done, f32[64,256]{1,0:T(8,128)S(1)} %copy-done.2, ...), custom_call_target="tpu_custom_call" | custom-call | tf_op jit(solution)/shard_map/pallas_call | solution.py:376
  (1 shorter events, 0.0 us)
Async XLA Ops:
  0.6 10.8 %copy-start = (f32[16,8192]{1,0:T(8,128)S(1)}, f32[16,8192]{1,0:T(8,128)}, u32[]{:S(2)}) copy-start(f32[16,8192]{1,0:T(8,128)} %part_ref.3) | copy-start | bytes 1572868
  3.3 13.2 %collective-permute-start = (bf16[16,640]{1,0:T(8,128)(2,1)}, bf16[16,640]{1,0:T(8,128)(2,1)S(1)}, u32[]{:S(2)}, u32[]{:S(2)}) collective-permute-start(bf16[16,640]{1,0:T(8,128)(2,1)} %get-tuple-element.27), channel_id=1, source_target_pairs={{0,8},{8,0},{16,24},{24,16},{1,9},{9,1},{17,25},{25,17},{2,10},{10... | collective-permute-start | bytes 61448 | tf_op jit(solution)/shard_map/ppermute | solution.py:65
  3.8 12.7 %collective-permute-start.1 = (bf16[16,640]{1,0:T(8,128)(2,1)}, bf16[16,640]{1,0:T(8,128)(2,1)S(1)}, u32[]{:S(2)}, u32[]{:S(2)}) collective-permute-start(bf16[16,640]{1,0:T(8,128)(2,1)} %get-tuple-element.28), channel_id=1, source_target_pairs={{0,24},{8,16},{16,8},{24,0},{1,25},{9,17},{17,9},{25,1},{2,26},{10... | collective-permute-start | bytes 61448 | tf_op jit(solution)/shard_map/ppermute | solution.py:65
  6.4 10.1 %collective-permute-start.2 = (bf16[16,640]{1,0:T(8,128)(2,1)}, bf16[16,640]{1,0:T(8,128)(2,1)S(1)}, u32[]{:S(2)}, u32[]{:S(2)}) collective-permute-start(bf16[16,640]{1,0:T(8,128)(2,1)} %get-tuple-element.29), channel_id=1, source_target_pairs={{0,1},{1,0},{2,3},{3,2},{4,5},{5,4},{6,7},{7,6},{8,9},{9,8},{10,11... | collective-permute-start | bytes 61448 | tf_op jit(solution)/shard_map/ppermute | solution.py:65
  7.9 8.6 %collective-permute-start.3 = (bf16[16,640]{1,0:T(8,128)(2,1)}, bf16[16,640]{1,0:T(8,128)(2,1)S(1)}, u32[]{:S(2)}, u32[]{:S(2)}) collective-permute-start(bf16[16,640]{1,0:T(8,128)(2,1)} %get-tuple-element.30), channel_id=1, source_target_pairs={{0,7},{1,2},{2,1},{3,4},{4,3},{5,6},{6,5},{7,0},{8,15},{9,10},{10,... | collective-permute-start | bytes 61448 | tf_op jit(solution)/shard_map/ppermute | solution.py:65
  11.5 0.8 %copy-start.1 = (f32[64,256]{1,0:T(8,128)S(1)}, f32[64,256]{1,0:T(8,128)}, u32[]{:S(2)}) copy-start(f32[64,256]{1,0:T(8,128)} %get-tuple-element.22.small_ref) | copy-start | bytes 196612
  39.7 3.4 %collective-permute-start.4 = (bf16[16,576]{1,0:T(8,128)(2,1)S(1)}, bf16[16,576]{1,0:T(8,128)(2,1)S(1)}, u32[]{:S(2)}, u32[]{:S(2)}) collective-permute-start(bf16[16,576]{1,0:T(8,128)(2,1)S(1)} %get-tuple-element.32), channel_id=1, source_target_pairs={{0,24},{8,16},{16,8},{24,0},{1,25},{9,17},{17,9},{25,1},{2,26},{10... | collective-permute-start | bytes 55304 | tf_op jit(solution)/shard_map/ppermute | solution.py:65
  40.3 2.8 %collective-permute-start.5 = (bf16[16,576]{1,0:T(8,128)(2,1)S(1)}, bf16[16,576]{1,0:T(8,128)(2,1)S(1)}, u32[]{:S(2)}, u32[]{:S(2)}) collective-permute-start(bf16[16,576]{1,0:T(8,128)(2,1)S(1)} %get-tuple-element.33), channel_id=1, source_target_pairs={{0,8},{8,0},{16,24},{24,16},{1,9},{9,1},{17,25},{25,17},{2,10},{10... | collective-permute-start | bytes 55304 | tf_op jit(solution)/shard_map/ppermute | solution.py:65
  43.3 6.5 %collective-permute-start.6 = (bf16[16,576]{1,0:T(8,128)(2,1)S(1)}, bf16[16,576]{1,0:T(8,128)(2,1)S(1)}, u32[]{:S(2)}, u32[]{:S(2)}) collective-permute-start(bf16[16,576]{1,0:T(8,128)(2,1)S(1)} %get-tuple-element.35), channel_id=1, source_target_pairs={{0,7},{1,2},{2,1},{3,4},{4,3},{5,6},{6,5},{7,0},{8,15},{9,10},{10,... | collective-permute-start | bytes 55304 | tf_op jit(solution)/shard_map/ppermute | solution.py:65
  44.9 4.9 %collective-permute-start.7 = (bf16[16,576]{1,0:T(8,128)(2,1)S(1)}, bf16[16,576]{1,0:T(8,128)(2,1)S(1)}, u32[]{:S(2)}, u32[]{:S(2)}) collective-permute-start(bf16[16,576]{1,0:T(8,128)(2,1)S(1)} %get-tuple-element.36), channel_id=1, source_target_pairs={{0,1},{1,0},{2,3},{3,2},{4,5},{5,4},{6,7},{7,6},{8,9},{9,8},{10,11... | collective-permute-start | bytes 55304 | tf_op jit(solution)/shard_map/ppermute | solution.py:65
  50.6 18.6 %copy-start.2 = (f32[64,256]{1,0:T(8,128)S(1)}, f32[64,256]{1,0:T(8,128)}, u32[]{:S(2)}) copy-start(f32[64,256]{1,0:T(8,128)} %get-tuple-element.22.small_ref) | copy-start | bytes 196612

commit v7 on v6

--- a/solution.py
+++ b/solution.py
@@ -158,8 +158,9 @@
 
 
 def side_by_side(ref, first, begin, width):
-    first = first + begin // GROUP
-    rows = [ref[r : r + 1, :] for r in range(first, first + width // GROUP)]
+    lanes = ref.shape[1]
+    first = first + begin // lanes
+    rows = [ref[r : r + 1, :] for r in range(first, first + width // lanes)]
     return jnp.concatenate(rows, axis=1)
 
 
@@ -172,7 +173,7 @@
 
 
 def deposit_kernel(
-    capacity, rows, leaving, part_ref, small_ref, sum_ref, code_ref, slot_ref, mark_ref, live_ref, columns_ref
+    capacity, rows, leaving, part_ref, small_ref, sum_ref, code_ref, slot_ref, mark_ref, live_ref
 ):
     channels, parts = part_ref.shape
     slots = code_ref.shape[1]
@@ -182,13 +183,11 @@
     closure = small_ref[closure_row:leave_row, :channels]
 
     leave = side_by_side(small_ref, leave_row, 0, leaving).astype(jnp.int32)
-    pieces = leaving // LANES
-    columns = [leave[:, k * LANES : (k + 1) * LANES] % GROUP for k in range(pieces)]
-    columns.append(jnp.zeros((LANES - pieces, LANES), jnp.int32))
-    columns = jnp.concatenate(columns, axis=0).astype(jnp.float32).T
-    lane = iota((LANES, GROUP), 1).astype(jnp.float32)
-    low = jnp.concatenate([one_hot(lane == columns[:, k : k + 1]) for k in range(pieces)], axis=0)
-    live_ref[...] = 1.0 - dot(ones(equal(groups, leave // GROUP)), low)
+    halves = [leave[:, : leaving // 2], leave[:, leaving // 2 :]]
+    high = jnp.concatenate([ones(equal(2 * groups, half // LANES)) for half in halves], axis=0)
+    low = jnp.concatenate([ones(equal(LANES, half % LANES)) for half in halves], axis=0)
+    hits = dot(high, low, NT)
+    live_ref[...] = 1.0 - (hits[: 2 * groups, :LANES] + hits[2 * groups :, LANES:])
 
     sizes, owners, offset = [small_ref[r : r + 1, :] for r in range(3)]
     offset = offset.astype(jnp.int32)
@@ -204,16 +203,14 @@
     earlier = ones((turned[:, 1:2] == owners) & (below < across))
     rank = dot(jnp.ones((8, tiles), jnp.bfloat16), earlier)[0:1]
     slot_ref[...] = (owners * capacity + rank).astype(jnp.int32)
-    columns_ref[0] = jnp.broadcast_to(start, (tiles, LANES)).astype(jnp.int16)
-    columns_ref[1] = jnp.broadcast_to(code_step, (tiles, LANES)).astype(jnp.int16)
+    starts = jnp.broadcast_to(start.astype(jnp.int16), (tiles, CHUNK))
+    steps = jnp.broadcast_to(code_step.astype(jnp.int16), (tiles, CHUNK))
     lines = iota(mark_ref.shape, 0)
     marks = jnp.where(lines == 0, offset // FZ, jnp.where(lines == 1, offset % FZ, 0))
     mark_ref[...] = marks.astype(jnp.float32).astype(jnp.bfloat16)
 
     def find(begin):
         cell = side_by_side(small_ref, cell_row, begin, CHUNK).astype(jnp.int32)
-        starts = jnp.concatenate([columns_ref[0]] * (CHUNK // LANES), axis=1)
-        steps = jnp.concatenate([columns_ref[1]] * (CHUNK // LANES), axis=1)
         found = jnp.where(cell.astype(jnp.int16) >= starts, steps, jnp.int16(0))
         while found.shape[0] > 16:
             half = found.shape[0] // 2
@@ -231,10 +228,8 @@
         state = part_ref[:, begin : begin + CHUNK] * live
         mixed, first = mix(closure, state.astype(jnp.bfloat16))
         added = dot(spread(mixed, first, place), ones(equal(tiles, tile)), NT)
-        if begin == 0:
-            sum_ref[...] = added
-        else:
-            sum_ref[...] += added
+        total = added if begin == 0 else total + added
+    sum_ref[...] = total
 
 
 def pack_kernel(rows, sum_ref, code_ref, slot_ref, mark_ref, small_ref, *refs):
@@ -423,8 +418,8 @@
     sums, code, slot, marks, live = call(
         functools.partial(deposit_kernel, capacity, rows, 4 * migr),
         [shape((width, tiles), f32), shape((1, slots), i32), shape((1, tiles), i32),
-         shape((lanes - width, tiles), bf16), shape((parts // GROUP, GROUP), f32)],
-        particles, small, scratch=[pltpu.VMEM((2, tiles, LANES), jnp.int16)],
+         shape((lanes - width, tiles), bf16), shape((parts // LANES, LANES), f32)],
+        particles, small,
     )
     (payload,) = call(
         functools.partial(pack_kernel, rows), [shape((count, lanes), bf16)],

time: 73.4 us -> 73.4 us (level)
  transfers between devices with their start and end apart: 8 -> 8, of which waited for: 2 -> 2; matrix products, arithmetic and copies ran while one was open for 0% -> 0% of each run, Pallas kernels for 6% -> 5%
where the time goes in v7:
time: 73.4 us; the launch traced here: 73.2 us
  blocking collectives  40.1 us (55%)
  Pallas kernels  13.4 us (18%)
  starting transfers between devices  11 us (15%)
  waiting for transfers between devices  7.11 us (10%)
  local copies, waits for them, and re-layouts  0.86 us (1%)
    all_to_all x1, blocking collectives, per_device(): lax.all_to_all(payload.reshape(devices, capacity, lanes), ('gx', 'gy'), s...  21.5 us
    all_to_all x1, blocking collectives, per_device(): lax.all_to_all(back.reshape(devices, capacity, rows * TILE), ('gx', 'gy')...  18.5 us
    pallas_call x7, Pallas kernels, call(): pl.pallas_call(kernel, out_shape=shapes, in_specs=[hbm if limit else vmem...  13.4 us
    ppermute x8, starting transfers between devices, exchange(): blocks[odd] = lax.ppermute(block, axis, pairs)  11 us
    ppermute x8, waiting for transfers between devices, exchange(): blocks[odd] = lax.ppermute(block, axis, pairs)  7.11 us
  transfers between devices with their start and end apart: 8, of which 2 were waited for; matrix products, arithmetic and copies ran while one was open for 0% of the time, Pallas kernels for 5%

profile of v7, /device:TPU:0, one launch (start us, length us, event | category | flops | bytes accessed | tf_op | source)
XLA Modules:
  0.0 73.2 jit_solution(12385435376568915147)
XLA Ops:
  0.6 0.0 copy-start
  0.6 2.6 %shard_map.104 = (bf16[16,640]{1,0:T(8,128)(2,1)}, bf16[16,640]{1,0:T(8,128)(2,1)}, bf16[16,640]{1,0:T(8,128)(2,1)}, bf16[16,640]{1,0:T(8,128)(2,1)}, f32[64,256]{1,0:T(8,128)}) custom-call(f32[16,8192]{1,0:T(8,128)} %part_ref.3, s32[4,512]{1,0:T(4,128)} %index_hbm.1, s32[1,4]{1,0:T(1,128)} %count_hbm.1, s32[1,256]{1,0:T(1,128)} %size_hbm.1, ...), custom_call_target="tpu_custom_call" | custom-call | tf_op jit(solution)/shard_map/pallas_call | solution.py:371
  3.3 0.5 collective-permute-start
  3.8 2.6 %collective-permute-start.1 = (bf16[16,640]{1,0:T(8,128)(2,1)}, bf16[16,640]{1,0:T(8,128)(2,1)S(1)}, u32[]{:S(2)}, u32[]{:S(2)}) collective-permute-start(bf16[16,640]{1,0:T(8,128)(2,1)} %get-tuple-element.28), channel_id=1, source_target_pairs={{0,24},{8,16},{16,8},{24,0},{1,25},{9,17},{17,9},{25,1},{2,26},{10... | collective-permute-start | bytes 61448 | tf_op jit(solution)/shard_map/ppermute | solution.py:65
  6.4 1.5 %collective-permute-start.2 = (bf16[16,640]{1,0:T(8,128)(2,1)}, bf16[16,640]{1,0:T(8,128)(2,1)S(1)}, u32[]{:S(2)}, u32[]{:S(2)}) collective-permute-start(bf16[16,640]{1,0:T(8,128)(2,1)} %get-tuple-element.29), channel_id=1, source_target_pairs={{0,1},{1,0},{2,3},{3,2},{4,5},{5,4},{6,7},{7,6},{8,9},{9,8},{10,11... | collective-permute-start | bytes 61448 | tf_op jit(solution)/shard_map/ppermute | solution.py:65
  7.9 3.5 %collective-permute-start.3 = (bf16[16,640]{1,0:T(8,128)(2,1)}, bf16[16,640]{1,0:T(8,128)(2,1)S(1)}, u32[]{:S(2)}, u32[]{:S(2)}) collective-permute-start(bf16[16,640]{1,0:T(8,128)(2,1)} %get-tuple-element.30), channel_id=1, source_target_pairs={{0,7},{1,2},{2,1},{3,4},{4,3},{5,6},{6,5},{7,0},{8,15},{9,10},{10,... | collective-permute-start | bytes 61448 | tf_op jit(solution)/shard_map/ppermute | solution.py:65
  11.5 0.0 copy-done
  11.5 0.0 copy-start.1
  11.5 0.8 %copy-done.1 = f32[64,256]{1,0:T(8,128)S(1)} copy-done((f32[64,256]{1,0:T(8,128)S(1)}, f32[64,256]{1,0:T(8,128)}, u32[]{:S(2)}) %copy-start.1) | copy-done | bytes 65560
  12.3 3.6 %shard_map.105 = (f32[576,256]{1,0:T(8,128)S(1)}, s32[1,10240]{1,0:T(1,128)S(1)}, s32[1,256]{1,0:T(1,128)S(1)}, bf16[64,256]{1,0:T(8,128)(2,1)S(1)}, f32[64,128]{1,0:T(8,128)S(1)}) custom-call(f32[16,8192]{1,0:T(8,128)S(1)} %copy-done, f32[64,256]{1,0:T(8,128)S(1)} %copy-done.1), custom_call_target="tpu_custom_call" | custom-call | tf_op jit(solution)/shard_map/pallas_call | solution.py:371
  15.9 0.0 collective-permute-done.refs_0_
  15.9 0.0 collective-permute-done.1.refs_1_
  15.9 0.0 collective-permute-done.2.refs_2_
  15.9 0.0 collective-permute-done.3.refs_3_
  16.0 1.6 %shard_map.106 = bf16[512,640]{1,0:T(8,128)(2,1)S(1)} custom-call(f32[576,256]{1,0:T(8,128)S(1)} %get-tuple-element.23.sum_ref, s32[1,10240]{1,0:T(1,128)S(1)} %get-tuple-element.24.code_ref, s32[1,256]{1,0:T(1,128)S(1)} %get-tuple-element.25.slot_ref, bf16[64,256]{1,0:T(8,128)(2,1)S(1)} %get-tuple-element.26.mark_ref, f32[64,256]{1,0:T(8,128)S(1)} %copy-done.1, ...), custom_call_target="tpu_custom_call" | custom-call | tf_op jit(solution)/shard_map/pallas_call | solution.py:371
  17.6 21.5 %all_to_all.10 = bf16[32,16,640]{2,1,0:T(8,128)(2,1)S(1)} all-to-all(bf16[32,16,640]{2,1,0:T(8,128)(2,1)S(1)} %bitcast.10), channel_id=1, replica_groups=mesh['gx'=4,'gy'=8] {'gx','gy'}, dimensions={0} | all-to-all | bytes 1310720 | tf_op jit(solution)/shard_map/all_to_all | solution.py:428
  39.1 0.6 shard_map.107
  39.7 0.5 collective-permute-start.4
  40.3 0.2 collective-permute-start.5
  40.5 2.6 %collective-permute-done.4.xb_ref = bf16[16,576]{1,0:T(8,128)(2,1)S(1)} collective-permute-done((bf16[16,576]{1,0:T(8,128)(2,1)S(1)}, bf16[16,576]{1,0:T(8,128)(2,1)S(1)}, u32[]{:S(2)}, u32[]{:S(2)}) %collective-permute-start.4) | collective-permute-done | bytes 18464 | tf_op jit(solution)/shard_map/ppermute | solution.py:65
  43.1 0.0 collective-permute-done.5.xa_ref
  43.1 0.2 shard_map.108
  43.3 1.7 %collective-permute-start.6 = (bf16[16,576]{1,0:T(8,128)(2,1)S(1)}, bf16[16,576]{1,0:T(8,128)(2,1)S(1)}, u32[]{:S(2)}, u32[]{:S(2)}) collective-permute-start(bf16[16,576]{1,0:T(8,128)(2,1)S(1)} %get-tuple-element.35), channel_id=1, source_target_pairs={{0,7},{1,2},{2,1},{3,4},{4,3},{5,6},{6,5},{7,0},{8,15},{9,10},{10,... | collective-permute-start | bytes 55304 | tf_op jit(solution)/shard_map/ppermute | solution.py:65
  44.9 0.4 collective-permute-start.7
  45.3 4.5 %collective-permute-done.6.yb_ref = bf16[16,576]{1,0:T(8,128)(2,1)S(1)} collective-permute-done((bf16[16,576]{1,0:T(8,128)(2,1)S(1)}, bf16[16,576]{1,0:T(8,128)(2,1)S(1)}, u32[]{:S(2)}, u32[]{:S(2)}) %collective-permute-start.6) | collective-permute-done | bytes 18464 | tf_op jit(solution)/shard_map/ppermute | solution.py:65
  49.8 0.0 collective-permute-done.7.ya_ref
  49.8 0.8 %shard_map.109 = (bf16[8,8,8,128]{3,2,1,0:T(8,128)(2,1)S(1)}, bf16[512,512]{1,0:T(8,128)(2,1)S(1)}) custom-call(bf16[512,128]{1,0:T(8,128)(2,1)S(1)} %slice.4.mark_ref, f32[64,1152]{1,0:T(8,128)S(1)} %get-tuple-element.34.along_ref, bf16[16,576]{1,0:T(8,128)(2,1)S(1)} %collective-permute-done.6.yb_ref, bf16[16,576]{1,0:T(8,128)(2,1)S(1)} %collective-permute-done.7.ya_ref), custom_call_target="tpu_custom_call" | custom-call | tf_op jit(solution)/shard_map/pallas_call | solution.py:371
  50.6 0.0 copy-start.2
  50.6 18.5 %all_to_all.11 = bf16[32,16,512]{2,1,0:T(8,128)(2,1)S(1)} all-to-all(bf16[32,16,512]{2,1,0:T(8,128)(2,1)S(1)} %bitcast.12), channel_id=1, replica_groups=mesh['gx'=4,'gy'=8] {'gx','gy'}, dimensions={0} | all-to-all | bytes 1048576 | tf_op jit(solution)/shard_map/all_to_all | solution.py:441
  69.1 0.0 copy-done.2
  69.1 4.0 %shard_map.110 = (f32[8,10240]{1,0:T(8,128)}, bf16[8,8,8,128]{3,2,1,0:T(8,128)(2,1)}) custom-call(bf16[512,512]{1,0:T(8,128)(2,1)S(1)} %bitcast.11, s32[1,256]{1,0:T(1,128)S(1)} %get-tuple-element.25.slot_ref, s32[1,10240]{1,0:T(1,128)S(1)} %get-tuple-element.24.code_ref, f32[16,8192]{1,0:T(8,128)S(1)} %copy-done, f32[64,256]{1,0:T(8,128)S(1)} %copy-done.2, ...), custom_call_target="tpu_custom_call" | custom-call | tf_op jit(solution)/shard_map/pallas_call | solution.py:371
  (1 shorter events, 0.0 us)
Async XLA Ops:
  0.6 10.8 %copy-start = (f32[16,8192]{1,0:T(8,128)S(1)}, f32[16,8192]{1,0:T(8,128)}, u32[]{:S(2)}) copy-start(f32[16,8192]{1,0:T(8,128)} %part_ref.3) | copy-start | bytes 1572868
  3.3 12.7 %collective-permute-start = (bf16[16,640]{1,0:T(8,128)(2,1)}, bf16[16,640]{1,0:T(8,128)(2,1)S(1)}, u32[]{:S(2)}, u32[]{:S(2)}) collective-permute-start(bf16[16,640]{1,0:T(8,128)(2,1)} %get-tuple-element.27), channel_id=1, source_target_pairs={{0,8},{8,0},{16,24},{24,16},{1,9},{9,1},{17,25},{25,17},{2,10},{10... | collective-permute-start | bytes 61448 | tf_op jit(solution)/shard_map/ppermute | solution.py:65
  3.8 12.2 %collective-permute-start.1 = (bf16[16,640]{1,0:T(8,128)(2,1)}, bf16[16,640]{1,0:T(8,128)(2,1)S(1)}, u32[]{:S(2)}, u32[]{:S(2)}) collective-permute-start(bf16[16,640]{1,0:T(8,128)(2,1)} %get-tuple-element.28), channel_id=1, source_target_pairs={{0,24},{8,16},{16,8},{24,0},{1,25},{9,17},{17,9},{25,1},{2,26},{10... | collective-permute-start | bytes 61448 | tf_op jit(solution)/shard_map/ppermute | solution.py:65
  6.4 9.5 %collective-permute-start.2 = (bf16[16,640]{1,0:T(8,128)(2,1)}, bf16[16,640]{1,0:T(8,128)(2,1)S(1)}, u32[]{:S(2)}, u32[]{:S(2)}) collective-permute-start(bf16[16,640]{1,0:T(8,128)(2,1)} %get-tuple-element.29), channel_id=1, source_target_pairs={{0,1},{1,0},{2,3},{3,2},{4,5},{5,4},{6,7},{7,6},{8,9},{9,8},{10,11... | collective-permute-start | bytes 61448 | tf_op jit(solution)/shard_map/ppermute | solution.py:65
  7.9 8.0 %collective-permute-start.3 = (bf16[16,640]{1,0:T(8,128)(2,1)}, bf16[16,640]{1,0:T(8,128)(2,1)S(1)}, u32[]{:S(2)}, u32[]{:S(2)}) collective-permute-start(bf16[16,640]{1,0:T(8,128)(2,1)} %get-tuple-element.30), channel_id=1, source_target_pairs={{0,7},{1,2},{2,1},{3,4},{4,3},{5,6},{6,5},{7,0},{8,15},{9,10},{10,... | collective-permute-start | bytes 61448 | tf_op jit(solution)/shard_map/ppermute | solution.py:65
  11.5 0.8 %copy-start.1 = (f32[64,256]{1,0:T(8,128)S(1)}, f32[64,256]{1,0:T(8,128)}, u32[]{:S(2)}) copy-start(f32[64,256]{1,0:T(8,128)} %get-tuple-element.22.small_ref) | copy-start | bytes 196612
  39.7 3.4 %collective-permute-start.4 = (bf16[16,576]{1,0:T(8,128)(2,1)S(1)}, bf16[16,576]{1,0:T(8,128)(2,1)S(1)}, u32[]{:S(2)}, u32[]{:S(2)}) collective-permute-start(bf16[16,576]{1,0:T(8,128)(2,1)S(1)} %get-tuple-element.32), channel_id=1, source_target_pairs={{0,24},{8,16},{16,8},{24,0},{1,25},{9,17},{17,9},{25,1},{2,26},{10... | collective-permute-start | bytes 55304 | tf_op jit(solution)/shard_map/ppermute | solution.py:65
  40.3 2.8 %collective-permute-start.5 = (bf16[16,576]{1,0:T(8,128)(2,1)S(1)}, bf16[16,576]{1,0:T(8,128)(2,1)S(1)}, u32[]{:S(2)}, u32[]{:S(2)}) collective-permute-start(bf16[16,576]{1,0:T(8,128)(2,1)S(1)} %get-tuple-element.33), channel_id=1, source_target_pairs={{0,8},{8,0},{16,24},{24,16},{1,9},{9,1},{17,25},{25,17},{2,10},{10... | collective-permute-start | bytes 55304 | tf_op jit(solution)/shard_map/ppermute | solution.py:65
  43.3 6.5 %collective-permute-start.6 = (bf16[16,576]{1,0:T(8,128)(2,1)S(1)}, bf16[16,576]{1,0:T(8,128)(2,1)S(1)}, u32[]{:S(2)}, u32[]{:S(2)}) collective-permute-start(bf16[16,576]{1,0:T(8,128)(2,1)S(1)} %get-tuple-element.35), channel_id=1, source_target_pairs={{0,7},{1,2},{2,1},{3,4},{4,3},{5,6},{6,5},{7,0},{8,15},{9,10},{10,... | collective-permute-start | bytes 55304 | tf_op jit(solution)/shard_map/ppermute | solution.py:65
  44.9 4.9 %collective-permute-start.7 = (bf16[16,576]{1,0:T(8,128)(2,1)S(1)}, bf16[16,576]{1,0:T(8,128)(2,1)S(1)}, u32[]{:S(2)}, u32[]{:S(2)}) collective-permute-start(bf16[16,576]{1,0:T(8,128)(2,1)S(1)} %get-tuple-element.36), channel_id=1, source_target_pairs={{0,1},{1,0},{2,3},{3,2},{4,5},{5,4},{6,7},{7,6},{8,9},{9,8},{10,11... | collective-permute-start | bytes 55304 | tf_op jit(solution)/shard_map/ppermute | solution.py:65
  50.6 18.6 %copy-start.2 = (f32[64,256]{1,0:T(8,128)S(1)}, f32[64,256]{1,0:T(8,128)}, u32[]{:S(2)}) copy-start(f32[64,256]{1,0:T(8,128)} %get-tuple-element.22.small_ref) | copy-start | bytes 196612

commit v8 on v7

--- a/solution.py
+++ b/solution.py
@@ -82,8 +82,8 @@
 
 
 def arrived_blocks(refs):
-    blocks = [ref[...].astype(jnp.float32) for ref in refs]
-    return ordered(blocks[0], blocks[1], "gx") + ordered(blocks[2], blocks[3], "gy")
+    yb, xb, ya, xa = [ref[...].astype(jnp.float32) for ref in refs]
+    return ordered(xa, xb, "gx") + ordered(ya, yb, "gy")
 
 
 def small_rows(rows, leaving, slots):
@@ -414,7 +414,8 @@
         + [pltpu.VMEM((4, channels, migr + LANES), bf16), pltpu.VMEM((small_count, GROUP), f32),
            pltpu.SemaphoreType.DMA((9,)), pltpu.SemaphoreType.DMA((5,))],
     )
-    arrived = exchange(*leaving[:2], "gx") + exchange(*leaving[2:], "gy")
+    (xa, xb), (ya, yb) = exchange(*leaving[:2], "gx"), exchange(*leaving[2:], "gy")
+    arrived = yb, xb, ya, xa
     sums, code, slot, marks, live = call(
         functools.partial(deposit_kernel, capacity, rows, 4 * migr),
         [shape((width, tiles), f32), shape((1, slots), i32), shape((1, tiles), i32),

time: 73.4 us -> 72.5 us (0.988)
  no operation moved by 1% of the time
where the time goes in v8:
time: 72.5 us; the launch traced here: 72.2 us
  blocking collectives  39.6 us (55%)
  Pallas kernels  13.4 us (18%)
  starting transfers between devices  10.5 us (14%)
  waiting for transfers between devices  7.12 us (10%)
  local copies, waits for them, and re-layouts  0.86 us (1%)
    all_to_all x1, blocking collectives, per_device(): lax.all_to_all(payload.reshape(devices, capacity, lanes), ('gx', 'gy'), s...  21.1 us
    all_to_all x1, blocking collectives, per_device(): lax.all_to_all(back.reshape(devices, capacity, rows * TILE), ('gx', 'gy')...  18.5 us
    pallas_call x7, Pallas kernels, call(): pl.pallas_call(kernel, out_shape=shapes, in_specs=[hbm if limit else vmem...  13.4 us
    ppermute x8, starting transfers between devices, exchange(): blocks[odd] = lax.ppermute(block, axis, pairs)  10.5 us
    ppermute x8, waiting for transfers between devices, exchange(): blocks[odd] = lax.ppermute(block, axis, pairs)  7.12 us
  transfers between devices with their start and end apart: 8, of which 2 were waited for; matrix products, arithmetic and copies ran while one was open for 0% of the time, Pallas kernels for 5%

profile of v8, /device:TPU:0, one launch (start us, length us, event | category | flops | bytes accessed | tf_op | source)
XLA Modules:
  0.0 72.2 jit_solution(8805596148640668331)
XLA Ops:
  0.6 0.0 copy-start
  0.6 2.6 %shard_map.104 = (bf16[16,640]{1,0:T(8,128)(2,1)}, bf16[16,640]{1,0:T(8,128)(2,1)}, bf16[16,640]{1,0:T(8,128)(2,1)}, bf16[16,640]{1,0:T(8,128)(2,1)}, f32[64,256]{1,0:T(8,128)}) custom-call(f32[16,8192]{1,0:T(8,128)} %part_ref.3, s32[4,512]{1,0:T(4,128)} %index_hbm.1, s32[1,4]{1,0:T(1,128)} %count_hbm.1, s32[1,256]{1,0:T(1,128)} %size_hbm.1, ...), custom_call_target="tpu_custom_call" | custom-call | tf_op jit(solution)/shard_map/pallas_call | solution.py:371
  3.3 6.1 %collective-permute-start = (bf16[16,640]{1,0:T(8,128)(2,1)}, bf16[16,640]{1,0:T(8,128)(2,1)S(1)}, u32[]{:S(2)}, u32[]{:S(2)}) collective-permute-start(bf16[16,640]{1,0:T(8,128)(2,1)} %get-tuple-element.27), channel_id=1, source_target_pairs={{0,7},{1,2},{2,1},{3,4},{4,3},{5,6},{6,5},{7,0},{8,15},{9,10},{10,... | collective-permute-start | bytes 61448 | tf_op jit(solution)/shard_map/ppermute | solution.py:65
  9.3 0.7 collective-permute-start.1
  10.0 0.0 collective-permute-start.2
  10.0 1.0 %collective-permute-start.3 = (bf16[16,640]{1,0:T(8,128)(2,1)}, bf16[16,640]{1,0:T(8,128)(2,1)S(1)}, u32[]{:S(2)}, u32[]{:S(2)}) collective-permute-start(bf16[16,640]{1,0:T(8,128)(2,1)} %get-tuple-element.30), channel_id=1, source_target_pairs={{0,8},{8,0},{16,24},{24,16},{1,9},{9,1},{17,25},{25,17},{2,10},{10... | collective-permute-start | bytes 61448 | tf_op jit(solution)/shard_map/ppermute | solution.py:65
  10.9 0.0 copy-done
  10.9 0.0 copy-start.1
  10.9 0.8 %copy-done.1 = f32[64,256]{1,0:T(8,128)S(1)} copy-done((f32[64,256]{1,0:T(8,128)S(1)}, f32[64,256]{1,0:T(8,128)}, u32[]{:S(2)}) %copy-start.1) | copy-done | bytes 65560
  11.8 3.6 %shard_map.105 = (f32[576,256]{1,0:T(8,128)S(1)}, s32[1,10240]{1,0:T(1,128)S(1)}, s32[1,256]{1,0:T(1,128)S(1)}, bf16[64,256]{1,0:T(8,128)(2,1)S(1)}, f32[64,128]{1,0:T(8,128)S(1)}) custom-call(f32[16,8192]{1,0:T(8,128)S(1)} %copy-done, f32[64,256]{1,0:T(8,128)S(1)} %copy-done.1), custom_call_target="tpu_custom_call" | custom-call | tf_op jit(solution)/shard_map/pallas_call | solution.py:371
  15.4 0.0 collective-permute-done.refs_0_
  15.4 0.0 collective-permute-done.1.refs_1_
  15.4 0.0 collective-permute-done.2.refs_2_
  15.4 0.0 collective-permute-done.3.refs_3_
  15.4 1.6 %shard_map.106 = bf16[512,640]{1,0:T(8,128)(2,1)S(1)} custom-call(f32[576,256]{1,0:T(8,128)S(1)} %get-tuple-element.23.sum_ref, s32[1,10240]{1,0:T(1,128)S(1)} %get-tuple-element.24.code_ref, s32[1,256]{1,0:T(1,128)S(1)} %get-tuple-element.25.slot_ref, bf16[64,256]{1,0:T(8,128)(2,1)S(1)} %get-tuple-element.26.mark_ref, f32[64,256]{1,0:T(8,128)S(1)} %copy-done.1, ...), custom_call_target="tpu_custom_call" | custom-call | tf_op jit(solution)/shard_map/pallas_call | solution.py:371
  17.1 21.1 %all_to_all.10 = bf16[32,16,640]{2,1,0:T(8,128)(2,1)S(1)} all-to-all(bf16[32,16,640]{2,1,0:T(8,128)(2,1)S(1)} %bitcast.10), channel_id=1, replica_groups=mesh['gx'=4,'gy'=8] {'gx','gy'}, dimensions={0} | all-to-all | bytes 1310720 | tf_op jit(solution)/shard_map/all_to_all | solution.py:429
  38.1 0.6 shard_map.107
  38.8 0.5 collective-permute-start.4
  39.3 0.2 collective-permute-start.5
  39.5 2.6 %collective-permute-done.4.xb_ref = bf16[16,576]{1,0:T(8,128)(2,1)S(1)} collective-permute-done((bf16[16,576]{1,0:T(8,128)(2,1)S(1)}, bf16[16,576]{1,0:T(8,128)(2,1)S(1)}, u32[]{:S(2)}, u32[]{:S(2)}) %collective-permute-start.4) | collective-permute-done | bytes 18464 | tf_op jit(solution)/shard_map/ppermute | solution.py:65
  42.1 0.0 collective-permute-done.5.xa_ref
  42.1 0.2 shard_map.108
  42.3 1.7 %collective-permute-start.6 = (bf16[16,576]{1,0:T(8,128)(2,1)S(1)}, bf16[16,576]{1,0:T(8,128)(2,1)S(1)}, u32[]{:S(2)}, u32[]{:S(2)}) collective-permute-start(bf16[16,576]{1,0:T(8,128)(2,1)S(1)} %get-tuple-element.35), channel_id=1, source_target_pairs={{0,7},{1,2},{2,1},{3,4},{4,3},{5,6},{6,5},{7,0},{8,15},{9,10},{10,... | collective-permute-start | bytes 55304 | tf_op jit(solution)/shard_map/ppermute | solution.py:65
  44.0 0.4 collective-permute-start.7
  44.4 4.5 %collective-permute-done.6.yb_ref = bf16[16,576]{1,0:T(8,128)(2,1)S(1)} collective-permute-done((bf16[16,576]{1,0:T(8,128)(2,1)S(1)}, bf16[16,576]{1,0:T(8,128)(2,1)S(1)}, u32[]{:S(2)}, u32[]{:S(2)}) %collective-permute-start.6) | collective-permute-done | bytes 18464 | tf_op jit(solution)/shard_map/ppermute | solution.py:65
  48.9 0.0 collective-permute-done.7.ya_ref
  48.9 0.8 %shard_map.109 = (bf16[8,8,8,128]{3,2,1,0:T(8,128)(2,1)S(1)}, bf16[512,512]{1,0:T(8,128)(2,1)S(1)}) custom-call(bf16[512,128]{1,0:T(8,128)(2,1)S(1)} %slice.4.mark_ref, f32[64,1152]{1,0:T(8,128)S(1)} %get-tuple-element.34.along_ref, bf16[16,576]{1,0:T(8,128)(2,1)S(1)} %collective-permute-done.6.yb_ref, bf16[16,576]{1,0:T(8,128)(2,1)S(1)} %collective-permute-done.7.ya_ref), custom_call_target="tpu_custom_call" | custom-call | tf_op jit(solution)/shard_map/pallas_call | solution.py:371
  49.6 0.0 copy-start.2
  49.6 18.5 %all_to_all.11 = bf16[32,16,512]{2,1,0:T(8,128)(2,1)S(1)} all-to-all(bf16[32,16,512]{2,1,0:T(8,128)(2,1)S(1)} %bitcast.12), channel_id=1, replica_groups=mesh['gx'=4,'gy'=8] {'gx','gy'}, dimensions={0} | all-to-all | bytes 1048576 | tf_op jit(solution)/shard_map/all_to_all | solution.py:442
  68.2 0.0 copy-done.2
  68.2 4.0 %shard_map.110 = (f32[8,10240]{1,0:T(8,128)}, bf16[8,8,8,128]{3,2,1,0:T(8,128)(2,1)}) custom-call(bf16[512,512]{1,0:T(8,128)(2,1)S(1)} %bitcast.11, s32[1,256]{1,0:T(1,128)S(1)} %get-tuple-element.25.slot_ref, s32[1,10240]{1,0:T(1,128)S(1)} %get-tuple-element.24.code_ref, f32[16,8192]{1,0:T(8,128)S(1)} %copy-done, f32[64,256]{1,0:T(8,128)S(1)} %copy-done.2, ...), custom_call_target="tpu_custom_call" | custom-call | tf_op jit(solution)/shard_map/pallas_call | solution.py:371
  (1 shorter events, 0.0 us)
Async XLA Ops:
  0.6 10.3 %copy-start = (f32[16,8192]{1,0:T(8,128)S(1)}, f32[16,8192]{1,0:T(8,128)}, u32[]{:S(2)}) copy-start(f32[16,8192]{1,0:T(8,128)} %part_ref.3) | copy-start | bytes 1572868
  3.3 12.1 %collective-permute-start = (bf16[16,640]{1,0:T(8,128)(2,1)}, bf16[16,640]{1,0:T(8,128)(2,1)S(1)}, u32[]{:S(2)}, u32[]{:S(2)}) collective-permute-start(bf16[16,640]{1,0:T(8,128)(2,1)} %get-tuple-element.27), channel_id=1, source_target_pairs={{0,7},{1,2},{2,1},{3,4},{4,3},{5,6},{6,5},{7,0},{8,15},{9,10},{10,... | collective-permute-start | bytes 61448 | tf_op jit(solution)/shard_map/ppermute | solution.py:65
  9.3 6.1 %collective-permute-start.1 = (bf16[16,640]{1,0:T(8,128)(2,1)}, bf16[16,640]{1,0:T(8,128)(2,1)S(1)}, u32[]{:S(2)}, u32[]{:S(2)}) collective-permute-start(bf16[16,640]{1,0:T(8,128)(2,1)} %get-tuple-element.28), channel_id=1, source_target_pairs={{0,24},{8,16},{16,8},{24,0},{1,25},{9,17},{17,9},{25,1},{2,26},{10... | collective-permute-start | bytes 61448 | tf_op jit(solution)/shard_map/ppermute | solution.py:65
  10.0 5.4 %collective-permute-start.2 = (bf16[16,640]{1,0:T(8,128)(2,1)}, bf16[16,640]{1,0:T(8,128)(2,1)S(1)}, u32[]{:S(2)}, u32[]{:S(2)}) collective-permute-start(bf16[16,640]{1,0:T(8,128)(2,1)} %get-tuple-element.29), channel_id=1, source_target_pairs={{0,1},{1,0},{2,3},{3,2},{4,5},{5,4},{6,7},{7,6},{8,9},{9,8},{10,11... | collective-permute-start | bytes 61448 | tf_op jit(solution)/shard_map/ppermute | solution.py:65
  10.0 5.4 %collective-permute-start.3 = (bf16[16,640]{1,0:T(8,128)(2,1)}, bf16[16,640]{1,0:T(8,128)(2,1)S(1)}, u32[]{:S(2)}, u32[]{:S(2)}) collective-permute-start(bf16[16,640]{1,0:T(8,128)(2,1)} %get-tuple-element.30), channel_id=1, source_target_pairs={{0,8},{8,0},{16,24},{24,16},{1,9},{9,1},{17,25},{25,17},{2,10},{10... | collective-permute-start | bytes 61448 | tf_op jit(solution)/shard_map/ppermute | solution.py:65
  10.9 0.8 %copy-start.1 = (f32[64,256]{1,0:T(8,128)S(1)}, f32[64,256]{1,0:T(8,128)}, u32[]{:S(2)}) copy-start(f32[64,256]{1,0:T(8,128)} %get-tuple-element.22.small_ref) | copy-start | bytes 196612
  38.8 3.3 %collective-permute-start.4 = (bf16[16,576]{1,0:T(8,128)(2,1)S(1)}, bf16[16,576]{1,0:T(8,128)(2,1)S(1)}, u32[]{:S(2)}, u32[]{:S(2)}) collective-permute-start(bf16[16,576]{1,0:T(8,128)(2,1)S(1)} %get-tuple-element.32), channel_id=1, source_target_pairs={{0,24},{8,16},{16,8},{24,0},{1,25},{9,17},{17,9},{25,1},{2,26},{10... | collective-permute-start | bytes 55304 | tf_op jit(solution)/shard_map/ppermute | solution.py:65
  39.3 2.8 %collective-permute-start.5 = (bf16[16,576]{1,0:T(8,128)(2,1)S(1)}, bf16[16,576]{1,0:T(8,128)(2,1)S(1)}, u32[]{:S(2)}, u32[]{:S(2)}) collective-permute-start(bf16[16,576]{1,0:T(8,128)(2,1)S(1)} %get-tuple-element.33), channel_id=1, source_target_pairs={{0,8},{8,0},{16,24},{24,16},{1,9},{9,1},{17,25},{25,17},{2,10},{10... | collective-permute-start | bytes 55304 | tf_op jit(solution)/shard_map/ppermute | solution.py:65
  42.3 6.5 %collective-permute-start.6 = (bf16[16,576]{1,0:T(8,128)(2,1)S(1)}, bf16[16,576]{1,0:T(8,128)(2,1)S(1)}, u32[]{:S(2)}, u32[]{:S(2)}) collective-permute-start(bf16[16,576]{1,0:T(8,128)(2,1)S(1)} %get-tuple-element.35), channel_id=1, source_target_pairs={{0,7},{1,2},{2,1},{3,4},{4,3},{5,6},{6,5},{7,0},{8,15},{9,10},{10,... | collective-permute-start | bytes 55304 | tf_op jit(solution)/shard_map/ppermute | solution.py:65
  44.0 4.9 %collective-permute-start.7 = (bf16[16,576]{1,0:T(8,128)(2,1)S(1)}, bf16[16,576]{1,0:T(8,128)(2,1)S(1)}, u32[]{:S(2)}, u32[]{:S(2)}) collective-permute-start(bf16[16,576]{1,0:T(8,128)(2,1)S(1)} %get-tuple-element.36), channel_id=1, source_target_pairs={{0,1},{1,0},{2,3},{3,2},{4,5},{5,4},{6,7},{7,6},{8,9},{9,8},{10,11... | collective-permute-start | bytes 55304 | tf_op jit(solution)/shard_map/ppermute | solution.py:65
  49.6 18.6 %copy-start.2 = (f32[64,256]{1,0:T(8,128)S(1)}, f32[64,256]{1,0:T(8,128)}, u32[]{:S(2)}) copy-start(f32[64,256]{1,0:T(8,128)} %get-tuple-element.22.small_ref) | copy-start | bytes 196612

commit v9 on v8

--- a/solution.py
+++ b/solution.py
@@ -246,15 +246,17 @@
     out_ref[...] = dot(match, table, NT).astype(jnp.bfloat16)
 
 
-def place_kernel(tile_ref, gas_ref, xa_ref, xb_ref):
-    even = is_even("gx")
+def place_kernel(tile_ref, gas_ref, xa_ref, xb_ref, ya_ref, yb_ref):
+    x_even, y_even = is_even("gx"), is_even("gy")
     count, lanes = tile_ref.shape
     width = gas_ref.shape[1] // 2
     marks = tile_ref[:, lanes - LANES :].astype(jnp.float32)
     column = marks[:, width % LANES : width % LANES + 1]
     height = marks[:, width % LANES + 1 : width % LANES + 2]
     lane = iota((1, LANES), 1)
-    hot = one_hot(column == lane.astype(jnp.float32))
+    edge = jnp.where(lane < COLS + FX, (lane - COLS) * FY, (lane - COLS - FX) * FY + FY - 1)
+    target = jnp.where(lane < COLS, lane, jnp.where(lane < COLS + 2 * FX, edge, -1))
+    hot = one_hot(column == target.astype(jnp.float32))
     place = (iota((1, width), 1) % TILE).astype(jnp.float32)
     values = tile_ref[:, :width].astype(jnp.float32)
     for half, mask in enumerate((place >= height, place < height)):
@@ -263,8 +265,11 @@
         gas_ref[:, where] = total[:COLS]
         rows = slice(half * FY, (half + 1) * FY)
         low, high = total[:FY], total[COLS - FY : COLS]
-        xa_ref[rows, :] = jnp.where(even, high, low).astype(jnp.bfloat16)
-        xb_ref[rows, :] = jnp.where(even, low, high).astype(jnp.bfloat16)
+        xa_ref[rows, :] = jnp.where(x_even, high, low).astype(jnp.bfloat16)
+        xb_ref[rows, :] = jnp.where(x_even, low, high).astype(jnp.bfloat16)
+        low, high = total[COLS : COLS + FX], total[COLS + FX : COLS + 2 * FX]
+        ya_ref[rows, :] = jnp.where(y_even, high, low).astype(jnp.bfloat16)
+        yb_ref[rows, :] = jnp.where(y_even, low, high).astype(jnp.bfloat16)
 
 
 def unfold(ref):
@@ -273,30 +278,39 @@
     return jnp.concatenate([edge[:half], edge[half:]], axis=1)
 
 
-def along_kernel(gas_ref, xb_ref, xa_ref, out_ref, ya_ref, yb_ref):
-    before, after = ordered(unfold(xa_ref), unfold(xb_ref), "gx")
-    blocks = [before] + [gas_ref[x * FY : (x + 1) * FY, :] for x in range(FX)] + [after]
-    along = [blocks[x] + 2.0 * blocks[x + 1] + blocks[x + 2] for x in range(FX)]
-    for x in range(FX):
-        out_ref[x * FY : (x + 1) * FY, :] = along[x]
-    width = ya_ref.shape[1]
+def corner_kernel(yb_ref, ya_ref, ca_ref, cb_ref):
+    even = is_even("gx")
+    sides = ordered(ya_ref[...].astype(jnp.float32), yb_ref[...].astype(jnp.float32), "gy")
+    rest = jnp.zeros((ca_ref.shape[0] - 4, ca_ref.shape[1]), jnp.float32)
+    low = jnp.concatenate([side[r : r + 1] for side in sides for r in (0, FX)] + [rest], axis=0)
+    high = jnp.concatenate([side[r : r + 1] for side in sides for r in (FX - 1, 2 * FX - 1)] + [rest], axis=0)
+    ca_ref[...] = jnp.where(even, high, low).astype(jnp.bfloat16)
+    cb_ref[...] = jnp.where(even, low, high).astype(jnp.bfloat16)
+
+
+def drag_kernel(
+    mark_ref, gas_ref, yb_ref, ya_ref, xb_ref, xa_ref, cb_ref, ca_ref, drag_ref, back_ref
+):
+    rows = drag_ref.shape[0]
+    width = gas_ref.shape[1] // 2
+    lanes = rows * TILE
+
+    def along(padded):
+        return padded[0:FX] + 2.0 * padded[1 : FX + 1] + padded[2 : FX + 2]
+
+    corners = ordered(ca_ref[...].astype(jnp.float32), cb_ref[...].astype(jnp.float32), "gx")
     edges = []
-    for row in (0, FY - 1):
-        edge = jnp.concatenate([along[x][row : row + 1] for x in range(FX)], axis=0)
-        edges.append(jnp.concatenate([edge[:, :width], edge[:, width:]], axis=0))
-    even = is_even("gy")
-    ya_ref[...] = jnp.where(even, edges[1], edges[0]).astype(jnp.bfloat16)
-    yb_ref[...] = jnp.where(even, edges[0], edges[1]).astype(jnp.bfloat16)
-
-
-def drag_kernel(mark_ref, along_ref, yb_ref, ya_ref, drag_ref, back_ref):
-    rows = drag_ref.shape[0]
-    width = along_ref.shape[1] // 2
-    lanes = rows * TILE
-    before, after = ordered(unfold(ya_ref), unfold(yb_ref), "gy")
+    for side, block in enumerate(ordered(unfold(ya_ref), unfold(yb_ref), "gy")):
+        first, last = [
+            jnp.concatenate([c[2 * side : 2 * side + 1], c[2 * side + 1 : 2 * side + 2]], axis=1) for c in corners
+        ]
+        edges.append(along(jnp.concatenate([first, block, last], axis=0)))
+    before, after = edges
+    first, last = ordered(unfold(xa_ref), unfold(xb_ref), "gx")
+    blocks = [first] + [gas_ref[x * FY : (x + 1) * FY, :] for x in range(FX)] + [last]
     smooth = []
     for x in range(FX):
-        block = along_ref[x * FY : (x + 1) * FY, :]
+        block = blocks[x] + 2.0 * blocks[x + 1] + blocks[x + 2]
         padded = jnp.concatenate([before[x : x + 1], block, after[x : x + 1]], axis=0)
         smooth.append((padded[0:FY] + 2.0 * block + padded[2 : FY + 2]) / 16.0)
     smooth = jnp.concatenate(smooth, axis=0)
@@ -430,14 +444,14 @@
         payload.reshape(devices, capacity, lanes), ("gx", "gy"), split_axis=0, concat_axis=0, tiled=True
     ).reshape(count, lanes)
     grid, edge = shape((COLS, 2 * width), f32), shape((2 * FX, width), bf16)
-    gas, xa, xb = call(place_kernel, [grid, edge, edge], received)
+    gas, xa, xb, ya, yb = call(place_kernel, [grid] + [edge] * 4, received)
+    ya, yb = exchange(ya, yb, "gy")
     xa, xb = exchange(xa, xb, "gx")
-    along, ya, yb = call(along_kernel, [grid, edge, edge], gas, xb, xa)
-    ya, yb = exchange(ya, yb, "gy")
+    ca, cb = exchange(*call(corner_kernel, [edge, edge], yb, ya), "gx")
     drag, back = call(
         drag_kernel,
         [shape((rows, FX, FY, FZ), bf16), shape((count, rows * TILE), bf16)],
-        received[:, lanes - LANES :], along, yb, ya,
+        received[:, lanes - LANES :], gas, yb, ya, xb, xa, cb, ca,
     )
     returned = lax.all_to_all(
         back.reshape(devices, capacity, rows * TILE), ("gx", "gy"), split_axis=0, concat_axis=0, tiled=True

time: 72.5 us -> 72.4 us (level)
  waiting for transfers between devices: 7.12 us -> 6.29 us
    ppermute x8 -> x10, waiting for transfers between devices: 7.12 us -> 6.29 us  [exchange(): blocks[odd] = lax.ppermute(block, axis, pairs)]
    ppermute x8 -> x10, starting transfers between devices: 10.5 us -> 11.2 us  [exchange(): blocks[odd] = lax.ppermute(block, axis, pairs)]
  transfers between devices with their start and end apart: 8 -> 10, of which waited for: 2 -> 2; matrix products, arithmetic and copies ran while one was open for 0% -> 0% of each run, Pallas kernels for 5% -> 5%
where the time goes in v9:
time: 72.4 us; the launch traced here: 72.2 us
  blocking collectives  39.8 us (55%)
  Pallas kernels  13.3 us (18%)
  starting transfers between devices  11.2 us (15%)
  waiting for transfers between devices  6.29 us (9%)
  local copies, waits for them, and re-layouts  0.86 us (1%)
  between operations  0.75 us (1%)
    all_to_all x1, blocking collectives, per_device(): lax.all_to_all(payload.reshape(devices, capacity, lanes), ('gx', 'gy'), s...  21.1 us
    all_to_all x1, blocking collectives, per_device(): lax.all_to_all(back.reshape(devices, capacity, rows * TILE), ('gx', 'gy')...  18.7 us
    pallas_call x7, Pallas kernels, call(): pl.pallas_call(kernel, out_shape=shapes, in_specs=[hbm if limit else vmem...  13.3 us
    ppermute x10, starting transfers between devices, exchange(): blocks[odd] = lax.ppermute(block, axis, pairs)  11.2 us
    ppermute x10, waiting for transfers between devices, exchange(): blocks[odd] = lax.ppermute(block, axis, pairs)  6.29 us
  transfers between devices with their start and end apart: 10, of which 2 were waited for; matrix products, arithmetic and copies ran while one was open for 0% of the time, Pallas kernels for 5%

profile of v9, /device:TPU:0, one launch (start us, length us, event | category | flops | bytes accessed | tf_op | source)
XLA Modules:
  0.0 72.2 jit_solution(12283125563157814985)
XLA Ops:
  0.6 0.0 copy-start
  0.6 2.6 %shard_map.104 = (bf16[16,640]{1,0:T(8,128)(2,1)}, bf16[16,640]{1,0:T(8,128)(2,1)}, bf16[16,640]{1,0:T(8,128)(2,1)}, bf16[16,640]{1,0:T(8,128)(2,1)}, f32[64,256]{1,0:T(8,128)}) custom-call(f32[16,8192]{1,0:T(8,128)} %part_ref.3, s32[4,512]{1,0:T(4,128)} %index_hbm.1, s32[1,4]{1,0:T(1,128)} %count_hbm.1, s32[1,256]{1,0:T(1,128)} %size_hbm.1, ...), custom_call_target="tpu_custom_call" | custom-call | tf_op jit(solution)/shard_map/pallas_call | solution.py:385
  3.2 6.1 %collective-permute-start = (bf16[16,640]{1,0:T(8,128)(2,1)}, bf16[16,640]{1,0:T(8,128)(2,1)S(1)}, u32[]{:S(2)}, u32[]{:S(2)}) collective-permute-start(bf16[16,640]{1,0:T(8,128)(2,1)} %get-tuple-element.28), channel_id=1, source_target_pairs={{0,7},{1,2},{2,1},{3,4},{4,3},{5,6},{6,5},{7,0},{8,15},{9,10},{10,... | collective-permute-start | bytes 61448 | tf_op jit(solution)/shard_map/ppermute | solution.py:65
  9.3 0.7 collective-permute-start.1
  10.0 0.0 collective-permute-start.2
  10.0 1.0 %collective-permute-start.3 = (bf16[16,640]{1,0:T(8,128)(2,1)}, bf16[16,640]{1,0:T(8,128)(2,1)S(1)}, u32[]{:S(2)}, u32[]{:S(2)}) collective-permute-start(bf16[16,640]{1,0:T(8,128)(2,1)} %get-tuple-element.31), channel_id=1, source_target_pairs={{0,8},{8,0},{16,24},{24,16},{1,9},{9,1},{17,25},{25,17},{2,10},{10... | collective-permute-start | bytes 61448 | tf_op jit(solution)/shard_map/ppermute | solution.py:65
  10.9 0.0 copy-done
  10.9 0.8 %copy-done.1 = f32[64,256]{1,0:T(8,128)S(1)} copy-done((f32[64,256]{1,0:T(8,128)S(1)}, f32[64,256]{1,0:T(8,128)}, u32[]{:S(2)}) %copy-start.1) | copy-done | bytes 65560
  11.8 3.6 %shard_map.105 = (f32[576,256]{1,0:T(8,128)S(1)}, s32[1,10240]{1,0:T(1,128)S(1)}, s32[1,256]{1,0:T(1,128)S(1)}, bf16[64,256]{1,0:T(8,128)(2,1)S(1)}, f32[64,128]{1,0:T(8,128)S(1)}) custom-call(f32[16,8192]{1,0:T(8,128)S(1)} %copy-done, f32[64,256]{1,0:T(8,128)S(1)} %copy-done.1), custom_call_target="tpu_custom_call" | custom-call | tf_op jit(solution)/shard_map/pallas_call | solution.py:385
  15.4 0.0 collective-permute-done.refs_0_
  15.4 0.0 collective-permute-done.1.refs_1_
  15.4 0.0 collective-permute-done.2.refs_2_
  15.4 0.0 collective-permute-done.3.refs_3_
  15.4 1.6 %shard_map.106 = bf16[512,640]{1,0:T(8,128)(2,1)S(1)} custom-call(f32[576,256]{1,0:T(8,128)S(1)} %get-tuple-element.24.sum_ref, s32[1,10240]{1,0:T(1,128)S(1)} %get-tuple-element.25.code_ref, s32[1,256]{1,0:T(1,128)S(1)} %get-tuple-element.26.slot_ref, bf16[64,256]{1,0:T(8,128)(2,1)S(1)} %get-tuple-element.27.mark_ref, f32[64,256]{1,0:T(8,128)S(1)} %copy-done.1, ...), custom_call_target="tpu_custom_call" | custom-call | tf_op jit(solution)/shard_map/pallas_call | solution.py:385
  17.0 21.1 %all_to_all.10 = bf16[32,16,640]{2,1,0:T(8,128)(2,1)S(1)} all-to-all(bf16[32,16,640]{2,1,0:T(8,128)(2,1)S(1)} %bitcast.10), channel_id=1, replica_groups=mesh['gx'=4,'gy'=8] {'gx','gy'}, dimensions={0} | all-to-all | bytes 1310720 | tf_op jit(solution)/shard_map/all_to_all | solution.py:443
  38.1 0.6 shard_map.107
  38.8 1.8 %collective-permute-start.4 = (bf16[16,576]{1,0:T(8,128)(2,1)S(1)}, bf16[16,576]{1,0:T(8,128)(2,1)S(1)}, u32[]{:S(2)}, u32[]{:S(2)}) collective-permute-start(bf16[16,576]{1,0:T(8,128)(2,1)S(1)} %get-tuple-element.33), channel_id=1, source_target_pairs={{0,7},{1,2},{2,1},{3,4},{4,3},{5,6},{6,5},{7,0},{8,15},{9,10},{10,... | collective-permute-start | bytes 55304 | tf_op jit(solution)/shard_map/ppermute | solution.py:65
  40.5 0.4 collective-permute-start.5
  40.9 0.0 collective-permute-start.6
  40.9 0.7 collective-permute-start.7
  41.5 3.8 %collective-permute-done.4.yb_ref = bf16[16,576]{1,0:T(8,128)(2,1)S(1)} collective-permute-done((bf16[16,576]{1,0:T(8,128)(2,1)S(1)}, bf16[16,576]{1,0:T(8,128)(2,1)S(1)}, u32[]{:S(2)}, u32[]{:S(2)}) %collective-permute-start.4) | collective-permute-done | bytes 18464 | tf_op jit(solution)/shard_map/ppermute | solution.py:65
  45.3 0.0 collective-permute-done.5.ya_ref
  45.3 0.1 collective-permute-start.8
  45.4 0.6 collective-permute-start.9
  46.1 0.0 collective-permute-done.6.xb_ref
  46.1 0.0 collective-permute-done.7.xa_ref
  46.1 2.5 %collective-permute-done.8.cb_ref = bf16[16,576]{1,0:T(8,128)(2,1)S(1)} collective-permute-done((bf16[16,576]{1,0:T(8,128)(2,1)S(1)}, bf16[16,576]{1,0:T(8,128)(2,1)S(1)}, u32[]{:S(2)}, u32[]{:S(2)}) %collective-permute-start.8) | collective-permute-done | bytes 18464 | tf_op jit(solution)/shard_map/ppermute | solution.py:65
  48.6 0.0 collective-permute-done.9.ca_ref
  48.6 0.8 %shard_map.109 = (bf16[8,8,8,128]{3,2,1,0:T(8,128)(2,1)S(1)}, bf16[512,512]{1,0:T(8,128)(2,1)S(1)}) custom-call(bf16[512,128]{1,0:T(8,128)(2,1)S(1)} %slice.4.mark_ref, f32[64,1152]{1,0:T(8,128)S(1)} %get-tuple-element.32.gas_ref, bf16[16,576]{1,0:T(8,128)(2,1)S(1)} %collective-permute-done.4.yb_ref, bf16[16,576]{1,0:T(8,128)(2,1)S(1)} %collective-permute-done.5.ya_ref, ...), custom_call_target="tpu_custom_call" | custom-call | tf_op jit(solution)/shard_map/pallas_call | solution.py:385
  49.4 0.0 copy-start.2
  49.4 18.7 %all_to_all.11 = bf16[32,16,512]{2,1,0:T(8,128)(2,1)S(1)} all-to-all(bf16[32,16,512]{2,1,0:T(8,128)(2,1)S(1)} %bitcast.12), channel_id=1, replica_groups=mesh['gx'=4,'gy'=8] {'gx','gy'}, dimensions={0} | all-to-all | bytes 1048576 | tf_op jit(solution)/shard_map/all_to_all | solution.py:456
  68.1 4.0 %shard_map.110 = (f32[8,10240]{1,0:T(8,128)}, bf16[8,8,8,128]{3,2,1,0:T(8,128)(2,1)}) custom-call(bf16[512,512]{1,0:T(8,128)(2,1)S(1)} %bitcast.11, s32[1,256]{1,0:T(1,128)S(1)} %get-tuple-element.26.slot_ref, s32[1,10240]{1,0:T(1,128)S(1)} %get-tuple-element.25.code_ref, f32[16,8192]{1,0:T(8,128)S(1)} %copy-done, f32[64,256]{1,0:T(8,128)S(1)} %copy-done.2, ...), custom_call_target="tpu_custom_call" | custom-call | tf_op jit(solution)/shard_map/pallas_call | solution.py:385
  (4 shorter events, 0.0 us)
Async XLA Ops:
  0.6 10.3 %copy-start = (f32[16,8192]{1,0:T(8,128)S(1)}, f32[16,8192]{1,0:T(8,128)}, u32[]{:S(2)}) copy-start(f32[16,8192]{1,0:T(8,128)} %part_ref.3) | copy-start | bytes 1572868
  3.2 12.1 %collective-permute-start = (bf16[16,640]{1,0:T(8,128)(2,1)}, bf16[16,640]{1,0:T(8,128)(2,1)S(1)}, u32[]{:S(2)}, u32[]{:S(2)}) collective-permute-start(bf16[16,640]{1,0:T(8,128)(2,1)} %get-tuple-element.28), channel_id=1, source_target_pairs={{0,7},{1,2},{2,1},{3,4},{4,3},{5,6},{6,5},{7,0},{8,15},{9,10},{10,... | collective-permute-start | bytes 61448 | tf_op jit(solution)/shard_map/ppermute | solution.py:65
  9.3 6.1 %collective-permute-start.1 = (bf16[16,640]{1,0:T(8,128)(2,1)}, bf16[16,640]{1,0:T(8,128)(2,1)S(1)}, u32[]{:S(2)}, u32[]{:S(2)}) collective-permute-start(bf16[16,640]{1,0:T(8,128)(2,1)} %get-tuple-element.29), channel_id=1, source_target_pairs={{0,24},{8,16},{16,8},{24,0},{1,25},{9,17},{17,9},{25,1},{2,26},{10... | collective-permute-start | bytes 61448 | tf_op jit(solution)/shard_map/ppermute | solution.py:65
  10.0 5.4 %collective-permute-start.2 = (bf16[16,640]{1,0:T(8,128)(2,1)}, bf16[16,640]{1,0:T(8,128)(2,1)S(1)}, u32[]{:S(2)}, u32[]{:S(2)}) collective-permute-start(bf16[16,640]{1,0:T(8,128)(2,1)} %get-tuple-element.30), channel_id=1, source_target_pairs={{0,1},{1,0},{2,3},{3,2},{4,5},{5,4},{6,7},{7,6},{8,9},{9,8},{10,11... | collective-permute-start | bytes 61448 | tf_op jit(solution)/shard_map/ppermute | solution.py:65
  10.0 5.4 %collective-permute-start.3 = (bf16[16,640]{1,0:T(8,128)(2,1)}, bf16[16,640]{1,0:T(8,128)(2,1)S(1)}, u32[]{:S(2)}, u32[]{:S(2)}) collective-permute-start(bf16[16,640]{1,0:T(8,128)(2,1)} %get-tuple-element.31), channel_id=1, source_target_pairs={{0,8},{8,0},{16,24},{24,16},{1,9},{9,1},{17,25},{25,17},{2,10},{10... | collective-permute-start | bytes 61448 | tf_op jit(solution)/shard_map/ppermute | solution.py:65
  10.9 0.8 %copy-start.1 = (f32[64,256]{1,0:T(8,128)S(1)}, f32[64,256]{1,0:T(8,128)}, u32[]{:S(2)}) copy-start(f32[64,256]{1,0:T(8,128)} %get-tuple-element.23.small_ref) | copy-start | bytes 196612
  38.8 6.5 %collective-permute-start.4 = (bf16[16,576]{1,0:T(8,128)(2,1)S(1)}, bf16[16,576]{1,0:T(8,128)(2,1)S(1)}, u32[]{:S(2)}, u32[]{:S(2)}) collective-permute-start(bf16[16,576]{1,0:T(8,128)(2,1)S(1)} %get-tuple-element.33), channel_id=1, source_target_pairs={{0,7},{1,2},{2,1},{3,4},{4,3},{5,6},{6,5},{7,0},{8,15},{9,10},{10,... | collective-permute-start | bytes 55304 | tf_op jit(solution)/shard_map/ppermute | solution.py:65
  40.5 4.8 %collective-permute-start.5 = (bf16[16,576]{1,0:T(8,128)(2,1)S(1)}, bf16[16,576]{1,0:T(8,128)(2,1)S(1)}, u32[]{:S(2)}, u32[]{:S(2)}) collective-permute-start(bf16[16,576]{1,0:T(8,128)(2,1)S(1)} %get-tuple-element.34), channel_id=1, source_target_pairs={{0,1},{1,0},{2,3},{3,2},{4,5},{5,4},{6,7},{7,6},{8,9},{9,8},{10,11... | collective-permute-start | bytes 55304 | tf_op jit(solution)/shard_map/ppermute | solution.py:65
  40.9 5.2 %collective-permute-start.6 = (bf16[16,576]{1,0:T(8,128)(2,1)S(1)}, bf16[16,576]{1,0:T(8,128)(2,1)S(1)}, u32[]{:S(2)}, u32[]{:S(2)}) collective-permute-start(bf16[16,576]{1,0:T(8,128)(2,1)S(1)} %get-tuple-element.35), channel_id=1, source_target_pairs={{0,24},{8,16},{16,8},{24,0},{1,25},{9,17},{17,9},{25,1},{2,26},{10... | collective-permute-start | bytes 55304 | tf_op jit(solution)/shard_map/ppermute | solution.py:65
  40.9 5.2 %collective-permute-start.7 = (bf16[16,576]{1,0:T(8,128)(2,1)S(1)}, bf16[16,576]{1,0:T(8,128)(2,1)S(1)}, u32[]{:S(2)}, u32[]{:S(2)}) collective-permute-start(bf16[16,576]{1,0:T(8,128)(2,1)S(1)} %get-tuple-element.36), channel_id=1, source_target_pairs={{0,8},{8,0},{16,24},{24,16},{1,9},{9,1},{17,25},{25,17},{2,10},{10... | collective-permute-start | bytes 55304 | tf_op jit(solution)/shard_map/ppermute | solution.py:65
  45.3 3.3 %collective-permute-start.8 = (bf16[16,576]{1,0:T(8,128)(2,1)S(1)}, bf16[16,576]{1,0:T(8,128)(2,1)S(1)}, u32[]{:S(2)}, u32[]{:S(2)}) collective-permute-start(bf16[16,576]{1,0:T(8,128)(2,1)S(1)} %get-tuple-element.37), channel_id=1, source_target_pairs={{0,24},{8,16},{16,8},{24,0},{1,25},{9,17},{17,9},{25,1},{2,26},{10... | collective-permute-start | bytes 55304 | tf_op jit(solution)/shard_map/ppermute | solution.py:65
  45.4 3.2 %collective-permute-start.9 = (bf16[16,576]{1,0:T(8,128)(2,1)S(1)}, bf16[16,576]{1,0:T(8,128)(2,1)S(1)}, u32[]{:S(2)}, u32[]{:S(2)}) collective-permute-start(bf16[16,576]{1,0:T(8,128)(2,1)S(1)} %get-tuple-element.38), channel_id=1, source_target_pairs={{0,8},{8,0},{16,24},{24,16},{1,9},{9,1},{17,25},{25,17},{2,10},{10... | collective-permute-start | bytes 55304 | tf_op jit(solution)/shard_map/ppermute | solution.py:65
  49.4 18.7 %copy-start.2 = (f32[64,256]{1,0:T(8,128)S(1)}, f32[64,256]{1,0:T(8,128)}, u32[]{:S(2)}) copy-start(f32[64,256]{1,0:T(8,128)} %get-tuple-element.23.small_ref) | copy-start | bytes 196612

commit v10 on v8

--- a/solution.py
+++ b/solution.py
@@ -246,19 +246,21 @@
     out_ref[...] = dot(match, table, NT).astype(jnp.bfloat16)
 
 
+def tile_marks(tile_ref, width):
+    marks = tile_ref[:, width // LANES * LANES :]
+    return marks[:, width % LANES : width % LANES + 1], marks[:, width % LANES + 1 : width % LANES + 2]
+
+
 def place_kernel(tile_ref, gas_ref, xa_ref, xb_ref):
     even = is_even("gx")
     count, lanes = tile_ref.shape
     width = gas_ref.shape[1] // 2
-    marks = tile_ref[:, lanes - LANES :].astype(jnp.float32)
-    column = marks[:, width % LANES : width % LANES + 1]
-    height = marks[:, width % LANES + 1 : width % LANES + 2]
-    lane = iota((1, LANES), 1)
-    hot = one_hot(column == lane.astype(jnp.float32))
-    place = (iota((1, width), 1) % TILE).astype(jnp.float32)
-    values = tile_ref[:, :width].astype(jnp.float32)
+    column, height = tile_marks(tile_ref, width)
+    hot = ones(column == iota((1, LANES), 1).astype(jnp.float32).astype(jnp.bfloat16))
+    place = (iota((1, width), 1) % TILE).astype(jnp.float32).astype(jnp.bfloat16)
+    values = tile_ref[:, :width]
     for half, mask in enumerate((place >= height, place < height)):
-        total = dot(hot, jnp.where(mask, values, 0.0).astype(jnp.bfloat16), TN)
+        total = dot(hot, jnp.where(mask, values, jnp.bfloat16(0)), TN)
         where = slice(half * width, (half + 1) * width)
         gas_ref[:, where] = total[:COLS]
         rows = slice(half * FY, (half + 1) * FY)
@@ -289,7 +291,7 @@
     yb_ref[...] = jnp.where(even, edges[0], edges[1]).astype(jnp.bfloat16)
 
 
-def drag_kernel(mark_ref, along_ref, yb_ref, ya_ref, drag_ref, back_ref):
+def drag_kernel(tile_ref, along_ref, yb_ref, ya_ref, drag_ref, back_ref):
     rows = drag_ref.shape[0]
     width = along_ref.shape[1] // 2
     lanes = rows * TILE
@@ -310,14 +312,12 @@
         where = slice(r * TILE, (r + 1) * TILE)
         both = jnp.concatenate([halves[0][:, where], halves[1][:, where]], axis=1)
         drag_ref[r] = both.reshape(FX, FY, FZ).astype(jnp.bfloat16)
-    mark = width % LANES
-    marks = mark_ref[...].astype(jnp.float32)
-    column, height = marks[:, mark : mark + 1], marks[:, mark + 1 : mark + 2]
-    hot = one_hot(column == iota((1, COLS), 1).astype(jnp.float32))
-    place = (iota((1, lanes), 1) % TILE).astype(jnp.float32)
+    column, height = tile_marks(tile_ref, width)
+    hot = ones(column == iota((1, COLS), 1).astype(jnp.float32).astype(jnp.bfloat16))
+    place = (iota((1, lanes), 1) % TILE).astype(jnp.float32).astype(jnp.bfloat16)
     low = dot(hot, halves[0].astype(jnp.bfloat16))
     high = dot(hot, halves[1].astype(jnp.bfloat16))
-    back_ref[...] = jnp.where(place >= height, low, high).astype(jnp.bfloat16)
+    back_ref[...] = jnp.where(place >= height, low.astype(jnp.bfloat16), high.astype(jnp.bfloat16))
 
 
 def force_kernel(back_ref, slot_ref, code_ref, part_ref, small_ref, live_ref, drag_ref, *refs):
@@ -437,7 +437,7 @@
     drag, back = call(
         drag_kernel,
         [shape((rows, FX, FY, FZ), bf16), shape((count, rows * TILE), bf16)],
-        received[:, lanes - LANES :], along, yb, ya,
+        received, along, yb, ya,
     )
     returned = lax.all_to_all(
         back.reshape(devices, capacity, rows * TILE), ("gx", "gy"), split_axis=0, concat_axis=0, tiled=True

time: 72.5 us -> 72.5 us (level)
  no operation moved by 1% of the time
where the time goes in v10:
time: 72.5 us; the launch traced here: 72.3 us
  blocking collectives  39.6 us (55%)
  Pallas kernels  13.5 us (19%)
  starting transfers between devices  10.5 us (14%)
  waiting for transfers between devices  7.12 us (10%)
  local copies, waits for them, and re-layouts  0.85 us (1%)
    all_to_all x1, blocking collectives, per_device(): lax.all_to_all(payload.reshape(devices, capacity, lanes), ('gx', 'gy'), s...  21.1 us
    all_to_all x1, blocking collectives, per_device(): lax.all_to_all(back.reshape(devices, capacity, rows * TILE), ('gx', 'gy')...  18.5 us
    pallas_call x7, Pallas kernels, call(): pl.pallas_call(kernel, out_shape=shapes, in_specs=[hbm if limit else vmem...  13.5 us
    ppermute x8, starting transfers between devices, exchange(): blocks[odd] = lax.ppermute(block, axis, pairs)  10.5 us
    ppermute x8, waiting for transfers between devices, exchange(): blocks[odd] = lax.ppermute(block, axis, pairs)  7.12 us
  transfers between devices with their start and end apart: 8, of which 2 were waited for; matrix products, arithmetic and copies ran while one was open for 0% of the time, Pallas kernels for 5%

profile of v10, /device:TPU:0, one launch (start us, length us, event | category | flops | bytes accessed | tf_op | source)
XLA Modules:
  0.0 72.3 jit_solution(8607722645137253821)
XLA Ops:
  0.6 0.0 copy-start
  0.6 2.6 %shard_map.104 = (bf16[16,640]{1,0:T(8,128)(2,1)}, bf16[16,640]{1,0:T(8,128)(2,1)}, bf16[16,640]{1,0:T(8,128)(2,1)}, bf16[16,640]{1,0:T(8,128)(2,1)}, f32[64,256]{1,0:T(8,128)}) custom-call(f32[16,8192]{1,0:T(8,128)} %part_ref.3, s32[4,512]{1,0:T(4,128)} %index_hbm.1, s32[1,4]{1,0:T(1,128)} %count_hbm.1, s32[1,256]{1,0:T(1,128)} %size_hbm.1, ...), custom_call_target="tpu_custom_call" | custom-call | tf_op jit(solution)/shard_map/pallas_call | solution.py:371
  3.3 6.1 %collective-permute-start = (bf16[16,640]{1,0:T(8,128)(2,1)}, bf16[16,640]{1,0:T(8,128)(2,1)S(1)}, u32[]{:S(2)}, u32[]{:S(2)}) collective-permute-start(bf16[16,640]{1,0:T(8,128)(2,1)} %get-tuple-element.27), channel_id=1, source_target_pairs={{0,7},{1,2},{2,1},{3,4},{4,3},{5,6},{6,5},{7,0},{8,15},{9,10},{10,... | collective-permute-start | bytes 61448 | tf_op jit(solution)/shard_map/ppermute | solution.py:65
  9.3 0.7 collective-permute-start.1
  10.0 0.0 collective-permute-start.2
  10.0 1.0 %collective-permute-start.3 = (bf16[16,640]{1,0:T(8,128)(2,1)}, bf16[16,640]{1,0:T(8,128)(2,1)S(1)}, u32[]{:S(2)}, u32[]{:S(2)}) collective-permute-start(bf16[16,640]{1,0:T(8,128)(2,1)} %get-tuple-element.30), channel_id=1, source_target_pairs={{0,8},{8,0},{16,24},{24,16},{1,9},{9,1},{17,25},{25,17},{2,10},{10... | collective-permute-start | bytes 61448 | tf_op jit(solution)/shard_map/ppermute | solution.py:65
  10.9 0.0 copy-done
  10.9 0.0 copy-start.1
  10.9 0.8 %copy-done.1 = f32[64,256]{1,0:T(8,128)S(1)} copy-done((f32[64,256]{1,0:T(8,128)S(1)}, f32[64,256]{1,0:T(8,128)}, u32[]{:S(2)}) %copy-start.1) | copy-done | bytes 65560
  11.8 3.6 %shard_map.105 = (f32[576,256]{1,0:T(8,128)S(1)}, s32[1,10240]{1,0:T(1,128)S(1)}, s32[1,256]{1,0:T(1,128)S(1)}, bf16[64,256]{1,0:T(8,128)(2,1)S(1)}, f32[64,128]{1,0:T(8,128)S(1)}) custom-call(f32[16,8192]{1,0:T(8,128)S(1)} %copy-done, f32[64,256]{1,0:T(8,128)S(1)} %copy-done.1), custom_call_target="tpu_custom_call" | custom-call | tf_op jit(solution)/shard_map/pallas_call | solution.py:371
  15.4 0.0 collective-permute-done.refs_0_
  15.4 0.0 collective-permute-done.1.refs_1_
  15.4 0.0 collective-permute-done.2.refs_2_
  15.4 0.0 collective-permute-done.3.refs_3_
  15.4 1.6 %shard_map.106 = bf16[512,640]{1,0:T(8,128)(2,1)S(1)} custom-call(f32[576,256]{1,0:T(8,128)S(1)} %get-tuple-element.23.sum_ref, s32[1,10240]{1,0:T(1,128)S(1)} %get-tuple-element.24.code_ref, s32[1,256]{1,0:T(1,128)S(1)} %get-tuple-element.25.slot_ref, bf16[64,256]{1,0:T(8,128)(2,1)S(1)} %get-tuple-element.26.mark_ref, f32[64,256]{1,0:T(8,128)S(1)} %copy-done.1, ...), custom_call_target="tpu_custom_call" | custom-call | tf_op jit(solution)/shard_map/pallas_call | solution.py:371
  17.1 21.1 %all_to_all.10 = bf16[32,16,640]{2,1,0:T(8,128)(2,1)S(1)} all-to-all(bf16[32,16,640]{2,1,0:T(8,128)(2,1)S(1)} %bitcast.10), channel_id=1, replica_groups=mesh['gx'=4,'gy'=8] {'gx','gy'}, dimensions={0} | all-to-all | bytes 1310720 | tf_op jit(solution)/shard_map/all_to_all | solution.py:429
  38.1 0.7 shard_map.107
  38.8 0.5 collective-permute-start.4
  39.4 0.2 collective-permute-start.5
  39.6 2.6 %collective-permute-done.4.xb_ref = bf16[16,576]{1,0:T(8,128)(2,1)S(1)} collective-permute-done((bf16[16,576]{1,0:T(8,128)(2,1)S(1)}, bf16[16,576]{1,0:T(8,128)(2,1)S(1)}, u32[]{:S(2)}, u32[]{:S(2)}) %collective-permute-start.4) | collective-permute-done | bytes 18464 | tf_op jit(solution)/shard_map/ppermute | solution.py:65
  42.2 0.0 collective-permute-done.5.xa_ref
  42.2 0.2 shard_map.108
  42.4 1.7 %collective-permute-start.6 = (bf16[16,576]{1,0:T(8,128)(2,1)S(1)}, bf16[16,576]{1,0:T(8,128)(2,1)S(1)}, u32[]{:S(2)}, u32[]{:S(2)}) collective-permute-start(bf16[16,576]{1,0:T(8,128)(2,1)S(1)} %get-tuple-element.35), channel_id=1, source_target_pairs={{0,7},{1,2},{2,1},{3,4},{4,3},{5,6},{6,5},{7,0},{8,15},{9,10},{10,... | collective-permute-start | bytes 55304 | tf_op jit(solution)/shard_map/ppermute | solution.py:65
  44.1 0.4 collective-permute-start.7
  44.4 4.5 %collective-permute-done.6.yb_ref = bf16[16,576]{1,0:T(8,128)(2,1)S(1)} collective-permute-done((bf16[16,576]{1,0:T(8,128)(2,1)S(1)}, bf16[16,576]{1,0:T(8,128)(2,1)S(1)}, u32[]{:S(2)}, u32[]{:S(2)}) %collective-permute-start.6) | collective-permute-done | bytes 18464 | tf_op jit(solution)/shard_map/ppermute | solution.py:65
  48.9 0.0 collective-permute-done.7.ya_ref
  48.9 0.8 %shard_map.109 = (bf16[8,8,8,128]{3,2,1,0:T(8,128)(2,1)S(1)}, bf16[512,512]{1,0:T(8,128)(2,1)S(1)}) custom-call(bf16[512,640]{1,0:T(8,128)(2,1)S(1)} %bitcast.9, f32[64,1152]{1,0:T(8,128)S(1)} %get-tuple-element.34.along_ref, bf16[16,576]{1,0:T(8,128)(2,1)S(1)} %collective-permute-done.6.yb_ref, bf16[16,576]{1,0:T(8,128)(2,1)S(1)} %collective-permute-done.7.ya_ref), custom_call_target="tpu_custom_call" | custom-call | tf_op jit(solution)/shard_map/pallas_call | solution.py:371
  49.7 0.0 copy-start.2
  49.7 18.5 %all_to_all.11 = bf16[32,16,512]{2,1,0:T(8,128)(2,1)S(1)} all-to-all(bf16[32,16,512]{2,1,0:T(8,128)(2,1)S(1)} %bitcast.12), channel_id=1, replica_groups=mesh['gx'=4,'gy'=8] {'gx','gy'}, dimensions={0} | all-to-all | bytes 1048576 | tf_op jit(solution)/shard_map/all_to_all | solution.py:442
  68.3 0.0 copy-done.2
  68.3 4.0 %shard_map.110 = (f32[8,10240]{1,0:T(8,128)}, bf16[8,8,8,128]{3,2,1,0:T(8,128)(2,1)}) custom-call(bf16[512,512]{1,0:T(8,128)(2,1)S(1)} %bitcast.11, s32[1,256]{1,0:T(1,128)S(1)} %get-tuple-element.25.slot_ref, s32[1,10240]{1,0:T(1,128)S(1)} %get-tuple-element.24.code_ref, f32[16,8192]{1,0:T(8,128)S(1)} %copy-done, f32[64,256]{1,0:T(8,128)S(1)} %copy-done.2, ...), custom_call_target="tpu_custom_call" | custom-call | tf_op jit(solution)/shard_map/pallas_call | solution.py:371
Async XLA Ops:
  0.6 10.3 %copy-start = (f32[16,8192]{1,0:T(8,128)S(1)}, f32[16,8192]{1,0:T(8,128)}, u32[]{:S(2)}) copy-start(f32[16,8192]{1,0:T(8,128)} %part_ref.3) | copy-start | bytes 1572868
  3.3 12.1 %collective-permute-start = (bf16[16,640]{1,0:T(8,128)(2,1)}, bf16[16,640]{1,0:T(8,128)(2,1)S(1)}, u32[]{:S(2)}, u32[]{:S(2)}) collective-permute-start(bf16[16,640]{1,0:T(8,128)(2,1)} %get-tuple-element.27), channel_id=1, source_target_pairs={{0,7},{1,2},{2,1},{3,4},{4,3},{5,6},{6,5},{7,0},{8,15},{9,10},{10,... | collective-permute-start | bytes 61448 | tf_op jit(solution)/shard_map/ppermute | solution.py:65
  9.3 6.1 %collective-permute-start.1 = (bf16[16,640]{1,0:T(8,128)(2,1)}, bf16[16,640]{1,0:T(8,128)(2,1)S(1)}, u32[]{:S(2)}, u32[]{:S(2)}) collective-permute-start(bf16[16,640]{1,0:T(8,128)(2,1)} %get-tuple-element.28), channel_id=1, source_target_pairs={{0,24},{8,16},{16,8},{24,0},{1,25},{9,17},{17,9},{25,1},{2,26},{10... | collective-permute-start | bytes 61448 | tf_op jit(solution)/shard_map/ppermute | solution.py:65
  10.0 5.4 %collective-permute-start.2 = (bf16[16,640]{1,0:T(8,128)(2,1)}, bf16[16,640]{1,0:T(8,128)(2,1)S(1)}, u32[]{:S(2)}, u32[]{:S(2)}) collective-permute-start(bf16[16,640]{1,0:T(8,128)(2,1)} %get-tuple-element.29), channel_id=1, source_target_pairs={{0,1},{1,0},{2,3},{3,2},{4,5},{5,4},{6,7},{7,6},{8,9},{9,8},{10,11... | collective-permute-start | bytes 61448 | tf_op jit(solution)/shard_map/ppermute | solution.py:65
  10.0 5.4 %collective-permute-start.3 = (bf16[16,640]{1,0:T(8,128)(2,1)}, bf16[16,640]{1,0:T(8,128)(2,1)S(1)}, u32[]{:S(2)}, u32[]{:S(2)}) collective-permute-start(bf16[16,640]{1,0:T(8,128)(2,1)} %get-tuple-element.30), channel_id=1, source_target_pairs={{0,8},{8,0},{16,24},{24,16},{1,9},{9,1},{17,25},{25,17},{2,10},{10... | collective-permute-start | bytes 61448 | tf_op jit(solution)/shard_map/ppermute | solution.py:65
  10.9 0.8 %copy-start.1 = (f32[64,256]{1,0:T(8,128)S(1)}, f32[64,256]{1,0:T(8,128)}, u32[]{:S(2)}) copy-start(f32[64,256]{1,0:T(8,128)} %get-tuple-element.22.small_ref) | copy-start | bytes 196612
  38.8 3.3 %collective-permute-start.4 = (bf16[16,576]{1,0:T(8,128)(2,1)S(1)}, bf16[16,576]{1,0:T(8,128)(2,1)S(1)}, u32[]{:S(2)}, u32[]{:S(2)}) collective-permute-start(bf16[16,576]{1,0:T(8,128)(2,1)S(1)} %get-tuple-element.32), channel_id=1, source_target_pairs={{0,24},{8,16},{16,8},{24,0},{1,25},{9,17},{17,9},{25,1},{2,26},{10... | collective-permute-start | bytes 55304 | tf_op jit(solution)/shard_map/ppermute | solution.py:65
  39.4 2.8 %collective-permute-start.5 = (bf16[16,576]{1,0:T(8,128)(2,1)S(1)}, bf16[16,576]{1,0:T(8,128)(2,1)S(1)}, u32[]{:S(2)}, u32[]{:S(2)}) collective-permute-start(bf16[16,576]{1,0:T(8,128)(2,1)S(1)} %get-tuple-element.33), channel_id=1, source_target_pairs={{0,8},{8,0},{16,24},{24,16},{1,9},{9,1},{17,25},{25,17},{2,10},{10... | collective-permute-start | bytes 55304 | tf_op jit(solution)/shard_map/ppermute | solution.py:65
  42.4 6.5 %collective-permute-start.6 = (bf16[16,576]{1,0:T(8,128)(2,1)S(1)}, bf16[16,576]{1,0:T(8,128)(2,1)S(1)}, u32[]{:S(2)}, u32[]{:S(2)}) collective-permute-start(bf16[16,576]{1,0:T(8,128)(2,1)S(1)} %get-tuple-element.35), channel_id=1, source_target_pairs={{0,7},{1,2},{2,1},{3,4},{4,3},{5,6},{6,5},{7,0},{8,15},{9,10},{10,... | collective-permute-start | bytes 55304 | tf_op jit(solution)/shard_map/ppermute | solution.py:65
  44.1 4.9 %collective-permute-start.7 = (bf16[16,576]{1,0:T(8,128)(2,1)S(1)}, bf16[16,576]{1,0:T(8,128)(2,1)S(1)}, u32[]{:S(2)}, u32[]{:S(2)}) collective-permute-start(bf16[16,576]{1,0:T(8,128)(2,1)S(1)} %get-tuple-element.36), channel_id=1, source_target_pairs={{0,1},{1,0},{2,3},{3,2},{4,5},{5,4},{6,7},{7,6},{8,9},{9,8},{10,11... | collective-permute-start | bytes 55304 | tf_op jit(solution)/shard_map/ppermute | solution.py:65
  49.7 18.6 %copy-start.2 = (f32[64,256]{1,0:T(8,128)S(1)}, f32[64,256]{1,0:T(8,128)}, u32[]{:S(2)}) copy-start(f32[64,256]{1,0:T(8,128)} %get-tuple-element.22.small_ref) | copy-start | bytes 196612

commit v11 on v8

--- a/solution.py
+++ b/solution.py
@@ -172,9 +172,10 @@
     )
 
 
-def deposit_kernel(
-    capacity, rows, leaving, part_ref, small_ref, sum_ref, code_ref, slot_ref, mark_ref, live_ref
-):
+def deposit_kernel(capacity, rows, part_ref, small_ref, *refs):
+    state_refs, (out_ref, code_ref, slot_ref, live_ref) = refs[:4], refs[4:]
+    migr = state_refs[0].shape[1] - LANES
+    leaving = 4 * migr
     channels, parts = part_ref.shape
     slots = code_ref.shape[1]
     tiles = slot_ref.shape[1]
@@ -205,9 +206,6 @@
     slot_ref[...] = (owners * capacity + rank).astype(jnp.int32)
     starts = jnp.broadcast_to(start.astype(jnp.int16), (tiles, CHUNK))
     steps = jnp.broadcast_to(code_step.astype(jnp.int16), (tiles, CHUNK))
-    lines = iota(mark_ref.shape, 0)
-    marks = jnp.where(lines == 0, offset // FZ, jnp.where(lines == 1, offset % FZ, 0))
-    mark_ref[...] = marks.astype(jnp.float32).astype(jnp.bfloat16)
 
     def find(begin):
         cell = side_by_side(small_ref, cell_row, begin, CHUNK).astype(jnp.int32)
@@ -218,30 +216,23 @@
         found = jnp.sum(found.astype(jnp.int32), axis=0, keepdims=True) & 0xFFFF
         return found // TILE, (found + cell) % TILE
 
-    for begin in range(parts, slots, CHUNK):
+    arrived = jnp.concatenate([block[:, :migr] for block in arrived_blocks(state_refs)], axis=1)
+    total = 0.0
+    for begin in range(0, slots, CHUNK):
         tile, place = find(begin)
         code_ref[:, begin : begin + CHUNK] = tile * TILE + place
-    for begin in range(0, parts, CHUNK):
-        tile, place = find(begin)
-        code_ref[:, begin : begin + CHUNK] = tile * TILE + place
-        live = side_by_side(live_ref, 0, begin, CHUNK)
-        state = part_ref[:, begin : begin + CHUNK] * live
+        if begin < parts:
+            live = side_by_side(live_ref, 0, begin, CHUNK)
+            state = part_ref[:, begin : begin + CHUNK] * live
+        else:
+            state = arrived[:, begin - parts : begin - parts + CHUNK]
         mixed, first = mix(closure, state.astype(jnp.bfloat16))
-        added = dot(spread(mixed, first, place), ones(equal(tiles, tile)), NT)
-        total = added if begin == 0 else total + added
-    sum_ref[...] = total
-
-
-def pack_kernel(rows, sum_ref, code_ref, slot_ref, mark_ref, small_ref, *refs):
-    state_refs, out_ref = refs[:4], refs[4]
-    channels, tiles = state_refs[0].shape[0], slot_ref.shape[1]
-    closure = small_ref[rows : 2 * rows, :channels]
-    migr = state_refs[0].shape[1] - LANES
-    code = code_ref[:, code_ref.shape[1] - 4 * migr :]
-    state = jnp.concatenate([block[:, :migr] for block in arrived_blocks(state_refs)], axis=1)
-    mixed, first = mix(closure, state)
-    total = sum_ref[...] + dot(spread(mixed, first, code % TILE), ones(equal(tiles, code // TILE)), NT)
-    table = jnp.concatenate([total.astype(jnp.bfloat16), mark_ref[...]], axis=0)
+        total = total + dot(spread(mixed, first, place), ones(equal(tiles, tile)), NT)
+
+    lines = iota((out_ref.shape[1] - total.shape[0], tiles), 0)
+    marks = jnp.where(lines == 0, offset // FZ, jnp.where(lines == 1, offset % FZ, 0))
+    marks = marks.astype(jnp.float32).astype(jnp.bfloat16)
+    table = jnp.concatenate([total.astype(jnp.bfloat16), marks], axis=0)
     match = one_hot(iota((out_ref.shape[0], tiles), 0) == slot_ref[...])
     out_ref[...] = dot(match, table, NT).astype(jnp.bfloat16)
 
@@ -416,15 +407,11 @@
     )
     (xa, xb), (ya, yb) = exchange(*leaving[:2], "gx"), exchange(*leaving[2:], "gy")
     arrived = yb, xb, ya, xa
-    sums, code, slot, marks, live = call(
-        functools.partial(deposit_kernel, capacity, rows, 4 * migr),
-        [shape((width, tiles), f32), shape((1, slots), i32), shape((1, tiles), i32),
-         shape((lanes - width, tiles), bf16), shape((parts // LANES, LANES), f32)],
-        particles, small,
-    )
-    (payload,) = call(
-        functools.partial(pack_kernel, rows), [shape((count, lanes), bf16)],
-        sums, code, slot, marks, small, *arrived,
+    payload, code, slot, live = call(
+        functools.partial(deposit_kernel, capacity, rows),
+        [shape((count, lanes), bf16), shape((1, slots), i32), shape((1, tiles), i32),
+         shape((parts // LANES, LANES), f32)],
+        particles, small, *arrived,
     )
     received = lax.all_to_all(
         payload.reshape(devices, capacity, lanes), ("gx", "gy"), split_axis=0, concat_axis=0, tiled=True

time: 72.5 us -> 76.5 us (1.055)
  waiting for transfers between devices: 7.12 us -> 10.3 us
  blocking collectives: 39.6 us -> 40.7 us
    ppermute x8, waiting for transfers between devices: 7.12 us -> 10.3 us  [exchange(): blocks[odd] = lax.ppermute(block, axis, pairs)]
    all_to_all x1, blocking collectives: 21.1 us -> 22.1 us  [per_device(): lax.all_to_all(payload.reshape(devices, capacity, lanes), ('gx', 'gy'), s...]
    pallas_call x7 -> x6, Pallas kernels: 13.4 us -> 13.2 us  [call(): pl.pallas_call(kernel, out_shape=shapes, in_specs=[hbm if limit else vmem...]
  transfers between devices with their start and end apart: 8 -> 8, of which waited for: 2 -> 5; matrix products, arithmetic and copies ran while one was open for 0% -> 0% of each run, Pallas kernels for 5% -> 0%
where the time goes in v11:
time: 76.5 us; the launch traced here: 76.3 us
  blocking collectives  40.7 us (53%)
  Pallas kernels  13.2 us (17%)
  starting transfers between devices  10.5 us (14%)
  waiting for transfers between devices  10.3 us (13%)
  local copies, waits for them, and re-layouts  0.86 us (1%)
    all_to_all x1, blocking collectives, per_device(): lax.all_to_all(payload.reshape(devices, capacity, lanes), ('gx', 'gy'), s...  22.1 us
    all_to_all x1, blocking collectives, per_device(): lax.all_to_all(back.reshape(devices, capacity, rows * TILE), ('gx', 'gy')...  18.5 us
    pallas_call x6, Pallas kernels, call(): pl.pallas_call(kernel, out_shape=shapes, in_specs=[hbm if limit else vmem...  13.2 us
    ppermute x8, starting transfers between devices, exchange(): blocks[odd] = lax.ppermute(block, axis, pairs)  10.5 us
    ppermute x8, waiting for transfers between devices, exchange(): blocks[odd] = lax.ppermute(block, axis, pairs)  10.3 us
  transfers between devices with their start and end apart: 8, of which 5 were waited for; matrix products, arithmetic and copies ran while one was open for 0% of the time, Pallas kernels for 0%

profile of v11, /device:TPU:0, one launch (start us, length us, event | category | flops | bytes accessed | tf_op | source)
XLA Modules:
  0.0 76.3 jit_solution(15191368061837679233)
XLA Ops:
  0.6 0.0 copy-start
  0.6 2.6 %shard_map.104 = (bf16[16,640]{1,0:T(8,128)(2,1)}, bf16[16,640]{1,0:T(8,128)(2,1)}, bf16[16,640]{1,0:T(8,128)(2,1)}, bf16[16,640]{1,0:T(8,128)(2,1)}, f32[64,256]{1,0:T(8,128)}) custom-call(f32[16,8192]{1,0:T(8,128)} %part_ref.3, s32[4,512]{1,0:T(4,128)} %index_hbm.1, s32[1,4]{1,0:T(1,128)} %count_hbm.1, s32[1,256]{1,0:T(1,128)} %size_hbm.1, ...), custom_call_target="tpu_custom_call" | custom-call | tf_op jit(solution)/shard_map/pallas_call | solution.py:362
  3.3 6.1 %collective-permute-start = (bf16[16,640]{1,0:T(8,128)(2,1)}, bf16[16,640]{1,0:T(8,128)(2,1)S(1)}, u32[]{:S(2)}, u32[]{:S(2)}) collective-permute-start(bf16[16,640]{1,0:T(8,128)(2,1)} %get-tuple-element.22), channel_id=1, source_target_pairs={{0,7},{1,2},{2,1},{3,4},{4,3},{5,6},{6,5},{7,0},{8,15},{9,10},{10,... | collective-permute-start | bytes 61448 | tf_op jit(solution)/shard_map/ppermute | solution.py:65
  9.3 0.7 collective-permute-start.1
  10.0 0.0 collective-permute-start.2
  10.0 1.0 %collective-permute-start.3 = (bf16[16,640]{1,0:T(8,128)(2,1)}, bf16[16,640]{1,0:T(8,128)(2,1)S(1)}, u32[]{:S(2)}, u32[]{:S(2)}) collective-permute-start(bf16[16,640]{1,0:T(8,128)(2,1)} %get-tuple-element.25), channel_id=1, source_target_pairs={{0,8},{8,0},{16,24},{24,16},{1,9},{9,1},{17,25},{25,17},{2,10},{10... | collective-permute-start | bytes 61448 | tf_op jit(solution)/shard_map/ppermute | solution.py:65
  10.9 0.4 collective-permute-done.refs_0_
  11.3 1.6 %collective-permute-done.1.refs_1_ = bf16[16,640]{1,0:T(8,128)(2,1)S(1)} collective-permute-done((bf16[16,640]{1,0:T(8,128)(2,1)}, bf16[16,640]{1,0:T(8,128)(2,1)S(1)}, u32[]{:S(2)}, u32[]{:S(2)}) %collective-permute-start.1) | collective-permute-done | bytes 20512 | tf_op jit(solution)/shard_map/ppermute | solution.py:65
  12.9 1.3 %collective-permute-done.2.refs_2_ = bf16[16,640]{1,0:T(8,128)(2,1)S(1)} collective-permute-done((bf16[16,640]{1,0:T(8,128)(2,1)}, bf16[16,640]{1,0:T(8,128)(2,1)S(1)}, u32[]{:S(2)}, u32[]{:S(2)}) %collective-permute-start.2) | collective-permute-done | bytes 20512 | tf_op jit(solution)/shard_map/ppermute | solution.py:65
  14.2 0.0 collective-permute-done.3.refs_3_
  14.2 0.0 copy-done
  14.2 0.0 copy-start.1
  14.2 0.8 %copy-done.1 = f32[64,256]{1,0:T(8,128)S(1)} copy-done((f32[64,256]{1,0:T(8,128)S(1)}, f32[64,256]{1,0:T(8,128)}, u32[]{:S(2)}) %copy-start.1) | copy-done | bytes 65560
  15.0 5.0 %shard_map.105 = (bf16[512,640]{1,0:T(8,128)(2,1)S(1)}, s32[1,10240]{1,0:T(1,128)S(1)}, s32[1,256]{1,0:T(1,128)S(1)}, f32[64,128]{1,0:T(8,128)S(1)}) custom-call(f32[16,8192]{1,0:T(8,128)S(1)} %copy-done, f32[64,256]{1,0:T(8,128)S(1)} %copy-done.1, bf16[16,640]{1,0:T(8,128)(2,1)S(1)} %collective-permute-done.refs_0_, ...), custom_call_target="tpu_custom_call" | custom-call | tf_op jit(solution)/shard_map/pallas_call | solution.py:362
  20.1 22.1 %all_to_all.10 = bf16[32,16,640]{2,1,0:T(8,128)(2,1)S(1)} all-to-all(bf16[32,16,640]{2,1,0:T(8,128)(2,1)S(1)} %bitcast.11), channel_id=1, replica_groups=mesh['gx'=4,'gy'=8] {'gx','gy'}, dimensions={0} | all-to-all | bytes 1310720 | tf_op jit(solution)/shard_map/all_to_all | solution.py:416
  42.2 0.6 shard_map.106
  42.8 0.5 collective-permute-start.4
  43.3 0.2 collective-permute-start.5
  43.5 2.6 %collective-permute-done.4.xb_ref = bf16[16,576]{1,0:T(8,128)(2,1)S(1)} collective-permute-done((bf16[16,576]{1,0:T(8,128)(2,1)S(1)}, bf16[16,576]{1,0:T(8,128)(2,1)S(1)}, u32[]{:S(2)}, u32[]{:S(2)}) %collective-permute-start.4) | collective-permute-done | bytes 18464 | tf_op jit(solution)/shard_map/ppermute | solution.py:65
  46.2 0.0 collective-permute-done.5.xa_ref
  46.2 0.2 shard_map.107
  46.4 1.7 %collective-permute-start.6 = (bf16[16,576]{1,0:T(8,128)(2,1)S(1)}, bf16[16,576]{1,0:T(8,128)(2,1)S(1)}, u32[]{:S(2)}, u32[]{:S(2)}) collective-permute-start(bf16[16,576]{1,0:T(8,128)(2,1)S(1)} %get-tuple-element.31), channel_id=1, source_target_pairs={{0,7},{1,2},{2,1},{3,4},{4,3},{5,6},{6,5},{7,0},{8,15},{9,10},{10,... | collective-permute-start | bytes 55304 | tf_op jit(solution)/shard_map/ppermute | solution.py:65
  48.0 0.4 collective-permute-start.7
  48.4 4.5 %collective-permute-done.6.yb_ref = bf16[16,576]{1,0:T(8,128)(2,1)S(1)} collective-permute-done((bf16[16,576]{1,0:T(8,128)(2,1)S(1)}, bf16[16,576]{1,0:T(8,128)(2,1)S(1)}, u32[]{:S(2)}, u32[]{:S(2)}) %collective-permute-start.6) | collective-permute-done | bytes 18464 | tf_op jit(solution)/shard_map/ppermute | solution.py:65
  52.9 0.0 collective-permute-done.7.ya_ref
  52.9 0.8 shard_map.108
  53.7 0.0 copy-start.2
  53.7 18.5 %all_to_all.11 = bf16[32,16,512]{2,1,0:T(8,128)(2,1)S(1)} all-to-all(bf16[32,16,512]{2,1,0:T(8,128)(2,1)S(1)} %bitcast.12), channel_id=1, replica_groups=mesh['gx'=4,'gy'=8] {'gx','gy'}, dimensions={0} | all-to-all | bytes 1048576 | tf_op jit(solution)/shard_map/all_to_all | solution.py:429
  72.2 0.0 copy-done.2
  72.2 4.0 %shard_map.109 = (f32[8,10240]{1,0:T(8,128)}, bf16[8,8,8,128]{3,2,1,0:T(8,128)(2,1)}) custom-call(bf16[512,512]{1,0:T(8,128)(2,1)S(1)} %bitcast.10, s32[1,256]{1,0:T(1,128)S(1)} %get-tuple-element.34.slot_ref, s32[1,10240]{1,0:T(1,128)S(1)} %get-tuple-element.35.code_ref, f32[16,8192]{1,0:T(8,128)S(1)} %copy-done, f32[64,256]{1,0:T(8,128)S(1)} %copy-done.2, ...), custom_call_target="tpu_custom_call" | custom-call | tf_op jit(solution)/shard_map/pallas_call | solution.py:362
  (1 shorter events, 0.0 us)
Async XLA Ops:
  0.6 13.6 %copy-start = (f32[16,8192]{1,0:T(8,128)S(1)}, f32[16,8192]{1,0:T(8,128)}, u32[]{:S(2)}) copy-start(f32[16,8192]{1,0:T(8,128)} %part_ref.3) | copy-start | bytes 1572868
  3.3 8.0 %collective-permute-start = (bf16[16,640]{1,0:T(8,128)(2,1)}, bf16[16,640]{1,0:T(8,128)(2,1)S(1)}, u32[]{:S(2)}, u32[]{:S(2)}) collective-permute-start(bf16[16,640]{1,0:T(8,128)(2,1)} %get-tuple-element.22), channel_id=1, source_target_pairs={{0,7},{1,2},{2,1},{3,4},{4,3},{5,6},{6,5},{7,0},{8,15},{9,10},{10,... | collective-permute-start | bytes 61448 | tf_op jit(solution)/shard_map/ppermute | solution.py:65
  9.3 3.6 %collective-permute-start.1 = (bf16[16,640]{1,0:T(8,128)(2,1)}, bf16[16,640]{1,0:T(8,128)(2,1)S(1)}, u32[]{:S(2)}, u32[]{:S(2)}) collective-permute-start(bf16[16,640]{1,0:T(8,128)(2,1)} %get-tuple-element.23), channel_id=1, source_target_pairs={{0,24},{8,16},{16,8},{24,0},{1,25},{9,17},{17,9},{25,1},{2,26},{10... | collective-permute-start | bytes 61448 | tf_op jit(solution)/shard_map/ppermute | solution.py:65
  10.0 4.2 %collective-permute-start.2 = (bf16[16,640]{1,0:T(8,128)(2,1)}, bf16[16,640]{1,0:T(8,128)(2,1)S(1)}, u32[]{:S(2)}, u32[]{:S(2)}) collective-permute-start(bf16[16,640]{1,0:T(8,128)(2,1)} %get-tuple-element.24), channel_id=1, source_target_pairs={{0,1},{1,0},{2,3},{3,2},{4,5},{5,4},{6,7},{7,6},{8,9},{9,8},{10,11... | collective-permute-start | bytes 61448 | tf_op jit(solution)/shard_map/ppermute | solution.py:65
  10.0 4.2 %collective-permute-start.3 = (bf16[16,640]{1,0:T(8,128)(2,1)}, bf16[16,640]{1,0:T(8,128)(2,1)S(1)}, u32[]{:S(2)}, u32[]{:S(2)}) collective-permute-start(bf16[16,640]{1,0:T(8,128)(2,1)} %get-tuple-element.25), channel_id=1, source_target_pairs={{0,8},{8,0},{16,24},{24,16},{1,9},{9,1},{17,25},{25,17},{2,10},{10... | collective-permute-start | bytes 61448 | tf_op jit(solution)/shard_map/ppermute | solution.py:65
  14.2 0.8 %copy-start.1 = (f32[64,256]{1,0:T(8,128)S(1)}, f32[64,256]{1,0:T(8,128)}, u32[]{:S(2)}) copy-start(f32[64,256]{1,0:T(8,128)} %get-tuple-element.21.small_ref) | copy-start | bytes 196612
  42.8 3.3 %collective-permute-start.4 = (bf16[16,576]{1,0:T(8,128)(2,1)S(1)}, bf16[16,576]{1,0:T(8,128)(2,1)S(1)}, u32[]{:S(2)}, u32[]{:S(2)}) collective-permute-start(bf16[16,576]{1,0:T(8,128)(2,1)S(1)} %get-tuple-element.28), channel_id=1, source_target_pairs={{0,24},{8,16},{16,8},{24,0},{1,25},{9,17},{17,9},{25,1},{2,26},{10... | collective-permute-start | bytes 55304 | tf_op jit(solution)/shard_map/ppermute | solution.py:65
  43.3 2.8 %collective-permute-start.5 = (bf16[16,576]{1,0:T(8,128)(2,1)S(1)}, bf16[16,576]{1,0:T(8,128)(2,1)S(1)}, u32[]{:S(2)}, u32[]{:S(2)}) collective-permute-start(bf16[16,576]{1,0:T(8,128)(2,1)S(1)} %get-tuple-element.29), channel_id=1, source_target_pairs={{0,8},{8,0},{16,24},{24,16},{1,9},{9,1},{17,25},{25,17},{2,10},{10... | collective-permute-start | bytes 55304 | tf_op jit(solution)/shard_map/ppermute | solution.py:65
  46.4 6.5 %collective-permute-start.6 = (bf16[16,576]{1,0:T(8,128)(2,1)S(1)}, bf16[16,576]{1,0:T(8,128)(2,1)S(1)}, u32[]{:S(2)}, u32[]{:S(2)}) collective-permute-start(bf16[16,576]{1,0:T(8,128)(2,1)S(1)} %get-tuple-element.31), channel_id=1, source_target_pairs={{0,7},{1,2},{2,1},{3,4},{4,3},{5,6},{6,5},{7,0},{8,15},{9,10},{10,... | collective-permute-start | bytes 55304 | tf_op jit(solution)/shard_map/ppermute | solution.py:65
  48.0 4.9 %collective-permute-start.7 = (bf16[16,576]{1,0:T(8,128)(2,1)S(1)}, bf16[16,576]{1,0:T(8,128)(2,1)S(1)}, u32[]{:S(2)}, u32[]{:S(2)}) collective-permute-start(bf16[16,576]{1,0:T(8,128)(2,1)S(1)} %get-tuple-element.32), channel_id=1, source_target_pairs={{0,1},{1,0},{2,3},{3,2},{4,5},{5,4},{6,7},{7,6},{8,9},{9,8},{10,11... | collective-permute-start | bytes 55304 | tf_op jit(solution)/shard_map/ppermute | solution.py:65
  53.7 18.6 %copy-start.2 = (f32[64,256]{1,0:T(8,128)S(1)}, f32[64,256]{1,0:T(8,128)}, u32[]{:S(2)}) copy-start(f32[64,256]{1,0:T(8,128)} %get-tuple-element.21.small_ref) | copy-start | bytes 196612

commit v12 on v8

--- a/solution.py
+++ b/solution.py
@@ -82,7 +82,7 @@
 
 
 def arrived_blocks(refs):
-    yb, xb, ya, xa = [ref[...].astype(jnp.float32) for ref in refs]
+    yb, ya, xb, xa = [ref[...].astype(jnp.float32) for ref in refs]
     return ordered(xa, xb, "gx") + ordered(ya, yb, "gy")
 
 
@@ -415,7 +415,7 @@
            pltpu.SemaphoreType.DMA((9,)), pltpu.SemaphoreType.DMA((5,))],
     )
     (xa, xb), (ya, yb) = exchange(*leaving[:2], "gx"), exchange(*leaving[2:], "gy")
-    arrived = yb, xb, ya, xa
+    arrived = yb, ya, xb, xa
     sums, code, slot, marks, live = call(
         functools.partial(deposit_kernel, capacity, rows, 4 * migr),
         [shape((width, tiles), f32), shape((1, slots), i32), shape((1, tiles), i32),

time: 72.5 us -> 72.7 us (level)
  no operation moved by 1% of the time
where the time goes in v12:
time: 72.7 us; the launch traced here: 72.5 us
  blocking collectives  39.9 us (55%)
  Pallas kernels  13.4 us (18%)
  starting transfers between devices  10.5 us (14%)
  waiting for transfers between devices  7.11 us (10%)
  local copies, waits for them, and re-layouts  0.86 us (1%)
    all_to_all x1, blocking collectives, per_device(): lax.all_to_all(payload.reshape(devices, capacity, lanes), ('gx', 'gy'), s...  21.4 us
    all_to_all x1, blocking collectives, per_device(): lax.all_to_all(back.reshape(devices, capacity, rows * TILE), ('gx', 'gy')...  18.5 us
    pallas_call x7, Pallas kernels, call(): pl.pallas_call(kernel, out_shape=shapes, in_specs=[hbm if limit else vmem...  13.4 us
    ppermute x8, starting transfers between devices, exchange(): blocks[odd] = lax.ppermute(block, axis, pairs)  10.5 us
    ppermute x8, waiting for transfers between devices, exchange(): blocks[odd] = lax.ppermute(block, axis, pairs)  7.11 us
  transfers between devices with their start and end apart: 8, of which 2 were waited for; matrix products, arithmetic and copies ran while one was open for 0% of the time, Pallas kernels for 5%

profile of v12, /device:TPU:0, one launch (start us, length us, event | category | flops | bytes accessed | tf_op | source)
XLA Modules:
  0.0 72.5 jit_solution(4840979202154907039)
XLA Ops:
  0.6 0.0 copy-start
  0.6 2.6 %shard_map.104 = (bf16[16,640]{1,0:T(8,128)(2,1)}, bf16[16,640]{1,0:T(8,128)(2,1)}, bf16[16,640]{1,0:T(8,128)(2,1)}, bf16[16,640]{1,0:T(8,128)(2,1)}, f32[64,256]{1,0:T(8,128)}) custom-call(f32[16,8192]{1,0:T(8,128)} %part_ref.3, s32[4,512]{1,0:T(4,128)} %index_hbm.1, s32[1,4]{1,0:T(1,128)} %count_hbm.1, s32[1,256]{1,0:T(1,128)} %size_hbm.1, ...), custom_call_target="tpu_custom_call" | custom-call | tf_op jit(solution)/shard_map/pallas_call | solution.py:371
  3.3 6.1 %collective-permute-start = (bf16[16,640]{1,0:T(8,128)(2,1)}, bf16[16,640]{1,0:T(8,128)(2,1)S(1)}, u32[]{:S(2)}, u32[]{:S(2)}) collective-permute-start(bf16[16,640]{1,0:T(8,128)(2,1)} %get-tuple-element.27), channel_id=1, source_target_pairs={{0,7},{1,2},{2,1},{3,4},{4,3},{5,6},{6,5},{7,0},{8,15},{9,10},{10,... | collective-permute-start | bytes 61448 | tf_op jit(solution)/shard_map/ppermute | solution.py:65
  9.3 0.0 collective-permute-start.1
  9.3 0.7 collective-permute-start.2
  10.0 1.0 %collective-permute-start.3 = (bf16[16,640]{1,0:T(8,128)(2,1)}, bf16[16,640]{1,0:T(8,128)(2,1)S(1)}, u32[]{:S(2)}, u32[]{:S(2)}) collective-permute-start(bf16[16,640]{1,0:T(8,128)(2,1)} %get-tuple-element.30), channel_id=1, source_target_pairs={{0,8},{8,0},{16,24},{24,16},{1,9},{9,1},{17,25},{25,17},{2,10},{10... | collective-permute-start | bytes 61448 | tf_op jit(solution)/shard_map/ppermute | solution.py:65
  10.9 0.0 copy-done
  10.9 0.0 copy-start.1
  10.9 0.8 %copy-done.1 = f32[64,256]{1,0:T(8,128)S(1)} copy-done((f32[64,256]{1,0:T(8,128)S(1)}, f32[64,256]{1,0:T(8,128)}, u32[]{:S(2)}) %copy-start.1) | copy-done | bytes 65560
  11.8 3.6 %shard_map.105 = (f32[576,256]{1,0:T(8,128)S(1)}, s32[1,10240]{1,0:T(1,128)S(1)}, s32[1,256]{1,0:T(1,128)S(1)}, bf16[64,256]{1,0:T(8,128)(2,1)S(1)}, f32[64,128]{1,0:T(8,128)S(1)}) custom-call(f32[16,8192]{1,0:T(8,128)S(1)} %copy-done, f32[64,256]{1,0:T(8,128)S(1)} %copy-done.1), custom_call_target="tpu_custom_call" | custom-call | tf_op jit(solution)/shard_map/pallas_call | solution.py:371
  15.4 0.0 collective-permute-done.refs_0_
  15.4 0.0 collective-permute-done.1.refs_1_
  15.4 0.0 collective-permute-done.2.refs_2_
  15.4 0.0 collective-permute-done.3.refs_3_
  15.4 1.6 %shard_map.106 = bf16[512,640]{1,0:T(8,128)(2,1)S(1)} custom-call(f32[576,256]{1,0:T(8,128)S(1)} %get-tuple-element.23.sum_ref, s32[1,10240]{1,0:T(1,128)S(1)} %get-tuple-element.24.code_ref, s32[1,256]{1,0:T(1,128)S(1)} %get-tuple-element.25.slot_ref, bf16[64,256]{1,0:T(8,128)(2,1)S(1)} %get-tuple-element.26.mark_ref, f32[64,256]{1,0:T(8,128)S(1)} %copy-done.1, ...), custom_call_target="tpu_custom_call" | custom-call | tf_op jit(solution)/shard_map/pallas_call | solution.py:371
  17.1 21.4 %all_to_all.10 = bf16[32,16,640]{2,1,0:T(8,128)(2,1)S(1)} all-to-all(bf16[32,16,640]{2,1,0:T(8,128)(2,1)S(1)} %bitcast.10), channel_id=1, replica_groups=mesh['gx'=4,'gy'=8] {'gx','gy'}, dimensions={0} | all-to-all | bytes 1310720 | tf_op jit(solution)/shard_map/all_to_all | solution.py:429
  38.4 0.6 shard_map.107
  39.0 0.5 collective-permute-start.4
  39.6 0.2 collective-permute-start.5
  39.8 2.6 %collective-permute-done.4.xb_ref = bf16[16,576]{1,0:T(8,128)(2,1)S(1)} collective-permute-done((bf16[16,576]{1,0:T(8,128)(2,1)S(1)}, bf16[16,576]{1,0:T(8,128)(2,1)S(1)}, u32[]{:S(2)}, u32[]{:S(2)}) %collective-permute-start.4) | collective-permute-done | bytes 18464 | tf_op jit(solution)/shard_map/ppermute | solution.py:65
  42.4 0.0 collective-permute-done.5.xa_ref
  42.4 0.2 shard_map.108
  42.6 1.7 %collective-permute-start.6 = (bf16[16,576]{1,0:T(8,128)(2,1)S(1)}, bf16[16,576]{1,0:T(8,128)(2,1)S(1)}, u32[]{:S(2)}, u32[]{:S(2)}) collective-permute-start(bf16[16,576]{1,0:T(8,128)(2,1)S(1)} %get-tuple-element.35), channel_id=1, source_target_pairs={{0,7},{1,2},{2,1},{3,4},{4,3},{5,6},{6,5},{7,0},{8,15},{9,10},{10,... | collective-permute-start | bytes 55304 | tf_op jit(solution)/shard_map/ppermute | solution.py:65
  44.3 0.4 collective-permute-start.7
  44.7 4.5 %collective-permute-done.6.yb_ref = bf16[16,576]{1,0:T(8,128)(2,1)S(1)} collective-permute-done((bf16[16,576]{1,0:T(8,128)(2,1)S(1)}, bf16[16,576]{1,0:T(8,128)(2,1)S(1)}, u32[]{:S(2)}, u32[]{:S(2)}) %collective-permute-start.6) | collective-permute-done | bytes 18464 | tf_op jit(solution)/shard_map/ppermute | solution.py:65
  49.1 0.0 collective-permute-done.7.ya_ref
  49.1 0.8 %shard_map.109 = (bf16[8,8,8,128]{3,2,1,0:T(8,128)(2,1)S(1)}, bf16[512,512]{1,0:T(8,128)(2,1)S(1)}) custom-call(bf16[512,128]{1,0:T(8,128)(2,1)S(1)} %slice.4.mark_ref, f32[64,1152]{1,0:T(8,128)S(1)} %get-tuple-element.34.along_ref, bf16[16,576]{1,0:T(8,128)(2,1)S(1)} %collective-permute-done.6.yb_ref, bf16[16,576]{1,0:T(8,128)(2,1)S(1)} %collective-permute-done.7.ya_ref), custom_call_target="tpu_custom_call" | custom-call | tf_op jit(solution)/shard_map/pallas_call | solution.py:371
  49.9 0.0 copy-start.2
  49.9 18.5 %all_to_all.11 = bf16[32,16,512]{2,1,0:T(8,128)(2,1)S(1)} all-to-all(bf16[32,16,512]{2,1,0:T(8,128)(2,1)S(1)} %bitcast.12), channel_id=1, replica_groups=mesh['gx'=4,'gy'=8] {'gx','gy'}, dimensions={0} | all-to-all | bytes 1048576 | tf_op jit(solution)/shard_map/all_to_all | solution.py:442
  68.5 0.0 copy-done.2
  68.5 4.0 %shard_map.110 = (f32[8,10240]{1,0:T(8,128)}, bf16[8,8,8,128]{3,2,1,0:T(8,128)(2,1)}) custom-call(bf16[512,512]{1,0:T(8,128)(2,1)S(1)} %bitcast.11, s32[1,256]{1,0:T(1,128)S(1)} %get-tuple-element.25.slot_ref, s32[1,10240]{1,0:T(1,128)S(1)} %get-tuple-element.24.code_ref, f32[16,8192]{1,0:T(8,128)S(1)} %copy-done, f32[64,256]{1,0:T(8,128)S(1)} %copy-done.2, ...), custom_call_target="tpu_custom_call" | custom-call | tf_op jit(solution)/shard_map/pallas_call | solution.py:371
  (1 shorter events, 0.0 us)
Async XLA Ops:
  0.6 10.3 %copy-start = (f32[16,8192]{1,0:T(8,128)S(1)}, f32[16,8192]{1,0:T(8,128)}, u32[]{:S(2)}) copy-start(f32[16,8192]{1,0:T(8,128)} %part_ref.3) | copy-start | bytes 1572868
  3.3 12.1 %collective-permute-start = (bf16[16,640]{1,0:T(8,128)(2,1)}, bf16[16,640]{1,0:T(8,128)(2,1)S(1)}, u32[]{:S(2)}, u32[]{:S(2)}) collective-permute-start(bf16[16,640]{1,0:T(8,128)(2,1)} %get-tuple-element.27), channel_id=1, source_target_pairs={{0,7},{1,2},{2,1},{3,4},{4,3},{5,6},{6,5},{7,0},{8,15},{9,10},{10,... | collective-permute-start | bytes 61448 | tf_op jit(solution)/shard_map/ppermute | solution.py:65
  9.3 6.1 %collective-permute-start.1 = (bf16[16,640]{1,0:T(8,128)(2,1)}, bf16[16,640]{1,0:T(8,128)(2,1)S(1)}, u32[]{:S(2)}, u32[]{:S(2)}) collective-permute-start(bf16[16,640]{1,0:T(8,128)(2,1)} %get-tuple-element.28), channel_id=1, source_target_pairs={{0,1},{1,0},{2,3},{3,2},{4,5},{5,4},{6,7},{7,6},{8,9},{9,8},{10,11... | collective-permute-start | bytes 61448 | tf_op jit(solution)/shard_map/ppermute | solution.py:65
  9.3 6.1 %collective-permute-start.2 = (bf16[16,640]{1,0:T(8,128)(2,1)}, bf16[16,640]{1,0:T(8,128)(2,1)S(1)}, u32[]{:S(2)}, u32[]{:S(2)}) collective-permute-start(bf16[16,640]{1,0:T(8,128)(2,1)} %get-tuple-element.29), channel_id=1, source_target_pairs={{0,24},{8,16},{16,8},{24,0},{1,25},{9,17},{17,9},{25,1},{2,26},{10... | collective-permute-start | bytes 61448 | tf_op jit(solution)/shard_map/ppermute | solution.py:65
  10.0 5.4 %collective-permute-start.3 = (bf16[16,640]{1,0:T(8,128)(2,1)}, bf16[16,640]{1,0:T(8,128)(2,1)S(1)}, u32[]{:S(2)}, u32[]{:S(2)}) collective-permute-start(bf16[16,640]{1,0:T(8,128)(2,1)} %get-tuple-element.30), channel_id=1, source_target_pairs={{0,8},{8,0},{16,24},{24,16},{1,9},{9,1},{17,25},{25,17},{2,10},{10... | collective-permute-start | bytes 61448 | tf_op jit(solution)/shard_map/ppermute | solution.py:65
  10.9 0.8 %copy-start.1 = (f32[64,256]{1,0:T(8,128)S(1)}, f32[64,256]{1,0:T(8,128)}, u32[]{:S(2)}) copy-start(f32[64,256]{1,0:T(8,128)} %get-tuple-element.22.small_ref) | copy-start | bytes 196612
  39.0 3.3 %collective-permute-start.4 = (bf16[16,576]{1,0:T(8,128)(2,1)S(1)}, bf16[16,576]{1,0:T(8,128)(2,1)S(1)}, u32[]{:S(2)}, u32[]{:S(2)}) collective-permute-start(bf16[16,576]{1,0:T(8,128)(2,1)S(1)} %get-tuple-element.32), channel_id=1, source_target_pairs={{0,24},{8,16},{16,8},{24,0},{1,25},{9,17},{17,9},{25,1},{2,26},{10... | collective-permute-start | bytes 55304 | tf_op jit(solution)/shard_map/ppermute | solution.py:65
  39.6 2.8 %collective-permute-start.5 = (bf16[16,576]{1,0:T(8,128)(2,1)S(1)}, bf16[16,576]{1,0:T(8,128)(2,1)S(1)}, u32[]{:S(2)}, u32[]{:S(2)}) collective-permute-start(bf16[16,576]{1,0:T(8,128)(2,1)S(1)} %get-tuple-element.33), channel_id=1, source_target_pairs={{0,8},{8,0},{16,24},{24,16},{1,9},{9,1},{17,25},{25,17},{2,10},{10... | collective-permute-start | bytes 55304 | tf_op jit(solution)/shard_map/ppermute | solution.py:65
  42.6 6.5 %collective-permute-start.6 = (bf16[16,576]{1,0:T(8,128)(2,1)S(1)}, bf16[16,576]{1,0:T(8,128)(2,1)S(1)}, u32[]{:S(2)}, u32[]{:S(2)}) collective-permute-start(bf16[16,576]{1,0:T(8,128)(2,1)S(1)} %get-tuple-element.35), channel_id=1, source_target_pairs={{0,7},{1,2},{2,1},{3,4},{4,3},{5,6},{6,5},{7,0},{8,15},{9,10},{10,... | collective-permute-start | bytes 55304 | tf_op jit(solution)/shard_map/ppermute | solution.py:65
  44.3 4.9 %collective-permute-start.7 = (bf16[16,576]{1,0:T(8,128)(2,1)S(1)}, bf16[16,576]{1,0:T(8,128)(2,1)S(1)}, u32[]{:S(2)}, u32[]{:S(2)}) collective-permute-start(bf16[16,576]{1,0:T(8,128)(2,1)S(1)} %get-tuple-element.36), channel_id=1, source_target_pairs={{0,1},{1,0},{2,3},{3,2},{4,5},{5,4},{6,7},{7,6},{8,9},{9,8},{10,11... | collective-permute-start | bytes 55304 | tf_op jit(solution)/shard_map/ppermute | solution.py:65
  49.9 18.6 %copy-start.2 = (f32[64,256]{1,0:T(8,128)S(1)}, f32[64,256]{1,0:T(8,128)}, u32[]{:S(2)}) copy-start(f32[64,256]{1,0:T(8,128)} %get-tuple-element.22.small_ref) | copy-start | bytes 196612

commit v13 on v8

--- a/solution.py
+++ b/solution.py
@@ -246,25 +246,27 @@
     out_ref[...] = dot(match, table, NT).astype(jnp.bfloat16)
 
 
-def place_kernel(tile_ref, gas_ref, xa_ref, xb_ref):
-    even = is_even("gx")
+def place_kernel(tile_ref, gas_ref, ya_ref, yb_ref):
+    even = is_even("gy")
     count, lanes = tile_ref.shape
     width = gas_ref.shape[1] // 2
     marks = tile_ref[:, lanes - LANES :].astype(jnp.float32)
     column = marks[:, width % LANES : width % LANES + 1]
     height = marks[:, width % LANES + 1 : width % LANES + 2]
     lane = iota((1, LANES), 1)
-    hot = one_hot(column == lane.astype(jnp.float32))
+    edge = jnp.where(lane < COLS + FX, (lane - COLS) * FY, (lane - COLS - FX) * FY + FY - 1)
+    target = jnp.where(lane < COLS, lane, jnp.where(lane < COLS + 2 * FX, edge, -1))
+    hot = one_hot(column == target.astype(jnp.float32))
     place = (iota((1, width), 1) % TILE).astype(jnp.float32)
     values = tile_ref[:, :width].astype(jnp.float32)
     for half, mask in enumerate((place >= height, place < height)):
         total = dot(hot, jnp.where(mask, values, 0.0).astype(jnp.bfloat16), TN)
         where = slice(half * width, (half + 1) * width)
         gas_ref[:, where] = total[:COLS]
-        rows = slice(half * FY, (half + 1) * FY)
-        low, high = total[:FY], total[COLS - FY : COLS]
-        xa_ref[rows, :] = jnp.where(even, high, low).astype(jnp.bfloat16)
-        xb_ref[rows, :] = jnp.where(even, low, high).astype(jnp.bfloat16)
+        rows = slice(half * FX, (half + 1) * FX)
+        low, high = total[COLS : COLS + FX], total[COLS + FX : COLS + 2 * FX]
+        ya_ref[rows, :] = jnp.where(even, high, low).astype(jnp.bfloat16)
+        yb_ref[rows, :] = jnp.where(even, low, high).astype(jnp.bfloat16)
 
 
 def unfold(ref):
@@ -273,32 +275,28 @@
     return jnp.concatenate([edge[:half], edge[half:]], axis=1)
 
 
-def along_kernel(gas_ref, xb_ref, xa_ref, out_ref, ya_ref, yb_ref):
-    before, after = ordered(unfold(xa_ref), unfold(xb_ref), "gx")
-    blocks = [before] + [gas_ref[x * FY : (x + 1) * FY, :] for x in range(FX)] + [after]
-    along = [blocks[x] + 2.0 * blocks[x + 1] + blocks[x + 2] for x in range(FX)]
+def along_kernel(gas_ref, yb_ref, ya_ref, out_ref, xa_ref, xb_ref):
+    before, after = ordered(unfold(ya_ref), unfold(yb_ref), "gy")
+    along = []
     for x in range(FX):
+        block = gas_ref[x * FY : (x + 1) * FY, :]
+        padded = jnp.concatenate([before[x : x + 1], block, after[x : x + 1]], axis=0)
+        along.append(padded[0:FY] + 2.0 * block + padded[2 : FY + 2])
         out_ref[x * FY : (x + 1) * FY, :] = along[x]
-    width = ya_ref.shape[1]
-    edges = []
-    for row in (0, FY - 1):
-        edge = jnp.concatenate([along[x][row : row + 1] for x in range(FX)], axis=0)
-        edges.append(jnp.concatenate([edge[:, :width], edge[:, width:]], axis=0))
-    even = is_even("gy")
-    ya_ref[...] = jnp.where(even, edges[1], edges[0]).astype(jnp.bfloat16)
-    yb_ref[...] = jnp.where(even, edges[0], edges[1]).astype(jnp.bfloat16)
-
-
-def drag_kernel(mark_ref, along_ref, yb_ref, ya_ref, drag_ref, back_ref):
+    width = xa_ref.shape[1]
+    low, high = [jnp.concatenate([along[x][:, :width], along[x][:, width:]], axis=0) for x in (0, FX - 1)]
+    even = is_even("gx")
+    xa_ref[...] = jnp.where(even, high, low).astype(jnp.bfloat16)
+    xb_ref[...] = jnp.where(even, low, high).astype(jnp.bfloat16)
+
+
+def drag_kernel(mark_ref, along_ref, xb_ref, xa_ref, drag_ref, back_ref):
     rows = drag_ref.shape[0]
     width = along_ref.shape[1] // 2
     lanes = rows * TILE
-    before, after = ordered(unfold(ya_ref), unfold(yb_ref), "gy")
-    smooth = []
-    for x in range(FX):
-        block = along_ref[x * FY : (x + 1) * FY, :]
-        padded = jnp.concatenate([before[x : x + 1], block, after[x : x + 1]], axis=0)
-        smooth.append((padded[0:FY] + 2.0 * block + padded[2 : FY + 2]) / 16.0)
+    first, last = ordered(unfold(xa_ref), unfold(xb_ref), "gx")
+    blocks = [first] + [along_ref[x * FY : (x + 1) * FY, :] for x in range(FX)] + [last]
+    smooth = [(blocks[x] + 2.0 * blocks[x + 1] + blocks[x + 2]) / 16.0 for x in range(FX)]
     smooth = jnp.concatenate(smooth, axis=0)
     halves = []
     for half in range(2):
@@ -430,14 +428,14 @@
         payload.reshape(devices, capacity, lanes), ("gx", "gy"), split_axis=0, concat_axis=0, tiled=True
     ).reshape(count, lanes)
     grid, edge = shape((COLS, 2 * width), f32), shape((2 * FX, width), bf16)
-    gas, xa, xb = call(place_kernel, [grid, edge, edge], received)
+    gas, ya, yb = call(place_kernel, [grid, edge, edge], received)
+    ya, yb = exchange(ya, yb, "gy")
+    along, xa, xb = call(along_kernel, [grid, edge, edge], gas, yb, ya)
     xa, xb = exchange(xa, xb, "gx")
-    along, ya, yb = call(along_kernel, [grid, edge, edge], gas, xb, xa)
-    ya, yb = exchange(ya, yb, "gy")
     drag, back = call(
         drag_kernel,
         [shape((rows, FX, FY, FZ), bf16), shape((count, rows * TILE), bf16)],
-        received[:, lanes - LANES :], along, yb, ya,
+        received[:, lanes - LANES :], along, xb, xa,
     )
     returned = lax.all_to_all(
         back.reshape(devices, capacity, rows * TILE), ("gx", "gy"), split_axis=0, concat_axis=0, tiled=True

time: 72.5 us -> 72.5 us (level)
  no operation moved by 1% of the time
where the time goes in v13:
time: 72.5 us; the launch traced here: 72.3 us
  blocking collectives  39.8 us (55%)
  Pallas kernels  13.4 us (18%)
  starting transfers between devices  10.5 us (14%)
  waiting for transfers between devices  6.97 us (10%)
  local copies, waits for them, and re-layouts  0.86 us (1%)
  between operations  0.73 us (1%)
    all_to_all x1, blocking collectives, per_device(): lax.all_to_all(payload.reshape(devices, capacity, lanes), ('gx', 'gy'), s...  21.1 us
    all_to_all x1, blocking collectives, per_device(): lax.all_to_all(back.reshape(devices, capacity, rows * TILE), ('gx', 'gy')...  18.7 us
    pallas_call x7, Pallas kernels, call(): pl.pallas_call(kernel, out_shape=shapes, in_specs=[hbm if limit else vmem...  13.4 us
    ppermute x8, starting transfers between devices, exchange(): blocks[odd] = lax.ppermute(block, axis, pairs)  10.5 us
    ppermute x8, waiting for transfers between devices, exchange(): blocks[odd] = lax.ppermute(block, axis, pairs)  6.97 us
  transfers between devices with their start and end apart: 8, of which 2 were waited for; matrix products, arithmetic and copies ran while one was open for 0% of the time, Pallas kernels for 5%

profile of v13, /device:TPU:0, one launch (start us, length us, event | category | flops | bytes accessed | tf_op | source)
XLA Modules:
  0.0 72.3 jit_solution(7584822295910399535)
XLA Ops:
  0.6 0.0 copy-start
  0.6 2.6 %shard_map.104 = (bf16[16,640]{1,0:T(8,128)(2,1)}, bf16[16,640]{1,0:T(8,128)(2,1)}, bf16[16,640]{1,0:T(8,128)(2,1)}, bf16[16,640]{1,0:T(8,128)(2,1)}, f32[64,256]{1,0:T(8,128)}) custom-call(f32[16,8192]{1,0:T(8,128)} %part_ref.3, s32[4,512]{1,0:T(4,128)} %index_hbm.1, s32[1,4]{1,0:T(1,128)} %count_hbm.1, s32[1,256]{1,0:T(1,128)} %size_hbm.1, ...), custom_call_target="tpu_custom_call" | custom-call | tf_op jit(solution)/shard_map/pallas_call | solution.py:369
  3.3 6.1 %collective-permute-start = (bf16[16,640]{1,0:T(8,128)(2,1)}, bf16[16,640]{1,0:T(8,128)(2,1)S(1)}, u32[]{:S(2)}, u32[]{:S(2)}) collective-permute-start(bf16[16,640]{1,0:T(8,128)(2,1)} %get-tuple-element.27), channel_id=1, source_target_pairs={{0,7},{1,2},{2,1},{3,4},{4,3},{5,6},{6,5},{7,0},{8,15},{9,10},{10,... | collective-permute-start | bytes 61448 | tf_op jit(solution)/shard_map/ppermute | solution.py:65
  9.3 0.7 collective-permute-start.1
  10.0 0.0 collective-permute-start.2
  10.0 1.0 %collective-permute-start.3 = (bf16[16,640]{1,0:T(8,128)(2,1)}, bf16[16,640]{1,0:T(8,128)(2,1)S(1)}, u32[]{:S(2)}, u32[]{:S(2)}) collective-permute-start(bf16[16,640]{1,0:T(8,128)(2,1)} %get-tuple-element.30), channel_id=1, source_target_pairs={{0,8},{8,0},{16,24},{24,16},{1,9},{9,1},{17,25},{25,17},{2,10},{10... | collective-permute-start | bytes 61448 | tf_op jit(solution)/shard_map/ppermute | solution.py:65
  10.9 0.0 copy-done
  10.9 0.0 copy-start.1
  10.9 0.8 %copy-done.1 = f32[64,256]{1,0:T(8,128)S(1)} copy-done((f32[64,256]{1,0:T(8,128)S(1)}, f32[64,256]{1,0:T(8,128)}, u32[]{:S(2)}) %copy-start.1) | copy-done | bytes 65560
  11.8 3.6 %shard_map.105 = (f32[576,256]{1,0:T(8,128)S(1)}, s32[1,10240]{1,0:T(1,128)S(1)}, s32[1,256]{1,0:T(1,128)S(1)}, bf16[64,256]{1,0:T(8,128)(2,1)S(1)}, f32[64,128]{1,0:T(8,128)S(1)}) custom-call(f32[16,8192]{1,0:T(8,128)S(1)} %copy-done, f32[64,256]{1,0:T(8,128)S(1)} %copy-done.1), custom_call_target="tpu_custom_call" | custom-call | tf_op jit(solution)/shard_map/pallas_call | solution.py:369
  15.4 0.0 collective-permute-done.refs_0_
  15.4 0.0 collective-permute-done.1.refs_1_
  15.4 0.0 collective-permute-done.2.refs_2_
  15.4 0.0 collective-permute-done.3.refs_3_
  15.4 1.6 %shard_map.106 = bf16[512,640]{1,0:T(8,128)(2,1)S(1)} custom-call(f32[576,256]{1,0:T(8,128)S(1)} %get-tuple-element.23.sum_ref, s32[1,10240]{1,0:T(1,128)S(1)} %get-tuple-element.24.code_ref, s32[1,256]{1,0:T(1,128)S(1)} %get-tuple-element.25.slot_ref, bf16[64,256]{1,0:T(8,128)(2,1)S(1)} %get-tuple-element.26.mark_ref, f32[64,256]{1,0:T(8,128)S(1)} %copy-done.1, ...), custom_call_target="tpu_custom_call" | custom-call | tf_op jit(solution)/shard_map/pallas_call | solution.py:369
  17.1 21.1 %all_to_all.10 = bf16[32,16,640]{2,1,0:T(8,128)(2,1)S(1)} all-to-all(bf16[32,16,640]{2,1,0:T(8,128)(2,1)S(1)} %bitcast.10), channel_id=1, replica_groups=mesh['gx'=4,'gy'=8] {'gx','gy'}, dimensions={0} | all-to-all | bytes 1310720 | tf_op jit(solution)/shard_map/all_to_all | solution.py:427
  38.1 0.6 shard_map.107
  38.8 1.7 %collective-permute-start.4 = (bf16[16,576]{1,0:T(8,128)(2,1)S(1)}, bf16[16,576]{1,0:T(8,128)(2,1)S(1)}, u32[]{:S(2)}, u32[]{:S(2)}) collective-permute-start(bf16[16,576]{1,0:T(8,128)(2,1)S(1)} %get-tuple-element.32), channel_id=1, source_target_pairs={{0,7},{1,2},{2,1},{3,4},{4,3},{5,6},{6,5},{7,0},{8,15},{9,10},{10,... | collective-permute-start | bytes 55304 | tf_op jit(solution)/shard_map/ppermute | solution.py:65
  40.5 0.4 collective-permute-start.5
  40.9 4.4 %collective-permute-done.4.yb_ref = bf16[16,576]{1,0:T(8,128)(2,1)S(1)} collective-permute-done((bf16[16,576]{1,0:T(8,128)(2,1)S(1)}, bf16[16,576]{1,0:T(8,128)(2,1)S(1)}, u32[]{:S(2)}, u32[]{:S(2)}) %collective-permute-start.4) | collective-permute-done | bytes 18464 | tf_op jit(solution)/shard_map/ppermute | solution.py:65
  45.3 0.0 collective-permute-done.5.ya_ref
  45.3 0.2 shard_map.108
  45.5 0.1 collective-permute-start.6
  45.6 0.6 collective-permute-start.7
  46.3 2.5 %collective-permute-done.6.xb_ref = bf16[16,576]{1,0:T(8,128)(2,1)S(1)} collective-permute-done((bf16[16,576]{1,0:T(8,128)(2,1)S(1)}, bf16[16,576]{1,0:T(8,128)(2,1)S(1)}, u32[]{:S(2)}, u32[]{:S(2)}) %collective-permute-start.6) | collective-permute-done | bytes 18464 | tf_op jit(solution)/shard_map/ppermute | solution.py:65
  48.8 0.0 collective-permute-done.7.xa_ref
  48.8 0.7 shard_map.109
  49.5 0.0 copy-start.2
  49.5 18.7 %all_to_all.11 = bf16[32,16,512]{2,1,0:T(8,128)(2,1)S(1)} all-to-all(bf16[32,16,512]{2,1,0:T(8,128)(2,1)S(1)} %bitcast.12), channel_id=1, replica_groups=mesh['gx'=4,'gy'=8] {'gx','gy'}, dimensions={0} | all-to-all | bytes 1048576 | tf_op jit(solution)/shard_map/all_to_all | solution.py:440
  68.3 0.0 copy-done.2
  68.3 4.0 %shard_map.110 = (f32[8,10240]{1,0:T(8,128)}, bf16[8,8,8,128]{3,2,1,0:T(8,128)(2,1)}) custom-call(bf16[512,512]{1,0:T(8,128)(2,1)S(1)} %bitcast.11, s32[1,256]{1,0:T(1,128)S(1)} %get-tuple-element.25.slot_ref, s32[1,10240]{1,0:T(1,128)S(1)} %get-tuple-element.24.code_ref, f32[16,8192]{1,0:T(8,128)S(1)} %copy-done, f32[64,256]{1,0:T(8,128)S(1)} %copy-done.2, ...), custom_call_target="tpu_custom_call" | custom-call | tf_op jit(solution)/shard_map/pallas_call | solution.py:369
  (1 shorter events, 0.0 us)
Async XLA Ops:
  0.6 10.3 %copy-start = (f32[16,8192]{1,0:T(8,128)S(1)}, f32[16,8192]{1,0:T(8,128)}, u32[]{:S(2)}) copy-start(f32[16,8192]{1,0:T(8,128)} %part_ref.3) | copy-start | bytes 1572868
  3.3 12.1 %collective-permute-start = (bf16[16,640]{1,0:T(8,128)(2,1)}, bf16[16,640]{1,0:T(8,128)(2,1)S(1)}, u32[]{:S(2)}, u32[]{:S(2)}) collective-permute-start(bf16[16,640]{1,0:T(8,128)(2,1)} %get-tuple-element.27), channel_id=1, source_target_pairs={{0,7},{1,2},{2,1},{3,4},{4,3},{5,6},{6,5},{7,0},{8,15},{9,10},{10,... | collective-permute-start | bytes 61448 | tf_op jit(solution)/shard_map/ppermute | solution.py:65
  9.3 6.1 %collective-permute-start.1 = (bf16[16,640]{1,0:T(8,128)(2,1)}, bf16[16,640]{1,0:T(8,128)(2,1)S(1)}, u32[]{:S(2)}, u32[]{:S(2)}) collective-permute-start(bf16[16,640]{1,0:T(8,128)(2,1)} %get-tuple-element.28), channel_id=1, source_target_pairs={{0,24},{8,16},{16,8},{24,0},{1,25},{9,17},{17,9},{25,1},{2,26},{10... | collective-permute-start | bytes 61448 | tf_op jit(solution)/shard_map/ppermute | solution.py:65
  10.0 5.4 %collective-permute-start.2 = (bf16[16,640]{1,0:T(8,128)(2,1)}, bf16[16,640]{1,0:T(8,128)(2,1)S(1)}, u32[]{:S(2)}, u32[]{:S(2)}) collective-permute-start(bf16[16,640]{1,0:T(8,128)(2,1)} %get-tuple-element.29), channel_id=1, source_target_pairs={{0,1},{1,0},{2,3},{3,2},{4,5},{5,4},{6,7},{7,6},{8,9},{9,8},{10,11... | collective-permute-start | bytes 61448 | tf_op jit(solution)/shard_map/ppermute | solution.py:65
  10.0 5.4 %collective-permute-start.3 = (bf16[16,640]{1,0:T(8,128)(2,1)}, bf16[16,640]{1,0:T(8,128)(2,1)S(1)}, u32[]{:S(2)}, u32[]{:S(2)}) collective-permute-start(bf16[16,640]{1,0:T(8,128)(2,1)} %get-tuple-element.30), channel_id=1, source_target_pairs={{0,8},{8,0},{16,24},{24,16},{1,9},{9,1},{17,25},{25,17},{2,10},{10... | collective-permute-start | bytes 61448 | tf_op jit(solution)/shard_map/ppermute | solution.py:65
  10.9 0.8 %copy-start.1 = (f32[64,256]{1,0:T(8,128)S(1)}, f32[64,256]{1,0:T(8,128)}, u32[]{:S(2)}) copy-start(f32[64,256]{1,0:T(8,128)} %get-tuple-element.22.small_ref) | copy-start | bytes 196612
  38.8 6.5 %collective-permute-start.4 = (bf16[16,576]{1,0:T(8,128)(2,1)S(1)}, bf16[16,576]{1,0:T(8,128)(2,1)S(1)}, u32[]{:S(2)}, u32[]{:S(2)}) collective-permute-start(bf16[16,576]{1,0:T(8,128)(2,1)S(1)} %get-tuple-element.32), channel_id=1, source_target_pairs={{0,7},{1,2},{2,1},{3,4},{4,3},{5,6},{6,5},{7,0},{8,15},{9,10},{10,... | collective-permute-start | bytes 55304 | tf_op jit(solution)/shard_map/ppermute | solution.py:65
  40.5 4.8 %collective-permute-start.5 = (bf16[16,576]{1,0:T(8,128)(2,1)S(1)}, bf16[16,576]{1,0:T(8,128)(2,1)S(1)}, u32[]{:S(2)}, u32[]{:S(2)}) collective-permute-start(bf16[16,576]{1,0:T(8,128)(2,1)S(1)} %get-tuple-element.33), channel_id=1, source_target_pairs={{0,1},{1,0},{2,3},{3,2},{4,5},{5,4},{6,7},{7,6},{8,9},{9,8},{10,11... | collective-permute-start | bytes 55304 | tf_op jit(solution)/shard_map/ppermute | solution.py:65
  45.5 3.3 %collective-permute-start.6 = (bf16[16,576]{1,0:T(8,128)(2,1)S(1)}, bf16[16,576]{1,0:T(8,128)(2,1)S(1)}, u32[]{:S(2)}, u32[]{:S(2)}) collective-permute-start(bf16[16,576]{1,0:T(8,128)(2,1)S(1)} %get-tuple-element.35), channel_id=1, source_target_pairs={{0,24},{8,16},{16,8},{24,0},{1,25},{9,17},{17,9},{25,1},{2,26},{10... | collective-permute-start | bytes 55304 | tf_op jit(solution)/shard_map/ppermute | solution.py:65
  45.6 3.2 %collective-permute-start.7 = (bf16[16,576]{1,0:T(8,128)(2,1)S(1)}, bf16[16,576]{1,0:T(8,128)(2,1)S(1)}, u32[]{:S(2)}, u32[]{:S(2)}) collective-permute-start(bf16[16,576]{1,0:T(8,128)(2,1)S(1)} %get-tuple-element.36), channel_id=1, source_target_pairs={{0,8},{8,0},{16,24},{24,16},{1,9},{9,1},{17,25},{25,17},{2,10},{10... | collective-permute-start | bytes 55304 | tf_op jit(solution)/shard_map/ppermute | solution.py:65
  49.5 18.7 %copy-start.2 = (f32[64,256]{1,0:T(8,128)S(1)}, f32[64,256]{1,0:T(8,128)}, u32[]{:S(2)}) copy-start(f32[64,256]{1,0:T(8,128)} %get-tuple-element.22.small_ref) | copy-start | bytes 196612

commit v14 on v8

--- a/solution.py
+++ b/solution.py
@@ -7,6 +7,7 @@
 from jax.experimental.pallas import tpu as pltpu
 from jax.sharding import PartitionSpec as P
 
+FREE = 32.0
 TILE = 64
 FX = 8
 FY = 8
@@ -132,17 +133,14 @@
     table = jnp.concatenate(
         [part_ref[:, g * GROUP : (g + 1) * GROUP].astype(jnp.bfloat16) for g in range(groups)], axis=0
     )
-    live = jnp.where(leave < parts, 1.0, 0.0)
+    free = jnp.where(iota((channels, migr), 0) == 0, FREE, 0.0)
     for r in range(4):
         where = slice(r * migr, (r + 1) * migr)
         found = dot(table, low[:, where])
-        picked = jnp.zeros((channels, migr), jnp.float32)
+        picked = free
         for g in range(groups):
             picked = jnp.where(high[:, where] == g, found[g * channels : (g + 1) * channels], picked)
-        out_ref[r, :, :migr] = picked.astype(jnp.bfloat16)
-        flags = [live[:, k : k + LANES] for k in range(r * migr, (r + 1) * migr, LANES)]
-        flags.append(jnp.zeros((channels - len(flags), LANES), jnp.float32))
-        out_ref[r, :, migr:] = jnp.concatenate(flags, axis=0).astype(jnp.bfloat16)
+        out_ref[r] = picked.astype(jnp.bfloat16)
         stores.append(pltpu.make_async_copy(out_ref.at[r], out_hbm[r], out_sems.at[r]))
         stores[-1].start()
     for store in stores:
@@ -236,9 +234,9 @@
     state_refs, out_ref = refs[:4], refs[4]
     channels, tiles = state_refs[0].shape[0], slot_ref.shape[1]
     closure = small_ref[rows : 2 * rows, :channels]
-    migr = state_refs[0].shape[1] - LANES
-    code = code_ref[:, code_ref.shape[1] - 4 * migr :]
-    state = jnp.concatenate([block[:, :migr] for block in arrived_blocks(state_refs)], axis=1)
+    code = code_ref[:, code_ref.shape[1] - 4 * state_refs[0].shape[1] :]
+    state = jnp.concatenate(arrived_blocks(state_refs), axis=1)
+    state = jnp.where(state[0:1] < FREE, state, 0.0)
     mixed, first = mix(closure, state)
     total = sum_ref[...] + dot(spread(mixed, first, code % TILE), ones(equal(tiles, code // TILE)), NT)
     table = jnp.concatenate([total.astype(jnp.bfloat16), mark_ref[...]], axis=0)
@@ -358,8 +356,8 @@
     drag = look(code_ref[:, parts:])
     for row, arrived in enumerate(arrived_blocks(state_refs)):
         begin = parts + row * migr
-        live = jnp.concatenate([arrived[k : k + 1, migr:] for k in range(migr // LANES)], axis=1)
-        force = drag[:, row * migr : (row + 1) * migr] - damping * arrived[:rows, :migr]
+        live = jnp.where(arrived[0:1] < FREE, 1.0, 0.0)
+        force = drag[:, row * migr : (row + 1) * migr] - damping * arrived[:rows]
         out_ref[:, begin : begin + migr] = live * force
     store(slice(parts, slots))
     for copy in stores:
@@ -408,10 +406,10 @@
     )
     *leaving, small = call(
         pick_kernel,
-        [shape((channels, migr + LANES), bf16)] * 4 + [shape((small_count, GROUP), f32)],
+        [shape((channels, migr), bf16)] * 4 + [shape((small_count, GROUP), f32)],
         *operands, limit=LARGE,
         scratch=[(pltpu.SMEM if i == 2 else pltpu.VMEM)(x.shape, x.dtype) for i, x in enumerate(operands)]
-        + [pltpu.VMEM((4, channels, migr + LANES), bf16), pltpu.VMEM((small_count, GROUP), f32),
+        + [pltpu.VMEM((4, channels, migr), bf16), pltpu.VMEM((small_count, GROUP), f32),
            pltpu.SemaphoreType.DMA((9,)), pltpu.SemaphoreType.DMA((5,))],
     )
     (xa, xb), (ya, yb) = exchange(*leaving[:2], "gx"), exchange(*leaving[2:], "gy")

time: 72.5 us -> 72.4 us (level)
  no operation moved by 1% of the time
where the time goes in v14:
time: 72.4 us; the launch traced here: 72.2 us
  blocking collectives  39.6 us (55%)
  Pallas kernels  13.4 us (19%)
  starting transfers between devices  10.5 us (15%)
  waiting for transfers between devices  7.11 us (10%)
  local copies, waits for them, and re-layouts  0.86 us (1%)
    all_to_all x1, blocking collectives, per_device(): lax.all_to_all(payload.reshape(devices, capacity, lanes), ('gx', 'gy'), s...  21.1 us
    all_to_all x1, blocking collectives, per_device(): lax.all_to_all(back.reshape(devices, capacity, rows * TILE), ('gx', 'gy')...  18.5 us
    pallas_call x7, Pallas kernels, call(): pl.pallas_call(kernel, out_shape=shapes, in_specs=[hbm if limit else vmem...  13.4 us
    ppermute x8, starting transfers between devices, exchange(): blocks[odd] = lax.ppermute(block, axis, pairs)  10.5 us
    ppermute x8, waiting for transfers between devices, exchange(): blocks[odd] = lax.ppermute(block, axis, pairs)  7.11 us
  transfers between devices with their start and end apart: 8, of which 2 were waited for; matrix products, arithmetic and copies ran while one was open for 0% of the time, Pallas kernels for 5%

profile of v14, /device:TPU:0, one launch (start us, length us, event | category | flops | bytes accessed | tf_op | source)
XLA Modules:
  0.0 72.2 jit_solution(5788895410917574700)
XLA Ops:
  0.6 0.0 copy-start
  0.6 2.6 %shard_map.104 = (bf16[16,512]{1,0:T(8,128)(2,1)}, bf16[16,512]{1,0:T(8,128)(2,1)}, bf16[16,512]{1,0:T(8,128)(2,1)}, bf16[16,512]{1,0:T(8,128)(2,1)}, f32[64,256]{1,0:T(8,128)}) custom-call(f32[16,8192]{1,0:T(8,128)} %part_ref.3, s32[4,512]{1,0:T(4,128)} %index_hbm.1, s32[1,4]{1,0:T(1,128)} %count_hbm.1, s32[1,256]{1,0:T(1,128)} %size_hbm.1, ...), custom_call_target="tpu_custom_call" | custom-call | tf_op jit(solution)/shard_map/pallas_call | solution.py:369
  3.3 6.1 %collective-permute-start = (bf16[16,512]{1,0:T(8,128)(2,1)}, bf16[16,512]{1,0:T(8,128)(2,1)S(1)}, u32[]{:S(2)}, u32[]{:S(2)}) collective-permute-start(bf16[16,512]{1,0:T(8,128)(2,1)} %get-tuple-element.27), channel_id=1, source_target_pairs={{0,7},{1,2},{2,1},{3,4},{4,3},{5,6},{6,5},{7,0},{8,15},{9,10},{10,... | collective-permute-start | bytes 49160 | tf_op jit(solution)/shard_map/ppermute | solution.py:66
  9.3 0.7 collective-permute-start.1
  10.0 0.0 collective-permute-start.2
  10.0 1.0 %collective-permute-start.3 = (bf16[16,512]{1,0:T(8,128)(2,1)}, bf16[16,512]{1,0:T(8,128)(2,1)S(1)}, u32[]{:S(2)}, u32[]{:S(2)}) collective-permute-start(bf16[16,512]{1,0:T(8,128)(2,1)} %get-tuple-element.30), channel_id=1, source_target_pairs={{0,8},{8,0},{16,24},{24,16},{1,9},{9,1},{17,25},{25,17},{2,10},{10... | collective-permute-start | bytes 49160 | tf_op jit(solution)/shard_map/ppermute | solution.py:66
  10.9 0.0 copy-done
  10.9 0.0 copy-start.1
  10.9 0.8 %copy-done.1 = f32[64,256]{1,0:T(8,128)S(1)} copy-done((f32[64,256]{1,0:T(8,128)S(1)}, f32[64,256]{1,0:T(8,128)}, u32[]{:S(2)}) %copy-start.1) | copy-done | bytes 65560
  11.8 3.6 %shard_map.105 = (f32[576,256]{1,0:T(8,128)S(1)}, s32[1,10240]{1,0:T(1,128)S(1)}, s32[1,256]{1,0:T(1,128)S(1)}, bf16[64,256]{1,0:T(8,128)(2,1)S(1)}, f32[64,128]{1,0:T(8,128)S(1)}) custom-call(f32[16,8192]{1,0:T(8,128)S(1)} %copy-done, f32[64,256]{1,0:T(8,128)S(1)} %copy-done.1), custom_call_target="tpu_custom_call" | custom-call | tf_op jit(solution)/shard_map/pallas_call | solution.py:369
  15.4 0.0 collective-permute-done.refs_0_
  15.4 0.0 collective-permute-done.1.refs_1_
  15.4 0.0 collective-permute-done.2.refs_2_
  15.4 0.0 collective-permute-done.3.refs_3_
  15.4 1.6 %shard_map.106 = bf16[512,640]{1,0:T(8,128)(2,1)S(1)} custom-call(f32[576,256]{1,0:T(8,128)S(1)} %get-tuple-element.23.sum_ref, s32[1,10240]{1,0:T(1,128)S(1)} %get-tuple-element.24.code_ref, s32[1,256]{1,0:T(1,128)S(1)} %get-tuple-element.25.slot_ref, bf16[64,256]{1,0:T(8,128)(2,1)S(1)} %get-tuple-element.26.mark_ref, f32[64,256]{1,0:T(8,128)S(1)} %copy-done.1, ...), custom_call_target="tpu_custom_call" | custom-call | tf_op jit(solution)/shard_map/pallas_call | solution.py:369
  17.1 21.1 %all_to_all.10 = bf16[32,16,640]{2,1,0:T(8,128)(2,1)S(1)} all-to-all(bf16[32,16,640]{2,1,0:T(8,128)(2,1)S(1)} %bitcast.10), channel_id=1, replica_groups=mesh['gx'=4,'gy'=8] {'gx','gy'}, dimensions={0} | all-to-all | bytes 1310720 | tf_op jit(solution)/shard_map/all_to_all | solution.py:427
  38.1 0.6 shard_map.107
  38.8 0.5 collective-permute-start.4
  39.3 0.2 collective-permute-start.5
  39.5 2.6 %collective-permute-done.4.xb_ref = bf16[16,576]{1,0:T(8,128)(2,1)S(1)} collective-permute-done((bf16[16,576]{1,0:T(8,128)(2,1)S(1)}, bf16[16,576]{1,0:T(8,128)(2,1)S(1)}, u32[]{:S(2)}, u32[]{:S(2)}) %collective-permute-start.4) | collective-permute-done | bytes 18464 | tf_op jit(solution)/shard_map/ppermute | solution.py:66
  42.1 0.0 collective-permute-done.5.xa_ref
  42.1 0.2 shard_map.108
  42.3 1.7 %collective-permute-start.6 = (bf16[16,576]{1,0:T(8,128)(2,1)S(1)}, bf16[16,576]{1,0:T(8,128)(2,1)S(1)}, u32[]{:S(2)}, u32[]{:S(2)}) collective-permute-start(bf16[16,576]{1,0:T(8,128)(2,1)S(1)} %get-tuple-element.35), channel_id=1, source_target_pairs={{0,7},{1,2},{2,1},{3,4},{4,3},{5,6},{6,5},{7,0},{8,15},{9,10},{10,... | collective-permute-start | bytes 55304 | tf_op jit(solution)/shard_map/ppermute | solution.py:66
  44.0 0.4 collective-permute-start.7
  44.4 4.5 %collective-permute-done.6.yb_ref = bf16[16,576]{1,0:T(8,128)(2,1)S(1)} collective-permute-done((bf16[16,576]{1,0:T(8,128)(2,1)S(1)}, bf16[16,576]{1,0:T(8,128)(2,1)S(1)}, u32[]{:S(2)}, u32[]{:S(2)}) %collective-permute-start.6) | collective-permute-done | bytes 18464 | tf_op jit(solution)/shard_map/ppermute | solution.py:66
  48.8 0.0 collective-permute-done.7.ya_ref
  48.8 0.8 %shard_map.109 = (bf16[8,8,8,128]{3,2,1,0:T(8,128)(2,1)S(1)}, bf16[512,512]{1,0:T(8,128)(2,1)S(1)}) custom-call(bf16[512,128]{1,0:T(8,128)(2,1)S(1)} %slice.4.mark_ref, f32[64,1152]{1,0:T(8,128)S(1)} %get-tuple-element.34.along_ref, bf16[16,576]{1,0:T(8,128)(2,1)S(1)} %collective-permute-done.6.yb_ref, bf16[16,576]{1,0:T(8,128)(2,1)S(1)} %collective-permute-done.7.ya_ref), custom_call_target="tpu_custom_call" | custom-call | tf_op jit(solution)/shard_map/pallas_call | solution.py:369
  49.6 0.0 copy-start.2
  49.6 18.5 %all_to_all.11 = bf16[32,16,512]{2,1,0:T(8,128)(2,1)S(1)} all-to-all(bf16[32,16,512]{2,1,0:T(8,128)(2,1)S(1)} %bitcast.12), channel_id=1, replica_groups=mesh['gx'=4,'gy'=8] {'gx','gy'}, dimensions={0} | all-to-all | bytes 1048576 | tf_op jit(solution)/shard_map/all_to_all | solution.py:440
  68.2 0.0 copy-done.2
  68.2 4.0 %shard_map.110 = (f32[8,10240]{1,0:T(8,128)}, bf16[8,8,8,128]{3,2,1,0:T(8,128)(2,1)}) custom-call(bf16[512,512]{1,0:T(8,128)(2,1)S(1)} %bitcast.11, s32[1,256]{1,0:T(1,128)S(1)} %get-tuple-element.25.slot_ref, s32[1,10240]{1,0:T(1,128)S(1)} %get-tuple-element.24.code_ref, f32[16,8192]{1,0:T(8,128)S(1)} %copy-done, f32[64,256]{1,0:T(8,128)S(1)} %copy-done.2, ...), custom_call_target="tpu_custom_call" | custom-call | tf_op jit(solution)/shard_map/pallas_call | solution.py:369
  (1 shorter events, 0.0 us)
Async XLA Ops:
  0.6 10.3 %copy-start = (f32[16,8192]{1,0:T(8,128)S(1)}, f32[16,8192]{1,0:T(8,128)}, u32[]{:S(2)}) copy-start(f32[16,8192]{1,0:T(8,128)} %part_ref.3) | copy-start | bytes 1572868
  3.3 12.1 %collective-permute-start = (bf16[16,512]{1,0:T(8,128)(2,1)}, bf16[16,512]{1,0:T(8,128)(2,1)S(1)}, u32[]{:S(2)}, u32[]{:S(2)}) collective-permute-start(bf16[16,512]{1,0:T(8,128)(2,1)} %get-tuple-element.27), channel_id=1, source_target_pairs={{0,7},{1,2},{2,1},{3,4},{4,3},{5,6},{6,5},{7,0},{8,15},{9,10},{10,... | collective-permute-start | bytes 49160 | tf_op jit(solution)/shard_map/ppermute | solution.py:66
  9.3 6.1 %collective-permute-start.1 = (bf16[16,512]{1,0:T(8,128)(2,1)}, bf16[16,512]{1,0:T(8,128)(2,1)S(1)}, u32[]{:S(2)}, u32[]{:S(2)}) collective-permute-start(bf16[16,512]{1,0:T(8,128)(2,1)} %get-tuple-element.28), channel_id=1, source_target_pairs={{0,24},{8,16},{16,8},{24,0},{1,25},{9,17},{17,9},{25,1},{2,26},{10... | collective-permute-start | bytes 49160 | tf_op jit(solution)/shard_map/ppermute | solution.py:66
  10.0 5.4 %collective-permute-start.2 = (bf16[16,512]{1,0:T(8,128)(2,1)}, bf16[16,512]{1,0:T(8,128)(2,1)S(1)}, u32[]{:S(2)}, u32[]{:S(2)}) collective-permute-start(bf16[16,512]{1,0:T(8,128)(2,1)} %get-tuple-element.29), channel_id=1, source_target_pairs={{0,1},{1,0},{2,3},{3,2},{4,5},{5,4},{6,7},{7,6},{8,9},{9,8},{10,11... | collective-permute-start | bytes 49160 | tf_op jit(solution)/shard_map/ppermute | solution.py:66
  10.0 5.5 %collective-permute-start.3 = (bf16[16,512]{1,0:T(8,128)(2,1)}, bf16[16,512]{1,0:T(8,128)(2,1)S(1)}, u32[]{:S(2)}, u32[]{:S(2)}) collective-permute-start(bf16[16,512]{1,0:T(8,128)(2,1)} %get-tuple-element.30), channel_id=1, source_target_pairs={{0,8},{8,0},{16,24},{24,16},{1,9},{9,1},{17,25},{25,17},{2,10},{10... | collective-permute-start | bytes 49160 | tf_op jit(solution)/shard_map/ppermute | solution.py:66
  10.9 0.8 %copy-start.1 = (f32[64,256]{1,0:T(8,128)S(1)}, f32[64,256]{1,0:T(8,128)}, u32[]{:S(2)}) copy-start(f32[64,256]{1,0:T(8,128)} %get-tuple-element.22.small_ref) | copy-start | bytes 196612
  38.8 3.3 %collective-permute-start.4 = (bf16[16,576]{1,0:T(8,128)(2,1)S(1)}, bf16[16,576]{1,0:T(8,128)(2,1)S(1)}, u32[]{:S(2)}, u32[]{:S(2)}) collective-permute-start(bf16[16,576]{1,0:T(8,128)(2,1)S(1)} %get-tuple-element.32), channel_id=1, source_target_pairs={{0,24},{8,16},{16,8},{24,0},{1,25},{9,17},{17,9},{25,1},{2,26},{10... | collective-permute-start | bytes 55304 | tf_op jit(solution)/shard_map/ppermute | solution.py:66
  39.3 2.8 %collective-permute-start.5 = (bf16[16,576]{1,0:T(8,128)(2,1)S(1)}, bf16[16,576]{1,0:T(8,128)(2,1)S(1)}, u32[]{:S(2)}, u32[]{:S(2)}) collective-permute-start(bf16[16,576]{1,0:T(8,128)(2,1)S(1)} %get-tuple-element.33), channel_id=1, source_target_pairs={{0,8},{8,0},{16,24},{24,16},{1,9},{9,1},{17,25},{25,17},{2,10},{10... | collective-permute-start | bytes 55304 | tf_op jit(solution)/shard_map/ppermute | solution.py:66
  42.3 6.5 %collective-permute-start.6 = (bf16[16,576]{1,0:T(8,128)(2,1)S(1)}, bf16[16,576]{1,0:T(8,128)(2,1)S(1)}, u32[]{:S(2)}, u32[]{:S(2)}) collective-permute-start(bf16[16,576]{1,0:T(8,128)(2,1)S(1)} %get-tuple-element.35), channel_id=1, source_target_pairs={{0,7},{1,2},{2,1},{3,4},{4,3},{5,6},{6,5},{7,0},{8,15},{9,10},{10,... | collective-permute-start | bytes 55304 | tf_op jit(solution)/shard_map/ppermute | solution.py:66
  44.0 4.9 %collective-permute-start.7 = (bf16[16,576]{1,0:T(8,128)(2,1)S(1)}, bf16[16,576]{1,0:T(8,128)(2,1)S(1)}, u32[]{:S(2)}, u32[]{:S(2)}) collective-permute-start(bf16[16,576]{1,0:T(8,128)(2,1)S(1)} %get-tuple-element.36), channel_id=1, source_target_pairs={{0,1},{1,0},{2,3},{3,2},{4,5},{5,4},{6,7},{7,6},{8,9},{9,8},{10,11... | collective-permute-start | bytes 55304 | tf_op jit(solution)/shard_map/ppermute | solution.py:66
  49.6 18.6 %copy-start.2 = (f32[64,256]{1,0:T(8,128)S(1)}, f32[64,256]{1,0:T(8,128)}, u32[]{:S(2)}) copy-start(f32[64,256]{1,0:T(8,128)} %get-tuple-element.22.small_ref) | copy-start | bytes 196612

commit v15 on v14

--- a/solution.py
+++ b/solution.py
@@ -309,7 +309,7 @@
         both = jnp.concatenate([halves[0][:, where], halves[1][:, where]], axis=1)
         drag_ref[r] = both.reshape(FX, FY, FZ).astype(jnp.bfloat16)
     mark = width % LANES
-    marks = mark_ref[...].astype(jnp.float32)
+    marks = mark_ref[:, mark_ref.shape[1] - LANES :].astype(jnp.float32)
     column, height = marks[:, mark : mark + 1], marks[:, mark + 1 : mark + 2]
     hot = one_hot(column == iota((1, COLS), 1).astype(jnp.float32))
     place = (iota((1, lanes), 1) % TILE).astype(jnp.float32)
@@ -435,7 +435,7 @@
     drag, back = call(
         drag_kernel,
         [shape((rows, FX, FY, FZ), bf16), shape((count, rows * TILE), bf16)],
-        received[:, lanes - LANES :], along, yb, ya,
+        received, along, yb, ya,
     )
     returned = lax.all_to_all(
         back.reshape(devices, capacity, rows * TILE), ("gx", "gy"), split_axis=0, concat_axis=0, tiled=True

time: 72.4 us -> 72.4 us (level)
  no operation moved by 1% of the time
where the time goes in v15:
time: 72.4 us; the launch traced here: 72.2 us
  blocking collectives  39.6 us (55%)
  Pallas kernels  13.4 us (19%)
  starting transfers between devices  10.5 us (15%)
  waiting for transfers between devices  7.12 us (10%)
  local copies, waits for them, and re-layouts  0.85 us (1%)
    all_to_all x1, blocking collectives, per_device(): lax.all_to_all(payload.reshape(devices, capacity, lanes), ('gx', 'gy'), s...  21.1 us
    all_to_all x1, blocking collectives, per_device(): lax.all_to_all(back.reshape(devices, capacity, rows * TILE), ('gx', 'gy')...  18.5 us
    pallas_call x7, Pallas kernels, call(): pl.pallas_call(kernel, out_shape=shapes, in_specs=[hbm if limit else vmem...  13.4 us
    ppermute x8, starting transfers between devices, exchange(): blocks[odd] = lax.ppermute(block, axis, pairs)  10.5 us
    ppermute x8, waiting for transfers between devices, exchange(): blocks[odd] = lax.ppermute(block, axis, pairs)  7.12 us
  transfers between devices with their start and end apart: 8, of which 2 were waited for; matrix products, arithmetic and copies ran while one was open for 0% of the time, Pallas kernels for 5%

profile of v15, /device:TPU:0, one launch (start us, length us, event | category | flops | bytes accessed | tf_op | source)
XLA Modules:
  0.0 72.2 jit_solution(3908065247178768435)
XLA Ops:
  0.6 0.0 copy-start
  0.6 2.6 %shard_map.104 = (bf16[16,512]{1,0:T(8,128)(2,1)}, bf16[16,512]{1,0:T(8,128)(2,1)}, bf16[16,512]{1,0:T(8,128)(2,1)}, bf16[16,512]{1,0:T(8,128)(2,1)}, f32[64,256]{1,0:T(8,128)}) custom-call(f32[16,8192]{1,0:T(8,128)} %part_ref.3, s32[4,512]{1,0:T(4,128)} %index_hbm.1, s32[1,4]{1,0:T(1,128)} %count_hbm.1, s32[1,256]{1,0:T(1,128)} %size_hbm.1, ...), custom_call_target="tpu_custom_call" | custom-call | tf_op jit(solution)/shard_map/pallas_call | solution.py:369
  3.3 6.1 %collective-permute-start = (bf16[16,512]{1,0:T(8,128)(2,1)}, bf16[16,512]{1,0:T(8,128)(2,1)S(1)}, u32[]{:S(2)}, u32[]{:S(2)}) collective-permute-start(bf16[16,512]{1,0:T(8,128)(2,1)} %get-tuple-element.27), channel_id=1, source_target_pairs={{0,7},{1,2},{2,1},{3,4},{4,3},{5,6},{6,5},{7,0},{8,15},{9,10},{10,... | collective-permute-start | bytes 49160 | tf_op jit(solution)/shard_map/ppermute | solution.py:66
  9.3 0.7 collective-permute-start.1
  10.0 0.0 collective-permute-start.2
  10.0 1.0 %collective-permute-start.3 = (bf16[16,512]{1,0:T(8,128)(2,1)}, bf16[16,512]{1,0:T(8,128)(2,1)S(1)}, u32[]{:S(2)}, u32[]{:S(2)}) collective-permute-start(bf16[16,512]{1,0:T(8,128)(2,1)} %get-tuple-element.30), channel_id=1, source_target_pairs={{0,8},{8,0},{16,24},{24,16},{1,9},{9,1},{17,25},{25,17},{2,10},{10... | collective-permute-start | bytes 49160 | tf_op jit(solution)/shard_map/ppermute | solution.py:66
  10.9 0.0 copy-done
  10.9 0.0 copy-start.1
  10.9 0.8 %copy-done.1 = f32[64,256]{1,0:T(8,128)S(1)} copy-done((f32[64,256]{1,0:T(8,128)S(1)}, f32[64,256]{1,0:T(8,128)}, u32[]{:S(2)}) %copy-start.1) | copy-done | bytes 65560
  11.8 3.6 %shard_map.105 = (f32[576,256]{1,0:T(8,128)S(1)}, s32[1,10240]{1,0:T(1,128)S(1)}, s32[1,256]{1,0:T(1,128)S(1)}, bf16[64,256]{1,0:T(8,128)(2,1)S(1)}, f32[64,128]{1,0:T(8,128)S(1)}) custom-call(f32[16,8192]{1,0:T(8,128)S(1)} %copy-done, f32[64,256]{1,0:T(8,128)S(1)} %copy-done.1), custom_call_target="tpu_custom_call" | custom-call | tf_op jit(solution)/shard_map/pallas_call | solution.py:369
  15.4 0.0 collective-permute-done.refs_0_
  15.4 0.0 collective-permute-done.1.refs_1_
  15.4 0.0 collective-permute-done.2.refs_2_
  15.4 0.0 collective-permute-done.3.refs_3_
  15.4 1.6 %shard_map.106 = bf16[512,640]{1,0:T(8,128)(2,1)S(1)} custom-call(f32[576,256]{1,0:T(8,128)S(1)} %get-tuple-element.23.sum_ref, s32[1,10240]{1,0:T(1,128)S(1)} %get-tuple-element.24.code_ref, s32[1,256]{1,0:T(1,128)S(1)} %get-tuple-element.25.slot_ref, bf16[64,256]{1,0:T(8,128)(2,1)S(1)} %get-tuple-element.26.mark_ref, f32[64,256]{1,0:T(8,128)S(1)} %copy-done.1, ...), custom_call_target="tpu_custom_call" | custom-call | tf_op jit(solution)/shard_map/pallas_call | solution.py:369
  17.1 21.1 %all_to_all.10 = bf16[32,16,640]{2,1,0:T(8,128)(2,1)S(1)} all-to-all(bf16[32,16,640]{2,1,0:T(8,128)(2,1)S(1)} %bitcast.10), channel_id=1, replica_groups=mesh['gx'=4,'gy'=8] {'gx','gy'}, dimensions={0} | all-to-all | bytes 1310720 | tf_op jit(solution)/shard_map/all_to_all | solution.py:427
  38.1 0.6 shard_map.107
  38.8 0.5 collective-permute-start.4
  39.3 0.2 collective-permute-start.5
  39.5 2.6 %collective-permute-done.4.xb_ref = bf16[16,576]{1,0:T(8,128)(2,1)S(1)} collective-permute-done((bf16[16,576]{1,0:T(8,128)(2,1)S(1)}, bf16[16,576]{1,0:T(8,128)(2,1)S(1)}, u32[]{:S(2)}, u32[]{:S(2)}) %collective-permute-start.4) | collective-permute-done | bytes 18464 | tf_op jit(solution)/shard_map/ppermute | solution.py:66
  42.1 0.0 collective-permute-done.5.xa_ref
  42.1 0.2 shard_map.108
  42.3 1.7 %collective-permute-start.6 = (bf16[16,576]{1,0:T(8,128)(2,1)S(1)}, bf16[16,576]{1,0:T(8,128)(2,1)S(1)}, u32[]{:S(2)}, u32[]{:S(2)}) collective-permute-start(bf16[16,576]{1,0:T(8,128)(2,1)S(1)} %get-tuple-element.35), channel_id=1, source_target_pairs={{0,7},{1,2},{2,1},{3,4},{4,3},{5,6},{6,5},{7,0},{8,15},{9,10},{10,... | collective-permute-start | bytes 55304 | tf_op jit(solution)/shard_map/ppermute | solution.py:66
  44.0 0.4 collective-permute-start.7
  44.4 4.5 %collective-permute-done.6.yb_ref = bf16[16,576]{1,0:T(8,128)(2,1)S(1)} collective-permute-done((bf16[16,576]{1,0:T(8,128)(2,1)S(1)}, bf16[16,576]{1,0:T(8,128)(2,1)S(1)}, u32[]{:S(2)}, u32[]{:S(2)}) %collective-permute-start.6) | collective-permute-done | bytes 18464 | tf_op jit(solution)/shard_map/ppermute | solution.py:66
  48.8 0.0 collective-permute-done.7.ya_ref
  48.8 0.8 %shard_map.109 = (bf16[8,8,8,128]{3,2,1,0:T(8,128)(2,1)S(1)}, bf16[512,512]{1,0:T(8,128)(2,1)S(1)}) custom-call(bf16[512,640]{1,0:T(8,128)(2,1)S(1)} %bitcast.9, f32[64,1152]{1,0:T(8,128)S(1)} %get-tuple-element.34.along_ref, bf16[16,576]{1,0:T(8,128)(2,1)S(1)} %collective-permute-done.6.yb_ref, bf16[16,576]{1,0:T(8,128)(2,1)S(1)} %collective-permute-done.7.ya_ref), custom_call_target="tpu_custom_call" | custom-call | tf_op jit(solution)/shard_map/pallas_call | solution.py:369
  49.6 0.0 copy-start.2
  49.6 18.5 %all_to_all.11 = bf16[32,16,512]{2,1,0:T(8,128)(2,1)S(1)} all-to-all(bf16[32,16,512]{2,1,0:T(8,128)(2,1)S(1)} %bitcast.12), channel_id=1, replica_groups=mesh['gx'=4,'gy'=8] {'gx','gy'}, dimensions={0} | all-to-all | bytes 1048576 | tf_op jit(solution)/shard_map/all_to_all | solution.py:440
  68.2 0.0 copy-done.2
  68.2 4.0 %shard_map.110 = (f32[8,10240]{1,0:T(8,128)}, bf16[8,8,8,128]{3,2,1,0:T(8,128)(2,1)}) custom-call(bf16[512,512]{1,0:T(8,128)(2,1)S(1)} %bitcast.11, s32[1,256]{1,0:T(1,128)S(1)} %get-tuple-element.25.slot_ref, s32[1,10240]{1,0:T(1,128)S(1)} %get-tuple-element.24.code_ref, f32[16,8192]{1,0:T(8,128)S(1)} %copy-done, f32[64,256]{1,0:T(8,128)S(1)} %copy-done.2, ...), custom_call_target="tpu_custom_call" | custom-call | tf_op jit(solution)/shard_map/pallas_call | solution.py:369
Async XLA Ops:
  0.6 10.3 %copy-start = (f32[16,8192]{1,0:T(8,128)S(1)}, f32[16,8192]{1,0:T(8,128)}, u32[]{:S(2)}) copy-start(f32[16,8192]{1,0:T(8,128)} %part_ref.3) | copy-start | bytes 1572868
  3.3 12.1 %collective-permute-start = (bf16[16,512]{1,0:T(8,128)(2,1)}, bf16[16,512]{1,0:T(8,128)(2,1)S(1)}, u32[]{:S(2)}, u32[]{:S(2)}) collective-permute-start(bf16[16,512]{1,0:T(8,128)(2,1)} %get-tuple-element.27), channel_id=1, source_target_pairs={{0,7},{1,2},{2,1},{3,4},{4,3},{5,6},{6,5},{7,0},{8,15},{9,10},{10,... | collective-permute-start | bytes 49160 | tf_op jit(solution)/shard_map/ppermute | solution.py:66
  9.3 6.1 %collective-permute-start.1 = (bf16[16,512]{1,0:T(8,128)(2,1)}, bf16[16,512]{1,0:T(8,128)(2,1)S(1)}, u32[]{:S(2)}, u32[]{:S(2)}) collective-permute-start(bf16[16,512]{1,0:T(8,128)(2,1)} %get-tuple-element.28), channel_id=1, source_target_pairs={{0,24},{8,16},{16,8},{24,0},{1,25},{9,17},{17,9},{25,1},{2,26},{10... | collective-permute-start | bytes 49160 | tf_op jit(solution)/shard_map/ppermute | solution.py:66
  10.0 5.4 %collective-permute-start.2 = (bf16[16,512]{1,0:T(8,128)(2,1)}, bf16[16,512]{1,0:T(8,128)(2,1)S(1)}, u32[]{:S(2)}, u32[]{:S(2)}) collective-permute-start(bf16[16,512]{1,0:T(8,128)(2,1)} %get-tuple-element.29), channel_id=1, source_target_pairs={{0,1},{1,0},{2,3},{3,2},{4,5},{5,4},{6,7},{7,6},{8,9},{9,8},{10,11... | collective-permute-start | bytes 49160 | tf_op jit(solution)/shard_map/ppermute | solution.py:66
  10.0 5.5 %collective-permute-start.3 = (bf16[16,512]{1,0:T(8,128)(2,1)}, bf16[16,512]{1,0:T(8,128)(2,1)S(1)}, u32[]{:S(2)}, u32[]{:S(2)}) collective-permute-start(bf16[16,512]{1,0:T(8,128)(2,1)} %get-tuple-element.30), channel_id=1, source_target_pairs={{0,8},{8,0},{16,24},{24,16},{1,9},{9,1},{17,25},{25,17},{2,10},{10... | collective-permute-start | bytes 49160 | tf_op jit(solution)/shard_map/ppermute | solution.py:66
  10.9 0.8 %copy-start.1 = (f32[64,256]{1,0:T(8,128)S(1)}, f32[64,256]{1,0:T(8,128)}, u32[]{:S(2)}) copy-start(f32[64,256]{1,0:T(8,128)} %get-tuple-element.22.small_ref) | copy-start | bytes 196612
  38.8 3.3 %collective-permute-start.4 = (bf16[16,576]{1,0:T(8,128)(2,1)S(1)}, bf16[16,576]{1,0:T(8,128)(2,1)S(1)}, u32[]{:S(2)}, u32[]{:S(2)}) collective-permute-start(bf16[16,576]{1,0:T(8,128)(2,1)S(1)} %get-tuple-element.32), channel_id=1, source_target_pairs={{0,24},{8,16},{16,8},{24,0},{1,25},{9,17},{17,9},{25,1},{2,26},{10... | collective-permute-start | bytes 55304 | tf_op jit(solution)/shard_map/ppermute | solution.py:66
  39.3 2.8 %collective-permute-start.5 = (bf16[16,576]{1,0:T(8,128)(2,1)S(1)}, bf16[16,576]{1,0:T(8,128)(2,1)S(1)}, u32[]{:S(2)}, u32[]{:S(2)}) collective-permute-start(bf16[16,576]{1,0:T(8,128)(2,1)S(1)} %get-tuple-element.33), channel_id=1, source_target_pairs={{0,8},{8,0},{16,24},{24,16},{1,9},{9,1},{17,25},{25,17},{2,10},{10... | collective-permute-start | bytes 55304 | tf_op jit(solution)/shard_map/ppermute | solution.py:66
  42.3 6.5 %collective-permute-start.6 = (bf16[16,576]{1,0:T(8,128)(2,1)S(1)}, bf16[16,576]{1,0:T(8,128)(2,1)S(1)}, u32[]{:S(2)}, u32[]{:S(2)}) collective-permute-start(bf16[16,576]{1,0:T(8,128)(2,1)S(1)} %get-tuple-element.35), channel_id=1, source_target_pairs={{0,7},{1,2},{2,1},{3,4},{4,3},{5,6},{6,5},{7,0},{8,15},{9,10},{10,... | collective-permute-start | bytes 55304 | tf_op jit(solution)/shard_map/ppermute | solution.py:66
  44.0 4.9 %collective-permute-start.7 = (bf16[16,576]{1,0:T(8,128)(2,1)S(1)}, bf16[16,576]{1,0:T(8,128)(2,1)S(1)}, u32[]{:S(2)}, u32[]{:S(2)}) collective-permute-start(bf16[16,576]{1,0:T(8,128)(2,1)S(1)} %get-tuple-element.36), channel_id=1, source_target_pairs={{0,1},{1,0},{2,3},{3,2},{4,5},{5,4},{6,7},{7,6},{8,9},{9,8},{10,11... | collective-permute-start | bytes 55304 | tf_op jit(solution)/shard_map/ppermute | solution.py:66
  49.6 18.6 %copy-start.2 = (f32[64,256]{1,0:T(8,128)S(1)}, f32[64,256]{1,0:T(8,128)}, u32[]{:S(2)}) copy-start(f32[64,256]{1,0:T(8,128)} %get-tuple-element.22.small_ref) | copy-start | bytes 196612
